TPU v7x, 32 devices: a whole 2x2x4 slice. The times are simulated.
32 devices in a mesh: rep: 4 (over y, x), fsdp: 8 (over z, core).
Axes of the slice: x: 2, y: 2, z: 4, core: 2. Of those that a mesh axis runs over, the one named last changes fastest.
Arguments:
- dec_in: bfloat16 [64, 512, 768], P(('rep', 'fsdp')), may hold values from -6 to 6
- memory: bfloat16 [64, 512, 768], P(('rep', 'fsdp')), may hold values from -6 to 6
- out_grad: bfloat16 [64, 512, 768], P(('rep', 'fsdp')), may hold values from -6 to 6
- dec_len: int32 [64], P(('rep', 'fsdp')), may hold values from 32 to 512, as said below
- enc_len: int32 [64], P(('rep', 'fsdp')), may hold values from 32 to 512, as said below
- buckets: int32 [512], replicated, may hold values from 0 to 31, as said below
- self_weight: float32 [4, 768, 768], P(None, 'fsdp'), as said below
- cross_weight: float32 [4, 768, 768], P(None, 'fsdp'), as said below
- ffn_in: float32 [2, 768, 2048], P(None, 'fsdp'), may hold values from -0.21875 to 0.21875
- ffn_out: float32 [2048, 768], P('fsdp'), may hold values from -0.1875 to 0.1875
- gains: float32 [3, 768], P(None, 'fsdp'), may hold values from 0.5 to 1.5
- table: float32 [32, 12], replicated, may hold values from -4 to 4
- self_rows: float32 [4, 768], P(None, 'fsdp'), as said below
- self_cols: float32 [4, 768], replicated, as said below
- cross_rows: float32 [4, 768], P(None, 'fsdp'), as said below
- cross_cols: float32 [4, 768], replicated, as said below
- in_rows: float32 [2, 768], P(None, 'fsdp'), as said below
- in_cols: float32 [2, 2048], replicated, as said below
- out_rows: float32 [2048], P('fsdp'), as said below
- out_cols: float32 [768], replicated, as said below
- gain_moment: float32 [3, 768], P(None, 'fsdp'), may hold values from 0.01 to 1
- table_moment: float32 [32, 12], replicated, may hold values from 0.01 to 1
Outputs:
- layer_out: bfloat16 [64, 512, 768], P(('rep', 'fsdp'))
- input_grad: float32 [64, 512, 768], P(('rep', 'fsdp'))
- memory_grad: float32 [64, 512, 768], P(('rep', 'fsdp'))
- self_grad: float32 [4, 768, 768], P(None, 'fsdp')
- cross_grad: float32 [4, 768, 768], P(None, 'fsdp')
- ffn_in_grad: float32 [2, 768, 2048], P(None, 'fsdp')
- feedforward_output_gradient: float32 [2048, 768], P('fsdp')
- gains_grad: float32 [3, 768], P(None, 'fsdp')
- table_grad: float32 [32, 12], replicated
- new_self: float32 [4, 768, 768], P(None, 'fsdp')
- new_cross: float32 [4, 768, 768], P(None, 'fsdp')
- new_ffn_in: float32 [2, 768, 2048], P(None, 'fsdp')
- new_ffn_out: float32 [2048, 768], P('fsdp')
- new_gains: float32 [3, 768], P(None, 'fsdp')
- new_table: float32 [32, 12], replicated
- new_self_rows: float32 [4, 768], P(None, 'fsdp')
- new_self_cols: float32 [4, 768], replicated
- new_cross_rows: float32 [4, 768], P(None, 'fsdp')
- new_cross_cols: float32 [4, 768], replicated
- new_in_rows: float32 [2, 768], P(None, 'fsdp')
- new_in_cols: float32 [2, 2048], replicated
- new_out_rows: float32 [2048], P('fsdp')
- new_out_cols: float32 [768], replicated
- new_gain_moment: float32 [3, 768], P(None, 'fsdp')
- new_table_moment: float32 [32, 12], replicated
Inputs may be any that keep to these rules, and one draw needn't show every extreme that they name: `dec_len`: a sequence's valid decoder tokens; some sequence has 512. `enc_len`: a sequence's valid memory tokens; some sequence has 512. `buckets`: never falls as the distance grows, is 0 at distance 0 and takes every bucket. `self_weight`: four 768 x 768 projections. `cross_weight`: four 768 x 768 projections. `self_rows`: positive running averages of squared gradients. `self_cols`: positive running averages of squared gradients. `cross_rows`: positive running averages of squared gradients. `cross_cols`: positive running averages of squared gradients. `in_rows`: positive running averages of squared gradients. `in_cols`: positive running averages of squared gradients. `out_rows`: positive running averages of squared gradients. `out_cols`: positive running averages of squared gradients.
All inputs are finite; a program needn't handle non-finite values.
Results may differ from a plain program's by a relative error of at most 0.03.
The roundings to bfloat16 on the way count: a program that leaves them out, or rounds other values in their place, can miss the bound.
Values may be sent and summed in bfloat16 or wider, within the bound.
No kernel may reach another device: no remote copies, remote signals or barrier semaphores. Data moves between devices by JAX's collectives and lax.ppermute only.
A program may use at most 320 MiB of HBM per device.

v0:
```python
import math

import jax
import jax.numpy as jnp
from jax import lax
from jax.sharding import PartitionSpec as P

H = 12
DH = 64
BUCKETS = 32


EXACT_ARITHMETIC = lax.Precision.HIGHEST
MASKED = -1000000000.0
DECAY_RATE = 0.8
STEP_RATE = 0.2
TINY_TERM = 1e-30


def rms_scale(vector, gain_row):
    return vector * lax.rsqrt(jnp.mean(vector * vector, axis=-1, keepdims=True) + 1e-06) * gain_row


def matmul(earlier_operand, later_operand):
    return jnp.dot(earlier_operand, later_operand, preferred_element_type=jnp.float32)


def inner_first(earlier_operand, later_operand):
    return lax.dot_general(
        earlier_operand, later_operand, (((0,), (0,)), ((), ())), preferred_element_type=jnp.float32
    )


def inner_last(earlier_operand, later_operand):
    return lax.dot_general(
        earlier_operand, later_operand, (((1,), (1,)), ((), ())), preferred_element_type=jnp.float32
    )


def split_heads(rows_in):
    return rows_in.reshape(rows_in.shape[0], H, DH)


def score_block(query_rows, key_rows, rel_bias, keep_mask):
    scores = jnp.einsum(
        "qhd,khd->hqk",
        split_heads(query_rows),
        split_heads(key_rows),
        preferred_element_type=jnp.float32,
    )
    if rel_bias is not None:
        scores = scores + rel_bias
    return jnp.where(keep_mask[None], scores, MASKED)


def attend(query_rows, key_rows, value_rows, rel_bias, keep_mask):
    scores = score_block(query_rows, key_rows, rel_bias, keep_mask)
    row_max = jnp.max(scores, axis=2, keepdims=True)
    log_total = row_max + jnp.log(jnp.sum(jnp.exp(scores - row_max), axis=2, keepdims=True))
    probability = jnp.exp(scores - log_total).astype(jnp.bfloat16)
    mixture = jnp.einsum(
        "hqk,khd->qhd", probability, split_heads(value_rows), preferred_element_type=jnp.float32
    )
    return (mixture.reshape(query_rows.shape).astype(jnp.bfloat16), log_total)


def attend_back(query_rows, key_rows, value_rows, grad_mix, log_total, rel_bias, keep_mask):
    scores = score_block(query_rows, key_rows, rel_bias, keep_mask)
    probability = jnp.exp(scores - log_total)
    heads_grad = split_heads(grad_mix)
    grad_prob = jnp.einsum(
        "qhd,khd->hqk", heads_grad, split_heads(value_rows), preferred_element_type=jnp.float32
    )
    grad_value = jnp.einsum(
        "hqk,qhd->khd",
        probability.astype(jnp.bfloat16),
        heads_grad,
        preferred_element_type=jnp.float32,
    )
    grad_score = (
        probability * (grad_prob - jnp.sum(probability * grad_prob, axis=2, keepdims=True))
    ).astype(jnp.bfloat16)
    grad_query = jnp.einsum(
        "hqk,khd->qhd", grad_score, split_heads(key_rows), preferred_element_type=jnp.float32
    )
    grad_key = jnp.einsum(
        "hqk,qhd->khd", grad_score, split_heads(query_rows), preferred_element_type=jnp.float32
    )
    return (
        grad_query.reshape(query_rows.shape).astype(jnp.bfloat16),
        grad_key.reshape(key_rows.shape).astype(jnp.bfloat16),
        grad_value.reshape(key_rows.shape).astype(jnp.bfloat16),
        grad_score,
    )


def gated_unit(gate_pre, up_pre):
    return jax.nn.gelu(gate_pre, approximate=True) * up_pre


def row_parts(gradient, weight, row_state):
    squares = gradient * gradient + TINY_TERM
    row_moment = DECAY_RATE * row_state + (1.0 - DECAY_RATE) * jnp.mean(squares, axis=2)
    return (
        row_moment,
        jnp.sum(squares, axis=1),
        jnp.sum(row_moment, axis=1),
        jnp.sum(weight * weight, axis=(1, 2)),
    )


def column_step(gradient, row_moment, col_state, col_sum, row_sum, whole_rows):
    col_moment = DECAY_RATE * col_state + (1.0 - DECAY_RATE) * col_sum / whole_rows
    row_mean = row_sum / whole_rows
    direction = gradient * lax.rsqrt(
        row_moment[:, :, None] * col_moment[:, None, :] / row_mean[:, None, None]
    )
    return (direction, col_moment)


def apply_optimizer_update(weight, direction, weight_square):
    step_size = STEP_RATE * jnp.sqrt(weight_square + 1e-06)
    ratio = step_size.reshape((-1,) + (1,) * (weight.ndim - 1))
    return weight - ratio * direction


def per_device(
    dec_in,
    memory,
    out_grad,
    dec_len,
    enc_len,
    buckets,
    self_weight,
    cross_weight,
    ffn_in,
    ffn_out,
    gains,
    table,
    self_rows,
    self_cols,
    cross_rows,
    cross_cols,
    in_rows,
    in_cols,
    out_rows,
    out_cols,
    gain_moment,
    table_moment,
):
    seq_count, seq_length, model_width = dec_in.shape
    mem_length = memory.shape[1]
    row_count = seq_count * seq_length
    shards = (
        self_weight.astype(jnp.bfloat16),
        cross_weight.astype(jnp.bfloat16),
        ffn_in.astype(jnp.bfloat16),
        ffn_out.astype(jnp.bfloat16),
        gains.astype(jnp.bfloat16),
    )
    gathered = (
        lax.all_gather(shards[0], "fsdp", axis=1, tiled=True),
        lax.all_gather(shards[1], "fsdp", axis=1, tiled=True),
        lax.all_gather(shards[2], "fsdp", axis=1, tiled=True),
        lax.all_gather(shards[3], "fsdp", axis=0, tiled=True),
        lax.all_gather(shards[4], "fsdp", axis=1, tiled=True),
    )
    col_whole = (self_cols, cross_cols, in_cols, out_cols)
    w_self, w_cross, w_in, w_out, gain_low = gathered
    gain_full = gain_low.astype(jnp.float32)
    positions = jnp.arange(seq_length)
    distance = positions[:, None] - positions[None, :]
    pair_bucket = jnp.take(buckets, jnp.maximum(distance, 0)).reshape(-1)
    one_hot = (pair_bucket[:, None] == jnp.arange(BUCKETS)[None, :]).astype(jnp.float32)
    rel_bias = jnp.dot(one_hot, table, precision=EXACT_ARITHMETIC).T.reshape(
        H, seq_length, seq_length
    )
    live_rows = (positions[None, :] < dec_len[:, None]).astype(jnp.float32).reshape(row_count, 1)
    mem_positions = jnp.arange(mem_length)

    def self_keep(seq_len):
        return (distance >= 0) & (positions[None, :] < seq_len)

    def cross_keep(seq_len):
        return jnp.broadcast_to(mem_positions[None, :] < seq_len, (seq_length, mem_length))

    def by_seq(rows_in, length_rows):
        return rows_in.reshape(seq_count, length_rows, model_width)

    residual = dec_in.reshape(row_count, model_width).astype(jnp.float32)
    mem_rows = memory.reshape(seq_count * mem_length, model_width)
    normed_one = rms_scale(residual, gain_full[0]).astype(jnp.bfloat16)
    query_one = matmul(normed_one, w_self[0]).astype(jnp.bfloat16)
    key_one = matmul(normed_one, w_self[1]).astype(jnp.bfloat16)
    value_one = matmul(normed_one, w_self[2]).astype(jnp.bfloat16)

    def self_forward(element):
        return attend(element[0], element[1], element[2], rel_bias, self_keep(element[3]))

    mix_one, total_one = lax.map(
        self_forward,
        (
            by_seq(query_one, seq_length),
            by_seq(key_one, seq_length),
            by_seq(value_one, seq_length),
            dec_len,
        ),
    )
    mix_one = mix_one.reshape(row_count, model_width)
    after_self = residual + matmul(mix_one, w_self[3])
    normed_two = rms_scale(after_self, gain_full[1]).astype(jnp.bfloat16)
    query_two = matmul(normed_two, w_cross[0]).astype(jnp.bfloat16)
    key_two = matmul(mem_rows, w_cross[1]).astype(jnp.bfloat16)
    value_two = matmul(mem_rows, w_cross[2]).astype(jnp.bfloat16)

    def cross_forward(element):
        return attend(element[0], element[1], element[2], None, cross_keep(element[3]))

    mix_two, total_two = lax.map(
        cross_forward,
        (
            by_seq(query_two, seq_length),
            by_seq(key_two, mem_length),
            by_seq(value_two, mem_length),
            enc_len,
        ),
    )
    mix_two = mix_two.reshape(row_count, model_width)
    after_cross = after_self + matmul(mix_two, w_cross[3])
    normed_three = rms_scale(after_cross, gain_full[2]).astype(jnp.bfloat16)
    gate_pre = matmul(normed_three, w_in[0])
    up_pre = matmul(normed_three, w_in[1])
    hidden = gated_unit(gate_pre, up_pre).astype(jnp.bfloat16)
    result = (after_cross + matmul(hidden, w_out)) * live_rows
    layer_out = result.astype(jnp.bfloat16).reshape(seq_count, seq_length, model_width)
    back_weights = (
        lax.all_gather(shards[0], "fsdp", axis=1, tiled=True),
        lax.all_gather(shards[1], "fsdp", axis=1, tiled=True),
        lax.all_gather(shards[2], "fsdp", axis=1, tiled=True),
        lax.all_gather(shards[3], "fsdp", axis=0, tiled=True),
        lax.all_gather(shards[4], "fsdp", axis=1, tiled=True),
    )
    back_self, back_cross, back_in, back_out, back_gain = back_weights
    back_gain = back_gain.astype(jnp.float32)
    grad_out = out_grad.reshape(row_count, model_width).astype(jnp.float32) * live_rows
    down_low = grad_out.astype(jnp.bfloat16)
    grad_down = inner_first(hidden, down_low)
    grad_hidden = inner_last(down_low, back_out)
    _, pullback = jax.vjp(gated_unit, gate_pre, up_pre)
    grad_gate, grad_up = pullback(grad_hidden)
    grad_gate = grad_gate.astype(jnp.bfloat16)
    grad_up = grad_up.astype(jnp.bfloat16)
    grad_inner = jnp.stack(
        [inner_first(normed_three, grad_gate), inner_first(normed_three, grad_up)]
    )
    grad_three = inner_last(grad_gate, back_in[0]) + inner_last(grad_up, back_in[1])
    _, pullback = jax.vjp(rms_scale, after_cross, back_gain[2])
    grad_cross, gain_three = pullback(grad_three)
    grad_cross = grad_out + grad_cross
    branch_two = grad_cross.astype(jnp.bfloat16)
    grad_co = inner_first(mix_two, branch_two)
    grad_mix_two = inner_last(branch_two, back_cross[3]).astype(jnp.bfloat16)

    def cross_backward(element):
        return attend_back(
            element[0], element[1], element[2], element[3], element[4], None, cross_keep(element[5])
        )[:3]

    grad_q_two, grad_k_two, grad_v_two = lax.map(
        cross_backward,
        (
            by_seq(query_two, seq_length),
            by_seq(key_two, mem_length),
            by_seq(value_two, mem_length),
            by_seq(grad_mix_two, seq_length),
            total_two,
            enc_len,
        ),
    )
    grad_q_two = grad_q_two.reshape(row_count, model_width)
    grad_k_two = grad_k_two.reshape(seq_count * mem_length, model_width)
    grad_v_two = grad_v_two.reshape(seq_count * mem_length, model_width)
    grad_cross_weights = jnp.stack(
        [
            inner_first(normed_two, grad_q_two),
            inner_first(mem_rows, grad_k_two),
            inner_first(mem_rows, grad_v_two),
            grad_co,
        ]
    )
    memory_grad = (
        inner_last(grad_k_two, back_cross[1]) + inner_last(grad_v_two, back_cross[2])
    ).reshape(seq_count, mem_length, model_width)
    _, pullback = jax.vjp(rms_scale, after_self, back_gain[1])
    grad_self, gain_two = pullback(inner_last(grad_q_two, back_cross[0]))
    grad_self = grad_cross + grad_self
    branch_one = grad_self.astype(jnp.bfloat16)
    grad_wo = inner_first(mix_one, branch_one)
    grad_mix_one = inner_last(branch_one, back_self[3]).astype(jnp.bfloat16)

    def self_backward(score_total, element):
        grad_query, grad_key, grad_value, grad_score = attend_back(
            element[0],
            element[1],
            element[2],
            element[3],
            element[4],
            rel_bias,
            self_keep(element[5]),
        )
        return (score_total + grad_score.astype(jnp.float32), (grad_query, grad_key, grad_value))

    score_total, (grad_q_one, grad_k_one, grad_v_one) = lax.scan(
        self_backward,
        jnp.zeros((H, seq_length, seq_length), jnp.float32),
        (
            by_seq(query_one, seq_length),
            by_seq(key_one, seq_length),
            by_seq(value_one, seq_length),
            by_seq(grad_mix_one, seq_length),
            total_one,
            dec_len,
        ),
    )
    table_part = jnp.dot(score_total.reshape(H, -1), one_hot, precision=EXACT_ARITHMETIC).T
    grad_q_one = grad_q_one.reshape(row_count, model_width)
    grad_k_one = grad_k_one.reshape(row_count, model_width)
    grad_v_one = grad_v_one.reshape(row_count, model_width)
    grad_self_weights = jnp.stack(
        [
            inner_first(normed_one, grad_q_one),
            inner_first(normed_one, grad_k_one),
            inner_first(normed_one, grad_v_one),
            grad_wo,
        ]
    )
    grad_normed = (
        inner_last(grad_q_one, back_self[0])
        + inner_last(grad_k_one, back_self[1])
        + inner_last(grad_v_one, back_self[2])
    )
    _, pullback = jax.vjp(rms_scale, residual, back_gain[0])
    grad_input, first_norm_gain = pullback(grad_normed)
    input_grad = (grad_self + grad_input).reshape(seq_count, seq_length, model_width)
    grad_gains = jnp.stack([first_norm_gain, gain_two, gain_three])
    owned = (
        lax.psum_scatter(grad_self_weights, "fsdp", scatter_dimension=1, tiled=True),
        lax.psum_scatter(grad_cross_weights, "fsdp", scatter_dimension=1, tiled=True),
        lax.psum_scatter(grad_inner, "fsdp", scatter_dimension=1, tiled=True),
        lax.psum_scatter(grad_down, "fsdp", scatter_dimension=0, tiled=True),
        lax.psum_scatter(grad_gains, "fsdp", scatter_dimension=1, tiled=True),
    )
    owned = (
        lax.psum(owned[0].astype(jnp.bfloat16), "rep").astype(jnp.float32),
        lax.psum(owned[1].astype(jnp.bfloat16), "rep").astype(jnp.float32),
        lax.psum(owned[2].astype(jnp.bfloat16), "rep").astype(jnp.float32),
        lax.psum(owned[3].astype(jnp.bfloat16), "rep").astype(jnp.float32),
        lax.psum(owned[4].astype(jnp.bfloat16), "rep").astype(jnp.float32),
    )
    table_total = lax.psum(table_part, ("rep", "fsdp"))
    fsdp_count = lax.axis_size("fsdp")
    grad_factor = 1.0 / math.sqrt(row_count * lax.axis_size("rep") * fsdp_count)
    self_grad, cross_grad, ffn_in_grad, feedforward_output_gradient, gains_grad = [
        member * grad_factor for member in owned
    ]
    table_grad = table_total * grad_factor
    batches = [
        (self_grad, self_weight, self_rows, col_whole[0]),
        (cross_grad, cross_weight, cross_rows, col_whole[1]),
        (ffn_in_grad, ffn_in, in_rows, col_whole[2]),
        (feedforward_output_gradient[None], ffn_out[None], out_rows[None], col_whole[3][None]),
    ]
    prepared = [
        row_parts(gradient, weight, row_state) for gradient, weight, row_state, col_state in batches
    ]
    gain_state = DECAY_RATE * gain_moment + (1.0 - DECAY_RATE) * (
        gains_grad * gains_grad + TINY_TERM
    )
    gain_direction = gains_grad * lax.rsqrt(gain_state)
    local_sums = []
    for parts in prepared:
        local_sums = local_sums + [parts[1], parts[2], parts[3]]
    local_sums = local_sums + [jnp.sum(gains * gains, axis=1)]
    totals = lax.psum(tuple(local_sums), "fsdp")
    updated = []
    col_results = []
    for place_index in range(len(batches)):
        gradient, weight, row_state, col_state = batches[place_index]
        whole_rows = weight.shape[1] * fsdp_count
        direction, col_moment = column_step(
            gradient,
            prepared[place_index][0],
            col_state,
            totals[3 * place_index],
            totals[3 * place_index + 1],
            whole_rows,
        )
        count_all = whole_rows * weight.shape[2]
        updated.append(
            apply_optimizer_update(weight, direction, totals[3 * place_index + 2] / count_all)
        )
        col_results.append(col_moment)
    gain_width = gains.shape[1] * fsdp_count
    gain_offset = 3 * len(batches)
    new_gains = apply_optimizer_update(gains, gain_direction, totals[gain_offset] / gain_width)
    table_state = DECAY_RATE * table_moment + (1.0 - DECAY_RATE) * (
        table_grad * table_grad + TINY_TERM
    )
    table_direction = table_grad * lax.rsqrt(table_state)
    new_table = apply_optimizer_update(table, table_direction, jnp.mean(table * table))
    return (
        layer_out,
        input_grad,
        memory_grad,
        self_grad,
        cross_grad,
        ffn_in_grad,
        feedforward_output_gradient,
        gains_grad,
        table_grad,
        updated[0],
        updated[1],
        updated[2],
        updated[3][0],
        new_gains,
        new_table,
        prepared[0][0],
        col_results[0],
        prepared[1][0],
        col_results[1],
        prepared[2][0],
        col_results[2],
        prepared[3][0][0],
        col_results[3][0],
        gain_state,
        table_state,
    )


def solution(mesh):
    placed = (
        P(("rep", "fsdp"), None, None),
        P(("rep", "fsdp"), None, None),
        P(("rep", "fsdp"), None, None),
        P(("rep", "fsdp")),
        P(("rep", "fsdp")),
        P(),
        P(None, "fsdp", None),
        P(None, "fsdp", None),
        P(None, "fsdp", None),
        P("fsdp", None),
        P(None, "fsdp"),
        P(),
        P(None, "fsdp"),
        P(),
        P(None, "fsdp"),
        P(),
        P(None, "fsdp"),
        P(),
        P("fsdp"),
        P(),
        P(None, "fsdp"),
        P(),
    )
    return jax.shard_map(
        per_device,
        mesh=mesh,
        in_specs=placed,
        out_specs=(
            P(("rep", "fsdp"), None, None),
            P(("rep", "fsdp"), None, None),
            P(("rep", "fsdp"), None, None),
            P(None, "fsdp", None),
            P(None, "fsdp", None),
            P(None, "fsdp", None),
            P("fsdp", None),
            P(None, "fsdp"),
            P(),
            P(None, "fsdp", None),
            P(None, "fsdp", None),
            P(None, "fsdp", None),
            P("fsdp", None),
            P(None, "fsdp"),
            P(),
            P(None, "fsdp"),
            P(),
            P(None, "fsdp"),
            P(),
            P(None, "fsdp"),
            P(),
            P("fsdp"),
            P(),
            P(None, "fsdp"),
            P(),
        ),
        check_vma=False,
    )
```

profile of v0, /device:TPU:0, one launch (start us, length us, event | category | flops | bytes accessed | tf_op | source)
XLA Modules:
  0.0 3655.9 jit_solution(9727375157479340790)
XLA Ops:
  22.6 13.6 all-gather
  43.1 2755.0 %gather_fusion = s32[262144]{0:T(1024)} fusion(s32[512]{0:T(512)S(1)} %copy-done.1, s32[262144]{0:T(1024)} %broadcast_clamp_fusion), kind=kCustom, calls=%fused_computation | custom fusion | bytes 3145728 | tf_op jit(solution)/shard_map/jit(_take)/gather | solution.py:173
  2799.9 10.7 fusion.39
  2810.6 19.3 copy.278
  2829.9 10.7 slice.80
  2840.5 12.8 copy.217
  2877.1 30.8 while.58
  2928.9 25.5 while.59
  2974.5 14.9 multiply_convert_fusion.2
  3025.3 82.8 %while.60 = (s32[]{:T(128)}, bf16[2,512,768]{2,1,0:T(8,128)(2,1)}, bf16[2,512,768]{1,2,0:T(8,128)(2,1)}, bf16[2,512,768]{1,2,0:T(8,128)(2,1)}, bf16[2,512,768]{1...) while((s32[]{:T(128)}, bf16[2,512,768]{2,1,0:T(8,128)(2,1)}, ...), condition=%wide.region_14.15_spmd.clone, body=%wide.region_12.14_spmd.clone.sunk | while | flops 2052188672 | bytes 192064432 | solution.py:269
  3038.9 11.2 multiply_reduce_fusion.16
  3080.4 11.2 multiply_reduce_fusion.16
  3135.5 114.5 %while.61 = (s32[]{:T(128)}, f32[12,512,512]{1,2,0:T(8,128)}, bf16[2,512,768]{1,2,0:T(8,128)(2,1)}, bf16[2,512,768]{1,2,0:T(8,128)(2,1)}, bf16[2,512,768]{1,2,0:...) while((s32[]{:T(128)}, f32[12,512,512]{1,2,0:T(8,128)}, ...), condition=%wide.region_18.19_spmd.clone, body=%wide.region_16.18_spmd.clone.sunk | while | flops 2052975104 | bytes 319940160 | solution.py:313
  3159.8 18.8 select_add_fusion.2
  3215.4 21.5 select_add_fusion.2
  3277.3 11.5 pad_maximum_fusion
  3309.1 12.8 copy.246
  3321.9 12.6 pad.14
  3334.5 15.4 copy.281
  3349.9 17.6 fusion.38
  3367.5 39.4 %psum.138 = f32[32,12]{0,1:T(8,128)S(1)} all-reduce(f32[32,12]{0,1:T(8,128)S(1)} %fusion.38), channel_id=1, replica_groups=mesh['rep'=4,'fsdp'=8] {'rep','fsdp'}, use_global_device_ids=true, to_apply=%region_33.34 | all-reduce | flops 384 | bytes 3072 | tf_op jit(solution)/shard_map/psum | solution.py:360
  3413.9 77.5 %reduce-scatter.12.cloned.1.call-done = f32[2,96,2048]{2,1,0:T(8,128)} async-done(((f32[2,768,2048]{2,1,0:T(8,128)}), f32[2,96,2048]{2,1,0:T(8,128)}) %reduce-scatter.12.cloned.1.call-update) | async-done | bytes 1572880 | tf_op jit(solution)/shard_map/reduce_scatter | solution.py:349
  3534.1 66.7 %all-reduce.4.cloned.1.call-done = (bf16[4,96,768]{2,1,0:T(8,128)(2,1)}, bf16[4,96,768]{2,1,0:T(8,128)(2,1)}, bf16[2,96,2048]{2,1,0:T(8,128)(2,1)}, bf16[256,768]{1,0:T(8,128)(2,1)}) async-done(((bf16[4,96,768]{2,1,0:T(8,128)(2,1)}, bf16[4,96,768]{2,1,0:T(8,128)(2,1)}, bf16[2,96,2048]{2,1,0:T(8,128)(2,1)}, bf16[256,768]{1,0:T(8,128)(2,1)}), (bf16[4,96,768]{2,1,0:T(8,128)(2,1)}, ...) | async-done | bytes 2359312 | tf_op jit(solution)/shard_map/psum | solution.py:354
  3609.1 30.1 all-reduce
  (563 shorter events, 452.8 us)
Async XLA Ops:
  7.2 2911.9 %copy-start = (bf16[2,512,768]{2,1,0:T(8,128)(2,1)S(1)}, bf16[2,512,768]{2,1,0:T(8,128)(2,1)}, u32[]{:S(2)}) copy-start(bf16[2,512,768]{2,1,0:T(8,128)(2,1)} %param.31) | copy-start | bytes 4718596
  7.2 2849.4 %all-gather.6.cloned.1.call-start = ((), (), s32[]{:S(2)}) async-start(), calls=%async_computation.5 | async-start | bytes 5308416 | tf_op jit(solution)/shard_map/all_gather | solution.py:162
  10.6 2903.3 %all-gather.8.cloned.1.call-start = ((), (), s32[]{:S(2)}) async-start(), calls=%async_computation.6 | async-start | bytes 5308416 | tf_op jit(solution)/shard_map/all_gather | solution.py:163
  13.8 2947.0 %all-gather.10.cloned.1.call-start = ((), (), s32[]{:S(2)}) async-start(), calls=%async_computation.7 | async-start | bytes 7077888 | tf_op jit(solution)/shard_map/all_gather | solution.py:164
  15.6 2958.9 %all-gather.12.cloned.1.call-start = ((), (), s32[]{:S(2)}) async-start(), calls=%async_computation.8 | async-start | bytes 3538944 | tf_op jit(solution)/shard_map/all_gather | solution.py:165
  18.7 3388.9 %reduce-scatter.14.cloned.1.call-start = ((), (), s32[]{:S(2)}) async-start(), calls=%async_computation.12 | async-start | bytes 7077888 | tf_op jit(solution)/shard_map/reduce_scatter | solution.py:350
  43.1 2755.0 %copy-start.61 = (s32[64,4,8,128]{3,1,2,0:T(4,128)S(1)}, s32[64,4,8,128]{3,1,2,0:T(4,128)}, u32[]{:S(2)}) copy-start(s32[64,4,8,128]{3,1,2,0:T(4,128)} %copy.275) | copy-start | bytes 3145732
  3011.2 398.4 %reduce-scatter.10.cloned.1.call-start = ((), (), s32[]{:S(2)}) async-start(), calls=%async_computation.10 | async-start | bytes 10616832 | tf_op jit(solution)/shard_map/reduce_scatter | solution.py:348
  3121.4 290.3 %reduce-scatter.8.cloned.1.call-start = ((), (), s32[]{:S(2)}) async-start(), calls=%async_computation.9 | async-start | bytes 10616832 | tf_op jit(solution)/shard_map/reduce_scatter | solution.py:347
  3215.4 26.4 copy-start.3
  3262.8 228.6 %reduce-scatter.12.cloned.1.call-start = ((), (), s32[]{:S(2)}) async-start(), calls=%async_computation.11 | async-start | bytes 14155776 | tf_op jit(solution)/shard_map/reduce_scatter | solution.py:349
  3288.8 234.4 %reduce-scatter.16.cloned.1.call-start = ((), (), s32[]{:S(2)}) async-start(), calls=%async_computation.13 | async-start | bytes 442368
  3349.9 57.1 %copy-start.97 = (f32[32,12]{0,1:T(8,128)S(1)}, f32[32,12]{0,1:T(8,128)}, u32[]{:S(2)}) copy-start(f32[32,12]{0,1:T(8,128)} %param.51) | copy-start | bytes 4612
  3407.0 193.8 %all-reduce.4.cloned.1.call-start = ((), (), s32[]{:S(2)}) async-start(), calls=%async_computation.14 | async-start | bytes 4718592 | tf_op jit(solution)/shard_map/psum | solution.py:354
  3603.2 37.6 %copy-start.89 = (f32[2,2048]{1,0:T(2,128)S(1)}, f32[2,2048]{1,0:T(2,128)}, u32[]{:S(2)}) copy-start(f32[2,2048]{1,0:T(2,128)} %param.47) | copy-start | bytes 49156
  3603.2 37.6 %copy-start.93 = (f32[4,768]{1,0:T(4,128)S(1)}, f32[4,768]{1,0:T(4,128)}, u32[]{:S(2)}) copy-start(f32[4,768]{1,0:T(4,128)} %param.45) | copy-start | bytes 36868
  3603.3 37.6 %copy-start.94 = (f32[4,768]{1,0:T(4,128)S(1)}, f32[4,768]{1,0:T(4,128)}, u32[]{:S(2)}) copy-start(f32[4,768]{1,0:T(4,128)} %param.43) | copy-start | bytes 36868
  3603.3 37.7 %copy-start.99 = (f32[3,96]{1,0:T(4,128)S(1)}, f32[3,96]{1,0:T(4,128)}, u32[]{:S(2)}) copy-start(f32[3,96]{1,0:T(4,128)} %param.40) | copy-start | bytes 3460
  3603.3 37.7 %copy-start.109 = (f32[3,96]{1,0:T(4,128)S(1)}, f32[3,96]{1,0:T(4,128)}, u32[]{:S(2)}) copy-start(f32[3,96]{1,0:T(4,128)} %param.50) | copy-start | bytes 3460
  3605.7 38.6 %copy-start.45 = (f32[2,96,2048]{2,1,0:T(8,128)S(1)}, f32[2,96,2048]{2,1,0:T(8,128)}, u32[]{:S(2)}) copy-start(f32[2,96,2048]{2,1,0:T(8,128)} %param.38) | copy-start | bytes 4718596
  3608.3 37.8 %copy-start.100 = (f32[2,96]{1,0:T(2,128)}, f32[2,96]{1,0:T(2,128)S(1)}, u32[]{:S(2)}) copy-start(f32[2,96]{1,0:T(2,128)S(1)} %get-tuple-element.675) | copy-start | bytes 2308
  3608.9 37.2 %copy-start.101 = (f32[256]{0:T(256)}, f32[256]{0:T(256)S(1)}, u32[]{:S(2)}) copy-start(f32[256]{0:T(256)S(1)} %get-tuple-element.672) | copy-start | bytes 3076
  3609.1 37.0 %copy-start.95 = (f32[4,96]{1,0:T(4,128)}, f32[4,96]{1,0:T(4,128)S(1)}, u32[]{:S(2)}) copy-start(f32[4,96]{1,0:T(4,128)S(1)} %get-tuple-element.678) | copy-start | bytes 4612
  3609.1 38.4 %copy-start.96 = (f32[4,96]{1,0:T(4,128)}, f32[4,96]{1,0:T(4,128)S(1)}, u32[]{:S(2)}) copy-start(f32[4,96]{1,0:T(4,128)S(1)} %get-tuple-element.722) | copy-start | bytes 4612
  (135 other events, 745.0 us)
Sparse Core Ops, SparseCore 0:
  10.7 54.3 all-gather.5
  67.2 50.5 all-gather.7
  120.0 63.5 all-gather.9
  185.1 36.9 all-gather.11
  3011.3 67.9 reduce-scatter.13
  3121.5 97.4 reduce-scatter.9
  3262.9 97.4 reduce-scatter.7
  3362.8 128.6 reduce-scatter.11
  3494.2 28.9 reduce-scatter.15
  3528.0 72.7 all-reduce.3
where the time goes:
time: 3660 us
  local copies, waits for them, and re-layouts  2960 us (81%)
  matrix products  291 us (8%)
  waiting for transfers between devices  151 us (4%)
  other arithmetic  141 us (4%)
  blocking collectives  93.1 us (3%)
    gather x1, local copies, waits for them, and re-layouts, per_device(): pair_bucket = jnp.take(buckets, jnp.maximum(distance, 0)).reshape(-1)  2750 us
    unnamed x225, local copies, waits for them, and re-layouts  92.1 us
    reduce_scatter x1, waiting for transfers between devices, per_device(): lax.psum_scatter(grad_inner, 'fsdp', scatter_dimension=1, tiled=True)  77.5 us
  transfers between devices with their start and end apart: 10, of which 3 were waited for; matrix products, arithmetic and copies ran while one was open for 91% of the time, Pallas kernels for 0%

commit v1 on v0

--- a/solution.py
+++ b/solution.py
@@ -170,8 +170,11 @@
     gain_full = gain_low.astype(jnp.float32)
     positions = jnp.arange(seq_length)
     distance = positions[:, None] - positions[None, :]
-    pair_bucket = jnp.take(buckets, jnp.maximum(distance, 0)).reshape(-1)
-    one_hot = (pair_bucket[:, None] == jnp.arange(BUCKETS)[None, :]).astype(jnp.float32)
+    first_distance = jnp.sum(buckets[:, None] < jnp.arange(BUCKETS + 1)[None, :], axis=0)
+    pair_distance = jnp.maximum(distance, 0).reshape(-1)[:, None]
+    one_hot = (
+        (pair_distance >= first_distance[None, :-1]) & (pair_distance < first_distance[None, 1:])
+    ).astype(jnp.float32)
     rel_bias = jnp.dot(one_hot, table, precision=EXACT_ARITHMETIC).T.reshape(
         H, seq_length, seq_length
     )
@@ -344,10 +347,10 @@
     input_grad = (grad_self + grad_input).reshape(seq_count, seq_length, model_width)
     grad_gains = jnp.stack([first_norm_gain, gain_two, gain_three])
     owned = (
-        lax.psum_scatter(grad_self_weights, "fsdp", scatter_dimension=1, tiled=True),
-        lax.psum_scatter(grad_cross_weights, "fsdp", scatter_dimension=1, tiled=True),
-        lax.psum_scatter(grad_inner, "fsdp", scatter_dimension=1, tiled=True),
-        lax.psum_scatter(grad_down, "fsdp", scatter_dimension=0, tiled=True),
+        lax.psum_scatter(grad_self_weights.astype(jnp.bfloat16), "fsdp", scatter_dimension=1, tiled=True),
+        lax.psum_scatter(grad_cross_weights.astype(jnp.bfloat16), "fsdp", scatter_dimension=1, tiled=True),
+        lax.psum_scatter(grad_inner.astype(jnp.bfloat16), "fsdp", scatter_dimension=1, tiled=True),
+        lax.psum_scatter(grad_down.astype(jnp.bfloat16), "fsdp", scatter_dimension=0, tiled=True),
         lax.psum_scatter(grad_gains, "fsdp", scatter_dimension=1, tiled=True),
     )
     owned = (

time: 3660 us -> 795 us (0.22)
  local copies, waits for them, and re-layouts: 2960 us -> 194 us
  waiting for transfers between devices: 151 us -> 82.7 us
    gather x1 -> x0, local copies, waits for them, and re-layouts: 2750 us -> none  [per_device(): pair_bucket = jnp.take(buckets, jnp.maximum(distance, 0)).reshape(-1)]
    reduce_scatter x4, waiting for transfers between devices: 77.6 us -> 0.02 us  [the longest x1 0.01 us: per_device(): lax.psum_scatter(grad_inner.astype(jnp.bfloat16), 'fsdp', scatter_dimensi...]
    unnamed x225 -> x219, local copies, waits for them, and re-layouts: 92.1 us -> 89 us
  transfers between devices with their start and end apart: 10 -> 10, of which waited for: 3 -> 4; matrix products, arithmetic and copies ran while one was open for 91% -> 67% of each run, Pallas kernels for 0% -> 0%
where the time goes in v1:
time: 795 us; the launch traced here: 783 us
  matrix products  280 us (35%)
  local copies, waits for them, and re-layouts  194 us (24%)
  other arithmetic  111 us (14%)
  blocking collectives  94.3 us (12%)
  waiting for transfers between devices  82.7 us (10%)
  between operations  18.1 us (2%)
    unnamed x219, local copies, waits for them, and re-layouts  89 us
    psum x1, waiting for transfers between devices, per_device(): lax.psum(owned[0].astype(jnp.bfloat16), 'rep').astype(jnp.float32)  65.5 us
    dot_general x11, matrix products, inner_last(): lax.dot_general(earlier_operand, later_operand, (((1,), (1,)), ((), ())),...  62 us
    dot_general x11, matrix products, matmul(): jnp.dot(earlier_operand, later_operand, preferred_element_type=jnp.float32)  47.6 us
    dynamic_slice x36, local copies, waits for them, and re-layouts, per_device(): lax.map(self_forward, (by_seq(query_one, seq_length), by_seq(key_one, seq...  43.2 us
    dot_general x8, matrix products, score_block(): jnp.einsum('qhd,khd->hqk', split_heads(query_rows), split_heads(key_rows)...  42.1 us
    psum x1, blocking collectives, per_device(): table_total = lax.psum(table_part, ('rep', 'fsdp'))  40.6 us
    add x2, other arithmetic, self_backward(): score_total + grad_score.astype(jnp.float32)  31.4 us
  transfers between devices with their start and end apart: 10, of which 4 were waited for; matrix products, arithmetic and copies ran while one was open for 67% of the time, Pallas kernels for 0%

profile of v1, /device:TPU:0, one launch (start us, length us, event | category | flops | bytes accessed | tf_op | source)
XLA Modules:
  0.0 782.5 jit_solution(15087694907863459823)
XLA Ops:
  22.0 13.6 %all-gather = bf16[8,96,3]{1,2,0:T(4,128)(2,1)S(1)} all-gather(bf16[1,96,3]{1,2,0:T(4,128)(2,1)S(1)} %get-tuple-element.713), channel_id=1, replica_groups=mesh['rep'=4,'fsdp'=8] {'fsdp'}, dimensions={0}, use_global_device_ids=true | all-gather | bytes 5184 | tf_op jit(solution)/shard_map/all_gather | solution.py:166
  37.9 12.2 %fusion.39 = f32[262144,12]{0,1:T(8,128)S(1)} fusion(f32[32,12]{0,1:T(8,128)S(1)} %copy-done.64, s32[262144]{0:T(1024)S(1)} %bitcast.446, s32[32]{0:T(128)S(1)} %get-tuple-element.715, s32[32]{0:T(128)S(1)} %get-tuple-element.714), kind=kOutput, calls=%fused_computation.80 | convolution fusion | flops 1233125376 | bytes 13633280 | tf_op jit(solution)/shard_map/dot_general | solution.py:178
  50.2 19.3 %copy.276 = f32[2,8,512,512]{3,2,1,0:T(8,128)} copy(f32[2,8,512,512]{3,1,2,0:T(8,128)S(1)} %bitcast.420) | data formatting | bytes 33554432
  69.5 10.9 %slice.86 = f32[12,512,512]{2,1,0:T(8,128)} slice(f32[16,512,512]{2,1,0:T(8,128)} %bitcast.418), slice={[0:12], [0:512], [0:512]} | slice | bytes 25165824 | tf_op jit(solution)/shard_map/reshape | solution.py:178
  80.4 12.7 %copy.217 = f32[12,512,512]{1,2,0:T(8,128)} copy(f32[12,512,512]{2,1,0:T(8,128)} %slice.86) | data formatting | bytes 25165824
  127.6 31.0 %while.58 = (s32[]{:T(128)}, bf16[2,512,768]{2,1,0:T(8,128)(2,1)}, f32[2,12,512,1]{2,1,3,0:T(8,128)S(1)}, bf16[2,512,768]{1,2,0:T(8,128)(2,1)}, s32[2]{0:T(128)S...) while((s32[]{:T(128)}, bf16[2,512,768]{2,1,0:T(8,128)(2,1)}, ...), condition=%wide.region_5.6_spmd.clone, body=%wide.region_2.5_spmd.clone.sunk | while | flops 828500480 | bytes 62096516 | solution.py:203
  169.4 25.6 %while.59 = (s32[]{:T(128)}, bf16[2,512,768]{2,1,0:T(8,128)(2,1)}, f32[2,12,512,1]{2,1,3,0:T(8,128)S(1)}, bf16[2,512,768]{1,2,0:T(8,128)(2,1)}, s32[2]{0:T(128)S...) while((s32[]{:T(128)}, bf16[2,512,768]{2,1,0:T(8,128)(2,1)}, ...), condition=%wide.region_10.11_spmd.clone, body=%wide.region_7.10_spmd.clone.sunk | while | flops 830859776 | bytes 48990332 | solution.py:222
  202.4 7.7 fusion.68
  222.8 15.0 %multiply_convert_fusion.2 = (bf16[1024,2048]{1,0:T(8,128)(2,1)}, bf16[1024,2048]{1,0:T(8,128)(2,1)}, bf16[1024,2048]{1,0:T(8,128)(2,1)S(1)}) fusion(f32[1024,2048]{1,0:T(8,128)} %fusion.66, f32[1024,2048]{1,0:T(8,128)} %fusion.68, bf16[1024,768]{1,0:T(8,128)(2,1)S(1)} %copy-done.43, bf16[2048,768]{1,0:T(8,128)(2,1)} %all-gather.12.cloned.1.call-done), kind=kOutput, calls=%fused_computation.96 | convolution fusion | flops 3275751424 | bytes 34078720 | tf_op jit(solution)/shard_map/dot_general | solution.py:35
  267.9 71.0 %while.60 = (s32[]{:T(128)}, bf16[2,512,768]{2,1,0:T(8,128)(2,1)}, bf16[2,512,768]{1,2,0:T(8,128)(2,1)}, bf16[2,512,768]{1,2,0:T(8,128)(2,1)}, bf16[2,512,768]{1...) while((s32[]{:T(128)}, bf16[2,512,768]{2,1,0:T(8,128)(2,1)}, ...), condition=%wide.region_15.16_spmd.clone, body=%wide.region_13.15_spmd.clone.sunk | while | flops 2052188672 | bytes 116566176 | solution.py:272
  369.1 107.2 %while.61 = (s32[]{:T(128)}, f32[12,512,512]{1,2,0:T(8,128)}, bf16[2,512,768]{1,2,0:T(8,128)(2,1)}, bf16[2,512,768]{1,2,0:T(8,128)(2,1)}, bf16[2,512,768]{1,2,0:...) while((s32[]{:T(128)}, f32[12,512,512]{1,2,0:T(8,128)}, ...), condition=%wide.region_19.20_spmd.clone, body=%wide.region_17.19_spmd.clone.sunk | while | flops 2052975104 | bytes 219276736 | solution.py:316
  380.5 10.3 %multiply_reduce_fusion.17 = (f32[12,512]{1,0:T(8,128)S(1)}, f32[12,512,512]{1,2,0:T(8,128)}) fusion(f32[12,512,512]{1,2,0:T(8,128)S(1)} %fusion.240, f32[12,512]{1,0:T(8,128)S(1)} %dynamic-slice_bitcast_fusion.5, f32[12,512,512]{1,2,0:T(8,128)} %get-tuple-element.1115, bf16[512,12,64]{0,2,1:T(8,128)(2,1)} %bitcast.399, ...), kind=kOutput, calls=%fused_computation.60.clone.1 | convolution fusion | flops 418375680 | bytes 39632896 | tf_op jit(solution)/shard_map/while/body/eval_jaxpr/qhd,khd->hqk/dot_general | solution.py:45
  397.5 13.8 %select_add_fusion.2 = (f32[12,512,512]{1,2,0:T(8,128)}, bf16[12,512,512]{1,2,0:T(8,128)(2,1)}) fusion(f32[12,512,512]{1,2,0:T(8,128)} %get-tuple-element.1094, pred[]{:T(512)S(6)} %compare.3, f32[12,512,512]{1,2,0:T(8,128)} %get-tuple-element.989, f32[12,512,512]{1,2,0:T(8,128)S(1)} %fusion.240, f32[12,512]{1,0:T(8,128)S(1)} %get-tuple-element.990), kind=kLoop, calls=%fused_computation.58.clone.1 | loop fusion | flops 18874368 | bytes 56647680 | tf_op jit(solution)/shard_map/while/body/eval_jaxpr/add | solution.py:314
  432.0 10.2 %multiply_reduce_fusion.17 = (f32[12,512]{1,0:T(8,128)S(1)}, f32[12,512,512]{1,2,0:T(8,128)}) fusion(f32[12,512,512]{1,2,0:T(8,128)S(1)} %fusion.240, f32[12,512]{1,0:T(8,128)S(1)} %dynamic-slice_bitcast_fusion.5, f32[12,512,512]{1,2,0:T(8,128)} %get-tuple-element.1115, bf16[512,12,64]{0,2,1:T(8,128)(2,1)} %bitcast.399, ...), kind=kOutput, calls=%fused_computation.60.clone.1 | convolution fusion | flops 418375680 | bytes 39632896 | tf_op jit(solution)/shard_map/while/body/eval_jaxpr/qhd,khd->hqk/dot_general | solution.py:45
  448.8 17.6 %select_add_fusion.2 = (f32[12,512,512]{1,2,0:T(8,128)}, bf16[12,512,512]{1,2,0:T(8,128)(2,1)}) fusion(f32[12,512,512]{1,2,0:T(8,128)} %get-tuple-element.1094, pred[]{:T(512)S(6)} %compare.3, f32[12,512,512]{1,2,0:T(8,128)} %get-tuple-element.989, f32[12,512,512]{1,2,0:T(8,128)S(1)} %fusion.240, f32[12,512]{1,0:T(8,128)S(1)} %get-tuple-element.990), kind=kLoop, calls=%fused_computation.58.clone.1 | loop fusion | flops 18874368 | bytes 56647680 | tf_op jit(solution)/shard_map/while/body/eval_jaxpr/add | solution.py:314
  508.1 12.7 %copy.246 = f32[12,512,512]{2,1,0:T(8,128)} copy(f32[12,512,512]{1,2,0:T(8,128)} %get-tuple-element.265) | data formatting | bytes 25165824 | tf_op jit(solution)/shard_map/while | solution.py:316
  532.2 12.5 %pad.13 = f32[16,512,512]{2,1,0:T(8,128)} pad(f32[12,512,512]{2,1,0:T(8,128)} %copy.246, f32[]{:T(128)} %constant.102.clone.1), padding=0_4x0_0x0_0 | pad | bytes 29360132
  544.7 15.3 %copy.279 = f32[2,8,512,512]{3,1,2,0:T(8,128)S(1)} copy(f32[2,8,512,512]{3,2,1,0:T(8,128)} %bitcast.417) | data formatting | bytes 33554432
  560.1 18.9 %fusion.38 = f32[32,12]{0,1:T(8,128)S(1)} fusion(f32[12,262144]{1,0:T(8,128)S(1)} %bitcast.419, s32[262144]{0:T(1024)S(1)} %bitcast.447, s32[32]{0:T(128)S(1)} %copy-done.102, s32[32]{0:T(128)S(1)} %copy-done.100), kind=kOutput, calls=%fused_computation.79 | convolution fusion | flops 1233125376 | bytes 13633280 | tf_op jit(solution)/shard_map/dot_general | solution.py:328
  579.0 40.6 %psum.138 = f32[32,12]{0,1:T(8,128)S(1)} all-reduce(f32[32,12]{0,1:T(8,128)S(1)} %fusion.38), channel_id=1, replica_groups=mesh['rep'=4,'fsdp'=8] {'rep','fsdp'}, use_global_device_ids=true, to_apply=%region_34.35 | all-reduce | flops 384 | bytes 3072 | tf_op jit(solution)/shard_map/psum | solution.py:363
  641.1 9.3 %reduce-scatter.16.cloned.1.call-done = f32[96,3]{1,0:T(8,128)} async-done(((f32[768,3]{1,0:T(8,128)}), f32[96,3]{1,0:T(8,128)}) %reduce-scatter.16.cloned.1.call-update) | async-done | bytes 1168
  651.3 10.0 %psum.137 = bf16[3,96]{1,0:T(4,128)(2,1)S(1)} all-reduce(bf16[3,96]{1,0:T(4,128)(2,1)S(1)} %copy.266), channel_id=1, replica_groups=mesh['rep'=4,'fsdp'=8] {'rep'}, use_global_device_ids=true, to_apply=%region_33.34 | all-reduce | flops 288 | bytes 1152 | tf_op jit(solution)/shard_map/psum | solution.py:361
  661.3 65.5 %all-reduce.4.cloned.1.call-done = (bf16[4,96,768]{2,1,0:T(8,128)(2,1)}, bf16[4,96,768]{2,1,0:T(8,128)(2,1)}, bf16[2,96,2048]{2,1,0:T(8,128)(2,1)}, bf16[256,768]{1,0:T(8,128)(2,1)}) async-done(((bf16[4,96,768]{2,1,0:T(8,128)(2,1)}, bf16[4,96,768]{2,1,0:T(8,128)(2,1)}, bf16[2,96,2048]{2,1,0:T(8,128)(2,1)}, bf16[256,768]{1,0:T(8,128)(2,1)}), (bf16[4,96,768]{2,1,0:T(8,128)(2,1)}, ...) | async-done | bytes 2359312 | tf_op jit(solution)/shard_map/psum | solution.py:357
  734.3 30.0 %all-reduce = (f32[4]{0:T(128)S(1)}, f32[4,768]{1,0:T(4,128)S(1)}, f32[4]{0:T(128)S(1)}, f32[4]{0:T(128)S(1)}, f32[4,768]{1,0:T(4,128)S(1)}, /*index=5*/f32[4]{0...) all-reduce(f32[4]{0:T(128)S(1)} %get-tuple-element.723, ...), channel_id=1, replica_groups=mesh['rep'=4,'fsdp'=8] {'fsdp'}, use_global_device_ids=true, to_apply=%region_41.42 | all-reduce | flops 11033 | bytes 88264 | tf_op jit(solution)/shard_map/psum | solution.py:387
  (488 shorter events, 404.0 us)
Async XLA Ops:
  7.2 110.7 %copy-start = (bf16[2,512,768]{2,1,0:T(8,128)(2,1)S(1)}, bf16[2,512,768]{2,1,0:T(8,128)(2,1)}, u32[]{:S(2)}) copy-start(bf16[2,512,768]{2,1,0:T(8,128)(2,1)} %param.31) | copy-start | bytes 4718596
  7.2 89.0 %all-gather.6.cloned.1.call-start = ((), (), s32[]{:S(2)}) async-start(), calls=%async_computation.5 | async-start | bytes 5308416 | tf_op jit(solution)/shard_map/all_gather | solution.py:162
  10.6 107.3 %all-gather.8.cloned.1.call-start = ((), (), s32[]{:S(2)}) async-start(), calls=%async_computation.6 | async-start | bytes 5308416 | tf_op jit(solution)/shard_map/all_gather | solution.py:163
  12.2 189.1 %all-gather.10.cloned.1.call-start = ((), (), s32[]{:S(2)}) async-start(), calls=%async_computation.7 | async-start | bytes 7077888 | tf_op jit(solution)/shard_map/all_gather | solution.py:164
  16.0 206.8 %all-gather.12.cloned.1.call-start = ((), (), s32[]{:S(2)}) async-start(), calls=%async_computation.8 | async-start | bytes 3538944 | tf_op jit(solution)/shard_map/all_gather | solution.py:165
  19.0 601.4 %reduce-scatter.14.cloned.1.call-start = ((), (), s32[]{:S(2)}) async-start(), calls=%async_computation.12 | async-start | bytes 3538944 | tf_op jit(solution)/shard_map/reduce_scatter | solution.py:353
  21.0 73.6 %copy-start.60 = (f32[1,4,2,128]{3,1,2,0:T(4,128)}, f32[1,4,2,128]{3,1,2,0:T(4,128)S(1)}, u32[]{:S(2)}) copy-start(f32[1,4,2,128]{3,1,2,0:T(4,128)S(1)} %copy.277) | copy-start | bytes 12292
  36.4 56.8 %copy-start.55 = (f32[768]{0:T(1024)}, f32[768]{0:T(1024)S(1)}, u32[]{:S(2)}) copy-start(f32[768]{0:T(1024)S(1)} %get-tuple-element.567) | copy-start | bytes 9220
  36.4 126.7 %copy-start.68 = (f32[768]{0:T(1024)}, f32[768]{0:T(1024)S(1)}, u32[]{:S(2)}) copy-start(f32[768]{0:T(1024)S(1)} %get-tuple-element.566) | copy-start | bytes 9220
  244.8 375.6 %reduce-scatter.10.cloned.1.call-start = ((), (), s32[]{:S(2)}) async-start(), calls=%async_computation.10 | async-start | bytes 5308416 | tf_op jit(solution)/shard_map/reduce_scatter | solution.py:351
  267.9 71.1 %copy-start.67 = (f32[1024]{0:T(1024)S(1)}, f32[1024]{0:T(1024)}, u32[]{:S(2)}) copy-start(f32[1024]{0:T(1024)} %copy-done.66) | copy-start | bytes 12292
  267.9 71.1 %copy-start.69 = (f32[768]{0:T(1024)S(1)}, f32[768]{0:T(1024)}, u32[]{:S(2)}) copy-start(f32[768]{0:T(1024)} %copy-done.68) | copy-start | bytes 9220
  355.9 264.4 %reduce-scatter.8.cloned.1.call-start = ((), (), s32[]{:S(2)}) async-start(), calls=%async_computation.9 | async-start | bytes 5308416 | tf_op jit(solution)/shard_map/reduce_scatter | solution.py:350
  487.6 132.8 %reduce-scatter.12.cloned.1.call-start = ((), (), s32[]{:S(2)}) async-start(), calls=%async_computation.11 | async-start | bytes 7077888 | tf_op jit(solution)/shard_map/reduce_scatter | solution.py:352
  502.0 148.5 %reduce-scatter.16.cloned.1.call-start = ((), (), s32[]{:S(2)}) async-start(), calls=%async_computation.13 | async-start | bytes 442368
  560.1 59.6 %copy-start.79 = (f32[32,12]{0,1:T(8,128)S(1)}, f32[32,12]{0,1:T(8,128)}, u32[]{:S(2)}) copy-start(f32[32,12]{0,1:T(8,128)} %param.51) | copy-start | bytes 4612
  579.0 41.4 %copy-start.28 = (bf16[2,512,768]{1,2,0:T(8,128)(2,1)S(1)}, bf16[2,512,768]{1,2,0:T(8,128)(2,1)}, u32[]{:S(2)}) copy-start(bf16[2,512,768]{1,2,0:T(8,128)(2,1)} %get-tuple-element.264) | copy-start | bytes 4718596
  619.7 107.2 %all-reduce.4.cloned.1.call-start = ((), (), s32[]{:S(2)}) async-start(), calls=%async_computation.14 | async-start | bytes 4718592 | tf_op jit(solution)/shard_map/psum | solution.py:357
  731.5 37.7 %copy-start.38 = (f32[4,96,768]{2,1,0:T(8,128)S(1)}, f32[4,96,768]{2,1,0:T(8,128)}, u32[]{:S(2)}) copy-start(f32[4,96,768]{2,1,0:T(8,128)} %param.37) | copy-start | bytes 3538948
  733.2 40.1 %copy-start.31 = (f32[2,96,2048]{2,1,0:T(8,128)}, f32[2,96,2048]{2,1,0:T(8,128)S(1)}, u32[]{:S(2)}) copy-start(f32[2,96,2048]{2,1,0:T(8,128)S(1)} %get-tuple-element.676) | copy-start | bytes 4718596
  733.9 39.4 %copy-start.82 = (f32[256]{0:T(256)}, f32[256]{0:T(256)S(1)}, u32[]{:S(2)}) copy-start(f32[256]{0:T(256)S(1)} %get-tuple-element.672) | copy-start | bytes 3076
  734.0 39.3 %copy-start.83 = (f32[2,96]{1,0:T(2,128)}, f32[2,96]{1,0:T(2,128)S(1)}, u32[]{:S(2)}) copy-start(f32[2,96]{1,0:T(2,128)S(1)} %get-tuple-element.675) | copy-start | bytes 2308
  734.2 39.1 %copy-start.77 = (f32[4,96]{1,0:T(4,128)}, f32[4,96]{1,0:T(4,128)S(1)}, u32[]{:S(2)}) copy-start(f32[4,96]{1,0:T(4,128)S(1)} %get-tuple-element.678) | copy-start | bytes 4612
  734.2 39.1 %copy-start.78 = (f32[4,96]{1,0:T(4,128)}, f32[4,96]{1,0:T(4,128)S(1)}, u32[]{:S(2)}) copy-start(f32[4,96]{1,0:T(4,128)S(1)} %get-tuple-element.724) | copy-start | bytes 4612
  (104 other events, 719.8 us)
Sparse Core Ops, SparseCore 0:
  10.7 54.4 all-gather.5
  67.3 50.4 all-gather.7
  120.0 63.5 all-gather.9
  185.7 37.0 all-gather.11
  244.9 39.2 reduce-scatter.13
  356.1 54.0 reduce-scatter.9
  487.7 54.0 reduce-scatter.7
  544.1 69.2 reduce-scatter.11
  619.8 30.6 reduce-scatter.15
  654.0 72.7 all-reduce.3

commit v2 on v0

v2 whole, which is shorter than its diff:
```python
import functools
import math

import jax
import jax.numpy as jnp
from jax import lax
from jax.experimental import pallas as pl
from jax.experimental.pallas import tpu as pltpu
from jax.sharding import PartitionSpec as P

H = 12
DH = 64
BUCKETS = 32
DECAY_RATE = 0.8
STEP_RATE = 0.2
TINY_TERM = 1e-30
EXACT_ARITHMETIC = lax.Precision.HIGHEST
PAIR = 2 * DH
GROUP = 4 * DH
HIDDEN = -1e30
VMEM_BYTES = 60 * 1024 * 1024
LOW = jnp.bfloat16
WIDE = jnp.float32


def nn(left, right):
    return lax.dot_general(left, right, (((1,), (0,)), ((), ())), preferred_element_type=WIDE)


def nt(left, right):
    return lax.dot_general(left, right, (((1,), (1,)), ((), ())), preferred_element_type=WIDE)


def tn(left, right):
    return lax.dot_general(left, right, (((0,), (0,)), ((), ())), preferred_element_type=WIDE)


def rms_rate(rows):
    return lax.rsqrt(jnp.mean(rows * rows, axis=-1, keepdims=True) + 1e-06)


def three_parts(column):
    high = column.astype(LOW)
    rest = column - high.astype(WIDE)
    middle = rest.astype(LOW)
    low = (rest - middle.astype(WIDE)).astype(LOW)
    return high, middle, low


def chunks(total, size):
    return [(at, min(size, total - at)) for at in range(0, total, size)]


def lanes(rows):
    return lax.broadcasted_iota(jnp.int32, (rows, PAIR), 1)


def own_lanes(rows, side):
    lane = lanes(rows)
    return (lane >= DH * side) & (lane < DH * (side + 1))


def key_extras(rows, side, length):
    lane = lanes(rows) - DH * (1 - side)
    dead = lax.broadcasted_iota(jnp.int32, (rows, PAIR), 0) >= length
    mask = jnp.where(dead, HIDDEN, 0.0)
    return jnp.where(
        (lane >= 0) & (lane < 3), 1.0, jnp.where(lane == 3, mask, 0.0)
    ).astype(LOW)


def row_extras(rows, side, column, last):
    lane = lanes(rows) - DH * (1 - side)
    high, middle, low = three_parts(column)
    wide = lambda part: jnp.broadcast_to(part.astype(WIDE), (rows, PAIR))
    return jnp.where(
        lane == 0,
        wide(high),
        jnp.where(
            lane == 1, wide(middle), jnp.where(lane == 2, wide(low), jnp.where(lane == 3, last, 0.0))
        ),
    ).astype(LOW)


def forward_body(causal, seq_count, length_ref, wave_ref, bias_ref, q_ref, k_ref, v_ref, mix_ref, total_ref, group):
    rows = q_ref.shape[0] // seq_count
    keys = k_ref.shape[0] // seq_count
    block = 256
    for pair in range(2):
        at = pair * PAIR
        for side in range(2):
            head = 2 * pair + side
            if causal:
                wave = wave_ref[pl.ds(group * 4 + head, 1), :]
                spread = pltpu.roll(
                    jnp.broadcast_to(wave, (rows, keys)), 0, 1, stride=1, stride_axis=0
                )
                row = lax.broadcasted_iota(jnp.int32, (rows, keys), 0)
                column = lax.broadcasted_iota(jnp.int32, (rows, keys), 1)
                bias_ref[side] = jnp.where(column <= row, spread, HIDDEN)
        for seq in range(seq_count):
            outs = []
            for side in range(2):
                own_q = own_lanes(rows, side)
                own_k = own_lanes(keys, side)
                query = jnp.where(
                    own_q,
                    q_ref[seq * rows : (seq + 1) * rows, at : at + PAIR],
                    (lanes(rows) == DH * (1 - side) + 3).astype(LOW),
                )
                key = jnp.where(
                    own_k,
                    k_ref[seq * keys : (seq + 1) * keys, at : at + PAIR],
                    key_extras(keys, side, length_ref[seq]),
                )
                value = jnp.where(
                    own_k,
                    v_ref[seq * keys : (seq + 1) * keys, at : at + PAIR],
                    jnp.ones((), LOW),
                )
                parts = []
                for start in range(0, rows, block):
                    span = start + block if causal else keys
                    scores = nt(query[start : start + block], key[:span])
                    if causal:
                        scores = scores + bias_ref[side, start : start + block, :span]
                    top = jnp.max(scores, axis=1, keepdims=True)
                    weight = jnp.exp(scores - top)
                    out = nn(weight.astype(LOW), value[:span])
                    total = out[:, DH * (1 - side) : DH * (1 - side) + 1]
                    parts.append(out * (1.0 / total))
                    spot = pl.ds(seq * rows + start, block)
                    lane = lanes(block)
                    seen = total_ref[spot, :] if (pair or side) else jnp.zeros((block, PAIR), WIDE)
                    total_ref[spot, :] = jnp.where(
                        lane == 2 * pair + side, top + jnp.log(total), seen
                    )
                outs.append(jnp.concatenate(parts, axis=0))
            mix_ref[seq * rows : (seq + 1) * rows, at : at + PAIR] = jnp.where(
                own_lanes(rows, 0), outs[0], outs[1]
            ).astype(LOW)


def forward_kernel(
    causal, seq_count, length_ref, x_ref, source_ref, gain_ref, wq_ref, wk_ref, wv_ref, wo_ref, wave_ref,
    q_ref, k_ref, v_ref, mix_ref, total_ref, after_ref, normed, bias,
):
    group = pl.program_id(0)

    @pl.when(group == 0)
    def _():
        for at, size in chunks(x_ref.shape[0], 256):
            rows = x_ref[at : at + size, :].astype(WIDE)
            normed[at : at + size, :] = (rows * rms_rate(rows) * gain_ref[...]).astype(LOW)
            after_ref[at : at + size, :] = rows

    source = normed if causal else source_ref
    q_ref[...] = nn(normed[...], wq_ref[...]).astype(LOW)
    k_ref[...] = nn(source[...], wk_ref[...]).astype(LOW)
    v_ref[...] = nn(source[...], wv_ref[...]).astype(LOW)
    forward_body(causal, seq_count, length_ref, wave_ref, bias, q_ref, k_ref, v_ref, mix_ref, total_ref, group)
    after_ref[...] += nn(mix_ref[...], wo_ref[...])


def weight_specs(width):
    across = lambda at: pl.BlockSpec((None, width, GROUP), lambda g, at=at: (at, 0, g))
    return [across(0), across(1), across(2), pl.BlockSpec((None, GROUP, width), lambda g: (3, g, 0))]


def whole(shape):
    return pl.BlockSpec(shape, lambda g: (0,) * len(shape))


def columns(rows):
    return pl.BlockSpec((rows, GROUP), lambda g: (0, g))


def attention_forward(causal, x, source, lengths, gain, weights, wave):
    row_count, width = x.shape
    seq_count = lengths.shape[0]
    source_rows = row_count if causal else source.shape[0]
    length = row_count // seq_count
    groups = width // GROUP
    low = lambda rows: jax.ShapeDtypeStruct((rows, width), LOW)
    args = [lengths, x, source, gain, weights, weights, weights, weights, wave]
    return pl.pallas_call(
        functools.partial(forward_kernel, causal, seq_count),
        grid=(groups,),
        in_specs=[
            pl.BlockSpec(memory_space=pltpu.SMEM),
            whole(x.shape),
            whole(source.shape),
            whole(gain.shape),
            *weight_specs(width),
            whole(wave.shape),
        ],
        out_specs=[
            columns(row_count),
            columns(source_rows),
            columns(source_rows),
            columns(row_count),
            pl.BlockSpec((None, row_count, PAIR), lambda g: (g, 0, 0)),
            whole((row_count, width)),
        ],
        out_shape=[
            low(row_count),
            low(source_rows),
            low(source_rows),
            low(row_count),
            jax.ShapeDtypeStruct((groups, row_count, PAIR), WIDE),
            jax.ShapeDtypeStruct((row_count, width), WIDE),
        ],
        scratch_shapes=[
            pltpu.VMEM((row_count, width), LOW),
            pltpu.VMEM((2, length, length) if causal else (1, 8, PAIR), WIDE),
        ],
        compiler_params=pltpu.CompilerParams(vmem_limit_bytes=VMEM_BYTES),
        name="self_forward" if causal else "cross_forward",
    )(*args)


def gelu_parts(gate):
    root = 0.7978845608028654
    square = gate * gate
    inner = jnp.tanh(root * gate * (1.0 + 0.044715 * square))
    half = 0.5 * (1.0 + inner)
    value = gate * half
    slope = half + 0.5 * gate * (1.0 - inner * inner) * (root * (1.0 + 3 * 0.044715 * square))
    return value, slope


def rms_back(rows, gain, grad):
    rate = rms_rate(rows)
    scaled = rows * rate
    low = grad * gain
    grad_rows = rate * (low - scaled * jnp.mean(scaled * low, axis=-1, keepdims=True))
    return grad_rows, jnp.sum(grad * scaled, axis=0, keepdims=True)


def feed_kernel(
    seq_count, length_ref, after_ref, out_grad_ref, gain_ref, wg_ref, wu_ref, wd_ref,
    layer_ref, grad_cross_ref, dwg_ref, dwu_ref, dwd_ref, dgain_ref,
    normed, normed_t, down, out_total, grad_total,
):
    step = pl.program_id(0)
    row_count = after_ref.shape[0]
    length = row_count // seq_count

    def live(at, size):
        position = lax.broadcasted_iota(jnp.int32, (size, 1), 0) + (at % length)
        return (position < length_ref[at // length]).astype(WIDE)

    @pl.when(step == 0)
    def _():
        for at, size in chunks(row_count, 256):
            rows = after_ref[at : at + size, :]
            low = (rows * rms_rate(rows) * gain_ref[...]).astype(LOW)
            normed[at : at + size, :] = low
            normed_t[:, at : at + size] = low.T
            down[at : at + size, :] = (
                out_grad_ref[at : at + size, :].astype(WIDE) * live(at, size)
            ).astype(LOW)
            out_total[at : at + size, :] = rows
            grad_total[at : at + size, :] = jnp.zeros((size, rows.shape[1]), WIDE)

    gate = nn(normed[...], wg_ref[...])
    up = nn(normed[...], wu_ref[...])
    value, slope = gelu_parts(gate)
    hidden = (value * up).astype(LOW)
    out_total[...] += nn(hidden, wd_ref[...])
    grad_hidden = nt(down[...], wd_ref[...])
    dwd_ref[...] = tn(hidden, down[...]).astype(LOW)
    grad_gate = (grad_hidden * up * slope).astype(LOW)
    grad_up = (grad_hidden * value).astype(LOW)
    dwg_ref[...] = nn(normed_t[...], grad_gate).astype(LOW)
    dwu_ref[...] = nn(normed_t[...], grad_up).astype(LOW)
    grad_total[...] += nt(grad_gate, wg_ref[...]) + nt(grad_up, wu_ref[...])

    @pl.when(step == pl.num_programs(0) - 1)
    def _():
        dgain = jnp.zeros(dgain_ref.shape, WIDE)
        for at, size in chunks(row_count, 256):
            part = slice(at, at + size)
            layer_ref[part, :] = (out_total[part, :] * live(at, size)).astype(LOW)
            grad_rows, gain_part = rms_back(after_ref[part, :], gain_ref[...], grad_total[part, :])
            dgain = dgain + gain_part
            grad_cross_ref[part, :] = (
                out_grad_ref[part, :].astype(WIDE) * live(at, size) + grad_rows
            )
        dgain_ref[...] = dgain


def feed_forward_both(after, out_grad, lengths, gain, w_in, w_out, block=256):
    row_count, width = after.shape
    hidden = w_out.shape[0]
    seq_count = lengths.shape[0]
    wide = pl.BlockSpec((None, width, block), lambda g: (0, 0, g))
    wide_up = pl.BlockSpec((None, width, block), lambda g: (1, 0, g))
    tall = pl.BlockSpec((block, width), lambda g: (g, 0))
    flat = pl.BlockSpec((width, block), lambda g: (0, g))
    return pl.pallas_call(
        functools.partial(feed_kernel, seq_count),
        grid=(hidden // block,),
        in_specs=[
            pl.BlockSpec(memory_space=pltpu.SMEM),
            whole(after.shape),
            whole(out_grad.shape),
            whole(gain.shape),
            wide,
            wide_up,
            tall,
        ],
        out_specs=[whole(after.shape), whole(after.shape), flat, flat, tall, whole((1, width))],
        out_shape=[
            jax.ShapeDtypeStruct((row_count, width), LOW),
            jax.ShapeDtypeStruct((row_count, width), WIDE),
            jax.ShapeDtypeStruct((width, hidden), LOW),
            jax.ShapeDtypeStruct((width, hidden), LOW),
            jax.ShapeDtypeStruct((hidden, width), LOW),
            jax.ShapeDtypeStruct((1, width), WIDE),
        ],
        scratch_shapes=[
            pltpu.VMEM((row_count, width), LOW),
            pltpu.VMEM((width, row_count), LOW),
            pltpu.VMEM((row_count, width), LOW),
            pltpu.VMEM((row_count, width), WIDE),
            pltpu.VMEM((row_count, width), WIDE),
        ],
        compiler_params=pltpu.CompilerParams(vmem_limit_bytes=VMEM_BYTES),
        name="feed_forward_both",
    )(lengths, after, out_grad, gain, w_in, w_in, w_out)


def backward_kernel(
    causal, seq_count, length_ref, x_ref, source_ref, grad_ref, gain_ref, wq_ref, wk_ref, wv_ref, wo_ref, wave_ref,
    q_ref, k_ref, v_ref, mix_ref, total_ref,
    grad_x_ref, gk_out_ref, gv_out_ref, dwq_ref, dwk_ref, dwv_ref, dwo_ref, dgain_ref, dist_ref,
    normed_t, source_t, branch, grad_mix, gq, bias, score_sum, grad_total,
):
    group = pl.program_id(0)
    row_count = x_ref.shape[0]
    rows = q_ref.shape[0] // seq_count
    keys = k_ref.shape[0] // seq_count
    block = 256

    @pl.when(group == 0)
    def _():
        for at, size in chunks(row_count, 256):
            value = x_ref[at : at + size, :].astype(WIDE)
            low = (value * rms_rate(value) * gain_ref[...]).astype(LOW)
            normed_t[:, at : at + size] = low.T
            branch[at : at + size, :] = grad_ref[at : at + size, :].astype(LOW)
            grad_total[at : at + size, :] = jnp.zeros((size, value.shape[1]), WIDE)
        if not causal:
            for at, size in chunks(source_ref.shape[0], 256):
                source_t[:, at : at + size] = source_ref[at : at + size, :].T

    grad_mix[...] = nt(branch[...], wo_ref[...]).astype(LOW)
    dwo_ref[...] = tn(mix_ref[...], branch[...]).astype(LOW)

    for pair in range(2):
        at = pair * PAIR
        if causal:
            for side in range(2):
                head = 2 * pair + side
                wave = wave_ref[pl.ds(group * 4 + head, 1), :]
                spread = pltpu.roll(
                    jnp.broadcast_to(wave, (keys, rows)), 0, 1, stride=1, stride_axis=0
                )
                row = lax.broadcasted_iota(jnp.int32, (keys, rows), 0)
                column = lax.broadcasted_iota(jnp.int32, (keys, rows), 1)
                bias[side] = jnp.where(column >= row, spread, HIDDEN)
        for seq in range(seq_count):
            span_q = slice(seq * rows, (seq + 1) * rows)
            span_k = slice(seq * keys, (seq + 1) * keys)
            sides = []
            for side in range(2):
                head = 2 * pair + side
                own_q = own_lanes(rows, side)
                own_k = own_lanes(keys, side)
                total = jnp.sum(
                    jnp.where(lanes(rows) == head, total_ref[span_q, :], 0.0), axis=1, keepdims=True
                )
                grad_low = grad_mix[span_q, at : at + PAIR]
                product = grad_low.astype(WIDE) * mix_ref[span_q, at : at + PAIR].astype(WIDE)
                delta = jnp.sum(jnp.where(own_q, product, 0.0), axis=1, keepdims=True)
                query = jnp.where(
                    own_q, q_ref[span_q, at : at + PAIR], row_extras(rows, side, -total, 1.0)
                )
                grad_out = jnp.where(own_q, grad_low, row_extras(rows, side, -delta, 0.0))
                key = jnp.where(
                    own_k,
                    k_ref[span_k, at : at + PAIR],
                    key_extras(keys, side, length_ref[seq]),
                )
                value = jnp.where(own_k, v_ref[span_k, at : at + PAIR], jnp.ones((), LOW))
                grad_query = []
                grad_key = None
                grad_value = None
                for start in range(0, rows, block):
                    span = start + block if causal else keys
                    scores = nt(key[:span], query[start : start + block])
                    if causal:
                        scores = scores + bias[side, :span, start : start + block]
                    weight = jnp.exp(scores)
                    low = weight.astype(LOW)
                    grad_weight = nt(value[:span], grad_out[start : start + block])
                    grad_score = (weight * grad_weight).astype(LOW)
                    if causal:
                        if seq == 0:
                            score_sum[side, :span, start : start + block] = grad_score.astype(WIDE)
                        else:
                            score_sum[side, :span, start : start + block] += grad_score.astype(WIDE)
                    key_part = nn(grad_score, query[start : start + block])
                    value_part = nn(low, grad_out[start : start + block])
                    grad_query.append(tn(grad_score, key[:span]))
                    if causal and start == 0 and rows > block:
                        rest = jnp.zeros((keys - span, PAIR), WIDE)
                        key_part = jnp.concatenate([key_part, rest], axis=0)
                        value_part = jnp.concatenate([value_part, rest], axis=0)
                    grad_key = key_part if grad_key is None else grad_key + key_part
                    grad_value = value_part if grad_value is None else grad_value + value_part
                sides.append((jnp.concatenate(grad_query, axis=0), grad_key, grad_value))
            pick_q = own_lanes(rows, 0)
            pick_k = own_lanes(keys, 0)
            gq[span_q, at : at + PAIR] = jnp.where(pick_q, sides[0][0], sides[1][0]).astype(LOW)
            gk_out_ref[span_k, at : at + PAIR] = jnp.where(pick_k, sides[0][1], sides[1][1]).astype(LOW)
            gv_out_ref[span_k, at : at + PAIR] = jnp.where(pick_k, sides[0][2], sides[1][2]).astype(LOW)
        if causal:
            for side in range(2):
                head = 2 * pair + side
                row = lax.broadcasted_iota(jnp.int32, (keys, rows), 0)
                column = lax.broadcasted_iota(jnp.int32, (keys, rows), 1)
                held = jnp.where(column >= row, score_sum[side], 0.0)
                while held.shape[0] > 1:
                    half = held.shape[0] // 2
                    held = held[:half] + pltpu.roll(held[half:], rows - half, 1)
                dist_ref[pl.ds(group * 4 + head, 1), :] = held

    if causal:
        source_t = normed_t
    dwq_ref[...] = nn(normed_t[...], gq[...]).astype(LOW)
    dwk_ref[...] = nn(source_t[...], gk_out_ref[...]).astype(LOW)
    dwv_ref[...] = nn(source_t[...], gv_out_ref[...]).astype(LOW)
    update = nt(gq[...], wq_ref[...])
    if causal:
        update = update + nt(gk_out_ref[...], wk_ref[...]) + nt(gv_out_ref[...], wv_ref[...])
    grad_total[...] += update

    @pl.when(group == pl.num_programs(0) - 1)
    def _():
        dgain = jnp.zeros(dgain_ref.shape, WIDE)
        for at, size in chunks(row_count, 256):
            part = slice(at, at + size)
            grad_rows, gain_part = rms_back(
                x_ref[part, :].astype(WIDE), gain_ref[...], grad_total[part, :]
            )
            dgain = dgain + gain_part
            grad_x_ref[part, :] = grad_ref[part, :] + grad_rows
        dgain_ref[...] = dgain


def attention_backward(causal, x, source, grad, lengths, gain, weights, wave, kept):
    row_count, width = x.shape
    seq_count = lengths.shape[0]
    source_rows = row_count if causal else source.shape[0]
    length = row_count // seq_count
    groups = width // GROUP
    low = lambda rows: jax.ShapeDtypeStruct((rows, width), LOW)
    grad_columns = pl.BlockSpec((width, GROUP), lambda g: (0, g))
    grad_rows = pl.BlockSpec((GROUP, width), lambda g: (g, 0))
    square = jax.ShapeDtypeStruct((width, width), LOW)
    score = (2, length, length) if causal else (1, 8, PAIR)
    return pl.pallas_call(
        functools.partial(backward_kernel, causal, seq_count),
        grid=(groups,),
        in_specs=[
            pl.BlockSpec(memory_space=pltpu.SMEM),
            whole(x.shape),
            whole(source.shape),
            whole(grad.shape),
            whole(gain.shape),
            *weight_specs(width),
            whole(wave.shape),
            columns(row_count),
            columns(source_rows),
            columns(source_rows),
            columns(row_count),
            pl.BlockSpec((None, row_count, PAIR), lambda g: (g, 0, 0)),
        ],
        out_specs=[
            whole((row_count, width)),
            columns(source_rows),
            columns(source_rows),
            grad_columns,
            grad_columns,
            grad_columns,
            grad_rows,
            whole((1, width)),
            whole(wave.shape),
        ],
        out_shape=[
            jax.ShapeDtypeStruct((row_count, width), WIDE),
            low(source_rows),
            low(source_rows),
            square,
            square,
            square,
            square,
            jax.ShapeDtypeStruct((1, width), WIDE),
            jax.ShapeDtypeStruct(wave.shape, WIDE),
        ],
        scratch_shapes=[
            pltpu.VMEM((width, row_count), LOW),
            pltpu.VMEM((width, source_rows) if not causal else (16, PAIR), LOW),
            pltpu.VMEM((row_count, width), LOW),
            pltpu.VMEM((row_count, GROUP), LOW),
            pltpu.VMEM((row_count, GROUP), LOW),
            pltpu.VMEM(score, WIDE),
            pltpu.VMEM(score, WIDE),
            pltpu.VMEM((row_count, width), WIDE),
        ],
        compiler_params=pltpu.CompilerParams(vmem_limit_bytes=VMEM_BYTES),
        name="self_backward" if causal else "cross_backward",
    )(lengths, x, source, grad, gain, weights, weights, weights, weights, wave, *kept)


def memory_kernel(gk_ref, gv_ref, wk_ref, wv_ref, out_ref):
    out_ref[...] = nt(gk_ref[...], wk_ref[...]) + nt(gv_ref[...], wv_ref[...])


def memory_gradient(grad_key, grad_value, weights):
    rows, width = grad_key.shape
    block = 256
    rowwise = pl.BlockSpec((block, width), lambda g: (g, 0))
    matrix = lambda at: pl.BlockSpec((None, width, width), lambda g: (at, 0, 0))
    return pl.pallas_call(
        memory_kernel,
        grid=(rows // block,),
        in_specs=[rowwise, rowwise, matrix(1), matrix(2)],
        out_specs=rowwise,
        out_shape=jax.ShapeDtypeStruct((rows, width), WIDE),
        compiler_params=pltpu.CompilerParams(vmem_limit_bytes=VMEM_BYTES),
        name="memory_gradient",
    )(grad_key, grad_value, weights, weights)


def row_parts(gradient, weight, row_state):
    squares = gradient * gradient + TINY_TERM
    row_moment = DECAY_RATE * row_state + (1.0 - DECAY_RATE) * jnp.mean(squares, axis=2)
    return (
        row_moment,
        jnp.sum(squares, axis=1),
        jnp.sum(row_moment, axis=1),
        jnp.sum(weight * weight, axis=(1, 2)),
    )


def column_step(gradient, row_moment, col_state, col_sum, row_sum, whole_rows):
    col_moment = DECAY_RATE * col_state + (1.0 - DECAY_RATE) * col_sum / whole_rows
    row_mean = row_sum / whole_rows
    direction = gradient * lax.rsqrt(
        row_moment[:, :, None] * col_moment[:, None, :] / row_mean[:, None, None]
    )
    return (direction, col_moment)


def apply_optimizer_update(weight, direction, weight_square):
    step_size = STEP_RATE * jnp.sqrt(weight_square + 1e-06)
    ratio = step_size.reshape((-1,) + (1,) * (weight.ndim - 1))
    return weight - ratio * direction


def per_device(
    dec_in,
    memory,
    out_grad,
    dec_len,
    enc_len,
    buckets,
    self_weight,
    cross_weight,
    ffn_in,
    ffn_out,
    gains,
    table,
    self_rows,
    self_cols,
    cross_rows,
    cross_cols,
    in_rows,
    in_cols,
    out_rows,
    out_cols,
    gain_moment,
    table_moment,
):
    seq_count, seq_length, model_width = dec_in.shape
    mem_length = memory.shape[1]
    row_count = seq_count * seq_length
    hidden_width = ffn_in.shape[2]
    w_self = lax.all_gather(self_weight.astype(LOW), "fsdp", axis=1, tiled=True)
    gain_full = lax.all_gather(gains.astype(LOW), "fsdp", axis=1, tiled=True).astype(WIDE)
    w_cross = lax.all_gather(cross_weight.astype(LOW), "fsdp", axis=1, tiled=True)
    w_in = lax.all_gather(ffn_in.astype(LOW), "fsdp", axis=1, tiled=True)
    w_out = lax.all_gather(ffn_out.astype(LOW), "fsdp", axis=0, tiled=True)
    col_whole = (self_cols, cross_cols, in_cols, out_cols)

    bucket_mask = (buckets[None, :] == jnp.arange(BUCKETS)[:, None]).astype(WIDE)
    by_distance = jnp.sum(table.T[:, :, None] * bucket_mask[None], axis=1)
    by_distance = jnp.pad(by_distance, ((0, 16 - H), (0, 0)))
    backwards = jnp.roll(by_distance[:, ::-1], 1, axis=1)
    no_bias = jnp.zeros((8, PAIR), WIDE)
    no_source = jnp.zeros((16, PAIR), LOW)

    dec_rows = dec_in.reshape(row_count, model_width)
    mem_rows = memory.reshape(seq_count * mem_length, model_width)
    grad_rows = out_grad.reshape(row_count, model_width)
    *kept_one, after_self = attention_forward(
        True, dec_rows, no_source, dec_len, gain_full[0:1], w_self, backwards
    )
    *kept_two, after_cross = attention_forward(
        False, after_self, mem_rows, enc_len, gain_full[1:2], w_cross, no_bias
    )
    layer_out, grad_cross, grad_wg, grad_wu, grad_wd, gain_three = feed_forward_both(
        after_cross, grad_rows, dec_len, gain_full[2:3], w_in, w_out
    )
    grad_self, grad_k_two, grad_v_two, *cross_parts, gain_two, _ = attention_backward(
        False, after_self, mem_rows, grad_cross, enc_len, gain_full[1:2], w_cross, no_bias, kept_two
    )
    memory_grad = memory_gradient(grad_k_two, grad_v_two, w_cross)
    input_grad, _, _, *self_parts, gain_one, dist_grad = attention_backward(
        True, dec_rows, no_source, grad_self, dec_len, gain_full[0:1], w_self, by_distance, kept_one
    )
    layer_out = layer_out.reshape(dec_in.shape)
    input_grad = input_grad.reshape(dec_in.shape)
    memory_grad = memory_grad.reshape(memory.shape)
    table_part = jnp.sum(bucket_mask[:, None, :] * dist_grad[None, :H, :], axis=2)

    owned = (
        lax.psum_scatter(jnp.stack(self_parts), "fsdp", scatter_dimension=1, tiled=True),
        lax.psum_scatter(jnp.stack(cross_parts), "fsdp", scatter_dimension=1, tiled=True),
        lax.psum_scatter(jnp.stack([grad_wg, grad_wu]), "fsdp", scatter_dimension=1, tiled=True),
        lax.psum_scatter(grad_wd, "fsdp", scatter_dimension=0, tiled=True),
    )
    owned = [lax.psum(member, "rep").astype(WIDE) for member in owned]
    small = jnp.concatenate(
        [gain_one.reshape(-1), gain_two.reshape(-1), gain_three.reshape(-1), table_part.reshape(-1)]
    )
    small = lax.psum(small, ("rep", "fsdp"))
    gain_total = small[: 3 * model_width].reshape(3, model_width)
    gain_mine = lax.dynamic_slice_in_dim(
        gain_total, lax.axis_index("fsdp") * gains.shape[1], gains.shape[1], axis=1
    )
    table_total = small[3 * model_width :].reshape(BUCKETS, H)
    owned.append(gain_mine)
    fsdp_count = lax.axis_size("fsdp")
    grad_factor = 1.0 / math.sqrt(row_count * lax.axis_size("rep") * fsdp_count)
    self_grad, cross_grad, ffn_in_grad, feedforward_output_gradient, gains_grad = [
        member * grad_factor for member in owned
    ]
    table_grad = table_total * grad_factor
    batches = [
        (self_grad, self_weight, self_rows, col_whole[0]),
        (cross_grad, cross_weight, cross_rows, col_whole[1]),
        (ffn_in_grad, ffn_in, in_rows, col_whole[2]),
        (feedforward_output_gradient[None], ffn_out[None], out_rows[None], col_whole[3][None]),
    ]
    prepared = [
        row_parts(gradient, weight, row_state) for gradient, weight, row_state, col_state in batches
    ]
    gain_state = DECAY_RATE * gain_moment + (1.0 - DECAY_RATE) * (
        gains_grad * gains_grad + TINY_TERM
    )
    gain_direction = gains_grad * lax.rsqrt(gain_state)
    local_sums = []
    for parts in prepared:
        local_sums = local_sums + [parts[1], parts[2], parts[3]]
    local_sums = local_sums + [jnp.sum(gains * gains, axis=1)]
    totals = lax.psum(tuple(local_sums), "fsdp")
    updated = []
    col_results = []
    for place_index in range(len(batches)):
        gradient, weight, row_state, col_state = batches[place_index]
        whole_rows = weight.shape[1] * fsdp_count
        direction, col_moment = column_step(
            gradient,
            prepared[place_index][0],
            col_state,
            totals[3 * place_index],
            totals[3 * place_index + 1],
            whole_rows,
        )
        count_all = whole_rows * weight.shape[2]
        updated.append(
            apply_optimizer_update(weight, direction, totals[3 * place_index + 2] / count_all)
        )
        col_results.append(col_moment)
    gain_width = gains.shape[1] * fsdp_count
    gain_offset = 3 * len(batches)
    new_gains = apply_optimizer_update(gains, gain_direction, totals[gain_offset] / gain_width)
    table_state = DECAY_RATE * table_moment + (1.0 - DECAY_RATE) * (
        table_grad * table_grad + TINY_TERM
    )
    table_direction = table_grad * lax.rsqrt(table_state)
    new_table = apply_optimizer_update(table, table_direction, jnp.mean(table * table))
    return (
        layer_out,
        input_grad,
        memory_grad,
        self_grad,
        cross_grad,
        ffn_in_grad,
        feedforward_output_gradient,
        gains_grad,
        table_grad,
        updated[0],
        updated[1],
        updated[2],
        updated[3][0],
        new_gains,
        new_table,
        prepared[0][0],
        col_results[0],
        prepared[1][0],
        col_results[1],
        prepared[2][0],
        col_results[2],
        prepared[3][0][0],
        col_results[3][0],
        gain_state,
        table_state,
    )


def solution(mesh):
    placed = (
        P(("rep", "fsdp"), None, None),
        P(("rep", "fsdp"), None, None),
        P(("rep", "fsdp"), None, None),
        P(("rep", "fsdp")),
        P(("rep", "fsdp")),
        P(),
        P(None, "fsdp", None),
        P(None, "fsdp", None),
        P(None, "fsdp", None),
        P("fsdp", None),
        P(None, "fsdp"),
        P(),
        P(None, "fsdp"),
        P(),
        P(None, "fsdp"),
        P(),
        P(None, "fsdp"),
        P(),
        P("fsdp"),
        P(),
        P(None, "fsdp"),
        P(),
    )
    return jax.shard_map(
        per_device,
        mesh=mesh,
        in_specs=placed,
        out_specs=(
            P(("rep", "fsdp"), None, None),
            P(("rep", "fsdp"), None, None),
            P(("rep", "fsdp"), None, None),
            P(None, "fsdp", None),
            P(None, "fsdp", None),
            P(None, "fsdp", None),
            P("fsdp", None),
            P(None, "fsdp"),
            P(),
            P(None, "fsdp", None),
            P(None, "fsdp", None),
            P(None, "fsdp", None),
            P("fsdp", None),
            P(None, "fsdp"),
            P(),
            P(None, "fsdp"),
            P(),
            P(None, "fsdp"),
            P(),
            P(None, "fsdp"),
            P(),
            P("fsdp"),
            P(),
            P(None, "fsdp"),
            P(),
        ),
        check_vma=False,
    )
```

time: 3660 us -> 635 us (0.17)
  local copies, waits for them, and re-layouts: 2960 us -> 6.79 us
  matrix products: 291 us -> 0 us
  Pallas kernels: 0 us -> 199 us
  waiting for transfers between devices: 151 us -> 287 us
  other arithmetic: 141 us -> 36.3 us
    gather x1 -> x0, local copies, waits for them, and re-layouts: 2750 us -> none  [per_device(): pair_bucket = jnp.take(buckets, jnp.maximum(distance, 0)).reshape(-1)]
    dot_general x63 -> x0, matrix products: 291 us -> none  [the longest x11 64.1 us: inner_last(): lax.dot_general(earlier_operand, later_operand, (((1,), (1,)), ((), ())),...]
    pallas_call x0 -> x6, Pallas kernels: none -> 199 us  [the longest x2 90.2 us: attention_backward(): pl.pallas_call(functools.partial(backward_kernel, causal, seq_count), gri...]
    all_gather x4, waiting for transfers between devices: 0.03 us -> 136 us  [the longest x1 65.6 us: per_device(): w_in = lax.all_gather(ffn_in.astype(LOW), 'fsdp', axis=1, tiled=True)]
    unnamed x225 -> x79, local copies, waits for them, and re-layouts: 92.1 us -> 3.92 us
    add x5 -> x1, other arithmetic: 47.7 us -> 0.01 us  [per_device(): DECAY_RATE * table_moment]
    dynamic_slice x36 -> x0, local copies, waits for them, and re-layouts: 46 us -> none  [per_device(): lax.map(self_forward, (by_seq(query_one, seq_length), by_seq(key_one, seq...]
    reduce_scatter x4, waiting for transfers between devices: 77.6 us -> 122 us  [the longest x1 70.5 us: per_device(): lax.psum_scatter(jnp.stack([grad_wg, grad_wu]), 'fsdp', scatter_dimension...]
  transfers between devices with their start and end apart: 10 -> 9, of which waited for: 3 -> 7; matrix products, arithmetic and copies ran while one was open for 91% -> 4% of each run, Pallas kernels for 0% -> 24%
where the time goes in v2:
time: 635 us; the launch traced here: 628 us
  waiting for transfers between devices  287 us (45%)
  Pallas kernels  199 us (31%)
  blocking collectives  82 us (13%)
  other arithmetic  36.3 us (6%)
  between operations  16.9 us (3%)
  local copies, waits for them, and re-layouts  6.79 us (1%)
    pallas_call x2, Pallas kernels, attention_backward(): pl.pallas_call(functools.partial(backward_kernel, causal, seq_count), gri...  90.2 us
    reduce_scatter x1, waiting for transfers between devices, per_device(): lax.psum_scatter(jnp.stack([grad_wg, grad_wu]), 'fsdp', scatter_dimension...  70.5 us
    all_gather x1, waiting for transfers between devices, per_device(): w_in = lax.all_gather(ffn_in.astype(LOW), 'fsdp', axis=1, tiled=True)  65.6 us
    pallas_call x2, Pallas kernels, attention_forward(): pl.pallas_call(functools.partial(forward_kernel, causal, seq_count), grid...  55.1 us
    reduce_scatter x1, waiting for transfers between devices, per_device(): lax.psum_scatter(jnp.stack(self_parts), 'fsdp', scatter_dimension=1, tile...  51.8 us
    pallas_call x1, Pallas kernels, feed_forward_both(): pl.pallas_call(functools.partial(feed_kernel, seq_count), grid=(hidden //...  46.5 us
    psum x1, blocking collectives, per_device(): small = lax.psum(small, ('rep', 'fsdp'))  38.4 us
    all_gather x1, waiting for transfers between devices, per_device(): w_self = lax.all_gather(self_weight.astype(LOW), 'fsdp', axis=1, tiled=True)  34.9 us
  transfers between devices with their start and end apart: 9, of which 7 were waited for; matrix products, arithmetic and copies ran while one was open for 4% of the time, Pallas kernels for 24%

profile of v2, /device:TPU:0, one launch (start us, length us, event | category | flops | bytes accessed | tf_op | source)
XLA Modules:
  0.0 627.7 jit_solution(14833450203087090501)
XLA Ops:
  7.3 2.7 multiply_reduce_fusion.2
  11.1 1.5 multiply_reduce_fusion.3
  14.8 13.6 %all-gather = bf16[8,96,3]{1,2,0:T(4,128)(2,1)S(1)} all-gather(bf16[1,96,3]{1,2,0:T(4,128)(2,1)S(1)} %get-tuple-element.245), channel_id=1, replica_groups=mesh['rep'=4,'fsdp'=8] {'fsdp'}, dimensions={0}, use_global_device_ids=true | all-gather | bytes 5184 | tf_op jit(solution)/shard_map/all_gather | solution.py:603
  29.7 34.9 %all-gather.6.cloned.1.call-done.wq_ref.wk_ref.wv_ref.wo_ref = bf16[4,768,768]{2,1,0:T(8,128)(2,1)} async-done(((bf16[4,96,768]{2,1,0:T(8,128)(2,1)}), bf16[4,768,768]{2,1,0:T(8,128)(2,1)}) %all-gather.6.cloned.1.call-update) | async-done | bytes 4718608 | tf_op jit(solution)/shard_map/all_gather | solution.py:602
  65.2 26.8 %self_forward.1 = (bf16[1024,768]{1,0:T(8,128)(2,1)}, bf16[1024,768]{1,0:T(8,128)(2,1)}, bf16[1024,768]{1,0:T(8,128)(2,1)}, bf16[1024,768]{1,0:T(8,128)(2,1)}, f...) custom-call(s32[2]{0:T(128)} %length_ref.9, bf16[1024,768]{1,0:T(8,128)(2,1)} %bitcast.33, ...), custom_call_target="tpu_custom_call" | custom-call | tf_op jit(solution)/shard_map/self_forward/pallas_call | solution.py:186
  92.0 25.4 %all-gather.8.cloned.1.call-done.wq_ref.wk_ref.wv_ref.wo_ref = bf16[4,768,768]{2,1,0:T(8,128)(2,1)} async-done(((bf16[4,96,768]{2,1,0:T(8,128)(2,1)}), bf16[4,768,768]{2,1,0:T(8,128)(2,1)}) %all-gather.8.cloned.1.call-update) | async-done | bytes 4718608 | tf_op jit(solution)/shard_map/all_gather | solution.py:604
  118.0 28.4 %cross_forward.1 = (bf16[1024,768]{1,0:T(8,128)(2,1)}, bf16[1024,768]{1,0:T(8,128)(2,1)}, bf16[1024,768]{1,0:T(8,128)(2,1)}, bf16[1024,768]{1,0:T(8,128)(2,1)}, ...) custom-call(s32[2]{0:T(128)} %length_ref.8, f32[1024,768]{1,0:T(8,128)} %get-tuple-element.58.x_ref, ...), custom_call_target="tpu_custom_call" | custom-call | tf_op jit(solution)/shard_map/cross_forward/pallas_call | solution.py:186
  146.4 10.4 %all-gather.12.cloned.1.call-done.wd_ref = bf16[2048,768]{1,0:T(8,128)(2,1)} async-done(((bf16[256,768]{1,0:T(8,128)(2,1)}), bf16[2048,768]{1,0:T(8,128)(2,1)}) %all-gather.12.cloned.1.call-update) | async-done | bytes 3145744 | tf_op jit(solution)/shard_map/all_gather | solution.py:606
  156.8 65.6 %all-gather.10.cloned.1.call-done.wg_ref.wu_ref = bf16[2,768,2048]{2,1,0:T(8,128)(2,1)} async-done(((bf16[2,96,2048]{2,1,0:T(8,128)(2,1)}), bf16[2,768,2048]{2,1,0:T(8,128)(2,1)}) %all-gather.10.cloned.1.call-update) | async-done | bytes 6291472 | tf_op jit(solution)/shard_map/all_gather | solution.py:605
  222.4 46.5 %feed_forward_both.1 = (bf16[1024,768]{1,0:T(8,128)(2,1)}, f32[1024,768]{1,0:T(8,128)}, bf16[768,2048]{1,0:T(8,128)(2,1)}, bf16[768,2048]{1,0:T(8,128)(2,1)}, bf...) custom-call(s32[2]{0:T(128)} %length_ref.9, f32[1024,768]{1,0:T(8,128)} %get-tuple-element.59.after_ref, ...), custom_call_target="tpu_custom_call" | custom-call | tf_op jit(solution)/shard_map/feed_forward_both/pallas_call | solution.py:301
  269.0 44.0 %cross_backward.1 = (f32[1024,768]{1,0:T(8,128)}, bf16[1024,768]{1,0:T(8,128)(2,1)}, bf16[1024,768]{1,0:T(8,128)(2,1)}, bf16[768,768]{1,0:T(8,128)(2,1)}, bf16[7...) custom-call(s32[2]{0:T(128)} %length_ref.8, ...), custom_call_target="tpu_custom_call" | custom-call | tf_op jit(solution)/shard_map/cross_backward/pallas_call | solution.py:474
  313.1 4.0 pad_maximum_fusion.2
  317.8 46.1 %self_backward.1 = (f32[1024,768]{1,0:T(8,128)}, bf16[1024,768]{1,0:T(8,128)(2,1)}, bf16[1024,768]{1,0:T(8,128)(2,1)}, bf16[768,768]{1,0:T(8,128)(2,1)}, bf16[76...) custom-call(s32[2]{0:T(128)} %length_ref.9, ...), custom_call_target="tpu_custom_call" | custom-call | tf_op jit(solution)/shard_map/self_backward/pallas_call | solution.py:474
  363.9 4.1 pad_maximum_fusion.1
  368.1 6.2 pad_maximum_fusion
  374.5 51.8 %reduce-scatter.5.cloned.1.call-done = bf16[4,96,768]{2,1,0:T(8,128)(2,1)} async-done(((bf16[4,768,768]{2,1,0:T(8,128)(2,1)}), bf16[4,96,768]{2,1,0:T(8,128)(2,1)}) %reduce-scatter.5.cloned.1.call-update) | async-done | bytes 589840 | tf_op jit(solution)/shard_map/reduce_scatter | solution.py:641
  426.3 70.5 %reduce-scatter.9.cloned.1.call-done = bf16[2,96,2048]{2,1,0:T(8,128)(2,1)} async-done(((bf16[2,768,2048]{2,1,0:T(8,128)(2,1)}), bf16[2,96,2048]{2,1,0:T(8,128)(2,1)}) %reduce-scatter.9.cloned.1.call-update) | async-done | bytes 786448 | tf_op jit(solution)/shard_map/reduce_scatter | solution.py:643
  498.8 38.4 %psum.130 = f32[2688]{0:T(1024)S(1)} all-reduce(f32[2688]{0:T(1024)S(1)} %pad_maximum_fusion.4), channel_id=1, replica_groups=mesh['rep'=4,'fsdp'=8] {'rep','fsdp'}, use_global_device_ids=true, to_apply=%region_10.11 | all-reduce | flops 2688 | bytes 21504 | tf_op jit(solution)/shard_map/psum | solution.py:650
  539.3 6.8 %memory_gradient.1 = f32[1024,768]{1,0:T(8,128)} custom-call(bf16[1024,768]{1,0:T(8,128)(2,1)} %get-tuple-element.74.gk_ref, bf16[1024,768]{1,0:T(8,128)(2,1)} %get-tuple-element.75.gv_ref, bf16[4,768,768]{2,1,0:T(8,128)(2,1)} %all-gather.8.cloned.1.call-done.wq_ref.wk_ref.wv_ref.wo_ref, ...), custom_call_target="tpu_custom_call" | custom-call | tf_op jit(solution)/shard_map/memory_gradient/pallas_call | solution.py:537
  546.1 27.9 %all-reduce.5.cloned.1.call-done = (bf16[4,96,768]{2,1,0:T(8,128)(2,1)}, bf16[4,96,768]{2,1,0:T(8,128)(2,1)}, bf16[2,96,2048]{2,1,0:T(8,128)(2,1)}, bf16[256,768]{1,0:T(8,128)(2,1)}) async-done(((bf16[4,96,768]{2,1,0:T(8,128)(2,1)}, bf16[4,96,768]{2,1,0:T(8,128)(2,1)}, bf16[2,96,2048]{2,1,0:T(8,128)(2,1)}, bf16[256,768]{1,0:T(8,128)(2,1)}), (bf16[4,96,768]{2,1,0:T(8,128)(2,1)}, ...) | async-done | bytes 2359312 | tf_op jit(solution)/shard_map/psum | solution.py:646
  574.0 2.4 fusion.4
  580.6 30.1 %all-reduce.1 = (f32[4]{0:T(128)S(1)}, f32[4,768]{1,0:T(4,128)S(1)}, f32[4]{0:T(128)S(1)}, f32[4]{0:T(128)S(1)}, f32[4,768]{1,0:T(4,128)S(1)}, /*index=5*/f32[4]...) all-reduce(f32[4]{0:T(128)S(1)} %get-tuple-element.246, ...), channel_id=1, replica_groups=mesh['rep'=4,'fsdp'=8] {'fsdp'}, use_global_device_ids=true, to_apply=%region_17.18 | all-reduce | flops 11033 | bytes 88264 | tf_op jit(solution)/shard_map/psum | solution.py:680
  613.0 2.5 multiply_subtract_fusion.3
  615.5 1.8 multiply_subtract_fusion
  (147 shorter events, 18.4 us)
Async XLA Ops:
  7.2 57.4 %all-gather.6.cloned.1.call-start = ((), (), s32[]{:S(2)}) async-start(), calls=%async_computation.4 | async-start | bytes 5308416 | tf_op jit(solution)/shard_map/all_gather | solution.py:602
  10.0 107.4 %all-gather.8.cloned.1.call-start = ((), (), s32[]{:S(2)}) async-start(), calls=%async_computation.5 | async-start | bytes 5308416 | tf_op jit(solution)/shard_map/all_gather | solution.py:604
  11.1 145.7 %all-gather.12.cloned.1.call-start = ((), (), s32[]{:S(2)}) async-start(), calls=%async_computation.7 | async-start | bytes 3538944 | tf_op jit(solution)/shard_map/all_gather | solution.py:606
  12.7 209.8 %all-gather.10.cloned.1.call-start = ((), (), s32[]{:S(2)}) async-start(), calls=%async_computation.6 | async-start | bytes 7077888 | tf_op jit(solution)/shard_map/all_gather | solution.py:605
  13.9 360.5 %reduce-scatter.11.cloned.1.call-start = ((), (), s32[]{:S(2)}) async-start(), calls=%async_computation.11 | async-start | bytes 3538944 | tf_op jit(solution)/shard_map/reduce_scatter | solution.py:644
  269.0 105.5 %reduce-scatter.7.cloned.1.call-start = ((), (), s32[]{:S(2)}) async-start(), calls=%async_computation.9 | async-start | bytes 5308416 | tf_op jit(solution)/shard_map/reduce_scatter | solution.py:642
  317.1 109.2 %reduce-scatter.5.cloned.1.call-start = ((), (), s32[]{:S(2)}) async-start(), calls=%async_computation.8 | async-start | bytes 5308416 | tf_op jit(solution)/shard_map/reduce_scatter | solution.py:641
  368.1 128.8 %reduce-scatter.9.cloned.1.call-start = ((), (), s32[]{:S(2)}) async-start(), calls=%async_computation.10 | async-start | bytes 7077888 | tf_op jit(solution)/shard_map/reduce_scatter | solution.py:643
  374.3 122.6 %copy-start.22 = (f32[32,12]{0,1:T(8,128)S(1)}, f32[32,12]{0,1:T(8,128)}, u32[]{:S(2)}) copy-start(f32[32,12]{0,1:T(8,128)} %param.43) | copy-start | bytes 4612
  374.3 124.0 %copy-start.26 = (f32[768]{0:T(1024)S(1)}, f32[768]{0:T(1024)}, u32[]{:S(2)}) copy-start(f32[768]{0:T(1024)} %param.41) | copy-start | bytes 9220
  374.3 124.0 %copy-start.15 = (f32[16,512]{1,0:T(8,128)S(1)}, f32[16,512]{1,0:T(8,128)}, u32[]{:S(2)}) copy-start(f32[16,512]{1,0:T(8,128)} %get-tuple-element.90) | copy-start | bytes 98308
  374.3 124.4 %copy-start.29 = (f32[1,768]{1,0:T(1,128)S(1)}, f32[1,768]{1,0:T(1,128)}, u32[]{:S(2)}) copy-start(f32[1,768]{1,0:T(1,128)} %get-tuple-element.87) | copy-start | bytes 9220
  374.4 124.4 %copy-start.28 = (f32[1,768]{1,0:T(1,128)S(1)}, f32[1,768]{1,0:T(1,128)}, u32[]{:S(2)}) copy-start(f32[1,768]{1,0:T(1,128)} %get-tuple-element.88) | copy-start | bytes 9220
  374.4 124.4 %copy-start.27 = (f32[1,768]{1,0:T(1,128)S(1)}, f32[1,768]{1,0:T(1,128)}, u32[]{:S(2)}) copy-start(f32[1,768]{1,0:T(1,128)} %get-tuple-element.89) | copy-start | bytes 9220
  374.4 199.6 %all-reduce.5.cloned.1.call-start = ((), (), s32[]{:S(2)}) async-start(), calls=%async_computation.12 | async-start | bytes 4718592 | tf_op jit(solution)/shard_map/psum | solution.py:646
  577.7 34.5 %copy-start.17 = (f32[2,2048]{1,0:T(2,128)S(1)}, f32[2,2048]{1,0:T(2,128)}, u32[]{:S(2)}) copy-start(f32[2,2048]{1,0:T(2,128)} %param.39) | copy-start | bytes 49156
  577.7 34.5 %copy-start.18 = (f32[4,768]{1,0:T(4,128)S(1)}, f32[4,768]{1,0:T(4,128)}, u32[]{:S(2)}) copy-start(f32[4,768]{1,0:T(4,128)} %param.37) | copy-start | bytes 36868
  577.7 34.5 %copy-start.19 = (f32[4,768]{1,0:T(4,128)S(1)}, f32[4,768]{1,0:T(4,128)}, u32[]{:S(2)}) copy-start(f32[4,768]{1,0:T(4,128)} %param.35) | copy-start | bytes 36868
  577.7 34.5 %copy-start.33 = (f32[3,96]{1,0:T(4,128)S(1)}, f32[3,96]{1,0:T(4,128)}, u32[]{:S(2)}) copy-start(f32[3,96]{1,0:T(4,128)} %param.42) | copy-start | bytes 3460
  578.2 37.3 %copy-start.1 = (f32[2,96,2048]{2,1,0:T(8,128)}, f32[2,96,2048]{2,1,0:T(8,128)S(1)}, u32[]{:S(2)}) copy-start(f32[2,96,2048]{2,1,0:T(8,128)S(1)} %get-tuple-element.224) | copy-start | bytes 4718596
  579.8 37.5 %copy-start.24 = (f32[2,96]{1,0:T(2,128)}, f32[2,96]{1,0:T(2,128)S(1)}, u32[]{:S(2)}) copy-start(f32[2,96]{1,0:T(2,128)S(1)} %get-tuple-element.223) | copy-start | bytes 2308
  580.5 36.9 %copy-start.25 = (f32[256]{0:T(256)}, f32[256]{0:T(256)S(1)}, u32[]{:S(2)}) copy-start(f32[256]{0:T(256)S(1)} %get-tuple-element.220) | copy-start | bytes 3076
  580.6 36.7 %copy-start.20 = (f32[4,96]{1,0:T(4,128)}, f32[4,96]{1,0:T(4,128)S(1)}, u32[]{:S(2)}) copy-start(f32[4,96]{1,0:T(4,128)S(1)} %get-tuple-element.226) | copy-start | bytes 4612
  580.6 38.1 %copy-start.21 = (f32[4,96]{1,0:T(4,128)}, f32[4,96]{1,0:T(4,128)S(1)}, u32[]{:S(2)}) copy-start(f32[4,96]{1,0:T(4,128)S(1)} %get-tuple-element.247) | copy-start | bytes 4612
  (21 other events, 58.0 us)
Sparse Core Ops, SparseCore 0:
  10.2 54.3 all-gather.5
  66.8 50.5 all-gather.7
  119.6 37.1 all-gather.11
  158.8 63.5 all-gather.9
  269.1 39.0 reduce-scatter.10
  317.3 53.3 reduce-scatter.6
  373.0 53.2 reduce-scatter.4
  428.6 68.1 reduce-scatter.8
  500.2 73.7 all-reduce.4

commit v3 on v2

--- a/solution.py
+++ b/solution.py
@@ -14,11 +14,11 @@
 DECAY_RATE = 0.8
 STEP_RATE = 0.2
 TINY_TERM = 1e-30
-EXACT_ARITHMETIC = lax.Precision.HIGHEST
 PAIR = 2 * DH
 GROUP = 4 * DH
 HIDDEN = -1e30
 VMEM_BYTES = 60 * 1024 * 1024
+PEAK = 1.15e9
 LOW = jnp.bfloat16
 WIDE = jnp.float32
 
@@ -214,6 +214,7 @@
             pltpu.VMEM((row_count, width), LOW),
             pltpu.VMEM((2, length, length) if causal else (1, 8, PAIR), WIDE),
         ],
+        cost_estimate=pl.CostEstimate(flops=int(27 * PEAK), bytes_accessed=20 << 20, transcendentals=0),
         compiler_params=pltpu.CompilerParams(vmem_limit_bytes=VMEM_BYTES),
         name="self_forward" if causal else "cross_forward",
     )(*args)
@@ -239,7 +240,7 @@
 
 def feed_kernel(
     seq_count, length_ref, after_ref, out_grad_ref, gain_ref, wg_ref, wu_ref, wd_ref,
-    layer_ref, grad_cross_ref, dwg_ref, dwu_ref, dwd_ref, dgain_ref,
+    layer_ref, grad_cross_ref, dwi_ref, dwd_ref, dgain_ref,
     normed, normed_t, down, out_total, grad_total,
 ):
     step = pl.program_id(0)
@@ -269,11 +270,11 @@
     hidden = (value * up).astype(LOW)
     out_total[...] += nn(hidden, wd_ref[...])
     grad_hidden = nt(down[...], wd_ref[...])
-    dwd_ref[...] = tn(hidden, down[...]).astype(LOW)
+    dwd_ref[...] = tn(hidden, down[...]).astype(LOW).reshape(dwd_ref.shape)
     grad_gate = (grad_hidden * up * slope).astype(LOW)
     grad_up = (grad_hidden * value).astype(LOW)
-    dwg_ref[...] = nn(normed_t[...], grad_gate).astype(LOW)
-    dwu_ref[...] = nn(normed_t[...], grad_up).astype(LOW)
+    dwi_ref[0] = nn(normed_t[...], grad_gate).astype(LOW)
+    dwi_ref[1] = nn(normed_t[...], grad_up).astype(LOW)
     grad_total[...] += nt(grad_gate, wg_ref[...]) + nt(grad_up, wu_ref[...])
 
     @pl.when(step == pl.num_programs(0) - 1)
@@ -297,7 +298,9 @@
     wide = pl.BlockSpec((None, width, block), lambda g: (0, 0, g))
     wide_up = pl.BlockSpec((None, width, block), lambda g: (1, 0, g))
     tall = pl.BlockSpec((block, width), lambda g: (g, 0))
-    flat = pl.BlockSpec((width, block), lambda g: (0, g))
+    both = pl.BlockSpec((2, width, block), lambda g: (0, 0, g))
+    quarter = block // 4
+    cut = pl.BlockSpec((4, None, quarter, width), lambda g: (0, g, 0, 0))
     return pl.pallas_call(
         functools.partial(feed_kernel, seq_count),
         grid=(hidden // block,),
@@ -310,13 +313,12 @@
             wide_up,
             tall,
         ],
-        out_specs=[whole(after.shape), whole(after.shape), flat, flat, tall, whole((1, width))],
+        out_specs=[whole(after.shape), whole(after.shape), both, cut, whole((1, width))],
         out_shape=[
             jax.ShapeDtypeStruct((row_count, width), LOW),
             jax.ShapeDtypeStruct((row_count, width), WIDE),
-            jax.ShapeDtypeStruct((width, hidden), LOW),
-            jax.ShapeDtypeStruct((width, hidden), LOW),
-            jax.ShapeDtypeStruct((hidden, width), LOW),
+            jax.ShapeDtypeStruct((2, width, hidden), LOW),
+            jax.ShapeDtypeStruct((4, hidden // block, quarter, width), LOW),
             jax.ShapeDtypeStruct((1, width), WIDE),
         ],
         scratch_shapes=[
@@ -326,6 +328,7 @@
             pltpu.VMEM((row_count, width), WIDE),
             pltpu.VMEM((row_count, width), WIDE),
         ],
+        cost_estimate=pl.CostEstimate(flops=int(46 * PEAK), bytes_accessed=40 << 20, transcendentals=0),
         compiler_params=pltpu.CompilerParams(vmem_limit_bytes=VMEM_BYTES),
         name="feed_forward_both",
     )(lengths, after, out_grad, gain, w_in, w_in, w_out)
@@ -333,9 +336,9 @@
 
 def backward_kernel(
     causal, seq_count, length_ref, x_ref, source_ref, grad_ref, gain_ref, wq_ref, wk_ref, wv_ref, wo_ref, wave_ref,
-    q_ref, k_ref, v_ref, mix_ref, total_ref,
-    grad_x_ref, gk_out_ref, gv_out_ref, dwq_ref, dwk_ref, dwv_ref, dwo_ref, dgain_ref, dist_ref,
-    normed_t, source_t, branch, grad_mix, gq, bias, score_sum, grad_total,
+    q_ref, k_ref, v_ref, mix_ref, total_ref, mix_all_ref,
+    grad_x_ref, gk_out_ref, gv_out_ref, dw_ref, dgain_ref, dist_ref,
+    normed_t, source_t, mix_t, branch, grad_mix, gq, bias, score_sum, grad_total,
 ):
     group = pl.program_id(0)
     row_count = x_ref.shape[0]
@@ -349,6 +352,7 @@
             value = x_ref[at : at + size, :].astype(WIDE)
             low = (value * rms_rate(value) * gain_ref[...]).astype(LOW)
             normed_t[:, at : at + size] = low.T
+            mix_t[:, at : at + size] = mix_all_ref[at : at + size, :].T
             branch[at : at + size, :] = grad_ref[at : at + size, :].astype(LOW)
             grad_total[at : at + size, :] = jnp.zeros((size, value.shape[1]), WIDE)
         if not causal:
@@ -356,7 +360,8 @@
                 source_t[:, at : at + size] = source_ref[at : at + size, :].T
 
     grad_mix[...] = nt(branch[...], wo_ref[...]).astype(LOW)
-    dwo_ref[...] = tn(mix_ref[...], branch[...]).astype(LOW)
+    across = pl.ds(pl.multiple_of(group * GROUP, GROUP), GROUP)
+    dw_ref[3] = nn(mix_t[...], branch[:, across]).astype(LOW)
 
     for pair in range(2):
         at = pair * PAIR
@@ -439,9 +444,9 @@
 
     if causal:
         source_t = normed_t
-    dwq_ref[...] = nn(normed_t[...], gq[...]).astype(LOW)
-    dwk_ref[...] = nn(source_t[...], gk_out_ref[...]).astype(LOW)
-    dwv_ref[...] = nn(source_t[...], gv_out_ref[...]).astype(LOW)
+    dw_ref[0] = nn(normed_t[...], gq[...]).astype(LOW)
+    dw_ref[1] = nn(source_t[...], gk_out_ref[...]).astype(LOW)
+    dw_ref[2] = nn(source_t[...], gv_out_ref[...]).astype(LOW)
     update = nt(gq[...], wq_ref[...])
     if causal:
         update = update + nt(gk_out_ref[...], wk_ref[...]) + nt(gv_out_ref[...], wv_ref[...])
@@ -467,9 +472,6 @@
     length = row_count // seq_count
     groups = width // GROUP
     low = lambda rows: jax.ShapeDtypeStruct((rows, width), LOW)
-    grad_columns = pl.BlockSpec((width, GROUP), lambda g: (0, g))
-    grad_rows = pl.BlockSpec((GROUP, width), lambda g: (g, 0))
-    square = jax.ShapeDtypeStruct((width, width), LOW)
     score = (2, length, length) if causal else (1, 8, PAIR)
     return pl.pallas_call(
         functools.partial(backward_kernel, causal, seq_count),
@@ -487,15 +489,13 @@
             columns(source_rows),
             columns(row_count),
             pl.BlockSpec((None, row_count, PAIR), lambda g: (g, 0, 0)),
+            whole((row_count, width)),
         ],
         out_specs=[
             whole((row_count, width)),
             columns(source_rows),
             columns(source_rows),
-            grad_columns,
-            grad_columns,
-            grad_columns,
-            grad_rows,
+            pl.BlockSpec((4, width, GROUP), lambda g: (0, 0, g)),
             whole((1, width)),
             whole(wave.shape),
         ],
@@ -503,16 +503,14 @@
             jax.ShapeDtypeStruct((row_count, width), WIDE),
             low(source_rows),
             low(source_rows),
-            square,
-            square,
-            square,
-            square,
+            jax.ShapeDtypeStruct(weights.shape, LOW),
             jax.ShapeDtypeStruct((1, width), WIDE),
             jax.ShapeDtypeStruct(wave.shape, WIDE),
         ],
         scratch_shapes=[
             pltpu.VMEM((width, row_count), LOW),
             pltpu.VMEM((width, source_rows) if not causal else (16, PAIR), LOW),
+            pltpu.VMEM((width, row_count), LOW),
             pltpu.VMEM((row_count, width), LOW),
             pltpu.VMEM((row_count, GROUP), LOW),
             pltpu.VMEM((row_count, GROUP), LOW),
@@ -520,9 +518,10 @@
             pltpu.VMEM(score, WIDE),
             pltpu.VMEM((row_count, width), WIDE),
         ],
+        cost_estimate=pl.CostEstimate(flops=int(45 * PEAK), bytes_accessed=40 << 20, transcendentals=0),
         compiler_params=pltpu.CompilerParams(vmem_limit_bytes=VMEM_BYTES),
         name="self_backward" if causal else "cross_backward",
-    )(lengths, x, source, grad, gain, weights, weights, weights, weights, wave, *kept)
+    )(lengths, x, source, grad, gain, weights, weights, weights, weights, wave, *kept, kept[3])
 
 
 def memory_kernel(gk_ref, gv_ref, wk_ref, wv_ref, out_ref):
@@ -540,35 +539,134 @@
         in_specs=[rowwise, rowwise, matrix(1), matrix(2)],
         out_specs=rowwise,
         out_shape=jax.ShapeDtypeStruct((rows, width), WIDE),
+        cost_estimate=pl.CostEstimate(flops=int(7 * PEAK), bytes_accessed=10 << 20, transcendentals=0),
         compiler_params=pltpu.CompilerParams(vmem_limit_bytes=VMEM_BYTES),
         name="memory_gradient",
     )(grad_key, grad_value, weights, weights)
 
 
-def row_parts(gradient, weight, row_state):
+def flat_permute(value, target):
+    reps, shards = lax.axis_size("rep"), lax.axis_size("fsdp")
+    pairs = []
+    for rep in range(reps):
+        for shard in range(shards):
+            to_rep, to_shard = target(rep, shard)
+            pairs.append((rep * shards + shard, to_rep * shards + to_shard))
+    return lax.ppermute(value, ("rep", "fsdp"), pairs)
+
+
+def from_rep(value, way):
+    return flat_permute(value, lambda rep, shard: (rep ^ way, shard))
+
+
+def from_shard(value, way):
+    return flat_permute(value, lambda rep, shard: (rep, shard ^ way))
+
+
+def from_line(value, hops):
+    shards = lax.axis_size("fsdp")
+    return flat_permute(value, lambda rep, shard: (rep, (shard + 2 * hops) % shards))
+
+
+def spread_quarter(piece):
+    hops = lax.axis_size("fsdp") // 2
+    line = jnp.stack([piece] + [from_line(piece, hop) for hop in range(1, hops)])
+    near = [line] + [from_rep(line, way) for way in range(1, 4)]
+    return near + [from_shard(part, 1) for part in near]
+
+
+def assemble_kernel(place, hops, where_ref, *refs):
+    parts, out_ref, sems = refs[:8], refs[8], refs[9]
+    rep, line, core = where_ref[0], where_ref[1], where_ref[2]
+    copies = []
+    for other in range(2):
+        for way in range(4):
+            for hop in range(hops):
+                shard = lax.rem(line - hop + hops, hops) * 2 + (core ^ other)
+                copies.append(
+                    pltpu.make_async_copy(
+                        parts[4 * other + way].at[hop],
+                        place(out_ref, rep ^ way, shard),
+                        sems.at[len(copies)],
+                    )
+                )
+    for copy in copies:
+        copy.start()
+    for copy in copies:
+        copy.wait()
+
+
+def assemble(parts, shape, place, name):
+    hops = parts[0].shape[0]
+    shard = lax.axis_index("fsdp")
+    where = jnp.stack([lax.axis_index("rep"), shard // 2, shard % 2]).astype(jnp.int32)
+    return pl.pallas_call(
+        functools.partial(assemble_kernel, place, hops),
+        in_specs=[pl.BlockSpec(memory_space=pltpu.SMEM)] + [pl.BlockSpec(memory_space=pl.ANY)] * 8,
+        out_specs=pl.BlockSpec(memory_space=pl.ANY),
+        out_shape=jax.ShapeDtypeStruct(shape, LOW),
+        scratch_shapes=[pltpu.SemaphoreType.DMA((8 * hops,))],
+        cost_estimate=pl.CostEstimate(flops=int(4 * PEAK), bytes_accessed=8 << 20, transcendentals=0),
+        compiler_params=pltpu.CompilerParams(vmem_limit_bytes=VMEM_BYTES),
+        name=name,
+    )(where, *parts)
+
+
+def rep_reduce(parts):
+    rep = lax.axis_index("rep")
+    pick = lambda at: lax.dynamic_index_in_dim(parts, at, 0, keepdims=False)
+    total = pick(rep).astype(WIDE)
+    for way in range(1, 4):
+        total = total + from_rep(pick(rep ^ way), way).astype(WIDE)
+    return total.astype(LOW)
+
+
+def rep_collect(piece):
+    rep = lax.axis_index("rep")
+    near = jnp.stack([piece] + [from_rep(piece, way) for way in range(1, 4)])
+    return jnp.stack([lax.dynamic_index_in_dim(near, at ^ rep, 0, keepdims=False) for at in range(4)])
+
+
+def butterfly(vector, move, size):
+    way = 1
+    while way < size:
+        vector = vector + move(vector, way)
+        way *= 2
+    return vector
+
+
+def after(value, *earlier):
+    return lax.optimization_barrier((value, *earlier))[0]
+
+
+def factored_update(gradient, weight, row_state, col_state, reduce):
+    count, rows, cols = weight.shape
     squares = gradient * gradient + TINY_TERM
     row_moment = DECAY_RATE * row_state + (1.0 - DECAY_RATE) * jnp.mean(squares, axis=2)
-    return (
-        row_moment,
-        jnp.sum(squares, axis=1),
-        jnp.sum(row_moment, axis=1),
-        jnp.sum(weight * weight, axis=(1, 2)),
-    )
-
-
-def column_step(gradient, row_moment, col_state, col_sum, row_sum, whole_rows):
+    local = jnp.concatenate(
+        [
+            jnp.sum(squares, axis=1).reshape(-1),
+            jnp.sum(row_moment, axis=1),
+            jnp.sum(weight * weight, axis=(1, 2)),
+        ]
+    )
+    total = reduce(local)
+    whole_rows = rows * lax.axis_size("fsdp")
+    col_sum = total[: count * cols].reshape(count, cols)
+    row_mean = total[count * cols : count * cols + count] / whole_rows
+    square = total[count * cols + count :] / (whole_rows * cols)
     col_moment = DECAY_RATE * col_state + (1.0 - DECAY_RATE) * col_sum / whole_rows
-    row_mean = row_sum / whole_rows
     direction = gradient * lax.rsqrt(
         row_moment[:, :, None] * col_moment[:, None, :] / row_mean[:, None, None]
     )
-    return (direction, col_moment)
-
-
-def apply_optimizer_update(weight, direction, weight_square):
-    step_size = STEP_RATE * jnp.sqrt(weight_square + 1e-06)
-    ratio = step_size.reshape((-1,) + (1,) * (weight.ndim - 1))
-    return weight - ratio * direction
+    step = STEP_RATE * jnp.sqrt(square + 1e-06)
+    return weight - step[:, None, None] * direction, row_moment, col_moment
+
+
+def plain_update(gradient, weight, moment, square):
+    moment = DECAY_RATE * moment + (1.0 - DECAY_RATE) * (gradient * gradient + TINY_TERM)
+    step = STEP_RATE * jnp.sqrt(square + 1e-06)
+    return weight - step * gradient * lax.rsqrt(moment), moment
 
 
 def per_device(
@@ -599,12 +697,36 @@
     mem_length = memory.shape[1]
     row_count = seq_count * seq_length
     hidden_width = ffn_in.shape[2]
+    reps, shards = lax.axis_size("rep"), lax.axis_size("fsdp")
+    rep, shard = lax.axis_index("rep"), lax.axis_index("fsdp")
+    quarters = reps == 4 and shards == 8
+    part_rows = hidden_width // shards
     w_self = lax.all_gather(self_weight.astype(LOW), "fsdp", axis=1, tiled=True)
     gain_full = lax.all_gather(gains.astype(LOW), "fsdp", axis=1, tiled=True).astype(WIDE)
-    w_cross = lax.all_gather(cross_weight.astype(LOW), "fsdp", axis=1, tiled=True)
     w_in = lax.all_gather(ffn_in.astype(LOW), "fsdp", axis=1, tiled=True)
-    w_out = lax.all_gather(ffn_out.astype(LOW), "fsdp", axis=0, tiled=True)
-    col_whole = (self_cols, cross_cols, in_cols, out_cols)
+    if quarters:
+        cross_quarter = lax.dynamic_index_in_dim(cross_weight, rep, 0, keepdims=False).astype(LOW)
+        out_quarter = lax.dynamic_index_in_dim(
+            ffn_out.reshape(4, part_rows // 4, model_width), rep, 0, keepdims=False
+        ).astype(LOW)
+        cross_pieces = spread_quarter(cross_quarter)
+        out_pieces = spread_quarter(out_quarter)
+        cross_rows_each, out_rows_each = cross_weight.shape[1], part_rows // 4
+        w_cross = assemble(
+            cross_pieces,
+            (4, model_width, model_width),
+            lambda ref, quarter, at: ref.at[quarter, pl.ds(at * cross_rows_each, cross_rows_each)],
+            "assemble_cross",
+        )
+        w_out = assemble(
+            out_pieces,
+            (hidden_width, model_width),
+            lambda ref, quarter, at: ref.at[pl.ds((at * 4 + quarter) * out_rows_each, out_rows_each)],
+            "assemble_out",
+        )
+    else:
+        w_cross = lax.all_gather(cross_weight.astype(LOW), "fsdp", axis=1, tiled=True)
+        w_out = lax.all_gather(ffn_out.astype(LOW), "fsdp", axis=0, tiled=True)
 
     bucket_mask = (buckets[None, :] == jnp.arange(BUCKETS)[:, None]).astype(WIDE)
     by_distance = jnp.sum(table.T[:, :, None] * bucket_mask[None], axis=1)
@@ -622,88 +744,76 @@
     *kept_two, after_cross = attention_forward(
         False, after_self, mem_rows, enc_len, gain_full[1:2], w_cross, no_bias
     )
-    layer_out, grad_cross, grad_wg, grad_wu, grad_wd, gain_three = feed_forward_both(
+    layer_out, grad_cross, grad_in, grad_out, gain_three = feed_forward_both(
         after_cross, grad_rows, dec_len, gain_full[2:3], w_in, w_out
     )
-    grad_self, grad_k_two, grad_v_two, *cross_parts, gain_two, _ = attention_backward(
+    grad_self, grad_k_two, grad_v_two, grad_cross_weights, gain_two, _ = attention_backward(
         False, after_self, mem_rows, grad_cross, enc_len, gain_full[1:2], w_cross, no_bias, kept_two
     )
-    memory_grad = memory_gradient(grad_k_two, grad_v_two, w_cross)
-    input_grad, _, _, *self_parts, gain_one, dist_grad = attention_backward(
+    input_grad, _, _, grad_self_weights, gain_one, dist_grad = attention_backward(
         True, dec_rows, no_source, grad_self, dec_len, gain_full[0:1], w_self, by_distance, kept_one
     )
+    memory_grad = memory_gradient(after(grad_k_two, gain_one), grad_v_two, w_cross)
     layer_out = layer_out.reshape(dec_in.shape)
     input_grad = input_grad.reshape(dec_in.shape)
     memory_grad = memory_grad.reshape(memory.shape)
     table_part = jnp.sum(bucket_mask[:, None, :] * dist_grad[None, :H, :], axis=2)
 
-    owned = (
-        lax.psum_scatter(jnp.stack(self_parts), "fsdp", scatter_dimension=1, tiled=True),
-        lax.psum_scatter(jnp.stack(cross_parts), "fsdp", scatter_dimension=1, tiled=True),
-        lax.psum_scatter(jnp.stack([grad_wg, grad_wu]), "fsdp", scatter_dimension=1, tiled=True),
-        lax.psum_scatter(grad_wd, "fsdp", scatter_dimension=0, tiled=True),
-    )
-    owned = [lax.psum(member, "rep").astype(WIDE) for member in owned]
+    scatter = lambda value, at: lax.psum_scatter(value, "fsdp", scatter_dimension=at, tiled=True)
     small = jnp.concatenate(
         [gain_one.reshape(-1), gain_two.reshape(-1), gain_three.reshape(-1), table_part.reshape(-1)]
     )
-    small = lax.psum(small, ("rep", "fsdp"))
-    gain_total = small[: 3 * model_width].reshape(3, model_width)
-    gain_mine = lax.dynamic_slice_in_dim(
-        gain_total, lax.axis_index("fsdp") * gains.shape[1], gains.shape[1], axis=1
-    )
-    table_total = small[3 * model_width :].reshape(BUCKETS, H)
-    owned.append(gain_mine)
-    fsdp_count = lax.axis_size("fsdp")
-    grad_factor = 1.0 / math.sqrt(row_count * lax.axis_size("rep") * fsdp_count)
-    self_grad, cross_grad, ffn_in_grad, feedforward_output_gradient, gains_grad = [
-        member * grad_factor for member in owned
+    if quarters:
+        cut = lambda value: value.reshape(4, -1, value.shape[-1])
+        own_in = scatter(grad_in, 1)
+        own_in = rep_collect(rep_reduce(cut(own_in))).reshape(own_in.shape)
+        own_out = scatter(rep_reduce(grad_out).reshape(-1, model_width), 0)
+        own_out = rep_collect(own_out).reshape(ffn_out.shape)
+        own_cross = rep_collect(scatter(rep_reduce(grad_cross_weights), 0))
+        own_self = scatter(grad_self_weights, 1)
+        own_self = rep_collect(rep_reduce(own_self))
+        over_shards = lambda vector: butterfly(vector, from_shard, shards)
+        small = butterfly(butterfly(small, from_shard, shards), from_rep, reps)
+    else:
+        over_reps = lambda value: lax.psum(value, "rep")
+        own_in = over_reps(scatter(grad_in, 1))
+        own_out = over_reps(
+            scatter(grad_out.transpose(1, 0, 2, 3).reshape(hidden_width, model_width), 0)
+        )
+        own_cross = over_reps(scatter(grad_cross_weights, 1))
+        own_self = over_reps(scatter(grad_self_weights, 1))
+        over_shards = lambda vector: lax.psum(vector, "fsdp")
+        small = lax.psum(small, ("rep", "fsdp"))
+
+    grad_factor = 1.0 / math.sqrt(row_count * reps * shards)
+    self_grad, cross_grad, ffn_in_grad, feedforward_output_gradient = [
+        member.astype(WIDE) * grad_factor for member in (own_self, own_cross, own_in, own_out)
     ]
-    table_grad = table_total * grad_factor
-    batches = [
-        (self_grad, self_weight, self_rows, col_whole[0]),
-        (cross_grad, cross_weight, cross_rows, col_whole[1]),
-        (ffn_in_grad, ffn_in, in_rows, col_whole[2]),
-        (feedforward_output_gradient[None], ffn_out[None], out_rows[None], col_whole[3][None]),
+    small = small * grad_factor
+    gains_grad = lax.dynamic_slice_in_dim(
+        small[: 3 * model_width].reshape(3, model_width), shard * gains.shape[1], gains.shape[1], axis=1
+    )
+    table_grad = small[3 * model_width :].reshape(BUCKETS, H)
+    new_ffn_in, new_in_rows, new_in_cols = factored_update(
+        ffn_in_grad, ffn_in, in_rows, in_cols, over_shards
+    )
+    new_ffn_out, new_out_rows, new_out_cols = [
+        member[0]
+        for member in factored_update(
+            feedforward_output_gradient[None], ffn_out[None], out_rows[None], out_cols[None], over_shards
+        )
     ]
-    prepared = [
-        row_parts(gradient, weight, row_state) for gradient, weight, row_state, col_state in batches
-    ]
-    gain_state = DECAY_RATE * gain_moment + (1.0 - DECAY_RATE) * (
-        gains_grad * gains_grad + TINY_TERM
-    )
-    gain_direction = gains_grad * lax.rsqrt(gain_state)
-    local_sums = []
-    for parts in prepared:
-        local_sums = local_sums + [parts[1], parts[2], parts[3]]
-    local_sums = local_sums + [jnp.sum(gains * gains, axis=1)]
-    totals = lax.psum(tuple(local_sums), "fsdp")
-    updated = []
-    col_results = []
-    for place_index in range(len(batches)):
-        gradient, weight, row_state, col_state = batches[place_index]
-        whole_rows = weight.shape[1] * fsdp_count
-        direction, col_moment = column_step(
-            gradient,
-            prepared[place_index][0],
-            col_state,
-            totals[3 * place_index],
-            totals[3 * place_index + 1],
-            whole_rows,
-        )
-        count_all = whole_rows * weight.shape[2]
-        updated.append(
-            apply_optimizer_update(weight, direction, totals[3 * place_index + 2] / count_all)
-        )
-        col_results.append(col_moment)
-    gain_width = gains.shape[1] * fsdp_count
-    gain_offset = 3 * len(batches)
-    new_gains = apply_optimizer_update(gains, gain_direction, totals[gain_offset] / gain_width)
-    table_state = DECAY_RATE * table_moment + (1.0 - DECAY_RATE) * (
-        table_grad * table_grad + TINY_TERM
-    )
-    table_direction = table_grad * lax.rsqrt(table_state)
-    new_table = apply_optimizer_update(table, table_direction, jnp.mean(table * table))
+    new_cross, new_cross_rows, new_cross_cols = factored_update(
+        cross_grad, cross_weight, cross_rows, cross_cols, over_shards
+    )
+    new_self, new_self_rows, new_self_cols = factored_update(
+        self_grad, self_weight, self_rows, self_cols, over_shards
+    )
+    gain_square = over_shards(jnp.sum(gains * gains, axis=1)) / model_width
+    new_gains, new_gain_moment = plain_update(gains_grad, gains, gain_moment, gain_square[:, None])
+    new_table, new_table_moment = plain_update(
+        table_grad, table, table_moment, jnp.mean(table * table)
+    )
     return (
         layer_out,
         input_grad,
@@ -714,22 +824,22 @@
         feedforward_output_gradient,
         gains_grad,
         table_grad,
-        updated[0],
-        updated[1],
-        updated[2],
-        updated[3][0],
+        new_self,
+        new_cross,
+        new_ffn_in,
+        new_ffn_out,
         new_gains,
         new_table,
-        prepared[0][0],
-        col_results[0],
-        prepared[1][0],
-        col_results[1],
-        prepared[2][0],
-        col_results[2],
-        prepared[3][0][0],
-        col_results[3][0],
-        gain_state,
-        table_state,
+        new_self_rows,
+        new_self_cols,
+        new_cross_rows,
+        new_cross_cols,
+        new_in_rows,
+        new_in_cols,
+        new_out_rows,
+        new_out_cols,
+        new_gain_moment,
+        new_table_moment,
     )
 
 

time: 635 us -> 795 us (1.25)
  Pallas kernels: 199 us -> 443 us
  waiting for transfers between devices: 287 us -> 185 us
  starting transfers between devices: 0.37 us -> 73.3 us
  blocking collectives: 82 us -> 13.8 us
  local copies, waits for them, and re-layouts: 6.79 us -> 19.5 us
    pallas_call x0 -> x2, Pallas kernels: none -> 242 us  [assemble(): pl.pallas_call(functools.partial(assemble_kernel, place, hops), in_specs=...]
    ppermute x0 -> x64, waiting for transfers between devices: none -> 139 us  [flat_permute(): return lax.ppermute(value, ('rep', 'fsdp'), pairs)]
    reduce_scatter x4, waiting for transfers between devices: 122 us -> 45.2 us  [per_device(): lax.psum_scatter(value, 'fsdp', scatter_dimension=at, tiled=True)]
    ppermute x0 -> x64, starting transfers between devices: none -> 73 us  [flat_permute(): return lax.ppermute(value, ('rep', 'fsdp'), pairs)]
    psum x2 -> x0, blocking collectives: 68.4 us -> none  [the longest x1 38.4 us: per_device(): small = lax.psum(small, ('rep', 'fsdp'))]
    all_gather x1, waiting for transfers between devices: 65.6 us -> 0.02 us  [per_device(): w_in = lax.all_gather(ffn_in.astype(LOW), 'fsdp', axis=1, tiled=True)]
    all_gather x2 -> x0, waiting for transfers between devices: 35.8 us -> none  [the longest x1 25.4 us: per_device(): lax.all_gather(cross_weight.astype(LOW), 'fsdp', axis=1, tiled=True)]
    all_gather x1, waiting for transfers between devices: 34.9 us -> 0.02 us  [per_device(): w_self = lax.all_gather(self_weight.astype(LOW), 'fsdp', axis=1, tiled=True)]
  transfers between devices with their start and end apart: 9 -> 70, of which waited for: 7 -> 31; matrix products, arithmetic and copies ran while one was open for 4% -> 5% of each run, Pallas kernels for 24% -> 50%
where the time goes in v3:
time: 795 us; the launch traced here: 787 us
  Pallas kernels  443 us (56%)
  waiting for transfers between devices  185 us (23%)
  starting transfers between devices  73.3 us (9%)
  other arithmetic  35.2 us (4%)
  local copies, waits for them, and re-layouts  19.5 us (2%)
  between operations  17.5 us (2%)
  blocking collectives  13.8 us (2%)
    pallas_call x2, Pallas kernels, assemble(): pl.pallas_call(functools.partial(assemble_kernel, place, hops), in_specs=...  242 us
    ppermute x64, waiting for transfers between devices, flat_permute(): return lax.ppermute(value, ('rep', 'fsdp'), pairs)  139 us
    pallas_call x2, Pallas kernels, attention_backward(): pl.pallas_call(functools.partial(backward_kernel, causal, seq_count), gri...  92 us
    ppermute x64, starting transfers between devices, flat_permute(): return lax.ppermute(value, ('rep', 'fsdp'), pairs)  73 us
    pallas_call x2, Pallas kernels, attention_forward(): pl.pallas_call(functools.partial(forward_kernel, causal, seq_count), grid...  55.4 us
    pallas_call x1, Pallas kernels, feed_forward_both(): pl.pallas_call(functools.partial(feed_kernel, seq_count), grid=(hidden //...  46.2 us
    reduce_scatter x4, waiting for transfers between devices, per_device(): lax.psum_scatter(value, 'fsdp', scatter_dimension=at, tiled=True)  45.2 us
  transfers between devices with their start and end apart: 70, of which 31 were waited for; matrix products, arithmetic and copies ran while one was open for 5% of the time, Pallas kernels for 50%

profile of v3, /device:TPU:0, one launch (start us, length us, event | category | flops | bytes accessed | tf_op | source)
XLA Modules:
  0.0 786.7 jit_solution(11529942912439132554)
XLA Ops:
  7.3 3.2 multiply_reduce_fusion.2
  24.9 6.3 collective-permute-done.10
  31.2 18.8 %collective-permute-done.11 = bf16[64,768]{1,0:T(8,128)(2,1)S(1)} collective-permute-done((bf16[64,768]{1,0:T(8,128)(2,1)S(1)}, bf16[64,768]{1,0:T(8,128)(2,1)S(1)}, u32[]{:S(2)}, u32[]{:S(2)}) %collective-permute-start.11) | collective-permute-done | bytes 98336 | tf_op jit(solution)/shard_map/ppermute | solution.py:555
  54.7 9.3 %collective-permute-done.2 = bf16[96,768]{1,0:T(8,128)(2,1)S(1)} collective-permute-done((bf16[96,768]{1,0:T(8,128)(2,1)S(1)}, bf16[96,768]{1,0:T(8,128)(2,1)S(1)}, u32[]{:S(2)}, u32[]{:S(2)}) %collective-permute-start.2) | collective-permute-done | bytes 147488 | tf_op jit(solution)/shard_map/ppermute | solution.py:555
  66.3 13.8 %all-gather = bf16[8,96,3]{1,2,0:T(4,128)(2,1)S(1)} all-gather(bf16[1,96,3]{1,2,0:T(4,128)(2,1)S(1)} %get-tuple-element.248), channel_id=1, replica_groups=mesh['rep'=4,'fsdp'=8] {'fsdp'}, dimensions={0}, use_global_device_ids=true | all-gather | bytes 5184 | tf_op jit(solution)/shard_map/all_gather | solution.py:705
  83.9 24.4 %collective-permute-done.4.refs_2_ = bf16[4,96,768]{2,1,0:T(8,128)(2,1)S(1)} collective-permute-done((bf16[4,96,768]{2,1,0:T(8,128)(2,1)S(1)}, bf16[4,96,768]{2,1,0:T(8,128)(2,1)S(1)}, u32[]{:S(2)}, u32[]{:S(2)}) %collective-permute-start.4) | collective-permute-done | bytes 589856 | tf_op jit(solution)/shard_map/ppermute | solution.py:555
  111.0 97.4 %assemble_out.1.wd_ref = bf16[2048,768]{1,0:T(8,128)(2,1)} custom-call(s32[3]{0:T(128)} %pad_add_fusion.where_ref, bf16[4,64,768]{2,1,0:T(8,128)(2,1)} %copy-done.11, bf16[4,64,768]{2,1,0:T(8,128)(2,1)} %collective-permute-done.13.refs_1_, bf16[4,64,768]{2,1,0:T(8,128)(2,1)} %collective-permute-done.14.refs_2_, ...), custom_call_target="tpu_custom_call" | custom-call | flops 4600000000 | bytes 8388608 | tf_op jit(solution)/shard_map/assemble_out/pallas_call | solution.py:603
  209.2 145.0 %assemble_cross.1.wq_ref.wk_ref.wv_ref.wo_ref = bf16[4,768,768]{2,1,0:T(8,128)(2,1)} custom-call(s32[3]{0:T(128)} %pad_add_fusion.where_ref, bf16[4,96,768]{2,1,0:T(8,128)(2,1)} %copy-done.6, bf16[4,96,768]{2,1,0:T(8,128)(2,1)} %copy-done.43, bf16[4,96,768]{2,1,0:T(8,128)(2,1)} %copy-done.44, bf16[4,96,768]{2,1,0:T(8,128)(2,1)} %copy-done.45, ...), custom_call_target="tpu_custom_call" | custom-call | flops 4600000000 | bytes 8388608 | tf_op jit(solution)/shard_map/assemble_cross/pallas_call | solution.py:603
  354.9 26.8 %self_forward.1 = (bf16[1024,768]{1,0:T(8,128)(2,1)}, bf16[1024,768]{1,0:T(8,128)(2,1)}, bf16[1024,768]{1,0:T(8,128)(2,1)}, bf16[1024,768]{1,0:T(8,128)(2,1)}, f...) custom-call(s32[2]{0:T(128)} %length_ref.9, bf16[1024,768]{1,0:T(8,128)(2,1)} %bitcast.134, ...), custom_call_target="tpu_custom_call" | custom-call | flops 31050000384 | bytes 20971520 | tf_op jit(solution)/shard_map/self_forward/pallas_call | solution.py:186
  382.2 28.6 %cross_forward.1 = (bf16[1024,768]{1,0:T(8,128)(2,1)}, bf16[1024,768]{1,0:T(8,128)(2,1)}, bf16[1024,768]{1,0:T(8,128)(2,1)}, bf16[1024,768]{1,0:T(8,128)(2,1)}, ...) custom-call(s32[2]{0:T(128)} %length_ref.8, f32[1024,768]{1,0:T(8,128)} %get-tuple-element.52.x_ref, ...), custom_call_target="tpu_custom_call" | custom-call | flops 31050000384 | bytes 20971520 | tf_op jit(solution)/shard_map/cross_forward/pallas_call | solution.py:186
  410.9 46.2 %feed_forward_both.1 = (bf16[1024,768]{1,0:T(8,128)(2,1)}, f32[1024,768]{1,0:T(8,128)}, bf16[2,768,2048]{2,1,0:T(8,128)(2,1)}, bf16[4,8,64,768]{3,2,1,0:T(8,128)(2,1)}, f32[1,768]{1,0:T(1,128)}) custom-call(s32[2]{0:T(128)} %length_ref.9, f32[1024,768]{1,0:T(8,128)} %get-tuple-element.53.after_ref, bf16[1024,768]{1,0:T(8,128)(2,1)} %bitcast.131, ...), custom_call_target="tpu_custom_call" | custom-call | flops 52899999744 | bytes 41943040 | tf_op jit(solution)/shard_map/feed_forward_both/pallas_call | solution.py:304
  463.2 44.9 %cross_backward.1 = (f32[1024,768]{1,0:T(8,128)}, bf16[1024,768]{1,0:T(8,128)(2,1)}, bf16[1024,768]{1,0:T(8,128)(2,1)}, bf16[4,768,768]{2,1,0:T(8,128)(2,1)}, f32[1,768]{1,0:T(1,128)}, /*index=5*/f32[8,128]{1,0:T(8,128)}) custom-call(s32[2]{0:T(128)} %length_ref.8, f32[1024,768]{1,0:T(8,128)} %get-tuple-element.52.x_ref, bf16[1024,768]{1,0:T(8,128)(2,1)} %bitcast.133, ...), custom_call_target="tpu_custom_call" | custom-call | flops 51749998592 | bytes 41943040 | tf_op jit(solution)/shard_map/cross_backward/pallas_call | solution.py:476
  517.1 24.8 %collective-permute-done.26 = bf16[768,768]{1,0:T(8,128)(2,1)S(1)} collective-permute-done((bf16[768,768]{1,0:T(8,128)(2,1)S(1)}, bf16[768,768]{1,0:T(8,128)(2,1)S(1)}, u32[]{:S(2)}, u32[]{:S(2)}) %collective-permute-start.26) | collective-permute-done | bytes 1179680 | tf_op jit(solution)/shard_map/ppermute | solution.py:555
  541.9 22.8 %collective-permute-done.27 = bf16[768,768]{1,0:T(8,128)(2,1)S(1)} collective-permute-done((bf16[768,768]{1,0:T(8,128)(2,1)S(1)}, bf16[768,768]{1,0:T(8,128)(2,1)S(1)}, u32[]{:S(2)}, u32[]{:S(2)}) %collective-permute-start.27) | collective-permute-done | bytes 1179680 | tf_op jit(solution)/shard_map/ppermute | solution.py:555
  569.4 47.1 %self_backward.1 = (f32[1024,768]{1,0:T(8,128)}, bf16[1024,768]{1,0:T(8,128)(2,1)}, bf16[1024,768]{1,0:T(8,128)(2,1)}, bf16[4,768,768]{2,1,0:T(8,128)(2,1)}, f32[1,768]{1,0:T(1,128)}, /*index=5*/f32[16,512]{1,0:T(8,128)}) custom-call(s32[2]{0:T(128)} %length_ref.9, bf16[1024,768]{1,0:T(8,128)(2,1)} %bitcast.135, bf16[16,128]{1,0:T(8,128)(2,1)} %broadcast_in_dim.4.source_ref, ...), custom_call_target="tpu_custom_call" | custom-call | flops 51749998592 | bytes 41943040 | tf_op jit(solution)/shard_map/self_backward/pallas_call | solution.py:476
  634.6 6.7 memory_gradient.1
  657.3 12.3 %reduce-scatter.5.cloned.1.call-done = bf16[4,96,768]{2,1,0:T(8,128)(2,1)} async-done(((bf16[4,768,768]{2,1,0:T(8,128)(2,1)}), bf16[4,96,768]{2,1,0:T(8,128)(2,1)}) %reduce-scatter.5.cloned.1.call-update) | async-done | bytes 589840 | tf_op jit(solution)/shard_map/reduce_scatter | solution.py:762
  692.0 4.0 collective-permute-start.53
  704.0 4.2 collective-permute-done.51
  708.3 33.0 %reduce-scatter.9.cloned.1.call-done = bf16[2,96,2048]{2,1,0:T(8,128)(2,1)} async-done(((bf16[2,768,2048]{2,1,0:T(8,128)(2,1)}), bf16[2,96,2048]{2,1,0:T(8,128)(2,1)}) %reduce-scatter.9.cloned.1.call-update) | async-done | bytes 786448 | tf_op jit(solution)/shard_map/reduce_scatter | solution.py:762
  746.0 3.3 collective-permute-done.32
  749.3 3.4 collective-permute-done.33
  765.1 5.1 collective-permute-start.56
  774.5 3.1 multiply_subtract_fusion.2
  (344 shorter events, 134.8 us)
Async XLA Ops:
  7.2 347.0 %all-gather.4.cloned.1.call-start = ((), (), s32[]{:S(2)}) async-start(), calls=%async_computation.4 | async-start | bytes 5308416 | tf_op jit(solution)/shard_map/all_gather | solution.py:704
  10.5 400.4 %all-gather.6.cloned.1.call-start = ((), (), s32[]{:S(2)}) async-start(), calls=%async_computation.5 | async-start | bytes 7077888 | tf_op jit(solution)/shard_map/all_gather | solution.py:706
  12.4 618.7 %reduce-scatter.11.cloned.1.call-start = ((), (), s32[]{:S(2)}) async-start(), calls=%async_computation.9 | async-start | bytes 884736 | tf_op jit(solution)/shard_map/reduce_scatter | solution.py:762
  13.4 40.8 %collective-permute-start = (bf16[96,768]{1,0:T(8,128)(2,1)S(1)}, bf16[96,768]{1,0:T(8,128)(2,1)S(1)}, u32[]{:S(2)}, u32[]{:S(2)}) collective-permute-start(bf16[96,768]{1,0:T(8,128)(2,1)S(1)} %fusion.39), channel_id=1, source_target_pairs={{0,2},{1,3},{2,4},{3,5},{4,6},{5,7},{6,0},{7,1},{8,10},{9,11},{10,... | collective-permute-start | bytes 442376 | tf_op jit(solution)/shard_map/ppermute | solution.py:555
  16.5 38.2 %collective-permute-start.1 = (bf16[96,768]{1,0:T(8,128)(2,1)S(1)}, bf16[96,768]{1,0:T(8,128)(2,1)S(1)}, u32[]{:S(2)}, u32[]{:S(2)}) collective-permute-start(bf16[96,768]{1,0:T(8,128)(2,1)S(1)} %fusion.39), channel_id=1, source_target_pairs={{0,4},{1,5},{2,6},{3,7},{4,0},{5,1},{6,2},{7,3},{8,12},{9,13},{10,... | collective-permute-start | bytes 442376 | tf_op jit(solution)/shard_map/ppermute | solution.py:555
  20.2 29.8 %collective-permute-start.11 = (bf16[64,768]{1,0:T(8,128)(2,1)S(1)}, bf16[64,768]{1,0:T(8,128)(2,1)S(1)}, u32[]{:S(2)}, u32[]{:S(2)}) collective-permute-start(bf16[64,768]{1,0:T(8,128)(2,1)S(1)} %fusion.38), channel_id=1, source_target_pairs={{0,4},{1,5},{2,6},{3,7},{4,0},{5,1},{6,2},{7,3},{8,12},{9,13},{10,... | collective-permute-start | bytes 294920 | tf_op jit(solution)/shard_map/ppermute | solution.py:555
  31.2 32.9 %collective-permute-start.2 = (bf16[96,768]{1,0:T(8,128)(2,1)S(1)}, bf16[96,768]{1,0:T(8,128)(2,1)S(1)}, u32[]{:S(2)}, u32[]{:S(2)}) collective-permute-start(bf16[96,768]{1,0:T(8,128)(2,1)S(1)} %fusion.39), channel_id=1, source_target_pairs={{0,6},{1,7},{2,0},{3,1},{4,2},{5,3},{6,4},{7,5},{8,14},{9,15},{10,... | collective-permute-start | bytes 442376 | tf_op jit(solution)/shard_map/ppermute | solution.py:555
  50.1 30.0 %collective-permute-start.13 = (bf16[4,64,768]{2,1,0:T(8,128)(2,1)S(1)}, bf16[4,64,768]{2,1,0:T(8,128)(2,1)}, u32[]{:S(2)}, u32[]{:S(2)}) collective-permute-start(bf16[4,64,768]{2,1,0:T(8,128)(2,1)S(1)} %pad_maximum_fusion.4.refs_0_), channel_id=1, source_target_pairs={{0,8},{1,9},{2,10},{3,11},{4,12},{5,13},{6,14},{7,15},{8,0},{9,1},... | collective-permute-start | bytes 1179656 | tf_op jit(solution)/shard_map/ppermute | solution.py:555
  51.6 30.0 %collective-permute-start.14 = (bf16[4,64,768]{2,1,0:T(8,128)(2,1)S(1)}, bf16[4,64,768]{2,1,0:T(8,128)(2,1)}, u32[]{:S(2)}, u32[]{:S(2)}) collective-permute-start(bf16[4,64,768]{2,1,0:T(8,128)(2,1)S(1)} %pad_maximum_fusion.4.refs_0_), channel_id=1, source_target_pairs={{0,16},{1,17},{2,18},{3,19},{4,20},{5,21},{6,22},{7,23},{8,24},{9,... | collective-permute-start | bytes 1179656 | tf_op jit(solution)/shard_map/ppermute | solution.py:555
  54.2 28.0 %collective-permute-start.15 = (bf16[4,64,768]{2,1,0:T(8,128)(2,1)S(1)}, bf16[4,64,768]{2,1,0:T(8,128)(2,1)}, u32[]{:S(2)}, u32[]{:S(2)}) collective-permute-start(bf16[4,64,768]{2,1,0:T(8,128)(2,1)S(1)} %pad_maximum_fusion.4.refs_0_), channel_id=1, source_target_pairs={{0,24},{1,25},{2,26},{3,27},{4,28},{5,29},{6,30},{7,31},{8,16},{9,... | collective-permute-start | bytes 1179656 | tf_op jit(solution)/shard_map/ppermute | solution.py:555
  80.1 28.2 %collective-permute-start.4 = (bf16[4,96,768]{2,1,0:T(8,128)(2,1)S(1)}, bf16[4,96,768]{2,1,0:T(8,128)(2,1)S(1)}, u32[]{:S(2)}, u32[]{:S(2)}) collective-permute-start(bf16[4,96,768]{2,1,0:T(8,128)(2,1)S(1)} %pad_maximum_fusion.1.refs_0_), channel_id=1, source_target_pairs={{0,16},{1,17},{2,18},{3,19},{4,20},{5,21},{6,22},{7,23},{8,24},{9,... | collective-permute-start | bytes 1769480 | tf_op jit(solution)/shard_map/ppermute | solution.py:555
  108.3 100.1 %collective-permute-start.6 = (bf16[4,96,768]{2,1,0:T(8,128)(2,1)S(1)}, bf16[4,96,768]{2,1,0:T(8,128)(2,1)S(1)}, u32[]{:S(2)}, u32[]{:S(2)}) collective-permute-start(bf16[4,96,768]{2,1,0:T(8,128)(2,1)S(1)} %pad_maximum_fusion.1.refs_0_), channel_id=1, source_target_pairs={{0,1},{1,0},{2,3},{3,2},{4,5},{5,4},{6,7},{7,6},{8,9},{9,8},{10,11... | collective-permute-start | bytes 1769480 | tf_op jit(solution)/shard_map/ppermute | solution.py:555
  108.3 100.1 %collective-permute-start.7 = (bf16[4,96,768]{2,1,0:T(8,128)(2,1)S(1)}, bf16[4,96,768]{2,1,0:T(8,128)(2,1)}, u32[]{:S(2)}, u32[]{:S(2)}) collective-permute-start(bf16[4,96,768]{2,1,0:T(8,128)(2,1)S(1)} %collective-permute-done.3.refs_1_), channel_id=1, source_target_pairs={{0,1},{1,0},{2,3},{3,2},{4,5},{5,4},{6,7},{7,6},{8,9},{9,8},{10,11... | collective-permute-start | bytes 1769480 | tf_op jit(solution)/shard_map/ppermute | solution.py:555
  108.8 99.6 %collective-permute-start.8 = (bf16[4,96,768]{2,1,0:T(8,128)(2,1)S(1)}, bf16[4,96,768]{2,1,0:T(8,128)(2,1)}, u32[]{:S(2)}, u32[]{:S(2)}) collective-permute-start(bf16[4,96,768]{2,1,0:T(8,128)(2,1)S(1)} %collective-permute-done.4.refs_2_), channel_id=1, source_target_pairs={{0,1},{1,0},{2,3},{3,2},{4,5},{5,4},{6,7},{7,6},{8,9},{9,8},{10,11... | collective-permute-start | bytes 1769480 | tf_op jit(solution)/shard_map/ppermute | solution.py:555
  108.9 99.6 %collective-permute-start.9 = (bf16[4,96,768]{2,1,0:T(8,128)(2,1)S(1)}, bf16[4,96,768]{2,1,0:T(8,128)(2,1)}, u32[]{:S(2)}, u32[]{:S(2)}) collective-permute-start(bf16[4,96,768]{2,1,0:T(8,128)(2,1)S(1)} %collective-permute-done.5.refs_3_), channel_id=1, source_target_pairs={{0,1},{1,0},{2,3},{3,2},{4,5},{5,4},{6,7},{7,6},{8,9},{9,8},{10,11... | collective-permute-start | bytes 1769480 | tf_op jit(solution)/shard_map/ppermute | solution.py:555
  459.8 48.4 %collective-permute-start.38 = (bf16[8,64,768]{2,1,0:T(8,128)(2,1)}, bf16[8,64,768]{2,1,0:T(8,128)(2,1)S(1)}, u32[]{:S(2)}, u32[]{:S(2)}) collective-permute-start(bf16[8,64,768]{2,1,0:T(8,128)(2,1)} %get-tuple-element.203), channel_id=1, source_target_pairs={{0,8},{1,9},{2,10},{3,11},{4,12},{5,13},{6,14},{7,15},{8,0},{9,1},... | collective-permute-start | bytes 2359304 | tf_op jit(solution)/shard_map/ppermute | solution.py:555
  460.4 47.8 %collective-permute-start.39 = (bf16[8,64,768]{2,1,0:T(8,128)(2,1)S(1)}, bf16[8,64,768]{2,1,0:T(8,128)(2,1)S(1)}, u32[]{:S(2)}, u32[]{:S(2)}) collective-permute-start(bf16[8,64,768]{2,1,0:T(8,128)(2,1)S(1)} %get-tuple-element.205), channel_id=1, source_target_pairs={{0,16},{1,17},{2,18},{3,19},{4,20},{5,21},{6,22},{7,23},{8,24},{9,... | collective-permute-start | bytes 2359304 | tf_op jit(solution)/shard_map/ppermute | solution.py:555
  461.8 46.3 %collective-permute-start.40 = (bf16[8,64,768]{2,1,0:T(8,128)(2,1)S(1)}, bf16[8,64,768]{2,1,0:T(8,128)(2,1)S(1)}, u32[]{:S(2)}, u32[]{:S(2)}) collective-permute-start(bf16[8,64,768]{2,1,0:T(8,128)(2,1)S(1)} %get-tuple-element.204), channel_id=1, source_target_pairs={{0,24},{1,25},{2,26},{3,27},{4,28},{5,29},{6,30},{7,31},{8,16},{9,... | collective-permute-start | bytes 2359304 | tf_op jit(solution)/shard_map/ppermute | solution.py:555
  510.6 139.6 %reduce-scatter.7.cloned.1.call-start = ((), (), s32[]{:S(2)}) async-start(), calls=%async_computation.7 | async-start | bytes 1327104 | tf_op jit(solution)/shard_map/reduce_scatter | solution.py:762
  512.9 29.0 %collective-permute-start.26 = (bf16[768,768]{1,0:T(8,128)(2,1)S(1)}, bf16[768,768]{1,0:T(8,128)(2,1)S(1)}, u32[]{:S(2)}, u32[]{:S(2)}) collective-permute-start(bf16[768,768]{1,0:T(8,128)(2,1)S(1)} %get-tuple-element.200), channel_id=1, source_target_pairs={{0,8},{1,9},{2,10},{3,11},{4,12},{5,13},{6,14},{7,15},{8,0},{9,1},... | collective-permute-start | bytes 3538952 | tf_op jit(solution)/shard_map/ppermute | solution.py:555
  513.6 51.1 %collective-permute-start.27 = (bf16[768,768]{1,0:T(8,128)(2,1)S(1)}, bf16[768,768]{1,0:T(8,128)(2,1)S(1)}, u32[]{:S(2)}, u32[]{:S(2)}) collective-permute-start(bf16[768,768]{1,0:T(8,128)(2,1)S(1)} %get-tuple-element.202), channel_id=1, source_target_pairs={{0,16},{1,17},{2,18},{3,19},{4,20},{5,21},{6,22},{7,23},{8,24},{9,... | collective-permute-start | bytes 3538952 | tf_op jit(solution)/shard_map/ppermute | solution.py:555
  515.1 51.3 %collective-permute-start.28 = (bf16[768,768]{1,0:T(8,128)(2,1)S(1)}, bf16[768,768]{1,0:T(8,128)(2,1)S(1)}, u32[]{:S(2)}, u32[]{:S(2)}) collective-permute-start(bf16[768,768]{1,0:T(8,128)(2,1)S(1)} %get-tuple-element.201), channel_id=1, source_target_pairs={{0,24},{1,25},{2,26},{3,27},{4,28},{5,29},{6,30},{7,31},{8,16},{9,... | collective-permute-start | bytes 3538952 | tf_op jit(solution)/shard_map/ppermute | solution.py:555
  569.3 100.2 %reduce-scatter.5.cloned.1.call-start = ((), (), s32[]{:S(2)}) async-start(), calls=%async_computation.6 | async-start | bytes 5308416 | tf_op jit(solution)/shard_map/reduce_scatter | solution.py:762
  616.5 124.8 %reduce-scatter.9.cloned.1.call-start = ((), (), s32[]{:S(2)}) async-start(), calls=%async_computation.8 | async-start | bytes 7077888 | tf_op jit(solution)/shard_map/reduce_scatter | solution.py:762
  (94 other events, 2015.2 us)
Sparse Core Ops, SparseCore 0:
  10.6 69.2 all-gather.3
  82.1 64.0 all-gather.5
  510.8 28.7 reduce-scatter.10
  569.4 30.3 reduce-scatter.6
  616.6 52.9 reduce-scatter.4
  671.8 69.3 reduce-scatter.8

commit v4 on v3

--- a/solution.py
+++ b/solution.py
@@ -568,11 +568,32 @@
     return flat_permute(value, lambda rep, shard: (rep, (shard + 2 * hops) % shards))
 
 
-def spread_quarter(piece):
+def along_line(piece):
     hops = lax.axis_size("fsdp") // 2
-    line = jnp.stack([piece] + [from_line(piece, hop) for hop in range(1, hops)])
-    near = [line] + [from_rep(line, way) for way in range(1, 4)]
-    return near + [from_shard(part, 1) for part in near]
+    return jnp.stack([piece] + [from_line(piece, hop) for hop in range(1, hops)])
+
+
+def across_reps(line):
+    return [line] + [from_rep(line, way) for way in range(1, 4)]
+
+
+def with_partner(parts):
+    return parts + [from_shard(part, 1) for part in parts]
+
+
+def scatter_line(quarter):
+    shards = quarter.shape[0]
+    hops = shards // 2
+    shard = lax.axis_index("fsdp")
+    line, core = shard // 2, shard % 2
+    halves = quarter.reshape(hops, 2, *quarter.shape[1:])
+    pick = lambda at: lax.dynamic_index_in_dim(halves, at, 1, keepdims=False)
+    chip = (pick(core).astype(WIDE) + from_shard(pick(core ^ 1), 1).astype(WIDE)).astype(LOW)
+    at_hop = lambda hop: lax.dynamic_index_in_dim(chip, (line + hop) % hops, 0, keepdims=False)
+    total = at_hop(0).astype(WIDE)
+    for hop in range(1, hops):
+        total = total + from_line(at_hop(hop), hop).astype(WIDE)
+    return total.astype(LOW)
 
 
 def assemble_kernel(place, hops, where_ref, *refs):
@@ -603,7 +624,7 @@
     return pl.pallas_call(
         functools.partial(assemble_kernel, place, hops),
         in_specs=[pl.BlockSpec(memory_space=pltpu.SMEM)] + [pl.BlockSpec(memory_space=pl.ANY)] * 8,
-        out_specs=pl.BlockSpec(memory_space=pl.ANY),
+        out_specs=pl.BlockSpec(memory_space=pltpu.VMEM),
         out_shape=jax.ShapeDtypeStruct(shape, LOW),
         scratch_shapes=[pltpu.SemaphoreType.DMA((8 * hops,))],
         cost_estimate=pl.CostEstimate(flops=int(4 * PEAK), bytes_accessed=8 << 20, transcendentals=0),
@@ -612,13 +633,14 @@
     )(where, *parts)
 
 
-def rep_reduce(parts):
+def rep_parts(parts):
     rep = lax.axis_index("rep")
     pick = lambda at: lax.dynamic_index_in_dim(parts, at, 0, keepdims=False)
-    total = pick(rep).astype(WIDE)
-    for way in range(1, 4):
-        total = total + from_rep(pick(rep ^ way), way).astype(WIDE)
-    return total.astype(LOW)
+    return [pick(rep)] + [from_rep(pick(rep ^ way), way) for way in range(1, 4)]
+
+
+def add_up(parts):
+    return sum(part.astype(WIDE) for part in parts).astype(LOW)
 
 
 def rep_collect(piece):
@@ -704,29 +726,6 @@
     w_self = lax.all_gather(self_weight.astype(LOW), "fsdp", axis=1, tiled=True)
     gain_full = lax.all_gather(gains.astype(LOW), "fsdp", axis=1, tiled=True).astype(WIDE)
     w_in = lax.all_gather(ffn_in.astype(LOW), "fsdp", axis=1, tiled=True)
-    if quarters:
-        cross_quarter = lax.dynamic_index_in_dim(cross_weight, rep, 0, keepdims=False).astype(LOW)
-        out_quarter = lax.dynamic_index_in_dim(
-            ffn_out.reshape(4, part_rows // 4, model_width), rep, 0, keepdims=False
-        ).astype(LOW)
-        cross_pieces = spread_quarter(cross_quarter)
-        out_pieces = spread_quarter(out_quarter)
-        cross_rows_each, out_rows_each = cross_weight.shape[1], part_rows // 4
-        w_cross = assemble(
-            cross_pieces,
-            (4, model_width, model_width),
-            lambda ref, quarter, at: ref.at[quarter, pl.ds(at * cross_rows_each, cross_rows_each)],
-            "assemble_cross",
-        )
-        w_out = assemble(
-            out_pieces,
-            (hidden_width, model_width),
-            lambda ref, quarter, at: ref.at[pl.ds((at * 4 + quarter) * out_rows_each, out_rows_each)],
-            "assemble_out",
-        )
-    else:
-        w_cross = lax.all_gather(cross_weight.astype(LOW), "fsdp", axis=1, tiled=True)
-        w_out = lax.all_gather(ffn_out.astype(LOW), "fsdp", axis=0, tiled=True)
 
     bucket_mask = (buckets[None, :] == jnp.arange(BUCKETS)[:, None]).astype(WIDE)
     by_distance = jnp.sum(table.T[:, :, None] * bucket_mask[None], axis=1)
@@ -741,37 +740,81 @@
     *kept_one, after_self = attention_forward(
         True, dec_rows, no_source, dec_len, gain_full[0:1], w_self, backwards
     )
+    if quarters:
+        cross_quarter = lax.dynamic_index_in_dim(cross_weight, rep, 0, keepdims=False).astype(LOW)
+        out_quarter = lax.dynamic_index_in_dim(
+            ffn_out.reshape(4, part_rows // 4, model_width), rep, 0, keepdims=False
+        ).astype(LOW)
+        cross_rows_each, out_rows_each = cross_weight.shape[1], part_rows // 4
+        cross_pieces = with_partner(across_reps(along_line(cross_quarter)))
+        w_cross = assemble(
+            list(lax.optimization_barrier((*cross_pieces, after_self))[:-1]),
+            (4, model_width, model_width),
+            lambda ref, quarter, at: ref.at[quarter, pl.ds(at * cross_rows_each, cross_rows_each)],
+            "assemble_cross",
+        )
+        out_line = along_line(after(out_quarter, w_self))
+        out_near = across_reps(after(out_line, after_self))
+    else:
+        w_cross = lax.all_gather(cross_weight.astype(LOW), "fsdp", axis=1, tiled=True)
+        w_out = lax.all_gather(ffn_out.astype(LOW), "fsdp", axis=0, tiled=True)
     *kept_two, after_cross = attention_forward(
         False, after_self, mem_rows, enc_len, gain_full[1:2], w_cross, no_bias
     )
+    if quarters:
+        out_near = list(lax.optimization_barrier((*out_near, after_cross))[:-1])
+        w_out = assemble(
+            with_partner(out_near),
+            (hidden_width, model_width),
+            lambda ref, quarter, at: ref.at[pl.ds((at * 4 + quarter) * out_rows_each, out_rows_each)],
+            "assemble_out",
+        )
     layer_out, grad_cross, grad_in, grad_out, gain_three = feed_forward_both(
         after_cross, grad_rows, dec_len, gain_full[2:3], w_in, w_out
     )
+    scatter = lambda value, at: lax.psum_scatter(value, "fsdp", scatter_dimension=at, tiled=True)
+    if quarters:
+        own_gate = scatter(grad_in[0], 0)
+        out_sum = rep_parts(grad_out)
     grad_self, grad_k_two, grad_v_two, grad_cross_weights, gain_two, _ = attention_backward(
         False, after_self, mem_rows, grad_cross, enc_len, gain_full[1:2], w_cross, no_bias, kept_two
     )
+    if quarters:
+        grad_self, own_gate, *out_sum = lax.optimization_barrier((grad_self, own_gate, *out_sum))
+        own_up = scatter(grad_in[1], 0)
+        cross_sum = rep_parts(grad_cross_weights)
     input_grad, _, _, grad_self_weights, gain_one, dist_grad = attention_backward(
         True, dec_rows, no_source, grad_self, dec_len, gain_full[0:1], w_self, by_distance, kept_one
     )
+    if quarters:
+        gain_one, own_gate, own_up, *sums = lax.optimization_barrier(
+            (gain_one, own_gate, own_up, *out_sum, *cross_sum)
+        )
+        out_sum, cross_sum = sums[:4], sums[4:]
     memory_grad = memory_gradient(after(grad_k_two, gain_one), grad_v_two, w_cross)
     layer_out = layer_out.reshape(dec_in.shape)
     input_grad = input_grad.reshape(dec_in.shape)
     memory_grad = memory_grad.reshape(memory.shape)
     table_part = jnp.sum(bucket_mask[:, None, :] * dist_grad[None, :H, :], axis=2)
 
-    scatter = lambda value, at: lax.psum_scatter(value, "fsdp", scatter_dimension=at, tiled=True)
     small = jnp.concatenate(
         [gain_one.reshape(-1), gain_two.reshape(-1), gain_three.reshape(-1), table_part.reshape(-1)]
     )
     if quarters:
-        cut = lambda value: value.reshape(4, -1, value.shape[-1])
-        own_in = scatter(grad_in, 1)
-        own_in = rep_collect(rep_reduce(cut(own_in))).reshape(own_in.shape)
-        own_out = scatter(rep_reduce(grad_out).reshape(-1, model_width), 0)
-        own_out = rep_collect(own_out).reshape(ffn_out.shape)
-        own_cross = rep_collect(scatter(rep_reduce(grad_cross_weights), 0))
         own_self = scatter(grad_self_weights, 1)
-        own_self = rep_collect(rep_reduce(own_self))
+        quarter = jnp.concatenate(
+            [
+                add_up(cross_sum).reshape(shards, -1, model_width),
+                add_up(out_sum).reshape(shards, -1, model_width),
+            ],
+            axis=1,
+        )
+        both = rep_collect(scatter_line(quarter))
+        own_cross, own_out = both[:, : cross_weight.shape[1]], both[:, cross_weight.shape[1] :]
+        own_out = own_out.reshape(ffn_out.shape)
+        own_in = jnp.stack([own_gate, own_up])
+        own_in = rep_collect(add_up(rep_parts(own_in.reshape(4, -1, hidden_width)))).reshape(ffn_in.shape)
+        own_self = rep_collect(add_up(rep_parts(own_self)))
         over_shards = lambda vector: butterfly(vector, from_shard, shards)
         small = butterfly(butterfly(small, from_shard, shards), from_rep, reps)
     else:

time: 795 us -> 546 us (0.69)
  Pallas kernels: 443 us -> 211 us
  waiting for transfers between devices: 185 us -> 99.1 us
  starting transfers between devices: 73.3 us -> 97.1 us
  local copies, waits for them, and re-layouts: 19.5 us -> 43.1 us
  other arithmetic: 35.2 us -> 52.7 us
    pallas_call x2, Pallas kernels: 242 us -> 10.1 us  [assemble(): pl.pallas_call(functools.partial(assemble_kernel, place, hops), in_specs=...]
    reduce_scatter x4 -> x3, waiting for transfers between devices: 45.2 us -> 0.04 us  [per_device(): lax.psum_scatter(value, 'fsdp', scatter_dimension=at, tiled=True)]
    ppermute x64 -> x65, waiting for transfers between devices: 139 us -> 96.4 us  [flat_permute(): return lax.ppermute(value, ('rep', 'fsdp'), pairs)]
    ppermute x64 -> x65, starting transfers between devices: 73 us -> 96.9 us  [flat_permute(): return lax.ppermute(value, ('rep', 'fsdp'), pairs)]
  transfers between devices with their start and end apart: 70 -> 70, of which waited for: 31 -> 24; matrix products, arithmetic and copies ran while one was open for 5% -> 13% of each run, Pallas kernels for 50% -> 31%
where the time goes in v4:
time: 546 us; the launch traced here: 537 us
  Pallas kernels  211 us (39%)
  waiting for transfers between devices  99.1 us (18%)
  starting transfers between devices  97.1 us (18%)
  other arithmetic  52.7 us (10%)
  local copies, waits for them, and re-layouts  43.1 us (8%)
  between operations  17.1 us (3%)
  blocking collectives  16.6 us (3%)
    ppermute x65, starting transfers between devices, flat_permute(): return lax.ppermute(value, ('rep', 'fsdp'), pairs)  96.9 us
    ppermute x65, waiting for transfers between devices, flat_permute(): return lax.ppermute(value, ('rep', 'fsdp'), pairs)  96.4 us
    pallas_call x2, Pallas kernels, attention_backward(): pl.pallas_call(functools.partial(backward_kernel, causal, seq_count), gri...  92.6 us
    pallas_call x2, Pallas kernels, attention_forward(): pl.pallas_call(functools.partial(forward_kernel, causal, seq_count), grid...  55.1 us
    pallas_call x1, Pallas kernels, feed_forward_both(): pl.pallas_call(functools.partial(feed_kernel, seq_count), grid=(hidden //...  46.7 us
    all_gather x1, blocking collectives, per_device(): lax.all_gather(gains.astype(LOW), 'fsdp', axis=1, tiled=True).astype(WIDE)  16.6 us
  transfers between devices with their start and end apart: 70, of which 24 were waited for; matrix products, arithmetic and copies ran while one was open for 13% of the time, Pallas kernels for 31%

profile of v4, /device:TPU:0, one launch (start us, length us, event | category | flops | bytes accessed | tf_op | source)
XLA Modules:
  0.0 536.8 jit_solution(15717177236130651037)
XLA Ops:
  21.0 16.6 %all-gather = bf16[8,96,3]{1,2,0:T(4,128)(2,1)S(1)} all-gather(bf16[1,96,3]{1,2,0:T(4,128)(2,1)S(1)} %get-tuple-element.313), channel_id=1, replica_groups=mesh['rep'=4,'fsdp'=8] {'fsdp'}, dimensions={0}, use_global_device_ids=true | all-gather | bytes 5184 | tf_op jit(solution)/shard_map/all_gather | solution.py:727
  46.5 9.4 %collective-permute-done.3.refs_1_ = bf16[4,96,768]{2,1,0:T(8,128)(2,1)S(1)} collective-permute-done((bf16[4,96,768]{2,1,0:T(8,128)(2,1)S(1)}, bf16[4,96,768]{2,1,0:T(8,128)(2,1)S(1)}, u32[]{:S(2)}, u32[]{:S(2)}) %collective-permute-start.3) | collective-permute-done | bytes 589856 | tf_op jit(solution)/shard_map/ppermute | solution.py:555
  55.9 13.1 %collective-permute-done.4.refs_2_ = bf16[4,96,768]{2,1,0:T(8,128)(2,1)S(1)} collective-permute-done((bf16[4,96,768]{2,1,0:T(8,128)(2,1)S(1)}, bf16[4,96,768]{2,1,0:T(8,128)(2,1)S(1)}, u32[]{:S(2)}, u32[]{:S(2)}) %collective-permute-start.4) | collective-permute-done | bytes 589856 | tf_op jit(solution)/shard_map/ppermute | solution.py:555
  72.1 9.7 %collective-permute-start.10 = (bf16[64,768]{1,0:T(8,128)(2,1)S(1)}, bf16[64,768]{1,0:T(8,128)(2,1)S(1)}, u32[]{:S(2)}, u32[]{:S(2)}) collective-permute-start(bf16[64,768]{1,0:T(8,128)(2,1)S(1)} %fusion.22), channel_id=1, source_target_pairs={{0,2},{1,3},{2,4},{3,5},{4,6},{5,7},{6,0},{7,1},{8,10},{9,11},{10,... | collective-permute-start | bytes 294920 | tf_op jit(solution)/shard_map/ppermute | solution.py:555
  82.3 26.8 %self_forward.1 = (bf16[1024,768]{1,0:T(8,128)(2,1)}, bf16[1024,768]{1,0:T(8,128)(2,1)}, bf16[1024,768]{1,0:T(8,128)(2,1)}, bf16[1024,768]{1,0:T(8,128)(2,1)}, f...) custom-call(s32[2]{0:T(128)} %length_ref.9, bf16[1024,768]{1,0:T(8,128)(2,1)} %bitcast.159, ...), custom_call_target="tpu_custom_call" | custom-call | flops 31050000384 | bytes 20971520 | tf_op jit(solution)/shard_map/self_forward/pallas_call | solution.py:186
  114.6 5.5 %assemble_cross.1.wq_ref.wk_ref.wv_ref.wo_ref = bf16[4,768,768]{2,1,0:T(8,128)(2,1)} custom-call(s32[3]{0:T(128)} %pad_add_fusion.where_ref, bf16[4,96,768]{2,1,0:T(8,128)(2,1)} %copy-done.17, bf16[4,96,768]{2,1,0:T(8,128)(2,1)} %copy-done.49, bf16[4,96,768]{2,1,0:T(8,128)(2,1)} %copy-done.50, bf16[4,96,768]{2,1,0:T(8,128)(2,1)} %copy-done.51, ...), custom_call_target="tpu_custom_call" | custom-call | flops 4600000000 | bytes 8388608 | tf_op jit(solution)/shard_map/assemble_cross/pallas_call | solution.py:624
  126.5 28.3 %cross_forward.1 = (bf16[1024,768]{1,0:T(8,128)(2,1)}, bf16[1024,768]{1,0:T(8,128)(2,1)}, bf16[1024,768]{1,0:T(8,128)(2,1)}, bf16[1024,768]{1,0:T(8,128)(2,1)}, ...) custom-call(s32[2]{0:T(128)} %length_ref.8, f32[1024,768]{1,0:T(8,128)} %get-tuple-element.83.x_ref, ...), custom_call_target="tpu_custom_call" | custom-call | flops 31050000384 | bytes 20971520 | tf_op jit(solution)/shard_map/cross_forward/pallas_call | solution.py:186
  159.3 4.6 assemble_out.1.wd_ref
  164.0 46.7 %feed_forward_both.1 = (bf16[1024,768]{1,0:T(8,128)(2,1)}, f32[1024,768]{1,0:T(8,128)}, bf16[2,768,2048]{2,1,0:T(8,128)(2,1)}, bf16[4,8,64,768]{3,2,1,0:T(8,128)(2,1)}, f32[1,768]{1,0:T(1,128)}) custom-call(s32[2]{0:T(128)} %length_ref.9, f32[1024,768]{1,0:T(8,128)} %get-tuple-element.92.after_ref, bf16[1024,768]{1,0:T(8,128)(2,1)} %bitcast.156, ...), custom_call_target="tpu_custom_call" | custom-call | flops 52899999744 | bytes 41943040 | tf_op jit(solution)/shard_map/feed_forward_both/pallas_call | solution.py:304
  210.7 6.7 %slice_bitcast_fusion = (bf16[768,2048]{1,0:T(8,128)(2,1)}, bf16[768,2048]{1,0:T(8,128)(2,1)}) fusion(bf16[2,768,2048]{2,1,0:T(8,128)(2,1)} %get-tuple-element.107), kind=kLoop, calls=%fused_computation | loop fusion | bytes 12582912 | tf_op jit(solution)/shard_map/squeeze | solution.py:784
  224.5 45.2 %cross_backward.1 = (f32[1024,768]{1,0:T(8,128)}, bf16[1024,768]{1,0:T(8,128)(2,1)}, bf16[1024,768]{1,0:T(8,128)(2,1)}, bf16[4,768,768]{2,1,0:T(8,128)(2,1)}, f32[1,768]{1,0:T(1,128)}, /*index=5*/f32[8,128]{1,0:T(8,128)}) custom-call(s32[2]{0:T(128)} %length_ref.8, f32[1024,768]{1,0:T(8,128)} %get-tuple-element.83.x_ref, bf16[1024,768]{1,0:T(8,128)(2,1)} %bitcast.158, ...), custom_call_target="tpu_custom_call" | custom-call | flops 51749998592 | bytes 41943040 | tf_op jit(solution)/shard_map/cross_backward/pallas_call | solution.py:476
  269.8 47.4 %self_backward.1 = (f32[1024,768]{1,0:T(8,128)}, bf16[1024,768]{1,0:T(8,128)(2,1)}, bf16[1024,768]{1,0:T(8,128)(2,1)}, bf16[4,768,768]{2,1,0:T(8,128)(2,1)}, f32[1,768]{1,0:T(1,128)}, /*index=5*/f32[16,512]{1,0:T(8,128)}) custom-call(s32[2]{0:T(128)} %length_ref.9, bf16[1024,768]{1,0:T(8,128)(2,1)} %bitcast.160, bf16[16,128]{1,0:T(8,128)(2,1)} %broadcast_in_dim.4.source_ref, ...), custom_call_target="tpu_custom_call" | custom-call | flops 51749998592 | bytes 41943040 | tf_op jit(solution)/shard_map/self_backward/pallas_call | solution.py:476
  317.3 4.4 dynamic-slice_bitcast_fusion
  330.1 8.5 %collective-permute-start.63 = (f32[3]{0:T(128)S(1)}, f32[3]{0:T(128)S(1)}, u32[]{:S(2)}, u32[]{:S(2)}) collective-permute-start(f32[3]{0:T(128)S(1)} %add.368), channel_id=1, source_target_pairs={{0,2},{1,3},{2,0},{3,1},{4,6},{5,7},{6,4},{7,5},{8,10},{9,11},{10,... | collective-permute-start | bytes 44 | tf_op jit(solution)/shard_map/ppermute | solution.py:555
  340.2 4.6 collective-permute-done.64
  345.4 5.5 %collective-permute-done.23 = bf16[768,768]{1,0:T(8,128)(2,1)} collective-permute-done((bf16[768,768]{1,0:T(8,128)(2,1)}, bf16[768,768]{1,0:T(8,128)(2,1)}, u32[]{:S(2)}, u32[]{:S(2)}) %collective-permute-start.23) | collective-permute-done | bytes 1179680 | tf_op jit(solution)/shard_map/ppermute | solution.py:555
  350.9 24.6 %collective-permute-done.24 = bf16[768,768]{1,0:T(8,128)(2,1)} collective-permute-done((bf16[768,768]{1,0:T(8,128)(2,1)}, bf16[768,768]{1,0:T(8,128)(2,1)}, u32[]{:S(2)}, u32[]{:S(2)}) %collective-permute-start.24) | collective-permute-done | bytes 1179680 | tf_op jit(solution)/shard_map/ppermute | solution.py:555
  384.1 8.5 %collective-permute-start.46 = (f32[2688]{0:T(1024)S(1)}, f32[2688]{0:T(1024)S(1)}, u32[]{:S(2)}, u32[]{:S(2)}) collective-permute-start(f32[2688]{0:T(1024)S(1)} %fusion.40), channel_id=1, source_target_pairs={{0,2},{1,3},{2,0},{3,1},{4,6},{5,7},{6,4},{7,5},{8,10},{9,11},{10,... | collective-permute-start | bytes 32264 | tf_op jit(solution)/shard_map/ppermute | solution.py:555
  395.4 3.7 collective-permute-done.47
  404.3 6.7 %memory_gradient.1 = f32[1024,768]{1,0:T(8,128)} custom-call(bf16[1024,768]{1,0:T(8,128)(2,1)} %get-tuple-element.125.gk_ref, bf16[1024,768]{1,0:T(8,128)(2,1)} %get-tuple-element.126.gv_ref, bf16[4,768,768]{2,1,0:T(8,128)(2,1)} %assemble_cross.1.wq_ref.wk_ref.wv_ref.wo_ref, bf16[4,768,768]{2,1,0:T(8,128)(2,1)} %assemble_cross.1.wq_ref.wk_ref.wv_ref.wo_ref), custom_call_target="tpu_custom_call" | custom-call | flops 8049999872 | bytes 10485760 | tf_op jit(solution)/shard_map/memory_gradient/pallas_call | solution.py:536
  445.9 4.0 collective-permute-done.33
  449.9 9.7 %collective-permute-done.34 = bf16[160,768]{1,0:T(8,128)(2,1)S(1)} collective-permute-done((bf16[160,768]{1,0:T(8,128)(2,1)S(1)}, bf16[160,768]{1,0:T(8,128)(2,1)S(1)}, u32[]{:S(2)}, u32[]{:S(2)}) %collective-permute-start.34) | collective-permute-done | bytes 245792 | tf_op jit(solution)/shard_map/ppermute | solution.py:555
  465.2 3.5 collective-permute-done.36
  481.5 5.8 %collective-permute-start.60 = (f32[770]{0:T(1024)S(1)}, f32[770]{0:T(1024)S(1)}, u32[]{:S(2)}, u32[]{:S(2)}) collective-permute-start(f32[770]{0:T(1024)S(1)} %fusion.39), channel_id=1, source_target_pairs={{0,2},{1,3},{2,0},{3,1},{4,6},{5,7},{6,4},{7,5},{8,10},{9,11},{10,... | collective-permute-start | bytes 9248 | tf_op jit(solution)/shard_map/ppermute | solution.py:555
  (369 shorter events, 170.2 us)
Async XLA Ops:
  7.2 64.9 %all-gather.4.cloned.1.call-start = ((), (), s32[]{:S(2)}) async-start(), calls=%async_computation.3 | async-start | bytes 5308416 | tf_op jit(solution)/shard_map/all_gather | solution.py:726
  10.6 153.4 %all-gather.6.cloned.1.call-start = ((), (), s32[]{:S(2)}) async-start(), calls=%async_computation.4 | async-start | bytes 7077888 | tf_op jit(solution)/shard_map/all_gather | solution.py:728
  12.4 257.4 %reduce-scatter.4.cloned.1.call-start = ((), (), s32[]{:S(2)}) async-start(), calls=%async_computation.5 | async-start | bytes 3538944 | tf_op jit(solution)/shard_map/reduce_scatter | solution.py:775
  13.4 26.1 %collective-permute-start = (bf16[96,768]{1,0:T(8,128)(2,1)S(1)}, bf16[96,768]{1,0:T(8,128)(2,1)S(1)}, u32[]{:S(2)}, u32[]{:S(2)}) collective-permute-start(bf16[96,768]{1,0:T(8,128)(2,1)S(1)} %fusion.41), channel_id=1, source_target_pairs={{0,2},{1,3},{2,4},{3,5},{4,6},{5,7},{6,0},{7,1},{8,10},{9,11},{10,... | collective-permute-start | bytes 442376 | tf_op jit(solution)/shard_map/ppermute | solution.py:555
  16.5 23.1 %collective-permute-start.1 = (bf16[96,768]{1,0:T(8,128)(2,1)S(1)}, bf16[96,768]{1,0:T(8,128)(2,1)S(1)}, u32[]{:S(2)}, u32[]{:S(2)}) collective-permute-start(bf16[96,768]{1,0:T(8,128)(2,1)S(1)} %fusion.41), channel_id=1, source_target_pairs={{0,4},{1,5},{2,6},{3,7},{4,0},{5,1},{6,2},{7,3},{8,12},{9,13},{10,... | collective-permute-start | bytes 442376 | tf_op jit(solution)/shard_map/ppermute | solution.py:555
  41.1 27.9 %collective-permute-start.4 = (bf16[4,96,768]{2,1,0:T(8,128)(2,1)S(1)}, bf16[4,96,768]{2,1,0:T(8,128)(2,1)S(1)}, u32[]{:S(2)}, u32[]{:S(2)}) collective-permute-start(bf16[4,96,768]{2,1,0:T(8,128)(2,1)S(1)} %pad_maximum_fusion.4.refs_0_), channel_id=1, source_target_pairs={{0,16},{1,17},{2,18},{3,19},{4,20},{5,21},{6,22},{7,23},{8,24},{9,... | collective-permute-start | bytes 1769480 | tf_op jit(solution)/shard_map/ppermute | solution.py:555
  42.6 26.4 %collective-permute-start.5 = (bf16[4,96,768]{2,1,0:T(8,128)(2,1)S(1)}, bf16[4,96,768]{2,1,0:T(8,128)(2,1)S(1)}, u32[]{:S(2)}, u32[]{:S(2)}) collective-permute-start(bf16[4,96,768]{2,1,0:T(8,128)(2,1)S(1)} %pad_maximum_fusion.4.refs_0_), channel_id=1, source_target_pairs={{0,24},{1,25},{2,26},{3,27},{4,28},{5,29},{6,30},{7,31},{8,16},{9,... | collective-permute-start | bytes 1769480 | tf_op jit(solution)/shard_map/ppermute | solution.py:555
  46.5 62.7 %collective-permute-start.6 = (bf16[4,96,768]{2,1,0:T(8,128)(2,1)S(1)}, bf16[4,96,768]{2,1,0:T(8,128)(2,1)}, u32[]{:S(2)}, u32[]{:S(2)}) collective-permute-start(bf16[4,96,768]{2,1,0:T(8,128)(2,1)S(1)} %pad_maximum_fusion.4.refs_0_), channel_id=1, source_target_pairs={{0,1},{1,0},{2,3},{3,2},{4,5},{5,4},{6,7},{7,6},{8,9},{9,8},{10,11... | collective-permute-start | bytes 1769480 | tf_op jit(solution)/shard_map/ppermute | solution.py:555
  55.9 55.7 %collective-permute-start.7 = (bf16[4,96,768]{2,1,0:T(8,128)(2,1)S(1)}, bf16[4,96,768]{2,1,0:T(8,128)(2,1)}, u32[]{:S(2)}, u32[]{:S(2)}) collective-permute-start(bf16[4,96,768]{2,1,0:T(8,128)(2,1)S(1)} %collective-permute-done.3.refs_1_), channel_id=1, source_target_pairs={{0,1},{1,0},{2,3},{3,2},{4,5},{5,4},{6,7},{7,6},{8,9},{9,8},{10,11... | collective-permute-start | bytes 1769480 | tf_op jit(solution)/shard_map/ppermute | solution.py:555
  69.0 45.6 %collective-permute-start.8 = (bf16[4,96,768]{2,1,0:T(8,128)(2,1)S(1)}, bf16[4,96,768]{2,1,0:T(8,128)(2,1)}, u32[]{:S(2)}, u32[]{:S(2)}) collective-permute-start(bf16[4,96,768]{2,1,0:T(8,128)(2,1)S(1)} %collective-permute-done.4.refs_2_), channel_id=1, source_target_pairs={{0,1},{1,0},{2,3},{3,2},{4,5},{5,4},{6,7},{7,6},{8,9},{9,8},{10,11... | collective-permute-start | bytes 1769480 | tf_op jit(solution)/shard_map/ppermute | solution.py:555
  69.0 45.6 %collective-permute-start.9 = (bf16[4,96,768]{2,1,0:T(8,128)(2,1)S(1)}, bf16[4,96,768]{2,1,0:T(8,128)(2,1)}, u32[]{:S(2)}, u32[]{:S(2)}) collective-permute-start(bf16[4,96,768]{2,1,0:T(8,128)(2,1)S(1)} %collective-permute-done.5.refs_3_), channel_id=1, source_target_pairs={{0,1},{1,0},{2,3},{3,2},{4,5},{5,4},{6,7},{7,6},{8,9},{9,8},{10,11... | collective-permute-start | bytes 1769480 | tf_op jit(solution)/shard_map/ppermute | solution.py:555
  72.1 48.0 %collective-permute-start.10 = (bf16[64,768]{1,0:T(8,128)(2,1)S(1)}, bf16[64,768]{1,0:T(8,128)(2,1)S(1)}, u32[]{:S(2)}, u32[]{:S(2)}) collective-permute-start(bf16[64,768]{1,0:T(8,128)(2,1)S(1)} %fusion.22), channel_id=1, source_target_pairs={{0,2},{1,3},{2,4},{3,5},{4,6},{5,7},{6,0},{7,1},{8,10},{9,11},{10,... | collective-permute-start | bytes 294920 | tf_op jit(solution)/shard_map/ppermute | solution.py:555
  122.4 32.4 %collective-permute-start.13 = (bf16[4,64,768]{2,1,0:T(8,128)(2,1)S(1)}, bf16[4,64,768]{2,1,0:T(8,128)(2,1)S(1)}, u32[]{:S(2)}, u32[]{:S(2)}) collective-permute-start(bf16[4,64,768]{2,1,0:T(8,128)(2,1)S(1)} %pad_maximum_fusion.6.refs_0_), channel_id=1, source_target_pairs={{0,8},{1,9},{2,10},{3,11},{4,12},{5,13},{6,14},{7,15},{8,0},{9,1},... | collective-permute-start | bytes 1179656 | tf_op jit(solution)/shard_map/ppermute | solution.py:555
  123.9 31.0 %collective-permute-start.14 = (bf16[4,64,768]{2,1,0:T(8,128)(2,1)S(1)}, bf16[4,64,768]{2,1,0:T(8,128)(2,1)S(1)}, u32[]{:S(2)}, u32[]{:S(2)}) collective-permute-start(bf16[4,64,768]{2,1,0:T(8,128)(2,1)S(1)} %pad_maximum_fusion.6.refs_0_), channel_id=1, source_target_pairs={{0,16},{1,17},{2,18},{3,19},{4,20},{5,21},{6,22},{7,23},{8,24},{9,... | collective-permute-start | bytes 1179656 | tf_op jit(solution)/shard_map/ppermute | solution.py:555
  125.4 29.5 %collective-permute-start.15 = (bf16[4,64,768]{2,1,0:T(8,128)(2,1)S(1)}, bf16[4,64,768]{2,1,0:T(8,128)(2,1)S(1)}, u32[]{:S(2)}, u32[]{:S(2)}) collective-permute-start(bf16[4,64,768]{2,1,0:T(8,128)(2,1)S(1)} %pad_maximum_fusion.6.refs_0_), channel_id=1, source_target_pairs={{0,24},{1,25},{2,26},{3,27},{4,28},{5,29},{6,30},{7,31},{8,16},{9,... | collective-permute-start | bytes 1179656 | tf_op jit(solution)/shard_map/ppermute | solution.py:555
  217.4 158.2 %reduce-scatter.6.cloned.1.call-start = ((), (), s32[]{:S(2)}) async-start(), calls=%async_computation.6 | async-start | bytes 3538944 | tf_op jit(solution)/shard_map/reduce_scatter | solution.py:775
  221.0 48.8 %collective-permute-start.20 = (bf16[8,64,768]{2,1,0:T(8,128)(2,1)}, bf16[8,64,768]{2,1,0:T(8,128)(2,1)S(1)}, u32[]{:S(2)}, u32[]{:S(2)}) collective-permute-start(bf16[8,64,768]{2,1,0:T(8,128)(2,1)} %get-tuple-element.271), channel_id=1, source_target_pairs={{0,8},{1,9},{2,10},{3,11},{4,12},{5,13},{6,14},{7,15},{8,0},{9,1},... | collective-permute-start | bytes 2359304 | tf_op jit(solution)/shard_map/ppermute | solution.py:555
  222.4 47.4 %collective-permute-start.21 = (bf16[8,64,768]{2,1,0:T(8,128)(2,1)}, bf16[8,64,768]{2,1,0:T(8,128)(2,1)S(1)}, u32[]{:S(2)}, u32[]{:S(2)}) collective-permute-start(bf16[8,64,768]{2,1,0:T(8,128)(2,1)} %get-tuple-element.270), channel_id=1, source_target_pairs={{0,16},{1,17},{2,18},{3,19},{4,20},{5,21},{6,22},{7,23},{8,24},{9,... | collective-permute-start | bytes 2359304 | tf_op jit(solution)/shard_map/ppermute | solution.py:555
  223.9 45.9 %collective-permute-start.22 = (bf16[8,64,768]{2,1,0:T(8,128)(2,1)}, bf16[8,64,768]{2,1,0:T(8,128)(2,1)S(1)}, u32[]{:S(2)}, u32[]{:S(2)}) collective-permute-start(bf16[8,64,768]{2,1,0:T(8,128)(2,1)} %get-tuple-element.269), channel_id=1, source_target_pairs={{0,24},{1,25},{2,26},{3,27},{4,28},{5,29},{6,30},{7,31},{8,16},{9,... | collective-permute-start | bytes 2359304 | tf_op jit(solution)/shard_map/ppermute | solution.py:555
  224.5 251.1 %reduce-scatter.8.cloned.1.call-start = ((), (), s32[]{:S(2)}) async-start(), calls=%async_computation.7 | async-start | bytes 5308416 | tf_op jit(solution)/shard_map/reduce_scatter | solution.py:775
  321.7 29.2 %collective-permute-start.23 = (bf16[768,768]{1,0:T(8,128)(2,1)}, bf16[768,768]{1,0:T(8,128)(2,1)}, u32[]{:S(2)}, u32[]{:S(2)}) collective-permute-start(bf16[768,768]{1,0:T(8,128)(2,1)} %get-tuple-element.267), channel_id=1, source_target_pairs={{0,8},{1,9},{2,10},{3,11},{4,12},{5,13},{6,14},{7,15},{8,0},{9,1},... | collective-permute-start | bytes 3538952 | tf_op jit(solution)/shard_map/ppermute | solution.py:555
  323.1 52.4 %collective-permute-start.24 = (bf16[768,768]{1,0:T(8,128)(2,1)}, bf16[768,768]{1,0:T(8,128)(2,1)}, u32[]{:S(2)}, u32[]{:S(2)}) collective-permute-start(bf16[768,768]{1,0:T(8,128)(2,1)} %get-tuple-element.266), channel_id=1, source_target_pairs={{0,16},{1,17},{2,18},{3,19},{4,20},{5,21},{6,22},{7,23},{8,24},{9,... | collective-permute-start | bytes 3538952 | tf_op jit(solution)/shard_map/ppermute | solution.py:555
  324.6 50.9 %collective-permute-start.25 = (bf16[768,768]{1,0:T(8,128)(2,1)}, bf16[768,768]{1,0:T(8,128)(2,1)}, u32[]{:S(2)}, u32[]{:S(2)}) collective-permute-start(bf16[768,768]{1,0:T(8,128)(2,1)} %get-tuple-element.265), channel_id=1, source_target_pairs={{0,24},{1,25},{2,26},{3,27},{4,28},{5,29},{6,30},{7,31},{8,16},{9,... | collective-permute-start | bytes 3538952 | tf_op jit(solution)/shard_map/ppermute | solution.py:555
  395.4 42.2 %collective-permute-start.32 = (bf16[4,160,768]{2,1,0:T(8,128)(2,1)}, bf16[4,160,768]{2,1,0:T(8,128)(2,1)}, u32[]{:S(2)}, u32[]{:S(2)}) collective-permute-start(bf16[4,160,768]{2,1,0:T(8,128)(2,1)} %fusion.8), channel_id=1, source_target_pairs={{0,1},{1,0},{2,3},{3,2},{4,5},{5,4},{6,7},{7,6},{8,9},{9,8},{10,11... | collective-permute-start | bytes 2949128 | tf_op jit(solution)/shard_map/ppermute | solution.py:555
  (105 other events, 1470.7 us)
Sparse Core Ops, SparseCore 0:
  10.7 61.3 all-gather.3
  74.2 69.8 all-gather.5
  217.5 45.7 reduce-scatter.3
  265.4 39.3 reduce-scatter.5
  317.4 60.3 reduce-scatter.7

commit v5 on v4

--- a/solution.py
+++ b/solution.py
@@ -335,11 +335,16 @@
 
 
 def backward_kernel(
-    causal, seq_count, length_ref, x_ref, source_ref, grad_ref, gain_ref, wq_ref, wk_ref, wv_ref, wo_ref, wave_ref,
-    q_ref, k_ref, v_ref, mix_ref, total_ref, mix_all_ref,
-    grad_x_ref, gk_out_ref, gv_out_ref, dw_ref, dgain_ref, dist_ref,
-    normed_t, source_t, mix_t, branch, grad_mix, gq, bias, score_sum, grad_total,
+    causal, seq_count, length_ref, x_ref, source_ref, grad_ref, gain_ref, wq_ref, wo_ref, wave_ref,
+    q_ref, k_ref, v_ref, mix_ref, total_ref, mix_all_ref, *refs,
 ):
+    if causal:
+        gq, gk_out_ref, gv_out_ref, dw_ref, dist_ref = refs[:5]
+        normed_t, branch, grad_mix, bias, score_sum = refs[5:]
+        source_t = normed_t
+    else:
+        grad_x_ref, gk_out_ref, gv_out_ref, dw_ref, dgain_ref, next_ref = refs[:6]
+        normed_t, branch, grad_mix, gq, source_t, mix_t, grad_total = refs[6:]
     group = pl.program_id(0)
     row_count = x_ref.shape[0]
     rows = q_ref.shape[0] // seq_count
@@ -352,16 +357,18 @@
             value = x_ref[at : at + size, :].astype(WIDE)
             low = (value * rms_rate(value) * gain_ref[...]).astype(LOW)
             normed_t[:, at : at + size] = low.T
-            mix_t[:, at : at + size] = mix_all_ref[at : at + size, :].T
             branch[at : at + size, :] = grad_ref[at : at + size, :].astype(LOW)
-            grad_total[at : at + size, :] = jnp.zeros((size, value.shape[1]), WIDE)
+            if not causal:
+                mix_t[:, at : at + size] = mix_all_ref[0, at : at + size, :].T
+                grad_total[at : at + size, :] = jnp.zeros((size, value.shape[1]), WIDE)
         if not causal:
             for at, size in chunks(source_ref.shape[0], 256):
                 source_t[:, at : at + size] = source_ref[at : at + size, :].T
 
     grad_mix[...] = nt(branch[...], wo_ref[...]).astype(LOW)
-    across = pl.ds(pl.multiple_of(group * GROUP, GROUP), GROUP)
-    dw_ref[3] = nn(mix_t[...], branch[:, across]).astype(LOW)
+    if not causal:
+        across = pl.ds(pl.multiple_of(group * GROUP, GROUP), GROUP)
+        dw_ref[3] = nn(mix_t[...], branch[:, across]).astype(LOW)
 
     for pair in range(2):
         at = pair * PAIR
@@ -442,15 +449,12 @@
                     held = held[:half] + pltpu.roll(held[half:], rows - half, 1)
                 dist_ref[pl.ds(group * 4 + head, 1), :] = held
 
-    if causal:
-        source_t = normed_t
     dw_ref[0] = nn(normed_t[...], gq[...]).astype(LOW)
     dw_ref[1] = nn(source_t[...], gk_out_ref[...]).astype(LOW)
     dw_ref[2] = nn(source_t[...], gv_out_ref[...]).astype(LOW)
-    update = nt(gq[...], wq_ref[...])
     if causal:
-        update = update + nt(gk_out_ref[...], wk_ref[...]) + nt(gv_out_ref[...], wv_ref[...])
-    grad_total[...] += update
+        return
+    grad_total[...] += nt(gq[...], wq_ref[...])
 
     @pl.when(group == pl.num_programs(0) - 1)
     def _():
@@ -461,18 +465,48 @@
                 x_ref[part, :].astype(WIDE), gain_ref[...], grad_total[part, :]
             )
             dgain = dgain + gain_part
-            grad_x_ref[part, :] = grad_ref[part, :] + grad_rows
+            grad_rows = grad_ref[part, :] + grad_rows
+            grad_x_ref[part, :] = grad_rows
+            branch[part, :] = grad_rows.astype(LOW)
+            mix_t[:, part] = mix_all_ref[1, part, :].T
         dgain_ref[...] = dgain
-
-
-def attention_backward(causal, x, source, grad, lengths, gain, weights, wave, kept):
+        next_ref[...] = nn(mix_t[...], branch[...]).astype(LOW)
+
+
+def attention_backward(causal, x, source, grad, lengths, gain, weights, wave, kept, mixes):
     row_count, width = x.shape
     seq_count = lengths.shape[0]
     source_rows = row_count if causal else source.shape[0]
     length = row_count // seq_count
     groups = width // GROUP
     low = lambda rows: jax.ShapeDtypeStruct((rows, width), LOW)
-    score = (2, length, length) if causal else (1, 8, PAIR)
+    matrices = 3 if causal else 4
+    gradients = pl.BlockSpec((matrices, width, GROUP), lambda g: (0, 0, g))
+    gradient_shape = jax.ShapeDtypeStruct((matrices, width, width), LOW)
+    if causal:
+        out_specs = [
+            columns(row_count), columns(source_rows), columns(source_rows), gradients, whole(wave.shape),
+        ]
+        out_shape = [
+            low(row_count), low(source_rows), low(source_rows), gradient_shape,
+            jax.ShapeDtypeStruct(wave.shape, WIDE),
+        ]
+        scratch = [pltpu.VMEM((2, length, length), WIDE)] * 2
+    else:
+        out_specs = [
+            whole((row_count, width)), columns(source_rows), columns(source_rows), gradients,
+            whole((1, width)), whole((width, width)),
+        ]
+        out_shape = [
+            jax.ShapeDtypeStruct((row_count, width), WIDE), low(source_rows), low(source_rows), gradient_shape,
+            jax.ShapeDtypeStruct((1, width), WIDE), jax.ShapeDtypeStruct((width, width), LOW),
+        ]
+        scratch = [
+            pltpu.VMEM((row_count, GROUP), LOW),
+            pltpu.VMEM((width, source_rows), LOW),
+            pltpu.VMEM((width, row_count), LOW),
+            pltpu.VMEM((row_count, width), WIDE),
+        ]
     return pl.pallas_call(
         functools.partial(backward_kernel, causal, seq_count),
         grid=(groups,),
@@ -482,46 +516,57 @@
             whole(source.shape),
             whole(grad.shape),
             whole(gain.shape),
-            *weight_specs(width),
+            weight_specs(width)[0],
+            weight_specs(width)[3],
             whole(wave.shape),
             columns(row_count),
             columns(source_rows),
             columns(source_rows),
             columns(row_count),
             pl.BlockSpec((None, row_count, PAIR), lambda g: (g, 0, 0)),
-            whole((row_count, width)),
+            whole(mixes.shape),
         ],
-        out_specs=[
-            whole((row_count, width)),
-            columns(source_rows),
-            columns(source_rows),
-            pl.BlockSpec((4, width, GROUP), lambda g: (0, 0, g)),
-            whole((1, width)),
-            whole(wave.shape),
-        ],
-        out_shape=[
-            jax.ShapeDtypeStruct((row_count, width), WIDE),
-            low(source_rows),
-            low(source_rows),
-            jax.ShapeDtypeStruct(weights.shape, LOW),
-            jax.ShapeDtypeStruct((1, width), WIDE),
-            jax.ShapeDtypeStruct(wave.shape, WIDE),
-        ],
+        out_specs=out_specs,
+        out_shape=out_shape,
         scratch_shapes=[
-            pltpu.VMEM((width, row_count), LOW),
-            pltpu.VMEM((width, source_rows) if not causal else (16, PAIR), LOW),
             pltpu.VMEM((width, row_count), LOW),
             pltpu.VMEM((row_count, width), LOW),
             pltpu.VMEM((row_count, GROUP), LOW),
-            pltpu.VMEM((row_count, GROUP), LOW),
-            pltpu.VMEM(score, WIDE),
-            pltpu.VMEM(score, WIDE),
-            pltpu.VMEM((row_count, width), WIDE),
+            *scratch,
         ],
         cost_estimate=pl.CostEstimate(flops=int(45 * PEAK), bytes_accessed=40 << 20, transcendentals=0),
         compiler_params=pltpu.CompilerParams(vmem_limit_bytes=VMEM_BYTES),
         name="self_backward" if causal else "cross_backward",
-    )(lengths, x, source, grad, gain, weights, weights, weights, weights, wave, *kept, kept[3])
+    )(lengths, x, source, grad, gain, weights, weights, wave, *kept, mixes)
+
+
+def input_kernel(gq_ref, gk_ref, gv_ref, wq_ref, wk_ref, wv_ref, x_ref, grad_ref, gain_ref, out_ref, dgain_ref):
+    total = nt(gq_ref[...], wq_ref[...]) + nt(gk_ref[...], wk_ref[...]) + nt(gv_ref[...], wv_ref[...])
+    grad_rows, dgain = rms_back(x_ref[...].astype(WIDE), gain_ref[...], total)
+    out_ref[...] = grad_ref[...] + grad_rows
+
+    @pl.when(pl.program_id(0) == 0)
+    def _():
+        dgain_ref[...] = jnp.zeros_like(dgain_ref)
+
+    dgain_ref[...] += dgain
+
+
+def input_gradient(grads, weights, x, grad, gain):
+    rows, width = x.shape
+    block = 256
+    rowwise = pl.BlockSpec((block, width), lambda g: (g, 0))
+    matrix = lambda at: pl.BlockSpec((None, width, width), lambda g: (at, 0, 0))
+    return pl.pallas_call(
+        input_kernel,
+        grid=(rows // block,),
+        in_specs=[rowwise, rowwise, rowwise, matrix(0), matrix(1), matrix(2), rowwise, rowwise, whole((1, width))],
+        out_specs=[rowwise, whole((1, width))],
+        out_shape=[jax.ShapeDtypeStruct((rows, width), WIDE), jax.ShapeDtypeStruct((1, width), WIDE)],
+        cost_estimate=pl.CostEstimate(flops=int(8 * PEAK), bytes_accessed=12 << 20, transcendentals=0),
+        compiler_params=pltpu.CompilerParams(vmem_limit_bytes=VMEM_BYTES),
+        name="input_gradient",
+    )(*grads, weights, weights, weights, x, grad, gain)
 
 
 def memory_kernel(gk_ref, gv_ref, wk_ref, wv_ref, out_ref):
@@ -776,22 +821,38 @@
     if quarters:
         own_gate = scatter(grad_in[0], 0)
         out_sum = rep_parts(grad_out)
-    grad_self, grad_k_two, grad_v_two, grad_cross_weights, gain_two, _ = attention_backward(
-        False, after_self, mem_rows, grad_cross, enc_len, gain_full[1:2], w_cross, no_bias, kept_two
+    grad_self, grad_k_two, grad_v_two, grad_cross_weights, gain_two, grad_wo = attention_backward(
+        False, after_self, mem_rows, grad_cross, enc_len, gain_full[1:2], w_cross, no_bias, kept_two,
+        jnp.stack([kept_two[3], kept_one[3]]),
     )
     if quarters:
         grad_self, own_gate, *out_sum = lax.optimization_barrier((grad_self, own_gate, *out_sum))
         own_up = scatter(grad_in[1], 0)
-        cross_sum = rep_parts(grad_cross_weights)
-    input_grad, _, _, grad_self_weights, gain_one, dist_grad = attention_backward(
-        True, dec_rows, no_source, grad_self, dec_len, gain_full[0:1], w_self, by_distance, kept_one
+        cut_wo = grad_wo.reshape(shards, 4, -1, model_width)
+        rep_pick = lambda at: jnp.concatenate(
+            [
+                lax.dynamic_index_in_dim(grad_cross_weights, at, 0, False).reshape(shards, -1, model_width),
+                lax.dynamic_index_in_dim(cut_wo, at, 1, False),
+            ],
+            axis=1,
+        )
+        grad_self, *cross_parts = lax.optimization_barrier(
+            (grad_self, *[rep_pick(rep ^ way) for way in range(4)])
+        )
+        cross_sum = cross_parts[:1] + [from_rep(cross_parts[way], way) for way in range(1, 4)]
+    *grads_one, grad_self_weights, dist_grad = attention_backward(
+        True, dec_rows, no_source, grad_self, dec_len, gain_full[0:1], w_self, by_distance, kept_one, no_source
     )
     if quarters:
-        gain_one, own_gate, own_up, *sums = lax.optimization_barrier(
-            (gain_one, own_gate, own_up, *out_sum, *cross_sum)
-        )
+        grad_self_weights, *near = lax.optimization_barrier((grad_self_weights, *cross_sum[:3]))
+        cross_sum = near + cross_sum[3:]
+        own_self = scatter(grad_self_weights, 1)
+        grads_one = list(lax.optimization_barrier((*grads_one, grad_self_weights))[:-1])
+    input_grad, gain_one = input_gradient(grads_one, w_self, dec_rows, grad_self, gain_full[0:1])
+    memory_grad = memory_gradient(after(grad_k_two, gain_one), grad_v_two, w_cross)
+    if quarters:
+        memory_grad, own_up, *sums = lax.optimization_barrier((memory_grad, own_up, *out_sum, *cross_sum))
         out_sum, cross_sum = sums[:4], sums[4:]
-    memory_grad = memory_gradient(after(grad_k_two, gain_one), grad_v_two, w_cross)
     layer_out = layer_out.reshape(dec_in.shape)
     input_grad = input_grad.reshape(dec_in.shape)
     memory_grad = memory_grad.reshape(memory.shape)
@@ -801,20 +862,24 @@
         [gain_one.reshape(-1), gain_two.reshape(-1), gain_three.reshape(-1), table_part.reshape(-1)]
     )
     if quarters:
-        own_self = scatter(grad_self_weights, 1)
-        quarter = jnp.concatenate(
+        in_parts = rep_parts(jnp.stack([own_gate, own_up]).reshape(4, -1, hidden_width))
+        quarter = scatter_line(
+            jnp.concatenate(
+                [add_up(cross_sum), add_up(out_sum).reshape(shards, -1, model_width)], axis=1
+            )
+        )
+        own_in = rep_collect(add_up(in_parts)).reshape(ffn_in.shape)
+        both = rep_collect(quarter)
+        cross_end = cross_weight.shape[1]
+        wo_end = cross_end + cross_weight.shape[1] // 4
+        own_cross, own_out = both[:, :cross_end], both[:, wo_end:].reshape(ffn_out.shape)
+        own_self = rep_collect(add_up(rep_parts(own_self.reshape(4, -1, model_width))))
+        own_self = jnp.concatenate(
             [
-                add_up(cross_sum).reshape(shards, -1, model_width),
-                add_up(out_sum).reshape(shards, -1, model_width),
-            ],
-            axis=1,
+                own_self.reshape(3, *self_weight.shape[1:]),
+                both[:, cross_end:wo_end].reshape(1, *self_weight.shape[1:]),
+            ]
         )
-        both = rep_collect(scatter_line(quarter))
-        own_cross, own_out = both[:, : cross_weight.shape[1]], both[:, cross_weight.shape[1] :]
-        own_out = own_out.reshape(ffn_out.shape)
-        own_in = jnp.stack([own_gate, own_up])
-        own_in = rep_collect(add_up(rep_parts(own_in.reshape(4, -1, hidden_width)))).reshape(ffn_in.shape)
-        own_self = rep_collect(add_up(rep_parts(own_self)))
         over_shards = lambda vector: butterfly(vector, from_shard, shards)
         small = butterfly(butterfly(small, from_shard, shards), from_rep, reps)
     else:
@@ -824,7 +889,7 @@
             scatter(grad_out.transpose(1, 0, 2, 3).reshape(hidden_width, model_width), 0)
         )
         own_cross = over_reps(scatter(grad_cross_weights, 1))
-        own_self = over_reps(scatter(grad_self_weights, 1))
+        own_self = over_reps(scatter(jnp.concatenate([grad_self_weights, grad_wo[None]]), 1))
         over_shards = lambda vector: lax.psum(vector, "fsdp")
         small = lax.psum(small, ("rep", "fsdp"))
 

time: 546 us -> 536 us (0.982)
  waiting for transfers between devices: 99.1 us -> 114 us
  local copies, waits for them, and re-layouts: 43.1 us -> 29.8 us
  starting transfers between devices: 97.1 us -> 85.2 us
    ppermute x65, waiting for transfers between devices: 96.4 us -> 110 us  [flat_permute(): return lax.ppermute(value, ('rep', 'fsdp'), pairs)]
    ppermute x65, starting transfers between devices: 96.9 us -> 85 us  [flat_permute(): return lax.ppermute(value, ('rep', 'fsdp'), pairs)]
    pallas_call x2, Pallas kernels: 92.6 us -> 81.2 us  [attention_backward(): pl.pallas_call(functools.partial(backward_kernel, causal, seq_count), gri...]
    pallas_call x0 -> x1, Pallas kernels: none -> 9.86 us  [input_gradient(): pl.pallas_call(input_kernel, grid=(rows // block,), in_specs=[rowwise, ro...]
  transfers between devices with their start and end apart: 70 -> 70, of which waited for: 24 -> 26; matrix products, arithmetic and copies ran while one was open for 13% -> 12% of each run, Pallas kernels for 31% -> 31%
where the time goes in v5:
time: 536 us; the launch traced here: 527 us
  Pallas kernels  210 us (39%)
  waiting for transfers between devices  114 us (21%)
  starting transfers between devices  85.2 us (16%)
  other arithmetic  55.1 us (10%)
  local copies, waits for them, and re-layouts  29.8 us (6%)
  between operations  17.2 us (3%)
  blocking collectives  15.8 us (3%)
    ppermute x65, waiting for transfers between devices, flat_permute(): return lax.ppermute(value, ('rep', 'fsdp'), pairs)  110 us
    ppermute x65, starting transfers between devices, flat_permute(): return lax.ppermute(value, ('rep', 'fsdp'), pairs)  85 us
    pallas_call x2, Pallas kernels, attention_backward(): pl.pallas_call(functools.partial(backward_kernel, causal, seq_count), gri...  81.2 us
    pallas_call x2, Pallas kernels, attention_forward(): pl.pallas_call(functools.partial(forward_kernel, causal, seq_count), grid...  55.5 us
    pallas_call x1, Pallas kernels, feed_forward_both(): pl.pallas_call(functools.partial(feed_kernel, seq_count), grid=(hidden //...  46.4 us
    all_gather x1, blocking collectives, per_device(): lax.all_gather(gains.astype(LOW), 'fsdp', axis=1, tiled=True).astype(WIDE)  15.8 us
  transfers between devices with their start and end apart: 70, of which 26 were waited for; matrix products, arithmetic and copies ran while one was open for 12% of the time, Pallas kernels for 31%

profile of v5, /device:TPU:0, one launch (start us, length us, event | category | flops | bytes accessed | tf_op | source)
XLA Modules:
  0.0 527.3 jit_solution(1793120393820796913)
XLA Ops:
  20.1 15.8 %all-gather = bf16[8,96,3]{1,2,0:T(4,128)(2,1)S(1)} all-gather(bf16[1,96,3]{1,2,0:T(4,128)(2,1)S(1)} %get-tuple-element.347), channel_id=1, replica_groups=mesh['rep'=4,'fsdp'=8] {'fsdp'}, dimensions={0}, use_global_device_ids=true | all-gather | bytes 5184 | tf_op jit(solution)/shard_map/all_gather | solution.py:772
  42.8 10.4 %collective-permute-done.3.refs_1_ = bf16[4,96,768]{2,1,0:T(8,128)(2,1)} collective-permute-done((bf16[4,96,768]{2,1,0:T(8,128)(2,1)S(1)}, bf16[4,96,768]{2,1,0:T(8,128)(2,1)}, u32[]{:S(2)}, u32[]{:S(2)}) %collective-permute-start.3) | collective-permute-done | bytes 589856 | tf_op jit(solution)/shard_map/ppermute | solution.py:600
  53.3 13.0 %collective-permute-done.4.refs_2_ = bf16[4,96,768]{2,1,0:T(8,128)(2,1)} collective-permute-done((bf16[4,96,768]{2,1,0:T(8,128)(2,1)S(1)}, bf16[4,96,768]{2,1,0:T(8,128)(2,1)}, u32[]{:S(2)}, u32[]{:S(2)}) %collective-permute-start.4) | collective-permute-done | bytes 589856 | tf_op jit(solution)/shard_map/ppermute | solution.py:600
  66.8 3.8 all-gather.4.cloned.1.call-done.wq_ref.wk_ref.wv_ref.wo_ref
  70.6 8.7 %collective-permute-start.10 = (bf16[64,768]{1,0:T(8,128)(2,1)S(1)}, bf16[64,768]{1,0:T(8,128)(2,1)S(1)}, u32[]{:S(2)}, u32[]{:S(2)}) collective-permute-start(bf16[64,768]{1,0:T(8,128)(2,1)S(1)} %fusion.18), channel_id=1, source_target_pairs={{0,2},{1,3},{2,4},{3,5},{4,6},{5,7},{6,0},{7,1},{8,10},{9,11},{10,... | collective-permute-start | bytes 294920 | tf_op jit(solution)/shard_map/ppermute | solution.py:600
  79.9 27.3 %self_forward.1 = (bf16[1024,768]{1,0:T(8,128)(2,1)}, bf16[1024,768]{1,0:T(8,128)(2,1)}, bf16[1024,768]{1,0:T(8,128)(2,1)}, bf16[1024,768]{1,0:T(8,128)(2,1)}, f...) custom-call(s32[2]{0:T(128)} %length_ref.9, bf16[1024,768]{1,0:T(8,128)(2,1)} %bitcast.171, ...), custom_call_target="tpu_custom_call" | custom-call | flops 31050000384 | bytes 20971520 | tf_op jit(solution)/shard_map/self_forward/pallas_call | solution.py:186
  112.3 5.6 %assemble_cross.1.wq_ref.wk_ref.wv_ref.wo_ref = bf16[4,768,768]{2,1,0:T(8,128)(2,1)} custom-call(s32[3]{0:T(128)} %pad_add_fusion.where_ref, bf16[4,96,768]{2,1,0:T(8,128)(2,1)} %copy-done.13, bf16[4,96,768]{2,1,0:T(8,128)(2,1)} %collective-permute-done.3.refs_1_, bf16[4,96,768]{2,1,0:T(8,128)(2,1)} %collective-permute-done.4.refs_2_, ...), custom_call_target="tpu_custom_call" | custom-call | flops 4600000000 | bytes 8388608 | tf_op jit(solution)/shard_map/assemble_cross/pallas_call | solution.py:669
  125.2 28.2 %cross_forward.1 = (bf16[1024,768]{1,0:T(8,128)(2,1)}, bf16[1024,768]{1,0:T(8,128)(2,1)}, bf16[1024,768]{1,0:T(8,128)(2,1)}, bf16[1024,768]{1,0:T(8,128)(2,1)}, ...) custom-call(s32[2]{0:T(128)} %length_ref.8, f32[1024,768]{1,0:T(8,128)} %get-tuple-element.98.x_ref, ...), custom_call_target="tpu_custom_call" | custom-call | flops 31050000384 | bytes 20971520 | tf_op jit(solution)/shard_map/cross_forward/pallas_call | solution.py:186
  157.8 4.5 assemble_out.1.wd_ref
  162.3 46.4 %feed_forward_both.1 = (bf16[1024,768]{1,0:T(8,128)(2,1)}, f32[1024,768]{1,0:T(8,128)}, bf16[2,768,2048]{2,1,0:T(8,128)(2,1)}, bf16[4,8,64,768]{3,2,1,0:T(8,128)(2,1)}, f32[1,768]{1,0:T(1,128)}) custom-call(s32[2]{0:T(128)} %length_ref.9, f32[1024,768]{1,0:T(8,128)} %get-tuple-element.107.after_ref, bf16[1024,768]{1,0:T(8,128)(2,1)} %bitcast.168, ...), custom_call_target="tpu_custom_call" | custom-call | flops 52899999744 | bytes 41943040 | tf_op jit(solution)/shard_map/feed_forward_both/pallas_call | solution.py:304
  208.7 6.6 %slice_bitcast_fusion = (bf16[768,2048]{1,0:T(8,128)(2,1)}, bf16[768,2048]{1,0:T(8,128)(2,1)}) fusion(bf16[2,768,2048]{2,1,0:T(8,128)(2,1)} %get-tuple-element.123), kind=kLoop, calls=%fused_computation.1 | loop fusion | bytes 12582912 | tf_op jit(solution)/shard_map/squeeze | solution.py:830
  221.9 6.9 %collective-permute-start.63 = (f32[3]{0:T(128)S(1)}, f32[3]{0:T(128)S(1)}, u32[]{:S(2)}, u32[]{:S(2)}) collective-permute-start(f32[3]{0:T(128)S(1)} %add.373), channel_id=1, source_target_pairs={{0,2},{1,3},{2,0},{3,1},{4,6},{5,7},{6,4},{7,5},{8,10},{9,11},{10,... | collective-permute-start | bytes 44 | tf_op jit(solution)/shard_map/ppermute | solution.py:600
  244.0 47.3 %cross_backward.1 = (f32[1024,768]{1,0:T(8,128)}, bf16[1024,768]{1,0:T(8,128)(2,1)}, bf16[1024,768]{1,0:T(8,128)(2,1)}, bf16[4,768,768]{2,1,0:T(8,128)(2,1)}, f3...) custom-call(s32[2]{0:T(128)} %length_ref.8, f32[1024,768]{1,0:T(8,128)} %get-tuple-element.98.x_ref, ...), custom_call_target="tpu_custom_call" | custom-call | flops 51749998592 | bytes 41943040 | tf_op jit(solution)/shard_map/cross_backward/pallas_call | solution.py:510
  293.6 3.7 constant_dynamic-slice_fusion.13
  306.1 33.9 %self_backward.1 = (bf16[1024,768]{1,0:T(8,128)(2,1)}, bf16[1024,768]{1,0:T(8,128)(2,1)}, bf16[1024,768]{1,0:T(8,128)(2,1)}, bf16[3,768,768]{2,1,0:T(8,128)(2,1)}, f32[16,512]{1,0:T(8,128)}) custom-call(s32[2]{0:T(128)} %length_ref.9, bf16[1024,768]{1,0:T(8,128)(2,1)} %bitcast.172, bf16[16,128]{1,0:T(8,128)(2,1)} %broadcast_in_dim.4.source_ref.mix_all_ref, ...), custom_call_target="tpu_custom_call" | custom-call | flops 51749998592 | bytes 41943040 | tf_op jit(solution)/shard_map/self_backward/pallas_call | solution.py:510
  341.1 26.9 %collective-permute-done.24 = bf16[8,120,768]{2,1,0:T(8,128)(2,1)} collective-permute-done((bf16[8,120,768]{2,1,0:T(8,128)(2,1)}, bf16[8,120,768]{2,1,0:T(8,128)(2,1)}, u32[]{:S(2)}, u32[]{:S(2)}) %collective-permute-start.24) | collective-permute-done | bytes 1474592 | tf_op jit(solution)/shard_map/ppermute | solution.py:600
  368.0 9.9 %input_gradient.1 = (f32[1024,768]{1,0:T(8,128)}, f32[1,768]{1,0:T(1,128)}) custom-call(bf16[1024,768]{1,0:T(8,128)(2,1)} %get-tuple-element.141.gq_ref, bf16[1024,768]{1,0:T(8,128)(2,1)} %get-tuple-element.142.gk_ref, bf16[1024,768]{1,0:T(8,128)(2,1)} %get-tuple-element.143.gv_ref, ...), custom_call_target="tpu_custom_call" | custom-call | flops 9200000000 | bytes 12582912 | tf_op jit(solution)/shard_map/input_gradient/pallas_call | solution.py:560
  378.6 7.0 %memory_gradient.1 = f32[1024,768]{1,0:T(8,128)} custom-call(bf16[1024,768]{1,0:T(8,128)(2,1)} %get-tuple-element.147.gk_ref, bf16[1024,768]{1,0:T(8,128)(2,1)} %get-tuple-element.148.gv_ref, bf16[4,768,768]{2,1,0:T(8,128)(2,1)} %assemble_cross.1.wq_ref.wk_ref.wv_ref.wo_ref, bf16[4,768,768]{2,1,0:T(8,128)(2,1)} %assemble_cross.1.wq_ref.wk_ref.wv_ref.wo_ref), custom_call_target="tpu_custom_call" | custom-call | flops 8049999872 | bytes 10485760 | tf_op jit(solution)/shard_map/memory_gradient/pallas_call | solution.py:581
  403.0 6.1 %collective-permute-done.48 = f32[2688]{0:T(1024)S(1)} collective-permute-done((f32[2688]{0:T(1024)S(1)}, f32[2688]{0:T(1024)S(1)}, u32[]{:S(2)}, u32[]{:S(2)}) %collective-permute-start.48) | collective-permute-done | bytes 10784 | tf_op jit(solution)/shard_map/ppermute | solution.py:600
  430.9 6.6 %collective-permute-done.33 = bf16[184,768]{1,0:T(8,128)(2,1)S(1)} collective-permute-done((bf16[184,768]{1,0:T(8,128)(2,1)S(1)}, bf16[184,768]{1,0:T(8,128)(2,1)S(1)}, u32[]{:S(2)}, u32[]{:S(2)}) %collective-permute-start.33) | collective-permute-done | bytes 282656 | tf_op jit(solution)/shard_map/ppermute | solution.py:600
  437.5 10.3 %collective-permute-done.34 = bf16[184,768]{1,0:T(8,128)(2,1)S(1)} collective-permute-done((bf16[184,768]{1,0:T(8,128)(2,1)S(1)}, bf16[184,768]{1,0:T(8,128)(2,1)S(1)}, u32[]{:S(2)}, u32[]{:S(2)}) %collective-permute-start.34) | collective-permute-done | bytes 282656 | tf_op jit(solution)/shard_map/ppermute | solution.py:600
  453.4 4.2 collective-permute-done.36
  457.6 5.8 %collective-permute-done.37 = bf16[184,768]{1,0:T(8,128)(2,1)S(1)} collective-permute-done((bf16[184,768]{1,0:T(8,128)(2,1)S(1)}, bf16[184,768]{1,0:T(8,128)(2,1)S(1)}, u32[]{:S(2)}, u32[]{:S(2)}) %collective-permute-start.37) | collective-permute-done | bytes 282656 | tf_op jit(solution)/shard_map/ppermute | solution.py:600
  469.9 6.6 %collective-permute-start.60 = (f32[770]{0:T(1024)S(1)}, f32[770]{0:T(1024)S(1)}, u32[]{:S(2)}, u32[]{:S(2)}) collective-permute-start(f32[770]{0:T(1024)S(1)} %fusion.35), channel_id=1, source_target_pairs={{0,2},{1,3},{2,0},{3,1},{4,6},{5,7},{6,4},{7,5},{8,10},{9,11},{10,... | collective-permute-start | bytes 9248 | tf_op jit(solution)/shard_map/ppermute | solution.py:600
  (361 shorter events, 164.7 us)
Async XLA Ops:
  7.2 63.4 %all-gather.4.cloned.1.call-start = ((), (), s32[]{:S(2)}) async-start(), calls=%async_computation.3 | async-start | bytes 5308416 | tf_op jit(solution)/shard_map/all_gather | solution.py:771
  10.6 151.8 %all-gather.6.cloned.1.call-start = ((), (), s32[]{:S(2)}) async-start(), calls=%async_computation.4 | async-start | bytes 7077888 | tf_op jit(solution)/shard_map/all_gather | solution.py:773
  12.4 290.2 %reduce-scatter.4.cloned.1.call-start = ((), (), s32[]{:S(2)}) async-start(), calls=%async_computation.5 | async-start | bytes 3538944 | tf_op jit(solution)/shard_map/reduce_scatter | solution.py:820
  12.4 24.4 %collective-permute-start = (bf16[96,768]{1,0:T(8,128)(2,1)S(1)}, bf16[96,768]{1,0:T(8,128)(2,1)S(1)}, u32[]{:S(2)}, u32[]{:S(2)}) collective-permute-start(bf16[96,768]{1,0:T(8,128)(2,1)S(1)} %fusion.37), channel_id=1, source_target_pairs={{0,2},{1,3},{2,4},{3,5},{4,6},{5,7},{6,0},{7,1},{8,10},{9,11},{10,... | collective-permute-start | bytes 442376 | tf_op jit(solution)/shard_map/ppermute | solution.py:600
  15.5 21.3 %collective-permute-start.1 = (bf16[96,768]{1,0:T(8,128)(2,1)S(1)}, bf16[96,768]{1,0:T(8,128)(2,1)S(1)}, u32[]{:S(2)}, u32[]{:S(2)}) collective-permute-start(bf16[96,768]{1,0:T(8,128)(2,1)S(1)} %fusion.37), channel_id=1, source_target_pairs={{0,4},{1,5},{2,6},{3,7},{4,0},{5,1},{6,2},{7,3},{8,12},{9,13},{10,... | collective-permute-start | bytes 442376 | tf_op jit(solution)/shard_map/ppermute | solution.py:600
  38.3 28.0 %collective-permute-start.4 = (bf16[4,96,768]{2,1,0:T(8,128)(2,1)S(1)}, bf16[4,96,768]{2,1,0:T(8,128)(2,1)}, u32[]{:S(2)}, u32[]{:S(2)}) collective-permute-start(bf16[4,96,768]{2,1,0:T(8,128)(2,1)S(1)} %pad_maximum_fusion.10.refs_0_), channel_id=1, source_target_pairs={{0,16},{1,17},{2,18},{3,19},{4,20},{5,21},{6,22},{7,23},{8,24},{9,... | collective-permute-start | bytes 1769480 | tf_op jit(solution)/shard_map/ppermute | solution.py:600
  39.8 26.5 %collective-permute-start.5 = (bf16[4,96,768]{2,1,0:T(8,128)(2,1)S(1)}, bf16[4,96,768]{2,1,0:T(8,128)(2,1)}, u32[]{:S(2)}, u32[]{:S(2)}) collective-permute-start(bf16[4,96,768]{2,1,0:T(8,128)(2,1)S(1)} %pad_maximum_fusion.10.refs_0_), channel_id=1, source_target_pairs={{0,24},{1,25},{2,26},{3,27},{4,28},{5,29},{6,30},{7,31},{8,16},{9,... | collective-permute-start | bytes 1769480 | tf_op jit(solution)/shard_map/ppermute | solution.py:600
  42.8 64.4 %collective-permute-start.6 = (bf16[4,96,768]{2,1,0:T(8,128)(2,1)S(1)}, bf16[4,96,768]{2,1,0:T(8,128)(2,1)S(1)}, u32[]{:S(2)}, u32[]{:S(2)}) collective-permute-start(bf16[4,96,768]{2,1,0:T(8,128)(2,1)S(1)} %pad_maximum_fusion.10.refs_0_), channel_id=1, source_target_pairs={{0,1},{1,0},{2,3},{3,2},{4,5},{5,4},{6,7},{7,6},{8,9},{9,8},{10,11... | collective-permute-start | bytes 1769480 | tf_op jit(solution)/shard_map/ppermute | solution.py:600
  53.3 56.0 %collective-permute-start.7 = (bf16[4,96,768]{2,1,0:T(8,128)(2,1)}, bf16[4,96,768]{2,1,0:T(8,128)(2,1)}, u32[]{:S(2)}, u32[]{:S(2)}) collective-permute-start(bf16[4,96,768]{2,1,0:T(8,128)(2,1)} %collective-permute-done.3.refs_1_), channel_id=1, source_target_pairs={{0,1},{1,0},{2,3},{3,2},{4,5},{5,4},{6,7},{7,6},{8,9},{9,8},{10,11... | collective-permute-start | bytes 1769480 | tf_op jit(solution)/shard_map/ppermute | solution.py:600
  66.3 46.0 %collective-permute-start.8 = (bf16[4,96,768]{2,1,0:T(8,128)(2,1)}, bf16[4,96,768]{2,1,0:T(8,128)(2,1)}, u32[]{:S(2)}, u32[]{:S(2)}) collective-permute-start(bf16[4,96,768]{2,1,0:T(8,128)(2,1)} %collective-permute-done.4.refs_2_), channel_id=1, source_target_pairs={{0,1},{1,0},{2,3},{3,2},{4,5},{5,4},{6,7},{7,6},{8,9},{9,8},{10,11... | collective-permute-start | bytes 1769480 | tf_op jit(solution)/shard_map/ppermute | solution.py:600
  66.3 46.0 %collective-permute-start.9 = (bf16[4,96,768]{2,1,0:T(8,128)(2,1)}, bf16[4,96,768]{2,1,0:T(8,128)(2,1)}, u32[]{:S(2)}, u32[]{:S(2)}) collective-permute-start(bf16[4,96,768]{2,1,0:T(8,128)(2,1)} %collective-permute-done.5.refs_3_), channel_id=1, source_target_pairs={{0,1},{1,0},{2,3},{3,2},{4,5},{5,4},{6,7},{7,6},{8,9},{9,8},{10,11... | collective-permute-start | bytes 1769480 | tf_op jit(solution)/shard_map/ppermute | solution.py:600
  70.6 47.3 %collective-permute-start.10 = (bf16[64,768]{1,0:T(8,128)(2,1)S(1)}, bf16[64,768]{1,0:T(8,128)(2,1)S(1)}, u32[]{:S(2)}, u32[]{:S(2)}) collective-permute-start(bf16[64,768]{1,0:T(8,128)(2,1)S(1)} %fusion.18), channel_id=1, source_target_pairs={{0,2},{1,3},{2,4},{3,5},{4,6},{5,7},{6,0},{7,1},{8,10},{9,11},{10,... | collective-permute-start | bytes 294920 | tf_op jit(solution)/shard_map/ppermute | solution.py:600
  121.1 32.3 %collective-permute-start.13 = (bf16[4,64,768]{2,1,0:T(8,128)(2,1)S(1)}, bf16[4,64,768]{2,1,0:T(8,128)(2,1)S(1)}, u32[]{:S(2)}, u32[]{:S(2)}) collective-permute-start(bf16[4,64,768]{2,1,0:T(8,128)(2,1)S(1)} %pad_maximum_fusion.13.refs_0_), channel_id=1, source_target_pairs={{0,8},{1,9},{2,10},{3,11},{4,12},{5,13},{6,14},{7,15},{8,0},{9,1},... | collective-permute-start | bytes 1179656 | tf_op jit(solution)/shard_map/ppermute | solution.py:600
  122.5 30.9 %collective-permute-start.14 = (bf16[4,64,768]{2,1,0:T(8,128)(2,1)S(1)}, bf16[4,64,768]{2,1,0:T(8,128)(2,1)S(1)}, u32[]{:S(2)}, u32[]{:S(2)}) collective-permute-start(bf16[4,64,768]{2,1,0:T(8,128)(2,1)S(1)} %pad_maximum_fusion.13.refs_0_), channel_id=1, source_target_pairs={{0,16},{1,17},{2,18},{3,19},{4,20},{5,21},{6,22},{7,23},{8,24},{9,... | collective-permute-start | bytes 1179656 | tf_op jit(solution)/shard_map/ppermute | solution.py:600
  123.8 29.7 %collective-permute-start.15 = (bf16[4,64,768]{2,1,0:T(8,128)(2,1)S(1)}, bf16[4,64,768]{2,1,0:T(8,128)(2,1)S(1)}, u32[]{:S(2)}, u32[]{:S(2)}) collective-permute-start(bf16[4,64,768]{2,1,0:T(8,128)(2,1)S(1)} %pad_maximum_fusion.13.refs_0_), channel_id=1, source_target_pairs={{0,24},{1,25},{2,26},{3,27},{4,28},{5,29},{6,30},{7,31},{8,16},{9,... | collective-permute-start | bytes 1179656 | tf_op jit(solution)/shard_map/ppermute | solution.py:600
  215.3 170.2 %reduce-scatter.6.cloned.1.call-start = ((), (), s32[]{:S(2)}) async-start(), calls=%async_computation.6 | async-start | bytes 3538944 | tf_op jit(solution)/shard_map/reduce_scatter | solution.py:820
  240.5 62.0 %collective-permute-start.20 = (bf16[8,64,768]{2,1,0:T(8,128)(2,1)}, bf16[8,64,768]{2,1,0:T(8,128)(2,1)}, u32[]{:S(2)}, u32[]{:S(2)}) collective-permute-start(bf16[8,64,768]{2,1,0:T(8,128)(2,1)} %get-tuple-element.301), channel_id=1, source_target_pairs={{0,8},{1,9},{2,10},{3,11},{4,12},{5,13},{6,14},{7,15},{8,0},{9,1},... | collective-permute-start | bytes 2359304 | tf_op jit(solution)/shard_map/ppermute | solution.py:600
  241.8 60.7 %collective-permute-start.21 = (bf16[8,64,768]{2,1,0:T(8,128)(2,1)}, bf16[8,64,768]{2,1,0:T(8,128)(2,1)}, u32[]{:S(2)}, u32[]{:S(2)}) collective-permute-start(bf16[8,64,768]{2,1,0:T(8,128)(2,1)} %get-tuple-element.300), channel_id=1, source_target_pairs={{0,16},{1,17},{2,18},{3,19},{4,20},{5,21},{6,22},{7,23},{8,24},{9,... | collective-permute-start | bytes 2359304 | tf_op jit(solution)/shard_map/ppermute | solution.py:600
  243.0 59.5 %collective-permute-start.22 = (bf16[8,64,768]{2,1,0:T(8,128)(2,1)}, bf16[8,64,768]{2,1,0:T(8,128)(2,1)}, u32[]{:S(2)}, u32[]{:S(2)}) collective-permute-start(bf16[8,64,768]{2,1,0:T(8,128)(2,1)} %get-tuple-element.299), channel_id=1, source_target_pairs={{0,24},{1,25},{2,26},{3,27},{4,28},{5,29},{6,30},{7,31},{8,16},{9,... | collective-permute-start | bytes 2359304 | tf_op jit(solution)/shard_map/ppermute | solution.py:600
  293.5 183.0 %reduce-scatter.8.cloned.1.call-start = ((), (), s32[]{:S(2)}) async-start(), calls=%async_computation.7 | async-start | bytes 3981312 | tf_op jit(solution)/shard_map/reduce_scatter | solution.py:820
  302.6 38.5 %collective-permute-start.23 = (bf16[8,120,768]{2,1,0:T(8,128)(2,1)}, bf16[8,120,768]{2,1,0:T(8,128)(2,1)}, u32[]{:S(2)}, u32[]{:S(2)}) collective-permute-start(bf16[8,120,768]{2,1,0:T(8,128)(2,1)} %pad_maximum_fusion.3), channel_id=1, source_target_pairs={{0,8},{1,9},{2,10},{3,11},{4,12},{5,13},{6,14},{7,15},{8,0},{9,1},... | collective-permute-start | bytes 4423688 | tf_op jit(solution)/shard_map/ppermute | solution.py:600
  304.0 63.9 %collective-permute-start.24 = (bf16[8,120,768]{2,1,0:T(8,128)(2,1)}, bf16[8,120,768]{2,1,0:T(8,128)(2,1)}, u32[]{:S(2)}, u32[]{:S(2)}) collective-permute-start(bf16[8,120,768]{2,1,0:T(8,128)(2,1)} %pad_maximum_fusion.4), channel_id=1, source_target_pairs={{0,16},{1,17},{2,18},{3,19},{4,20},{5,21},{6,22},{7,23},{8,24},{9,... | collective-permute-start | bytes 4423688 | tf_op jit(solution)/shard_map/ppermute | solution.py:600
  305.3 80.3 %collective-permute-start.25 = (bf16[8,120,768]{2,1,0:T(8,128)(2,1)}, bf16[8,120,768]{2,1,0:T(8,128)(2,1)}, u32[]{:S(2)}, u32[]{:S(2)}) collective-permute-start(bf16[8,120,768]{2,1,0:T(8,128)(2,1)} %pad_maximum_fusion.5), channel_id=1, source_target_pairs={{0,24},{1,25},{2,26},{3,27},{4,28},{5,29},{6,30},{7,31},{8,16},{9,... | collective-permute-start | bytes 4423688 | tf_op jit(solution)/shard_map/ppermute | solution.py:600
  402.9 21.2 %collective-permute-start.32 = (bf16[4,184,768]{2,1,0:T(8,128)(2,1)S(1)}, bf16[4,184,768]{2,1,0:T(8,128)(2,1)}, u32[]{:S(2)}, u32[]{:S(2)}) collective-permute-start(bf16[4,184,768]{2,1,0:T(8,128)(2,1)S(1)} %dynamic-slice_bitcast_fusion), channel_id=1, source_target_pairs={{0,1},{1,0},{2,3},{3,2},{4,5},{5,4},{6,7},{7,6},{8,9},{9,8},{10,11... | collective-permute-start | bytes 3391496 | tf_op jit(solution)/shard_map/ppermute | solution.py:600
  (96 other events, 961.7 us)
Sparse Core Ops, SparseCore 0:
  10.6 59.9 all-gather.3
  72.8 70.3 all-gather.5
  215.4 44.4 reduce-scatter.3
  293.6 39.4 reduce-scatter.5
  378.7 42.8 reduce-scatter.7

commit v6 on v5

--- a/solution.py
+++ b/solution.py
@@ -19,6 +19,8 @@
 HIDDEN = -1e30
 VMEM_BYTES = 60 * 1024 * 1024
 PEAK = 1.15e9
+LINE = 4
+LINE_CORES = 2
 LOW = jnp.bfloat16
 WIDE = jnp.float32
 
@@ -238,11 +240,16 @@
     return grad_rows, jnp.sum(grad * scaled, axis=0, keepdims=True)
 
 
+def shard_slot(where_ref, shard):
+    return (shard % LINE_CORES) ^ where_ref[2], lax.rem(shard // LINE_CORES - where_ref[1] + LINE, LINE)
+
+
 def feed_kernel(
-    seq_count, length_ref, after_ref, out_grad_ref, gain_ref, wg_ref, wu_ref, wd_ref,
-    layer_ref, grad_cross_ref, dwi_ref, dwd_ref, dgain_ref,
-    normed, normed_t, down, out_total, grad_total,
+    seq_count, length_ref, where_ref, after_ref, out_grad_ref, gain_ref, wg_ref, wu_ref, wd_ref,
+    layer_ref, grad_cross_ref, dwg_ref, dwu_ref, *refs,
 ):
+    near_refs = refs[:4]
+    dgain_ref, normed, normed_t, down, out_total, grad_total, cut = refs[4:]
     step = pl.program_id(0)
     row_count = after_ref.shape[0]
     length = row_count // seq_count
@@ -270,11 +277,14 @@
     hidden = (value * up).astype(LOW)
     out_total[...] += nn(hidden, wd_ref[...])
     grad_hidden = nt(down[...], wd_ref[...])
-    dwd_ref[...] = tn(hidden, down[...]).astype(LOW).reshape(dwd_ref.shape)
+    cut[...] = tn(hidden, down[...]).astype(LOW).reshape(cut.shape)
+    core, hop = shard_slot(where_ref, step)
+    for way in range(4):
+        near_refs[way][core, hop] = cut[where_ref[0] ^ way]
     grad_gate = (grad_hidden * up * slope).astype(LOW)
     grad_up = (grad_hidden * value).astype(LOW)
-    dwi_ref[0] = nn(normed_t[...], grad_gate).astype(LOW)
-    dwi_ref[1] = nn(normed_t[...], grad_up).astype(LOW)
+    dwg_ref[...] = nn(normed_t[...], grad_gate).astype(LOW)
+    dwu_ref[...] = nn(normed_t[...], grad_up).astype(LOW)
     grad_total[...] += nt(grad_gate, wg_ref[...]) + nt(grad_up, wu_ref[...])
 
     @pl.when(step == pl.num_programs(0) - 1)
@@ -291,20 +301,21 @@
         dgain_ref[...] = dgain
 
 
-def feed_forward_both(after, out_grad, lengths, gain, w_in, w_out, block=256):
+def feed_forward_both(after, out_grad, lengths, where, gain, w_in, w_out):
     row_count, width = after.shape
     hidden = w_out.shape[0]
+    block = hidden // (LINE * LINE_CORES)
     seq_count = lengths.shape[0]
     wide = pl.BlockSpec((None, width, block), lambda g: (0, 0, g))
     wide_up = pl.BlockSpec((None, width, block), lambda g: (1, 0, g))
     tall = pl.BlockSpec((block, width), lambda g: (g, 0))
-    both = pl.BlockSpec((2, width, block), lambda g: (0, 0, g))
-    quarter = block // 4
-    cut = pl.BlockSpec((4, None, quarter, width), lambda g: (0, g, 0, 0))
+    flat = pl.BlockSpec((width, block), lambda g: (0, g))
+    near = (LINE_CORES, LINE, block // 4, width)
     return pl.pallas_call(
         functools.partial(feed_kernel, seq_count),
         grid=(hidden // block,),
         in_specs=[
+            pl.BlockSpec(memory_space=pltpu.SMEM),
             pl.BlockSpec(memory_space=pltpu.SMEM),
             whole(after.shape),
             whole(out_grad.shape),
@@ -313,12 +324,13 @@
             wide_up,
             tall,
         ],
-        out_specs=[whole(after.shape), whole(after.shape), both, cut, whole((1, width))],
+        out_specs=[whole(after.shape), whole(after.shape), flat, flat, *[whole(near)] * 4, whole((1, width))],
         out_shape=[
             jax.ShapeDtypeStruct((row_count, width), LOW),
             jax.ShapeDtypeStruct((row_count, width), WIDE),
-            jax.ShapeDtypeStruct((2, width, hidden), LOW),
-            jax.ShapeDtypeStruct((4, hidden // block, quarter, width), LOW),
+            jax.ShapeDtypeStruct((width, hidden), LOW),
+            jax.ShapeDtypeStruct((width, hidden), LOW),
+            *[jax.ShapeDtypeStruct(near, LOW)] * 4,
             jax.ShapeDtypeStruct((1, width), WIDE),
         ],
         scratch_shapes=[
@@ -327,24 +339,26 @@
             pltpu.VMEM((row_count, width), LOW),
             pltpu.VMEM((row_count, width), WIDE),
             pltpu.VMEM((row_count, width), WIDE),
+            pltpu.VMEM((4, block // 4, width), LOW),
         ],
         cost_estimate=pl.CostEstimate(flops=int(46 * PEAK), bytes_accessed=40 << 20, transcendentals=0),
         compiler_params=pltpu.CompilerParams(vmem_limit_bytes=VMEM_BYTES),
         name="feed_forward_both",
-    )(lengths, after, out_grad, gain, w_in, w_in, w_out)
+    )(lengths, where, after, out_grad, gain, w_in, w_in, w_out)
 
 
 def backward_kernel(
-    causal, seq_count, length_ref, x_ref, source_ref, grad_ref, gain_ref, wq_ref, wo_ref, wave_ref,
-    q_ref, k_ref, v_ref, mix_ref, total_ref, mix_all_ref, *refs,
+    causal, seq_count, length_ref, where_ref, x_ref, source_ref, grad_ref, gain_ref, wq_ref, wo_ref, wave_ref,
+    q_ref, k_ref, v_ref, mix_ref, total_ref, mix_all_ref, mix_past_ref, *refs,
 ):
     if causal:
         gq, gk_out_ref, gv_out_ref, dw_ref, dist_ref = refs[:5]
         normed_t, branch, grad_mix, bias, score_sum = refs[5:]
         source_t = normed_t
     else:
-        grad_x_ref, gk_out_ref, gv_out_ref, dw_ref, dgain_ref, next_ref = refs[:6]
-        normed_t, branch, grad_mix, gq, source_t, mix_t, grad_total = refs[6:]
+        grad_x_ref, gk_out_ref, gv_out_ref, dgain_ref = refs[:4]
+        near_refs, far_ref = refs[4:8], refs[8]
+        normed_t, branch, grad_mix, gq, source_t, mix_t, grad_total, dw_ref, past = refs[9:]
     group = pl.program_id(0)
     row_count = x_ref.shape[0]
     rows = q_ref.shape[0] // seq_count
@@ -359,7 +373,7 @@
             normed_t[:, at : at + size] = low.T
             branch[at : at + size, :] = grad_ref[at : at + size, :].astype(LOW)
             if not causal:
-                mix_t[:, at : at + size] = mix_all_ref[0, at : at + size, :].T
+                mix_t[:, at : at + size] = mix_all_ref[at : at + size, :].T
                 grad_total[at : at + size, :] = jnp.zeros((size, value.shape[1]), WIDE)
         if not causal:
             for at, size in chunks(source_ref.shape[0], 256):
@@ -368,7 +382,8 @@
     grad_mix[...] = nt(branch[...], wo_ref[...]).astype(LOW)
     if not causal:
         across = pl.ds(pl.multiple_of(group * GROUP, GROUP), GROUP)
-        dw_ref[3] = nn(mix_t[...], branch[:, across]).astype(LOW)
+        put = lambda at, value: dw_ref.__setitem__(at, value.astype(LOW).reshape(dw_ref.shape[1:]))
+        put(3, nn(mix_t[...], branch[:, across]))
 
     for pair in range(2):
         at = pair * PAIR
@@ -449,12 +464,25 @@
                     held = held[:half] + pltpu.roll(held[half:], rows - half, 1)
                 dist_ref[pl.ds(group * 4 + head, 1), :] = held
 
-    dw_ref[0] = nn(normed_t[...], gq[...]).astype(LOW)
-    dw_ref[1] = nn(source_t[...], gk_out_ref[...]).astype(LOW)
-    dw_ref[2] = nn(source_t[...], gv_out_ref[...]).astype(LOW)
     if causal:
+        dw_ref[0] = nn(normed_t[...], gq[...]).astype(LOW)
+        dw_ref[1] = nn(source_t[...], gk_out_ref[...]).astype(LOW)
+        dw_ref[2] = nn(source_t[...], gv_out_ref[...]).astype(LOW)
         return
+    put(0, nn(normed_t[...], gq[...]))
+    put(1, nn(source_t[...], gk_out_ref[...]))
+    put(2, nn(source_t[...], gv_out_ref[...]))
     grad_total[...] += nt(gq[...], wq_ref[...])
+    rep, line, core = where_ref[0], where_ref[1], where_ref[2]
+    held = dw_ref.shape[2]
+    slots = []
+    for way in range(4):
+        for hop in range(LINE):
+            at = lax.rem(line + hop, LINE) * LINE_CORES
+            slots.append((near_refs[way].at[hop], rep ^ way, at + core))
+            slots.append((far_ref.at[way, hop], rep ^ way, at + (core ^ 1)))
+    for slot, quarter, shard in slots:
+        slot[0:held, across] = dw_ref[quarter, shard]
 
     @pl.when(group == pl.num_programs(0) - 1)
     def _():
@@ -468,49 +496,58 @@
             grad_rows = grad_ref[part, :] + grad_rows
             grad_x_ref[part, :] = grad_rows
             branch[part, :] = grad_rows.astype(LOW)
-            mix_t[:, part] = mix_all_ref[1, part, :].T
+            mix_t[:, part] = mix_past_ref[part, :].T
         dgain_ref[...] = dgain
-        next_ref[...] = nn(mix_t[...], branch[...]).astype(LOW)
-
-
-def attention_backward(causal, x, source, grad, lengths, gain, weights, wave, kept, mixes):
+        thirds = nn(mix_t[...], branch[...]).astype(LOW)
+        past[:, 0:3] = thirds.reshape(past.shape[0], 3, *past.shape[2:])
+        past[:, 3] = jnp.zeros_like(past[:, 3])
+        for slot, quarter, shard in slots:
+            slot[held:, :] = past[shard, quarter]
+
+
+def attention_backward(causal, x, source, grad, lengths, where, gain, weights, wave, kept, mix, past):
     row_count, width = x.shape
     seq_count = lengths.shape[0]
     source_rows = row_count if causal else source.shape[0]
     length = row_count // seq_count
     groups = width // GROUP
     low = lambda rows: jax.ShapeDtypeStruct((rows, width), LOW)
-    matrices = 3 if causal else 4
-    gradients = pl.BlockSpec((matrices, width, GROUP), lambda g: (0, 0, g))
-    gradient_shape = jax.ShapeDtypeStruct((matrices, width, width), LOW)
     if causal:
         out_specs = [
-            columns(row_count), columns(source_rows), columns(source_rows), gradients, whole(wave.shape),
+            columns(row_count), columns(source_rows), columns(source_rows),
+            pl.BlockSpec((3, width, GROUP), lambda g: (0, 0, g)), whole(wave.shape),
         ]
         out_shape = [
-            low(row_count), low(source_rows), low(source_rows), gradient_shape,
-            jax.ShapeDtypeStruct(wave.shape, WIDE),
+            low(row_count), low(source_rows), low(source_rows),
+            jax.ShapeDtypeStruct((3, width, width), LOW), jax.ShapeDtypeStruct(wave.shape, WIDE),
         ]
         scratch = [pltpu.VMEM((2, length, length), WIDE)] * 2
     else:
+        shards = LINE * LINE_CORES
+        each, third = width // shards, width // shards // 3
+        near = (LINE, each + third, width)
         out_specs = [
-            whole((row_count, width)), columns(source_rows), columns(source_rows), gradients,
-            whole((1, width)), whole((width, width)),
+            whole((row_count, width)), columns(source_rows), columns(source_rows), whole((1, width)),
+            *[whole(near)] * 4, whole((4, *near)),
         ]
         out_shape = [
-            jax.ShapeDtypeStruct((row_count, width), WIDE), low(source_rows), low(source_rows), gradient_shape,
-            jax.ShapeDtypeStruct((1, width), WIDE), jax.ShapeDtypeStruct((width, width), LOW),
+            jax.ShapeDtypeStruct((row_count, width), WIDE), low(source_rows), low(source_rows),
+            jax.ShapeDtypeStruct((1, width), WIDE), *[jax.ShapeDtypeStruct(near, LOW)] * 4,
+            jax.ShapeDtypeStruct((4, *near), LOW),
         ]
         scratch = [
             pltpu.VMEM((row_count, GROUP), LOW),
             pltpu.VMEM((width, source_rows), LOW),
             pltpu.VMEM((width, row_count), LOW),
             pltpu.VMEM((row_count, width), WIDE),
+            pltpu.VMEM((4, shards, each, GROUP), LOW),
+            pltpu.VMEM((shards, 4, third, width), LOW),
         ]
     return pl.pallas_call(
         functools.partial(backward_kernel, causal, seq_count),
         grid=(groups,),
         in_specs=[
+            pl.BlockSpec(memory_space=pltpu.SMEM),
             pl.BlockSpec(memory_space=pltpu.SMEM),
             whole(x.shape),
             whole(source.shape),
@@ -524,7 +561,8 @@
             columns(source_rows),
             columns(row_count),
             pl.BlockSpec((None, row_count, PAIR), lambda g: (g, 0, 0)),
-            whole(mixes.shape),
+            whole(mix.shape),
+            whole(past.shape),
         ],
         out_specs=out_specs,
         out_shape=out_shape,
@@ -537,7 +575,7 @@
         cost_estimate=pl.CostEstimate(flops=int(45 * PEAK), bytes_accessed=40 << 20, transcendentals=0),
         compiler_params=pltpu.CompilerParams(vmem_limit_bytes=VMEM_BYTES),
         name="self_backward" if causal else "cross_backward",
-    )(lengths, x, source, grad, gain, weights, weights, wave, *kept, mixes)
+    )(lengths, where, x, source, grad, gain, weights, weights, wave, *kept, mix, past)
 
 
 def input_kernel(gq_ref, gk_ref, gv_ref, wq_ref, wk_ref, wv_ref, x_ref, grad_ref, gain_ref, out_ref, dgain_ref):
@@ -626,19 +664,8 @@
     return parts + [from_shard(part, 1) for part in parts]
 
 
-def scatter_line(quarter):
-    shards = quarter.shape[0]
-    hops = shards // 2
-    shard = lax.axis_index("fsdp")
-    line, core = shard // 2, shard % 2
-    halves = quarter.reshape(hops, 2, *quarter.shape[1:])
-    pick = lambda at: lax.dynamic_index_in_dim(halves, at, 1, keepdims=False)
-    chip = (pick(core).astype(WIDE) + from_shard(pick(core ^ 1), 1).astype(WIDE)).astype(LOW)
-    at_hop = lambda hop: lax.dynamic_index_in_dim(chip, (line + hop) % hops, 0, keepdims=False)
-    total = at_hop(0).astype(WIDE)
-    for hop in range(1, hops):
-        total = total + from_line(at_hop(hop), hop).astype(WIDE)
-    return total.astype(LOW)
+def add_line(parts):
+    return [parts[0]] + [from_line(parts[hop], hop) for hop in range(1, LINE)]
 
 
 def assemble_kernel(place, hops, where_ref, *refs):
@@ -662,10 +689,8 @@
         copy.wait()
 
 
-def assemble(parts, shape, place, name):
+def assemble(parts, where, shape, place, name):
     hops = parts[0].shape[0]
-    shard = lax.axis_index("fsdp")
-    where = jnp.stack([lax.axis_index("rep"), shard // 2, shard % 2]).astype(jnp.int32)
     return pl.pallas_call(
         functools.partial(assemble_kernel, place, hops),
         in_specs=[pl.BlockSpec(memory_space=pltpu.SMEM)] + [pl.BlockSpec(memory_space=pl.ANY)] * 8,
@@ -688,10 +713,18 @@
     return sum(part.astype(WIDE) for part in parts).astype(LOW)
 
 
-def rep_collect(piece):
+def rep_near(piece):
+    return [piece] + [from_rep(piece, way) for way in range(1, 4)]
+
+
+def rep_order(near):
     rep = lax.axis_index("rep")
-    near = jnp.stack([piece] + [from_rep(piece, way) for way in range(1, 4)])
+    near = jnp.stack(near)
     return jnp.stack([lax.dynamic_index_in_dim(near, at ^ rep, 0, keepdims=False) for at in range(4)])
+
+
+def hold(*values):
+    return lax.optimization_barrier(values)
 
 
 def butterfly(vector, move, size):
@@ -706,8 +739,7 @@
     return lax.optimization_barrier((value, *earlier))[0]
 
 
-def factored_update(gradient, weight, row_state, col_state, reduce):
-    count, rows, cols = weight.shape
+def factored_sums(gradient, weight, row_state):
     squares = gradient * gradient + TINY_TERM
     row_moment = DECAY_RATE * row_state + (1.0 - DECAY_RATE) * jnp.mean(squares, axis=2)
     local = jnp.concatenate(
@@ -717,7 +749,11 @@
             jnp.sum(weight * weight, axis=(1, 2)),
         ]
     )
-    total = reduce(local)
+    return row_moment, local
+
+
+def factored_update(gradient, weight, row_moment, col_state, total):
+    count, rows, cols = weight.shape
     whole_rows = rows * lax.axis_size("fsdp")
     col_sum = total[: count * cols].reshape(count, cols)
     row_mean = total[count * cols : count * cols + count] / whole_rows
@@ -727,7 +763,7 @@
         row_moment[:, :, None] * col_moment[:, None, :] / row_mean[:, None, None]
     )
     step = STEP_RATE * jnp.sqrt(square + 1e-06)
-    return weight - step[:, None, None] * direction, row_moment, col_moment
+    return weight - step[:, None, None] * direction, col_moment
 
 
 def plain_update(gradient, weight, moment, square):
@@ -768,6 +804,7 @@
     rep, shard = lax.axis_index("rep"), lax.axis_index("fsdp")
     quarters = reps == 4 and shards == 8
     part_rows = hidden_width // shards
+    where = jnp.stack([rep, shard // 2, shard % 2]).astype(jnp.int32) * int(quarters)
     w_self = lax.all_gather(self_weight.astype(LOW), "fsdp", axis=1, tiled=True)
     gain_full = lax.all_gather(gains.astype(LOW), "fsdp", axis=1, tiled=True).astype(WIDE)
     w_in = lax.all_gather(ffn_in.astype(LOW), "fsdp", axis=1, tiled=True)
@@ -793,7 +830,8 @@
         cross_rows_each, out_rows_each = cross_weight.shape[1], part_rows // 4
         cross_pieces = with_partner(across_reps(along_line(cross_quarter)))
         w_cross = assemble(
-            list(lax.optimization_barrier((*cross_pieces, after_self))[:-1]),
+            hold(*cross_pieces, after_self)[:-1],
+            where,
             (4, model_width, model_width),
             lambda ref, quarter, at: ref.at[quarter, pl.ds(at * cross_rows_each, cross_rows_each)],
             "assemble_cross",
@@ -807,89 +845,90 @@
         False, after_self, mem_rows, enc_len, gain_full[1:2], w_cross, no_bias
     )
     if quarters:
-        out_near = list(lax.optimization_barrier((*out_near, after_cross))[:-1])
+        out_near = list(hold(*out_near, after_cross)[:-1])
         w_out = assemble(
             with_partner(out_near),
+            where,
             (hidden_width, model_width),
             lambda ref, quarter, at: ref.at[pl.ds((at * 4 + quarter) * out_rows_each, out_rows_each)],
             "assemble_out",
         )
-    layer_out, grad_cross, grad_in, grad_out, gain_three = feed_forward_both(
-        after_cross, grad_rows, dec_len, gain_full[2:3], w_in, w_out
+    layer_out, grad_cross, grad_gate, grad_up, *out_near, gain_three = feed_forward_both(
+        after_cross, grad_rows, dec_len, where, gain_full[2:3], w_in, w_out
     )
     scatter = lambda value, at: lax.psum_scatter(value, "fsdp", scatter_dimension=at, tiled=True)
     if quarters:
-        own_gate = scatter(grad_in[0], 0)
-        out_sum = rep_parts(grad_out)
-    grad_self, grad_k_two, grad_v_two, grad_cross_weights, gain_two, grad_wo = attention_backward(
-        False, after_self, mem_rows, grad_cross, enc_len, gain_full[1:2], w_cross, no_bias, kept_two,
-        jnp.stack([kept_two[3], kept_one[3]]),
+        own_gate = scatter(grad_gate, 0)
+        out_near = out_near[:1] + [from_rep(out_near[way], way) for way in range(1, 4)]
+    grad_self, grad_k_two, grad_v_two, gain_two, *cross_near, cross_far = attention_backward(
+        False, after_self, mem_rows, grad_cross, enc_len, where, gain_full[1:2], w_cross, no_bias, kept_two,
+        kept_two[3], kept_one[3],
     )
     if quarters:
-        grad_self, own_gate, *out_sum = lax.optimization_barrier((grad_self, own_gate, *out_sum))
-        own_up = scatter(grad_in[1], 0)
-        cut_wo = grad_wo.reshape(shards, 4, -1, model_width)
-        rep_pick = lambda at: jnp.concatenate(
-            [
-                lax.dynamic_index_in_dim(grad_cross_weights, at, 0, False).reshape(shards, -1, model_width),
-                lax.dynamic_index_in_dim(cut_wo, at, 1, False),
-            ],
-            axis=1,
-        )
-        grad_self, *cross_parts = lax.optimization_barrier(
-            (grad_self, *[rep_pick(rep ^ way) for way in range(4)])
-        )
-        cross_sum = cross_parts[:1] + [from_rep(cross_parts[way], way) for way in range(1, 4)]
+        cross_far, grad_k_two, *out_near = hold(cross_far, grad_k_two, *out_near)
+        pair = from_shard(cross_far, 1)
+        memory_grad = memory_gradient(grad_k_two, grad_v_two, w_cross)
+        memory_grad, pair, own_gate = hold(memory_grad, pair, own_gate)
+        own_up = scatter(grad_up, 0)
+        cross_chip = [add_up([cross_near[way], pair[way]]) for way in range(4)]
+        grad_self, *cross_chip = hold(grad_self, *cross_chip)
+        cross_near = cross_chip[:1] + [from_rep(cross_chip[way], way) for way in range(1, 4)]
+    else:
+        memory_grad = memory_gradient(grad_k_two, grad_v_two, w_cross)
     *grads_one, grad_self_weights, dist_grad = attention_backward(
-        True, dec_rows, no_source, grad_self, dec_len, gain_full[0:1], w_self, by_distance, kept_one, no_source
+        True, dec_rows, no_source, grad_self, dec_len, where, gain_full[0:1], w_self, by_distance, kept_one,
+        no_source, no_source,
     )
     if quarters:
-        grad_self_weights, *near = lax.optimization_barrier((grad_self_weights, *cross_sum[:3]))
-        cross_sum = near + cross_sum[3:]
         own_self = scatter(grad_self_weights, 1)
-        grads_one = list(lax.optimization_barrier((*grads_one, grad_self_weights))[:-1])
-    input_grad, gain_one = input_gradient(grads_one, w_self, dec_rows, grad_self, gain_full[0:1])
-    memory_grad = memory_gradient(after(grad_k_two, gain_one), grad_v_two, w_cross)
-    if quarters:
-        memory_grad, own_up, *sums = lax.optimization_barrier((memory_grad, own_up, *out_sum, *cross_sum))
-        out_sum, cross_sum = sums[:4], sums[4:]
+        dist_grad, own_up, *rest = hold(dist_grad, own_up, *grads_one, *cross_near)
+        grads_one, cross_near = rest[:3], rest[3:]
+        in_parts = rep_parts(jnp.stack([own_gate, own_up]).reshape(4, -1, hidden_width))
+        out_sum = add_up(out_near)
+        out_pair = from_shard(out_sum[1], 1)
+        input_grad, gain_one = input_gradient(grads_one, w_self, dec_rows, grad_self, gain_full[0:1])
+        input_grad, out_pair = hold(input_grad, out_pair)
+        line = jnp.concatenate([add_up(cross_near), add_up([out_sum[0], out_pair])], axis=1)
+        line_parts = add_line(line)
+    else:
+        input_grad, gain_one = input_gradient(grads_one, w_self, dec_rows, grad_self, gain_full[0:1])
     layer_out = layer_out.reshape(dec_in.shape)
     input_grad = input_grad.reshape(dec_in.shape)
     memory_grad = memory_grad.reshape(memory.shape)
     table_part = jnp.sum(bucket_mask[:, None, :] * dist_grad[None, :H, :], axis=2)
-
     small = jnp.concatenate(
         [gain_one.reshape(-1), gain_two.reshape(-1), gain_three.reshape(-1), table_part.reshape(-1)]
     )
+    each = model_width // (LINE * LINE_CORES)
     if quarters:
-        in_parts = rep_parts(jnp.stack([own_gate, own_up]).reshape(4, -1, hidden_width))
-        quarter = scatter_line(
-            jnp.concatenate(
-                [add_up(cross_sum), add_up(out_sum).reshape(shards, -1, model_width)], axis=1
-            )
-        )
-        own_in = rep_collect(add_up(in_parts)).reshape(ffn_in.shape)
-        both = rep_collect(quarter)
-        cross_end = cross_weight.shape[1]
-        wo_end = cross_end + cross_weight.shape[1] // 4
-        own_cross, own_out = both[:, :cross_end], both[:, wo_end:].reshape(ffn_out.shape)
-        own_self = rep_collect(add_up(rep_parts(own_self.reshape(4, -1, model_width))))
+        small = butterfly(butterfly(small, from_shard, shards), from_rep, reps)
+        in_near = rep_near(add_up(in_parts))
+        both_near = rep_near(add_up(line_parts))
+        self_parts = rep_parts(own_self.reshape(4, -1, model_width))
+        rest = hold(small, *in_near, *both_near, *self_parts)
+        small, in_near, both_near, self_parts = rest[0], rest[1:5], rest[5:9], rest[9:]
+        own_in = rep_order(in_near).reshape(ffn_in.shape)
+        both = rep_order(both_near)
+        own_cross = both[:, :each]
+        own_out = both[:, each + each // 3 :].reshape(ffn_out.shape)
         own_self = jnp.concatenate(
             [
-                own_self.reshape(3, *self_weight.shape[1:]),
-                both[:, cross_end:wo_end].reshape(1, *self_weight.shape[1:]),
+                rep_order(rep_near(add_up(self_parts))).reshape(3, *self_weight.shape[1:]),
+                both[:3, each : each + each // 3].reshape(1, *self_weight.shape[1:]),
             ]
         )
         over_shards = lambda vector: butterfly(vector, from_shard, shards)
-        small = butterfly(butterfly(small, from_shard, shards), from_rep, reps)
     else:
         over_reps = lambda value: lax.psum(value, "rep")
-        own_in = over_reps(scatter(grad_in, 1))
-        own_out = over_reps(
-            scatter(grad_out.transpose(1, 0, 2, 3).reshape(hidden_width, model_width), 0)
-        )
-        own_cross = over_reps(scatter(grad_cross_weights, 1))
-        own_self = over_reps(scatter(jnp.concatenate([grad_self_weights, grad_wo[None]]), 1))
+        own_in = over_reps(scatter(jnp.stack([grad_gate, grad_up]), 1))
+        grad_out = jnp.stack(out_near)
+        grad_out = grad_out.transpose(2, 1, 0, 3, 4).reshape(hidden_width, model_width)
+        own_out = over_reps(scatter(grad_out, 0))
+        packed = jnp.stack([jnp.stack(cross_near), cross_far]).transpose(1, 2, 0, 3, 4)
+        cross_parts = packed[..., :each, :].reshape(4, model_width, model_width)
+        past = packed[:3, ..., each:, :].transpose(1, 2, 0, 3, 4).reshape(1, model_width, model_width)
+        own_cross = over_reps(scatter(cross_parts, 1))
+        own_self = over_reps(scatter(jnp.concatenate([grad_self_weights, past]), 1))
         over_shards = lambda vector: lax.psum(vector, "fsdp")
         small = lax.psum(small, ("rep", "fsdp"))
 
@@ -902,22 +941,28 @@
         small[: 3 * model_width].reshape(3, model_width), shard * gains.shape[1], gains.shape[1], axis=1
     )
     table_grad = small[3 * model_width :].reshape(BUCKETS, H)
-    new_ffn_in, new_in_rows, new_in_cols = factored_update(
-        ffn_in_grad, ffn_in, in_rows, in_cols, over_shards
-    )
-    new_ffn_out, new_out_rows, new_out_cols = [
-        member[0]
-        for member in factored_update(
-            feedforward_output_gradient[None], ffn_out[None], out_rows[None], out_cols[None], over_shards
-        )
+    groups = (
+        (ffn_in_grad, ffn_in, in_rows, in_cols),
+        (feedforward_output_gradient[None], ffn_out[None], out_rows[None], out_cols[None]),
+        (cross_grad, cross_weight, cross_rows, cross_cols),
+        (self_grad, self_weight, self_rows, self_cols),
+    )
+    sums = [factored_sums(gradient, weight, row_state) for gradient, weight, row_state, _ in groups]
+    vectors = [member[1] for member in sums] + [jnp.sum(gains * gains, axis=1)]
+    total = over_shards(jnp.concatenate(vectors))
+    totals = []
+    for vector in vectors:
+        totals.append(total[: vector.shape[0]])
+        total = total[vector.shape[0] :]
+    updated = [
+        factored_update(gradient, weight, sums[at][0], col_state, totals[at])
+        for at, (gradient, weight, _, col_state) in enumerate(groups)
     ]
-    new_cross, new_cross_rows, new_cross_cols = factored_update(
-        cross_grad, cross_weight, cross_rows, cross_cols, over_shards
-    )
-    new_self, new_self_rows, new_self_cols = factored_update(
-        self_grad, self_weight, self_rows, self_cols, over_shards
-    )
-    gain_square = over_shards(jnp.sum(gains * gains, axis=1)) / model_width
+    new_ffn_in, new_ffn_out, new_cross, new_self = [member[0] for member in updated]
+    new_in_cols, new_out_cols, new_cross_cols, new_self_cols = [member[1] for member in updated]
+    new_in_rows, new_out_rows, new_cross_rows, new_self_rows = [member[0] for member in sums]
+    new_ffn_out, new_out_rows, new_out_cols = new_ffn_out[0], new_out_rows[0], new_out_cols[0]
+    gain_square = totals[4] / model_width
     new_gains, new_gain_moment = plain_update(gains_grad, gains, gain_moment, gain_square[:, None])
     new_table, new_table_moment = plain_update(
         table_grad, table, table_moment, jnp.mean(table * table)

time: 536 us -> 486 us (0.907)
  other arithmetic: 55.1 us -> 36.6 us
  waiting for transfers between devices: 114 us -> 99.8 us
  local copies, waits for them, and re-layouts: 29.8 us -> 18.3 us
  starting transfers between devices: 85.2 us -> 78.2 us
    ppermute x65 -> x54, waiting for transfers between devices: 110 us -> 97.1 us  [flat_permute(): return lax.ppermute(value, ('rep', 'fsdp'), pairs)]
    squeeze x4 -> x1, local copies, waits for them, and re-layouts: 8.93 us -> 0.03 us  [per_device(): out_pair = from_shard(out_sum[1], 1)]
    ppermute x65 -> x54, starting transfers between devices: 85 us -> 78 us  [flat_permute(): return lax.ppermute(value, ('rep', 'fsdp'), pairs)]
    concatenate x6 -> x0, other arithmetic: 6.67 us -> none  [the longest x4 5.15 us: per_device(): jnp.concatenate([lax.dynamic_index_in_dim(grad_cross_weights, at, 0, Fals...]
  transfers between devices with their start and end apart: 70 -> 59, of which waited for: 26 -> 22; matrix products, arithmetic and copies ran while one was open for 12% -> 7% of each run, Pallas kernels for 31% -> 34%
where the time goes in v6:
time: 486 us; the launch traced here: 479 us
  Pallas kernels  212 us (44%)
  waiting for transfers between devices  99.8 us (21%)
  starting transfers between devices  78.2 us (16%)
  other arithmetic  36.6 us (8%)
  local copies, waits for them, and re-layouts  18.3 us (4%)
  between operations  17.3 us (4%)
  blocking collectives  16.6 us (3%)
    ppermute x54, waiting for transfers between devices, flat_permute(): return lax.ppermute(value, ('rep', 'fsdp'), pairs)  97.1 us
    pallas_call x2, Pallas kernels, attention_backward(): pl.pallas_call(functools.partial(backward_kernel, causal, seq_count), gri...  82.7 us
    ppermute x54, starting transfers between devices, flat_permute(): return lax.ppermute(value, ('rep', 'fsdp'), pairs)  78 us
    pallas_call x2, Pallas kernels, attention_forward(): pl.pallas_call(functools.partial(forward_kernel, causal, seq_count), grid...  55 us
    pallas_call x1, Pallas kernels, feed_forward_both(): pl.pallas_call(functools.partial(feed_kernel, seq_count), grid=(hidden //...  47.4 us
    all_gather x1, blocking collectives, per_device(): lax.all_gather(gains.astype(LOW), 'fsdp', axis=1, tiled=True).astype(WIDE)  16.6 us
    convert_element_type x7, other arithmetic, add_up(): return sum((part.astype(WIDE) for part in parts)).astype(LOW)  10.6 us
    pallas_call x2, Pallas kernels, assemble(): pl.pallas_call(functools.partial(assemble_kernel, place, hops), in_specs=...  10 us
  transfers between devices with their start and end apart: 59, of which 22 were waited for; matrix products, arithmetic and copies ran while one was open for 7% of the time, Pallas kernels for 34%

profile of v6, /device:TPU:0, one launch (start us, length us, event | category | flops | bytes accessed | tf_op | source)
XLA Modules:
  0.0 478.6 jit_solution(10082748171364201650)
XLA Ops:
  7.3 3.2 multiply_reduce_fusion.1
  13.4 3.1 collective-permute-start
  21.0 16.6 %all-gather = bf16[8,96,3]{1,2,0:T(4,128)(2,1)S(1)} all-gather(bf16[1,96,3]{1,2,0:T(4,128)(2,1)S(1)} %get-tuple-element.372), channel_id=1, replica_groups=mesh['rep'=4,'fsdp'=8] {'fsdp'}, dimensions={0}, use_global_device_ids=true | all-gather | bytes 5184 | tf_op jit(solution)/shard_map/all_gather | solution.py:809
  46.5 9.4 %collective-permute-done.3.refs_1_ = bf16[4,96,768]{2,1,0:T(8,128)(2,1)S(1)} collective-permute-done((bf16[4,96,768]{2,1,0:T(8,128)(2,1)S(1)}, bf16[4,96,768]{2,1,0:T(8,128)(2,1)S(1)}, u32[]{:S(2)}, u32[]{:S(2)}) %collective-permute-start.3) | collective-permute-done | bytes 589856 | tf_op jit(solution)/shard_map/ppermute | solution.py:638
  55.9 13.1 %collective-permute-done.4.refs_2_ = bf16[4,96,768]{2,1,0:T(8,128)(2,1)S(1)} collective-permute-done((bf16[4,96,768]{2,1,0:T(8,128)(2,1)S(1)}, bf16[4,96,768]{2,1,0:T(8,128)(2,1)S(1)}, u32[]{:S(2)}, u32[]{:S(2)}) %collective-permute-start.4) | collective-permute-done | bytes 589856 | tf_op jit(solution)/shard_map/ppermute | solution.py:638
  72.1 9.7 %collective-permute-start.10 = (bf16[64,768]{1,0:T(8,128)(2,1)S(1)}, bf16[64,768]{1,0:T(8,128)(2,1)S(1)}, u32[]{:S(2)}, u32[]{:S(2)}) collective-permute-start(bf16[64,768]{1,0:T(8,128)(2,1)S(1)} %fusion.26), channel_id=1, source_target_pairs={{0,2},{1,3},{2,4},{3,5},{4,6},{5,7},{6,0},{7,1},{8,10},{9,11},{10,... | collective-permute-start | bytes 294920 | tf_op jit(solution)/shard_map/ppermute | solution.py:638
  82.3 26.8 %self_forward.1 = (bf16[1024,768]{1,0:T(8,128)(2,1)}, bf16[1024,768]{1,0:T(8,128)(2,1)}, bf16[1024,768]{1,0:T(8,128)(2,1)}, bf16[1024,768]{1,0:T(8,128)(2,1)}, f...) custom-call(s32[2]{0:T(128)} %length_ref.9, bf16[1024,768]{1,0:T(8,128)(2,1)} %bitcast.146, ...), custom_call_target="tpu_custom_call" | custom-call | flops 31050000384 | bytes 20971520 | tf_op jit(solution)/shard_map/self_forward/pallas_call | solution.py:188
  111.6 3.2 collective-permute-start.12
  114.8 5.5 %assemble_cross.1.wq_ref.wk_ref.wv_ref.wo_ref = bf16[4,768,768]{2,1,0:T(8,128)(2,1)} custom-call(s32[3]{0:T(128)} %pad_add_fusion.where_ref, bf16[4,96,768]{2,1,0:T(8,128)(2,1)} %copy-done.16, bf16[4,96,768]{2,1,0:T(8,128)(2,1)} %copy-done.51, bf16[4,96,768]{2,1,0:T(8,128)(2,1)} %copy-done.52, bf16[4,96,768]{2,1,0:T(8,128)(2,1)} %copy-done.53, ...), custom_call_target="tpu_custom_call" | custom-call | flops 4600000000 | bytes 8388608 | tf_op jit(solution)/shard_map/assemble_cross/pallas_call | solution.py:694
  126.6 28.3 %cross_forward.1 = (bf16[1024,768]{1,0:T(8,128)(2,1)}, bf16[1024,768]{1,0:T(8,128)(2,1)}, bf16[1024,768]{1,0:T(8,128)(2,1)}, bf16[1024,768]{1,0:T(8,128)(2,1)}, ...) custom-call(s32[2]{0:T(128)} %length_ref.8, f32[1024,768]{1,0:T(8,128)} %get-tuple-element.114.x_ref, ...), custom_call_target="tpu_custom_call" | custom-call | flops 31050000384 | bytes 20971520 | tf_op jit(solution)/shard_map/cross_forward/pallas_call | solution.py:188
  159.3 4.6 assemble_out.1.wd_ref
  164.0 47.4 %feed_forward_both.1 = (bf16[1024,768]{1,0:T(8,128)(2,1)}, f32[1024,768]{1,0:T(8,128)}, bf16[768,2048]{1,0:T(8,128)(2,1)}, bf16[768,2048]{1,0:T(8,128)(2,1)}, bf...) custom-call(s32[2]{0:T(128)} %length_ref.9, ...), custom_call_target="tpu_custom_call" | custom-call | flops 52899999744 | bytes 41943040 | tf_op jit(solution)/shard_map/feed_forward_both/pallas_call | solution.py:314
  215.0 48.7 %cross_backward.1 = (f32[1024,768]{1,0:T(8,128)}, bf16[1024,768]{1,0:T(8,128)(2,1)}, bf16[1024,768]{1,0:T(8,128)(2,1)}, f32[1,768]{1,0:T(1,128)}, bf16[4,128,768...) custom-call(s32[2]{0:T(128)} %length_ref.8, ...), custom_call_target="tpu_custom_call" | custom-call | flops 51749998592 | bytes 41943040 | tf_op jit(solution)/shard_map/cross_backward/pallas_call | solution.py:546
  266.6 6.7 %memory_gradient.1 = f32[1024,768]{1,0:T(8,128)} custom-call(bf16[1024,768]{1,0:T(8,128)(2,1)} %get-tuple-element.146.gk_ref, bf16[1024,768]{1,0:T(8,128)(2,1)} %get-tuple-element.147.gv_ref, bf16[4,768,768]{2,1,0:T(8,128)(2,1)} %assemble_cross.1.wq_ref.wk_ref.wv_ref.wo_ref, bf16[4,768,768]{2,1,0:T(8,128)(2,1)} %assemble_cross.1.wq_ref.wk_ref.wv_ref.wo_ref), custom_call_target="tpu_custom_call" | custom-call | flops 8049999872 | bytes 10485760 | tf_op jit(solution)/shard_map/memory_gradient/pallas_call | solution.py:619
  273.3 4.0 fusion
  277.3 34.0 %self_backward.1 = (bf16[1024,768]{1,0:T(8,128)(2,1)}, bf16[1024,768]{1,0:T(8,128)(2,1)}, bf16[1024,768]{1,0:T(8,128)(2,1)}, bf16[3,768,768]{2,1,0:T(8,128)(2,1)}, f32[16,512]{1,0:T(8,128)}) custom-call(s32[2]{0:T(128)} %length_ref.9, s32[3]{0:T(128)} %pad_add_fusion.where_ref, bf16[1024,768]{1,0:T(8,128)(2,1)} %bitcast.147, ...), custom_call_target="tpu_custom_call" | custom-call | flops 51749998592 | bytes 41943040 | tf_op jit(solution)/shard_map/self_backward/pallas_call | solution.py:546
  318.4 14.5 %collective-permute-done.24 = bf16[4,128,768]{2,1,0:T(8,128)(2,1)} collective-permute-done((bf16[4,128,768]{2,1,0:T(8,128)(2,1)S(1)}, bf16[4,128,768]{2,1,0:T(8,128)(2,1)}, u32[]{:S(2)}, u32[]{:S(2)}) %collective-permute-start.24) | collective-permute-done | bytes 786464 | tf_op jit(solution)/shard_map/ppermute | solution.py:638
  332.9 17.7 %collective-permute-done.25 = bf16[4,128,768]{2,1,0:T(8,128)(2,1)} collective-permute-done((bf16[4,128,768]{2,1,0:T(8,128)(2,1)S(1)}, bf16[4,128,768]{2,1,0:T(8,128)(2,1)}, u32[]{:S(2)}, u32[]{:S(2)}) %collective-permute-start.25) | collective-permute-done | bytes 786464 | tf_op jit(solution)/shard_map/ppermute | solution.py:638
  356.1 9.9 %input_gradient.1 = (f32[1024,768]{1,0:T(8,128)}, f32[1,768]{1,0:T(1,128)}) custom-call(bf16[1024,768]{1,0:T(8,128)(2,1)} %get-tuple-element.168.gq_ref, bf16[1024,768]{1,0:T(8,128)(2,1)} %get-tuple-element.169.gk_ref, bf16[1024,768]{1,0:T(8,128)(2,1)} %get-tuple-element.170.gv_ref, ...), custom_call_target="tpu_custom_call" | custom-call | flops 9200000000 | bytes 12582912 | tf_op jit(solution)/shard_map/input_gradient/pallas_call | solution.py:598
  369.2 8.8 %collective-permute-start.29 = (f32[2688]{0:T(1024)S(1)}, f32[2688]{0:T(1024)S(1)}, u32[]{:S(2)}, u32[]{:S(2)}) collective-permute-start(f32[2688]{0:T(1024)S(1)} %fusion.47), channel_id=1, source_target_pairs={{0,2},{1,3},{2,0},{3,1},{4,6},{5,7},{6,4},{7,5},{8,10},{9,11},{10,... | collective-permute-start | bytes 32264 | tf_op jit(solution)/shard_map/ppermute | solution.py:638
  381.8 13.7 %collective-permute-done.30 = f32[2688]{0:T(1024)S(1)} collective-permute-done((f32[2688]{0:T(1024)S(1)}, f32[2688]{0:T(1024)S(1)}, u32[]{:S(2)}, u32[]{:S(2)}) %collective-permute-start.30) | collective-permute-done | bytes 10784 | tf_op jit(solution)/shard_map/ppermute | solution.py:638
  398.8 7.5 %collective-permute-done.40 = bf16[192,768]{1,0:T(8,128)(2,1)S(1)} collective-permute-done((bf16[192,768]{1,0:T(8,128)(2,1)S(1)}, bf16[192,768]{1,0:T(8,128)(2,1)S(1)}, u32[]{:S(2)}, u32[]{:S(2)}) %collective-permute-start.40) | collective-permute-done | bytes 294944 | tf_op jit(solution)/shard_map/ppermute | solution.py:638
  415.7 8.6 %collective-permute-done.37 = bf16[48,2048]{1,0:T(8,128)(2,1)S(1)} collective-permute-done((bf16[48,2048]{1,0:T(8,128)(2,1)S(1)}, bf16[48,2048]{1,0:T(8,128)(2,1)S(1)}, u32[]{:S(2)}, u32[]{:S(2)}) %collective-permute-start.37) | collective-permute-done | bytes 196640 | tf_op jit(solution)/shard_map/ppermute | solution.py:638
  447.1 6.4 %collective-permute-start.52 = (f32[11033]{0:T(1024)S(1)}, f32[11033]{0:T(1024)S(1)}, u32[]{:S(2)}, u32[]{:S(2)}) collective-permute-start(f32[11033]{0:T(1024)S(1)} %add.263), channel_id=1, source_target_pairs={{0,2},{1,3},{2,0},{3,1},{4,6},{5,7},{6,4},{7,5},{8,10},{9,11},{10,... | collective-permute-start | bytes 132404 | tf_op jit(solution)/shard_map/ppermute | solution.py:638
  (339 shorter events, 110.0 us)
Async XLA Ops:
  7.2 64.9 %all-gather.4.cloned.1.call-start = ((), (), s32[]{:S(2)}) async-start(), calls=%async_computation.3 | async-start | bytes 5308416 | tf_op jit(solution)/shard_map/all_gather | solution.py:808
  10.5 153.4 %all-gather.6.cloned.1.call-start = ((), (), s32[]{:S(2)}) async-start(), calls=%async_computation.4 | async-start | bytes 7077888 | tf_op jit(solution)/shard_map/all_gather | solution.py:810
  12.3 261.0 %reduce-scatter.4.cloned.1.call-start = ((), (), s32[]{:S(2)}) async-start(), calls=%async_computation.5 | async-start | bytes 3538944 | tf_op jit(solution)/shard_map/reduce_scatter | solution.py:859
  41.1 27.9 %collective-permute-start.4 = (bf16[4,96,768]{2,1,0:T(8,128)(2,1)S(1)}, bf16[4,96,768]{2,1,0:T(8,128)(2,1)S(1)}, u32[]{:S(2)}, u32[]{:S(2)}) collective-permute-start(bf16[4,96,768]{2,1,0:T(8,128)(2,1)S(1)} %pad_maximum_fusion.4.refs_0_), channel_id=1, source_target_pairs={{0,16},{1,17},{2,18},{3,19},{4,20},{5,21},{6,22},{7,23},{8,24},{9,... | collective-permute-start | bytes 1769480 | tf_op jit(solution)/shard_map/ppermute | solution.py:638
  42.6 26.4 %collective-permute-start.5 = (bf16[4,96,768]{2,1,0:T(8,128)(2,1)S(1)}, bf16[4,96,768]{2,1,0:T(8,128)(2,1)S(1)}, u32[]{:S(2)}, u32[]{:S(2)}) collective-permute-start(bf16[4,96,768]{2,1,0:T(8,128)(2,1)S(1)} %pad_maximum_fusion.4.refs_0_), channel_id=1, source_target_pairs={{0,24},{1,25},{2,26},{3,27},{4,28},{5,29},{6,30},{7,31},{8,16},{9,... | collective-permute-start | bytes 1769480 | tf_op jit(solution)/shard_map/ppermute | solution.py:638
  46.5 62.7 %collective-permute-start.6 = (bf16[4,96,768]{2,1,0:T(8,128)(2,1)S(1)}, bf16[4,96,768]{2,1,0:T(8,128)(2,1)S(1)}, u32[]{:S(2)}, u32[]{:S(2)}) collective-permute-start(bf16[4,96,768]{2,1,0:T(8,128)(2,1)S(1)} %pad_maximum_fusion.4.refs_0_), channel_id=1, source_target_pairs={{0,1},{1,0},{2,3},{3,2},{4,5},{5,4},{6,7},{7,6},{8,9},{9,8},{10,11... | collective-permute-start | bytes 1769480 | tf_op jit(solution)/shard_map/ppermute | solution.py:638
  55.9 55.7 %collective-permute-start.7 = (bf16[4,96,768]{2,1,0:T(8,128)(2,1)S(1)}, bf16[4,96,768]{2,1,0:T(8,128)(2,1)}, u32[]{:S(2)}, u32[]{:S(2)}) collective-permute-start(bf16[4,96,768]{2,1,0:T(8,128)(2,1)S(1)} %collective-permute-done.3.refs_1_), channel_id=1, source_target_pairs={{0,1},{1,0},{2,3},{3,2},{4,5},{5,4},{6,7},{7,6},{8,9},{9,8},{10,11... | collective-permute-start | bytes 1769480 | tf_op jit(solution)/shard_map/ppermute | solution.py:638
  69.0 45.8 %collective-permute-start.8 = (bf16[4,96,768]{2,1,0:T(8,128)(2,1)S(1)}, bf16[4,96,768]{2,1,0:T(8,128)(2,1)}, u32[]{:S(2)}, u32[]{:S(2)}) collective-permute-start(bf16[4,96,768]{2,1,0:T(8,128)(2,1)S(1)} %collective-permute-done.4.refs_2_), channel_id=1, source_target_pairs={{0,1},{1,0},{2,3},{3,2},{4,5},{5,4},{6,7},{7,6},{8,9},{9,8},{10,11... | collective-permute-start | bytes 1769480 | tf_op jit(solution)/shard_map/ppermute | solution.py:638
  69.0 45.8 %collective-permute-start.9 = (bf16[4,96,768]{2,1,0:T(8,128)(2,1)S(1)}, bf16[4,96,768]{2,1,0:T(8,128)(2,1)}, u32[]{:S(2)}, u32[]{:S(2)}) collective-permute-start(bf16[4,96,768]{2,1,0:T(8,128)(2,1)S(1)} %collective-permute-done.5.refs_3_), channel_id=1, source_target_pairs={{0,1},{1,0},{2,3},{3,2},{4,5},{5,4},{6,7},{7,6},{8,9},{9,8},{10,11... | collective-permute-start | bytes 1769480 | tf_op jit(solution)/shard_map/ppermute | solution.py:638
  72.1 48.2 %collective-permute-start.10 = (bf16[64,768]{1,0:T(8,128)(2,1)S(1)}, bf16[64,768]{1,0:T(8,128)(2,1)S(1)}, u32[]{:S(2)}, u32[]{:S(2)}) collective-permute-start(bf16[64,768]{1,0:T(8,128)(2,1)S(1)} %fusion.26), channel_id=1, source_target_pairs={{0,2},{1,3},{2,4},{3,5},{4,6},{5,7},{6,0},{7,1},{8,10},{9,11},{10,... | collective-permute-start | bytes 294920 | tf_op jit(solution)/shard_map/ppermute | solution.py:638
  122.4 32.4 %collective-permute-start.13 = (bf16[4,64,768]{2,1,0:T(8,128)(2,1)S(1)}, bf16[4,64,768]{2,1,0:T(8,128)(2,1)S(1)}, u32[]{:S(2)}, u32[]{:S(2)}) collective-permute-start(bf16[4,64,768]{2,1,0:T(8,128)(2,1)S(1)} %pad_maximum_fusion.7.refs_0_), channel_id=1, source_target_pairs={{0,8},{1,9},{2,10},{3,11},{4,12},{5,13},{6,14},{7,15},{8,0},{9,1},... | collective-permute-start | bytes 1179656 | tf_op jit(solution)/shard_map/ppermute | solution.py:638
  124.0 30.9 %collective-permute-start.14 = (bf16[4,64,768]{2,1,0:T(8,128)(2,1)S(1)}, bf16[4,64,768]{2,1,0:T(8,128)(2,1)S(1)}, u32[]{:S(2)}, u32[]{:S(2)}) collective-permute-start(bf16[4,64,768]{2,1,0:T(8,128)(2,1)S(1)} %pad_maximum_fusion.7.refs_0_), channel_id=1, source_target_pairs={{0,16},{1,17},{2,18},{3,19},{4,20},{5,21},{6,22},{7,23},{8,24},{9,... | collective-permute-start | bytes 1179656 | tf_op jit(solution)/shard_map/ppermute | solution.py:638
  125.5 29.4 %collective-permute-start.15 = (bf16[4,64,768]{2,1,0:T(8,128)(2,1)S(1)}, bf16[4,64,768]{2,1,0:T(8,128)(2,1)S(1)}, u32[]{:S(2)}, u32[]{:S(2)}) collective-permute-start(bf16[4,64,768]{2,1,0:T(8,128)(2,1)S(1)} %pad_maximum_fusion.7.refs_0_), channel_id=1, source_target_pairs={{0,24},{1,25},{2,26},{3,27},{4,28},{5,29},{6,30},{7,31},{8,16},{9,... | collective-permute-start | bytes 1179656 | tf_op jit(solution)/shard_map/ppermute | solution.py:638
  211.4 52.4 %collective-permute-start.20 = (bf16[2,4,64,768]{3,2,1,0:T(8,128)(2,1)}, bf16[2,4,64,768]{3,2,1,0:T(8,128)(2,1)S(1)}, u32[]{:S(2)}, u32[]{:S(2)}) collective-permute-start(bf16[2,4,64,768]{3,2,1,0:T(8,128)(2,1)} %get-tuple-element.143), channel_id=1, source_target_pairs={{0,8},{1,9},{2,10},{3,11},{4,12},{5,13},{6,14},{7,15},{8,0},{9,1},... | collective-permute-start | bytes 2359304 | tf_op jit(solution)/shard_map/ppermute | solution.py:638
  213.0 50.8 %collective-permute-start.21 = (bf16[2,4,64,768]{3,2,1,0:T(8,128)(2,1)}, bf16[2,4,64,768]{3,2,1,0:T(8,128)(2,1)S(1)}, u32[]{:S(2)}, u32[]{:S(2)}) collective-permute-start(bf16[2,4,64,768]{3,2,1,0:T(8,128)(2,1)} %get-tuple-element.144), channel_id=1, source_target_pairs={{0,16},{1,17},{2,18},{3,19},{4,20},{5,21},{6,22},{7,23},{8,24},{9,... | collective-permute-start | bytes 2359304 | tf_op jit(solution)/shard_map/ppermute | solution.py:638
  214.5 49.4 %collective-permute-start.22 = (bf16[2,4,64,768]{3,2,1,0:T(8,128)(2,1)}, bf16[2,4,64,768]{3,2,1,0:T(8,128)(2,1)S(1)}, u32[]{:S(2)}, u32[]{:S(2)}) collective-permute-start(bf16[2,4,64,768]{3,2,1,0:T(8,128)(2,1)} %get-tuple-element.145), channel_id=1, source_target_pairs={{0,24},{1,25},{2,26},{3,27},{4,28},{5,29},{6,30},{7,31},{8,16},{9,... | collective-permute-start | bytes 2359304 | tf_op jit(solution)/shard_map/ppermute | solution.py:638
  215.0 103.4 %reduce-scatter.6.cloned.1.call-start = ((), (), s32[]{:S(2)}) async-start(), calls=%async_computation.6 | async-start | bytes 3538944 | tf_op jit(solution)/shard_map/reduce_scatter | solution.py:859
  265.2 149.4 %reduce-scatter.8.cloned.1.call-start = ((), (), s32[]{:S(2)}) async-start(), calls=%async_computation.7 | async-start | bytes 3981312 | tf_op jit(solution)/shard_map/reduce_scatter | solution.py:859
  314.0 36.6 %collective-permute-start.25 = (bf16[4,128,768]{2,1,0:T(8,128)(2,1)S(1)}, bf16[4,128,768]{2,1,0:T(8,128)(2,1)}, u32[]{:S(2)}, u32[]{:S(2)}) collective-permute-start(bf16[4,128,768]{2,1,0:T(8,128)(2,1)S(1)} %copy-done.11), channel_id=1, source_target_pairs={{0,16},{1,17},{2,18},{3,19},{4,20},{5,21},{6,22},{7,23},{8,24},{9,... | collective-permute-start | bytes 2359304 | tf_op jit(solution)/shard_map/ppermute | solution.py:638
  315.5 35.1 %collective-permute-start.26 = (bf16[4,128,768]{2,1,0:T(8,128)(2,1)S(1)}, bf16[4,128,768]{2,1,0:T(8,128)(2,1)}, u32[]{:S(2)}, u32[]{:S(2)}) collective-permute-start(bf16[4,128,768]{2,1,0:T(8,128)(2,1)S(1)} %copy-done.10), channel_id=1, source_target_pairs={{0,24},{1,25},{2,26},{3,27},{4,28},{5,29},{6,30},{7,31},{8,16},{9,... | collective-permute-start | bytes 2359304 | tf_op jit(solution)/shard_map/ppermute | solution.py:638
  318.3 50.9 %collective-permute-start.27 = (bf16[4,64,768]{2,1,0:T(8,128)(2,1)S(1)}, bf16[4,64,768]{2,1,0:T(8,128)(2,1)}, u32[]{:S(2)}, u32[]{:S(2)}) collective-permute-start(bf16[4,64,768]{2,1,0:T(8,128)(2,1)S(1)} %slice_bitcast_fusion.1), channel_id=1, source_target_pairs={{0,1},{1,0},{2,3},{3,2},{4,5},{5,4},{6,7},{7,6},{8,9},{9,8},{10,11... | collective-permute-start | bytes 1179656 | tf_op jit(solution)/shard_map/ppermute | solution.py:638
  352.6 42.9 %collective-permute-start.33 = (bf16[48,2048]{1,0:T(8,128)(2,1)}, bf16[48,2048]{1,0:T(8,128)(2,1)S(1)}, u32[]{:S(2)}, u32[]{:S(2)}) collective-permute-start(bf16[48,2048]{1,0:T(8,128)(2,1)} %get-tuple-element.345), channel_id=1, source_target_pairs={{0,8},{1,9},{2,10},{3,11},{4,12},{5,13},{6,14},{7,15},{8,0},{9,1},... | collective-permute-start | bytes 589832 | tf_op jit(solution)/shard_map/ppermute | solution.py:638
  353.8 41.8 %collective-permute-start.34 = (bf16[48,2048]{1,0:T(8,128)(2,1)}, bf16[48,2048]{1,0:T(8,128)(2,1)S(1)}, u32[]{:S(2)}, u32[]{:S(2)}) collective-permute-start(bf16[48,2048]{1,0:T(8,128)(2,1)} %get-tuple-element.347), channel_id=1, source_target_pairs={{0,16},{1,17},{2,18},{3,19},{4,20},{5,21},{6,22},{7,23},{8,24},{9,... | collective-permute-start | bytes 589832 | tf_op jit(solution)/shard_map/ppermute | solution.py:638
  354.7 41.7 %collective-permute-start.35 = (bf16[48,2048]{1,0:T(8,128)(2,1)S(1)}, bf16[48,2048]{1,0:T(8,128)(2,1)}, u32[]{:S(2)}, u32[]{:S(2)}) collective-permute-start(bf16[48,2048]{1,0:T(8,128)(2,1)S(1)} %get-tuple-element.346), channel_id=1, source_target_pairs={{0,24},{1,25},{2,26},{3,27},{4,28},{5,29},{6,30},{7,31},{8,16},{9,... | collective-permute-start | bytes 589832 | tf_op jit(solution)/shard_map/ppermute | solution.py:638
  (97 other events, 1188.1 us)
Sparse Core Ops, SparseCore 0:
  10.6 61.3 all-gather.3
  74.2 69.8 all-gather.5
  215.1 45.7 reduce-scatter.3
  265.4 46.1 reduce-scatter.5
  313.8 47.4 reduce-scatter.7

commit v7 on v6

--- a/solution.py
+++ b/solution.py
@@ -880,16 +880,17 @@
         no_source, no_source,
     )
     if quarters:
+        dist_grad, own_up, grad_self_weights, *rest = hold(
+            dist_grad, own_up, grad_self_weights, *grads_one, *cross_near, *out_near
+        )
+        grads_one, cross_near, out_near = rest[:3], rest[3:7], rest[7:]
         own_self = scatter(grad_self_weights, 1)
-        dist_grad, own_up, *rest = hold(dist_grad, own_up, *grads_one, *cross_near)
-        grads_one, cross_near = rest[:3], rest[3:]
-        in_parts = rep_parts(jnp.stack([own_gate, own_up]).reshape(4, -1, hidden_width))
         out_sum = add_up(out_near)
         out_pair = from_shard(out_sum[1], 1)
-        input_grad, gain_one = input_gradient(grads_one, w_self, dec_rows, grad_self, gain_full[0:1])
-        input_grad, out_pair = hold(input_grad, out_pair)
+        in_parts = rep_parts(jnp.stack([own_gate, own_up]).reshape(4, -1, hidden_width))
         line = jnp.concatenate([add_up(cross_near), add_up([out_sum[0], out_pair])], axis=1)
         line_parts = add_line(line)
+        input_grad, gain_one = input_gradient(grads_one, w_self, dec_rows, grad_self, gain_full[0:1])
     else:
         input_grad, gain_one = input_gradient(grads_one, w_self, dec_rows, grad_self, gain_full[0:1])
     layer_out = layer_out.reshape(dec_in.shape)
@@ -901,7 +902,7 @@
     )
     each = model_width // (LINE * LINE_CORES)
     if quarters:
-        small = butterfly(butterfly(small, from_shard, shards), from_rep, reps)
+        small = butterfly(small, from_rep, reps)
         in_near = rep_near(add_up(in_parts))
         both_near = rep_near(add_up(line_parts))
         self_parts = rep_parts(own_self.reshape(4, -1, model_width))
@@ -930,17 +931,12 @@
         own_cross = over_reps(scatter(cross_parts, 1))
         own_self = over_reps(scatter(jnp.concatenate([grad_self_weights, past]), 1))
         over_shards = lambda vector: lax.psum(vector, "fsdp")
-        small = lax.psum(small, ("rep", "fsdp"))
+        small = lax.psum(small, "rep")
 
     grad_factor = 1.0 / math.sqrt(row_count * reps * shards)
     self_grad, cross_grad, ffn_in_grad, feedforward_output_gradient = [
         member.astype(WIDE) * grad_factor for member in (own_self, own_cross, own_in, own_out)
     ]
-    small = small * grad_factor
-    gains_grad = lax.dynamic_slice_in_dim(
-        small[: 3 * model_width].reshape(3, model_width), shard * gains.shape[1], gains.shape[1], axis=1
-    )
-    table_grad = small[3 * model_width :].reshape(BUCKETS, H)
     groups = (
         (ffn_in_grad, ffn_in, in_rows, in_cols),
         (feedforward_output_gradient[None], ffn_out[None], out_rows[None], out_cols[None]),
@@ -948,7 +944,7 @@
         (self_grad, self_weight, self_rows, self_cols),
     )
     sums = [factored_sums(gradient, weight, row_state) for gradient, weight, row_state, _ in groups]
-    vectors = [member[1] for member in sums] + [jnp.sum(gains * gains, axis=1)]
+    vectors = [member[1] for member in sums] + [jnp.sum(gains * gains, axis=1), small]
     total = over_shards(jnp.concatenate(vectors))
     totals = []
     for vector in vectors:
@@ -963,6 +959,11 @@
     new_in_rows, new_out_rows, new_cross_rows, new_self_rows = [member[0] for member in sums]
     new_ffn_out, new_out_rows, new_out_cols = new_ffn_out[0], new_out_rows[0], new_out_cols[0]
     gain_square = totals[4] / model_width
+    small = totals[5] * grad_factor
+    gains_grad = lax.dynamic_slice_in_dim(
+        small[: 3 * model_width].reshape(3, model_width), shard * gains.shape[1], gains.shape[1], axis=1
+    )
+    table_grad = small[3 * model_width :].reshape(BUCKETS, H)
     new_gains, new_gain_moment = plain_update(gains_grad, gains, gain_moment, gain_square[:, None])
     new_table, new_table_moment = plain_update(
         table_grad, table, table_moment, jnp.mean(table * table)

time: 486 us -> 469 us (0.965)
  waiting for transfers between devices: 99.8 us -> 78.4 us
    ppermute x54 -> x51, waiting for transfers between devices: 97.1 us -> 75.6 us  [flat_permute(): return lax.ppermute(value, ('rep', 'fsdp'), pairs)]
    ppermute x54 -> x51, starting transfers between devices: 78 us -> 81.6 us  [flat_permute(): return lax.ppermute(value, ('rep', 'fsdp'), pairs)]
  transfers between devices with their start and end apart: 59 -> 56, of which waited for: 22 -> 22; matrix products, arithmetic and copies ran while one was open for 7% -> 7% of each run, Pallas kernels for 34% -> 36%
where the time goes in v7:
time: 469 us; the launch traced here: 461 us
  Pallas kernels  212 us (45%)
  starting transfers between devices  81.8 us (17%)
  waiting for transfers between devices  78.4 us (17%)
  other arithmetic  34.8 us (7%)
  local copies, waits for them, and re-layouts  20.5 us (4%)
  between operations  17.3 us (4%)
  blocking collectives  16.6 us (4%)
    pallas_call x2, Pallas kernels, attention_backward(): pl.pallas_call(functools.partial(backward_kernel, causal, seq_count), gri...  82.9 us
    ppermute x51, starting transfers between devices, flat_permute(): return lax.ppermute(value, ('rep', 'fsdp'), pairs)  81.6 us
    ppermute x51, waiting for transfers between devices, flat_permute(): return lax.ppermute(value, ('rep', 'fsdp'), pairs)  75.6 us
    pallas_call x2, Pallas kernels, attention_forward(): pl.pallas_call(functools.partial(forward_kernel, causal, seq_count), grid...  55.1 us
    pallas_call x1, Pallas kernels, feed_forward_both(): pl.pallas_call(functools.partial(feed_kernel, seq_count), grid=(hidden //...  47.5 us
    all_gather x1, blocking collectives, per_device(): lax.all_gather(gains.astype(LOW), 'fsdp', axis=1, tiled=True).astype(WIDE)  16.6 us
    pallas_call x2, Pallas kernels, assemble(): pl.pallas_call(functools.partial(assemble_kernel, place, hops), in_specs=...  10 us
    pallas_call x1, Pallas kernels, input_gradient(): pl.pallas_call(input_kernel, grid=(rows // block,), in_specs=[rowwise, ro...  9.86 us
  transfers between devices with their start and end apart: 56, of which 22 were waited for; matrix products, arithmetic and copies ran while one was open for 7% of the time, Pallas kernels for 36%

profile of v7, /device:TPU:0, one launch (start us, length us, event | category | flops | bytes accessed | tf_op | source)
XLA Modules:
  0.0 461.3 jit_solution(11580802622843854804)
XLA Ops:
  7.3 3.2 multiply_reduce_fusion.1
  13.4 3.1 collective-permute-start
  16.5 2.6 collective-permute-start.1
  21.0 16.6 %all-gather = bf16[8,96,3]{1,2,0:T(4,128)(2,1)S(1)} all-gather(bf16[1,96,3]{1,2,0:T(4,128)(2,1)S(1)} %get-tuple-element.378), channel_id=1, replica_groups=mesh['rep'=4,'fsdp'=8] {'fsdp'}, dimensions={0}, use_global_device_ids=true | all-gather | bytes 5184 | tf_op jit(solution)/shard_map/all_gather | solution.py:809
  46.5 9.4 %collective-permute-done.3.refs_1_ = bf16[4,96,768]{2,1,0:T(8,128)(2,1)S(1)} collective-permute-done((bf16[4,96,768]{2,1,0:T(8,128)(2,1)S(1)}, bf16[4,96,768]{2,1,0:T(8,128)(2,1)S(1)}, u32[]{:S(2)}, u32[]{:S(2)}) %collective-permute-start.3) | collective-permute-done | bytes 589856 | tf_op jit(solution)/shard_map/ppermute | solution.py:638
  55.9 13.1 %collective-permute-done.4.refs_2_ = bf16[4,96,768]{2,1,0:T(8,128)(2,1)S(1)} collective-permute-done((bf16[4,96,768]{2,1,0:T(8,128)(2,1)S(1)}, bf16[4,96,768]{2,1,0:T(8,128)(2,1)S(1)}, u32[]{:S(2)}, u32[]{:S(2)}) %collective-permute-start.4) | collective-permute-done | bytes 589856 | tf_op jit(solution)/shard_map/ppermute | solution.py:638
  72.1 9.7 %collective-permute-start.10 = (bf16[64,768]{1,0:T(8,128)(2,1)S(1)}, bf16[64,768]{1,0:T(8,128)(2,1)S(1)}, u32[]{:S(2)}, u32[]{:S(2)}) collective-permute-start(bf16[64,768]{1,0:T(8,128)(2,1)S(1)} %fusion.26), channel_id=1, source_target_pairs={{0,2},{1,3},{2,4},{3,5},{4,6},{5,7},{6,0},{7,1},{8,10},{9,11},{10,... | collective-permute-start | bytes 294920 | tf_op jit(solution)/shard_map/ppermute | solution.py:638
  82.3 26.8 %self_forward.1 = (bf16[1024,768]{1,0:T(8,128)(2,1)}, bf16[1024,768]{1,0:T(8,128)(2,1)}, bf16[1024,768]{1,0:T(8,128)(2,1)}, bf16[1024,768]{1,0:T(8,128)(2,1)}, f...) custom-call(s32[2]{0:T(128)} %length_ref.9, bf16[1024,768]{1,0:T(8,128)(2,1)} %bitcast.146, ...), custom_call_target="tpu_custom_call" | custom-call | flops 31050000384 | bytes 20971520 | tf_op jit(solution)/shard_map/self_forward/pallas_call | solution.py:188
  111.6 3.2 collective-permute-start.12
  114.8 5.5 %assemble_cross.1.wq_ref.wk_ref.wv_ref.wo_ref = bf16[4,768,768]{2,1,0:T(8,128)(2,1)} custom-call(s32[3]{0:T(128)} %pad_add_fusion.where_ref, bf16[4,96,768]{2,1,0:T(8,128)(2,1)} %copy-done.20, bf16[4,96,768]{2,1,0:T(8,128)(2,1)} %copy-done.57, bf16[4,96,768]{2,1,0:T(8,128)(2,1)} %copy-done.58, bf16[4,96,768]{2,1,0:T(8,128)(2,1)} %copy-done.59, ...), custom_call_target="tpu_custom_call" | custom-call | flops 4600000000 | bytes 8388608 | tf_op jit(solution)/shard_map/assemble_cross/pallas_call | solution.py:694
  126.6 28.3 %cross_forward.1 = (bf16[1024,768]{1,0:T(8,128)(2,1)}, bf16[1024,768]{1,0:T(8,128)(2,1)}, bf16[1024,768]{1,0:T(8,128)(2,1)}, bf16[1024,768]{1,0:T(8,128)(2,1)}, ...) custom-call(s32[2]{0:T(128)} %length_ref.8, f32[1024,768]{1,0:T(8,128)} %get-tuple-element.117.x_ref, ...), custom_call_target="tpu_custom_call" | custom-call | flops 31050000384 | bytes 20971520 | tf_op jit(solution)/shard_map/cross_forward/pallas_call | solution.py:188
  159.4 4.5 assemble_out.1.wd_ref
  163.9 47.5 %feed_forward_both.1 = (bf16[1024,768]{1,0:T(8,128)(2,1)}, f32[1024,768]{1,0:T(8,128)}, bf16[768,2048]{1,0:T(8,128)(2,1)}, bf16[768,2048]{1,0:T(8,128)(2,1)}, bf...) custom-call(s32[2]{0:T(128)} %length_ref.9, ...), custom_call_target="tpu_custom_call" | custom-call | flops 52899999744 | bytes 41943040 | tf_op jit(solution)/shard_map/feed_forward_both/pallas_call | solution.py:314
  215.0 48.7 %cross_backward.1 = (f32[1024,768]{1,0:T(8,128)}, bf16[1024,768]{1,0:T(8,128)(2,1)}, bf16[1024,768]{1,0:T(8,128)(2,1)}, f32[1,768]{1,0:T(1,128)}, bf16[4,128,768...) custom-call(s32[2]{0:T(128)} %length_ref.8, ...), custom_call_target="tpu_custom_call" | custom-call | flops 51749998592 | bytes 41943040 | tf_op jit(solution)/shard_map/cross_backward/pallas_call | solution.py:546
  266.6 6.7 %memory_gradient.1 = f32[1024,768]{1,0:T(8,128)} custom-call(bf16[1024,768]{1,0:T(8,128)(2,1)} %get-tuple-element.149.gk_ref, bf16[1024,768]{1,0:T(8,128)(2,1)} %get-tuple-element.150.gv_ref, bf16[4,768,768]{2,1,0:T(8,128)(2,1)} %assemble_cross.1.wq_ref.wk_ref.wv_ref.wo_ref, bf16[4,768,768]{2,1,0:T(8,128)(2,1)} %assemble_cross.1.wq_ref.wk_ref.wv_ref.wo_ref), custom_call_target="tpu_custom_call" | custom-call | flops 8049999872 | bytes 10485760 | tf_op jit(solution)/shard_map/memory_gradient/pallas_call | solution.py:619
  273.3 4.0 fusion
  280.8 34.1 %self_backward.1 = (bf16[1024,768]{1,0:T(8,128)(2,1)}, bf16[1024,768]{1,0:T(8,128)(2,1)}, bf16[1024,768]{1,0:T(8,128)(2,1)}, bf16[3,768,768]{2,1,0:T(8,128)(2,1)}, f32[16,512]{1,0:T(8,128)}) custom-call(s32[2]{0:T(128)} %length_ref.9, s32[3]{0:T(128)} %pad_add_fusion.where_ref, bf16[1024,768]{1,0:T(8,128)(2,1)} %bitcast.147, ...), custom_call_target="tpu_custom_call" | custom-call | flops 51749998592 | bytes 41943040 | tf_op jit(solution)/shard_map/self_backward/pallas_call | solution.py:546
  324.9 9.9 %input_gradient.1 = (f32[1024,768]{1,0:T(8,128)}, f32[1,768]{1,0:T(1,128)}) custom-call(bf16[1024,768]{1,0:T(8,128)(2,1)} %get-tuple-element.176.gq_ref, bf16[1024,768]{1,0:T(8,128)(2,1)} %get-tuple-element.177.gk_ref, bf16[1024,768]{1,0:T(8,128)(2,1)} %get-tuple-element.178.gv_ref, ...), custom_call_target="tpu_custom_call" | custom-call | flops 9200000000 | bytes 12582912 | tf_op jit(solution)/shard_map/input_gradient/pallas_call | solution.py:598
  340.3 8.2 %collective-permute-start.36 = (bf16[192,768]{1,0:T(8,128)(2,1)S(1)}, bf16[192,768]{1,0:T(8,128)(2,1)S(1)}, u32[]{:S(2)}, u32[]{:S(2)}) collective-permute-start(bf16[192,768]{1,0:T(8,128)(2,1)S(1)} %get-tuple-element.343), channel_id=1, source_target_pairs={{0,2},{1,3},{2,4},{3,5},{4,6},{5,7},{6,0},{7,1},{8,10},{9,11},{10,... | collective-permute-start | bytes 884744 | tf_op jit(solution)/shard_map/ppermute | solution.py:638
  353.6 5.1 %collective-permute-done.36 = bf16[192,768]{1,0:T(8,128)(2,1)S(1)} collective-permute-done((bf16[192,768]{1,0:T(8,128)(2,1)S(1)}, bf16[192,768]{1,0:T(8,128)(2,1)S(1)}, u32[]{:S(2)}, u32[]{:S(2)}) %collective-permute-start.36) | collective-permute-done | bytes 294944 | tf_op jit(solution)/shard_map/ppermute | solution.py:638
  358.7 18.3 %collective-permute-done.37 = bf16[192,768]{1,0:T(8,128)(2,1)S(1)} collective-permute-done((bf16[192,768]{1,0:T(8,128)(2,1)S(1)}, bf16[192,768]{1,0:T(8,128)(2,1)S(1)}, u32[]{:S(2)}, u32[]{:S(2)}) %collective-permute-start.37) | collective-permute-done | bytes 294944 | tf_op jit(solution)/shard_map/ppermute | solution.py:638
  377.0 2.7 collective-permute-done.38
  389.6 12.4 %collective-permute-done.33 = bf16[48,2048]{1,0:T(8,128)(2,1)S(1)} collective-permute-done((bf16[48,2048]{1,0:T(8,128)(2,1)S(1)}, bf16[48,2048]{1,0:T(8,128)(2,1)S(1)}, u32[]{:S(2)}, u32[]{:S(2)}) %collective-permute-start.33) | collective-permute-done | bytes 196640 | tf_op jit(solution)/shard_map/ppermute | solution.py:638
  423.9 10.0 %collective-permute-start.49 = (f32[13721]{0:T(1024)S(1)}, f32[13721]{0:T(1024)S(1)}, u32[]{:S(2)}, u32[]{:S(2)}) collective-permute-start(f32[13721]{0:T(1024)S(1)} %add.250), channel_id=1, source_target_pairs={{0,2},{1,3},{2,0},{3,1},{4,6},{5,7},{6,4},{7,5},{8,10},{9,11},{10,... | collective-permute-start | bytes 164660 | tf_op jit(solution)/shard_map/ppermute | solution.py:638
  (342 shorter events, 110.4 us)
Async XLA Ops:
  7.2 64.8 %all-gather.4.cloned.1.call-start = ((), (), s32[]{:S(2)}) async-start(), calls=%async_computation.3 | async-start | bytes 5308416 | tf_op jit(solution)/shard_map/all_gather | solution.py:808
  10.5 153.4 %all-gather.6.cloned.1.call-start = ((), (), s32[]{:S(2)}) async-start(), calls=%async_computation.4 | async-start | bytes 7077888 | tf_op jit(solution)/shard_map/all_gather | solution.py:810
  12.3 260.9 %reduce-scatter.4.cloned.1.call-start = ((), (), s32[]{:S(2)}) async-start(), calls=%async_computation.5 | async-start | bytes 3538944 | tf_op jit(solution)/shard_map/reduce_scatter | solution.py:859
  41.0 27.9 %collective-permute-start.4 = (bf16[4,96,768]{2,1,0:T(8,128)(2,1)S(1)}, bf16[4,96,768]{2,1,0:T(8,128)(2,1)S(1)}, u32[]{:S(2)}, u32[]{:S(2)}) collective-permute-start(bf16[4,96,768]{2,1,0:T(8,128)(2,1)S(1)} %pad_maximum_fusion.4.refs_0_), channel_id=1, source_target_pairs={{0,16},{1,17},{2,18},{3,19},{4,20},{5,21},{6,22},{7,23},{8,24},{9,... | collective-permute-start | bytes 1769480 | tf_op jit(solution)/shard_map/ppermute | solution.py:638
  46.5 62.7 %collective-permute-start.6 = (bf16[4,96,768]{2,1,0:T(8,128)(2,1)S(1)}, bf16[4,96,768]{2,1,0:T(8,128)(2,1)S(1)}, u32[]{:S(2)}, u32[]{:S(2)}) collective-permute-start(bf16[4,96,768]{2,1,0:T(8,128)(2,1)S(1)} %pad_maximum_fusion.4.refs_0_), channel_id=1, source_target_pairs={{0,1},{1,0},{2,3},{3,2},{4,5},{5,4},{6,7},{7,6},{8,9},{9,8},{10,11... | collective-permute-start | bytes 1769480 | tf_op jit(solution)/shard_map/ppermute | solution.py:638
  55.9 55.7 %collective-permute-start.7 = (bf16[4,96,768]{2,1,0:T(8,128)(2,1)S(1)}, bf16[4,96,768]{2,1,0:T(8,128)(2,1)}, u32[]{:S(2)}, u32[]{:S(2)}) collective-permute-start(bf16[4,96,768]{2,1,0:T(8,128)(2,1)S(1)} %collective-permute-done.3.refs_1_), channel_id=1, source_target_pairs={{0,1},{1,0},{2,3},{3,2},{4,5},{5,4},{6,7},{7,6},{8,9},{9,8},{10,11... | collective-permute-start | bytes 1769480 | tf_op jit(solution)/shard_map/ppermute | solution.py:638
  69.0 45.8 %collective-permute-start.8 = (bf16[4,96,768]{2,1,0:T(8,128)(2,1)S(1)}, bf16[4,96,768]{2,1,0:T(8,128)(2,1)}, u32[]{:S(2)}, u32[]{:S(2)}) collective-permute-start(bf16[4,96,768]{2,1,0:T(8,128)(2,1)S(1)} %collective-permute-done.4.refs_2_), channel_id=1, source_target_pairs={{0,1},{1,0},{2,3},{3,2},{4,5},{5,4},{6,7},{7,6},{8,9},{9,8},{10,11... | collective-permute-start | bytes 1769480 | tf_op jit(solution)/shard_map/ppermute | solution.py:638
  69.0 45.8 %collective-permute-start.9 = (bf16[4,96,768]{2,1,0:T(8,128)(2,1)S(1)}, bf16[4,96,768]{2,1,0:T(8,128)(2,1)}, u32[]{:S(2)}, u32[]{:S(2)}) collective-permute-start(bf16[4,96,768]{2,1,0:T(8,128)(2,1)S(1)} %collective-permute-done.5.refs_3_), channel_id=1, source_target_pairs={{0,1},{1,0},{2,3},{3,2},{4,5},{5,4},{6,7},{7,6},{8,9},{9,8},{10,11... | collective-permute-start | bytes 1769480 | tf_op jit(solution)/shard_map/ppermute | solution.py:638
  72.1 48.2 %collective-permute-start.10 = (bf16[64,768]{1,0:T(8,128)(2,1)S(1)}, bf16[64,768]{1,0:T(8,128)(2,1)S(1)}, u32[]{:S(2)}, u32[]{:S(2)}) collective-permute-start(bf16[64,768]{1,0:T(8,128)(2,1)S(1)} %fusion.26), channel_id=1, source_target_pairs={{0,2},{1,3},{2,4},{3,5},{4,6},{5,7},{6,0},{7,1},{8,10},{9,11},{10,... | collective-permute-start | bytes 294920 | tf_op jit(solution)/shard_map/ppermute | solution.py:638
  122.4 32.4 %collective-permute-start.13 = (bf16[4,64,768]{2,1,0:T(8,128)(2,1)S(1)}, bf16[4,64,768]{2,1,0:T(8,128)(2,1)S(1)}, u32[]{:S(2)}, u32[]{:S(2)}) collective-permute-start(bf16[4,64,768]{2,1,0:T(8,128)(2,1)S(1)} %pad_maximum_fusion.7.refs_0_), channel_id=1, source_target_pairs={{0,8},{1,9},{2,10},{3,11},{4,12},{5,13},{6,14},{7,15},{8,0},{9,1},... | collective-permute-start | bytes 1179656 | tf_op jit(solution)/shard_map/ppermute | solution.py:638
  124.0 30.9 %collective-permute-start.14 = (bf16[4,64,768]{2,1,0:T(8,128)(2,1)S(1)}, bf16[4,64,768]{2,1,0:T(8,128)(2,1)S(1)}, u32[]{:S(2)}, u32[]{:S(2)}) collective-permute-start(bf16[4,64,768]{2,1,0:T(8,128)(2,1)S(1)} %pad_maximum_fusion.7.refs_0_), channel_id=1, source_target_pairs={{0,16},{1,17},{2,18},{3,19},{4,20},{5,21},{6,22},{7,23},{8,24},{9,... | collective-permute-start | bytes 1179656 | tf_op jit(solution)/shard_map/ppermute | solution.py:638
  125.5 29.4 %collective-permute-start.15 = (bf16[4,64,768]{2,1,0:T(8,128)(2,1)S(1)}, bf16[4,64,768]{2,1,0:T(8,128)(2,1)S(1)}, u32[]{:S(2)}, u32[]{:S(2)}) collective-permute-start(bf16[4,64,768]{2,1,0:T(8,128)(2,1)S(1)} %pad_maximum_fusion.7.refs_0_), channel_id=1, source_target_pairs={{0,24},{1,25},{2,26},{3,27},{4,28},{5,29},{6,30},{7,31},{8,16},{9,... | collective-permute-start | bytes 1179656 | tf_op jit(solution)/shard_map/ppermute | solution.py:638
  211.4 52.4 %collective-permute-start.20 = (bf16[2,4,64,768]{3,2,1,0:T(8,128)(2,1)}, bf16[2,4,64,768]{3,2,1,0:T(8,128)(2,1)S(1)}, u32[]{:S(2)}, u32[]{:S(2)}) collective-permute-start(bf16[2,4,64,768]{3,2,1,0:T(8,128)(2,1)} %get-tuple-element.146), channel_id=1, source_target_pairs={{0,8},{1,9},{2,10},{3,11},{4,12},{5,13},{6,14},{7,15},{8,0},{9,1},... | collective-permute-start | bytes 2359304 | tf_op jit(solution)/shard_map/ppermute | solution.py:638
  212.9 50.9 %collective-permute-start.21 = (bf16[2,4,64,768]{3,2,1,0:T(8,128)(2,1)}, bf16[2,4,64,768]{3,2,1,0:T(8,128)(2,1)S(1)}, u32[]{:S(2)}, u32[]{:S(2)}) collective-permute-start(bf16[2,4,64,768]{3,2,1,0:T(8,128)(2,1)} %get-tuple-element.147), channel_id=1, source_target_pairs={{0,16},{1,17},{2,18},{3,19},{4,20},{5,21},{6,22},{7,23},{8,24},{9,... | collective-permute-start | bytes 2359304 | tf_op jit(solution)/shard_map/ppermute | solution.py:638
  214.4 49.4 %collective-permute-start.22 = (bf16[2,4,64,768]{3,2,1,0:T(8,128)(2,1)}, bf16[2,4,64,768]{3,2,1,0:T(8,128)(2,1)S(1)}, u32[]{:S(2)}, u32[]{:S(2)}) collective-permute-start(bf16[2,4,64,768]{3,2,1,0:T(8,128)(2,1)} %get-tuple-element.148), channel_id=1, source_target_pairs={{0,24},{1,25},{2,26},{3,27},{4,28},{5,29},{6,30},{7,31},{8,16},{9,... | collective-permute-start | bytes 2359304 | tf_op jit(solution)/shard_map/ppermute | solution.py:638
  215.0 100.0 %reduce-scatter.6.cloned.1.call-start = ((), (), s32[]{:S(2)}) async-start(), calls=%async_computation.6 | async-start | bytes 3538944 | tf_op jit(solution)/shard_map/reduce_scatter | solution.py:859
  265.2 123.3 %reduce-scatter.8.cloned.1.call-start = ((), (), s32[]{:S(2)}) async-start(), calls=%async_computation.7 | async-start | bytes 3981312 | tf_op jit(solution)/shard_map/reduce_scatter | solution.py:859
  277.3 37.7 %collective-permute-start.24 = (bf16[4,128,768]{2,1,0:T(8,128)(2,1)}, bf16[4,128,768]{2,1,0:T(8,128)(2,1)S(1)}, u32[]{:S(2)}, u32[]{:S(2)}) collective-permute-start(bf16[4,128,768]{2,1,0:T(8,128)(2,1)} %get-tuple-element.169), channel_id=1, source_target_pairs={{0,8},{1,9},{2,10},{3,11},{4,12},{5,13},{6,14},{7,15},{8,0},{9,1},... | collective-permute-start | bytes 2359304 | tf_op jit(solution)/shard_map/ppermute | solution.py:638
  278.8 36.7 %collective-permute-start.25 = (bf16[4,128,768]{2,1,0:T(8,128)(2,1)}, bf16[4,128,768]{2,1,0:T(8,128)(2,1)S(1)}, u32[]{:S(2)}, u32[]{:S(2)}) collective-permute-start(bf16[4,128,768]{2,1,0:T(8,128)(2,1)} %get-tuple-element.170), channel_id=1, source_target_pairs={{0,16},{1,17},{2,18},{3,19},{4,20},{5,21},{6,22},{7,23},{8,24},{9,... | collective-permute-start | bytes 2359304 | tf_op jit(solution)/shard_map/ppermute | solution.py:638
  280.3 35.2 %collective-permute-start.26 = (bf16[4,128,768]{2,1,0:T(8,128)(2,1)}, bf16[4,128,768]{2,1,0:T(8,128)(2,1)S(1)}, u32[]{:S(2)}, u32[]{:S(2)}) collective-permute-start(bf16[4,128,768]{2,1,0:T(8,128)(2,1)} %get-tuple-element.171), channel_id=1, source_target_pairs={{0,24},{1,25},{2,26},{3,27},{4,28},{5,29},{6,30},{7,31},{8,16},{9,... | collective-permute-start | bytes 2359304 | tf_op jit(solution)/shard_map/ppermute | solution.py:638
  335.9 45.6 %collective-permute-start.27 = (f32[2688]{0:T(1024)S(1)}, f32[2688]{0:T(1024)S(1)}, u32[]{:S(2)}, u32[]{:S(2)}) collective-permute-start(f32[2688]{0:T(1024)S(1)} %pad_maximum_fusion.12), channel_id=1, source_target_pairs={{0,8},{1,9},{2,10},{3,11},{4,12},{5,13},{6,14},{7,15},{8,0},{9,1},... | collective-permute-start | bytes 32264 | tf_op jit(solution)/shard_map/ppermute | solution.py:638
  348.4 28.6 %collective-permute-start.37 = (bf16[192,768]{1,0:T(8,128)(2,1)S(1)}, bf16[192,768]{1,0:T(8,128)(2,1)S(1)}, u32[]{:S(2)}, u32[]{:S(2)}) collective-permute-start(bf16[192,768]{1,0:T(8,128)(2,1)S(1)} %get-tuple-element.345), channel_id=1, source_target_pairs={{0,4},{1,5},{2,6},{3,7},{4,0},{5,1},{6,2},{7,3},{8,12},{9,13},{10,... | collective-permute-start | bytes 884744 | tf_op jit(solution)/shard_map/ppermute | solution.py:638
  348.5 31.2 %collective-permute-start.38 = (bf16[192,768]{1,0:T(8,128)(2,1)S(1)}, bf16[192,768]{1,0:T(8,128)(2,1)S(1)}, u32[]{:S(2)}, u32[]{:S(2)}) collective-permute-start(bf16[192,768]{1,0:T(8,128)(2,1)S(1)} %get-tuple-element.344), channel_id=1, source_target_pairs={{0,6},{1,7},{2,0},{3,1},{4,2},{5,3},{6,4},{7,5},{8,14},{9,15},{10,... | collective-permute-start | bytes 884744 | tf_op jit(solution)/shard_map/ppermute | solution.py:638
  352.0 35.1 %collective-permute-start.32 = (bf16[48,2048]{1,0:T(8,128)(2,1)S(1)}, bf16[48,2048]{1,0:T(8,128)(2,1)S(1)}, u32[]{:S(2)}, u32[]{:S(2)}) collective-permute-start(bf16[48,2048]{1,0:T(8,128)(2,1)S(1)} %fusion.18), channel_id=1, source_target_pairs={{0,8},{1,9},{2,10},{3,11},{4,12},{5,13},{6,14},{7,15},{8,0},{9,1},... | collective-permute-start | bytes 589832 | tf_op jit(solution)/shard_map/ppermute | solution.py:638
  (100 other events, 1358.2 us)
Sparse Core Ops, SparseCore 0:
  10.6 61.3 all-gather.3
  74.2 69.8 all-gather.5
  215.1 45.7 reduce-scatter.3
  265.4 46.2 reduce-scatter.5
  316.6 68.5 reduce-scatter.7

commit v8 on v7

--- a/solution.py
+++ b/solution.py
@@ -17,7 +17,7 @@
 PAIR = 2 * DH
 GROUP = 4 * DH
 HIDDEN = -1e30
-VMEM_BYTES = 60 * 1024 * 1024
+MEGABYTE = 1024 * 1024
 PEAK = 1.15e9
 LINE = 4
 LINE_CORES = 2
@@ -87,7 +87,7 @@
 def forward_body(causal, seq_count, length_ref, wave_ref, bias_ref, q_ref, k_ref, v_ref, mix_ref, total_ref, group):
     rows = q_ref.shape[0] // seq_count
     keys = k_ref.shape[0] // seq_count
-    block = 256
+    block = rows
     for pair in range(2):
         at = pair * PAIR
         for side in range(2):
@@ -170,7 +170,7 @@
 
 
 def whole(shape):
-    return pl.BlockSpec(shape, lambda g: (0,) * len(shape))
+    return pl.BlockSpec(shape, lambda g: (0,) * len(shape), pipeline_mode=pl.Buffered(1))
 
 
 def columns(rows):
@@ -217,7 +217,7 @@
             pltpu.VMEM((2, length, length) if causal else (1, 8, PAIR), WIDE),
         ],
         cost_estimate=pl.CostEstimate(flops=int(27 * PEAK), bytes_accessed=20 << 20, transcendentals=0),
-        compiler_params=pltpu.CompilerParams(vmem_limit_bytes=VMEM_BYTES),
+        compiler_params=pltpu.CompilerParams(vmem_limit_bytes=36 * MEGABYTE),
         name="self_forward" if causal else "cross_forward",
     )(*args)
 
@@ -342,7 +342,7 @@
             pltpu.VMEM((4, block // 4, width), LOW),
         ],
         cost_estimate=pl.CostEstimate(flops=int(46 * PEAK), bytes_accessed=40 << 20, transcendentals=0),
-        compiler_params=pltpu.CompilerParams(vmem_limit_bytes=VMEM_BYTES),
+        compiler_params=pltpu.CompilerParams(vmem_limit_bytes=40 * MEGABYTE),
         name="feed_forward_both",
     )(lengths, where, after, out_grad, gain, w_in, w_in, w_out)
 
@@ -363,7 +363,7 @@
     row_count = x_ref.shape[0]
     rows = q_ref.shape[0] // seq_count
     keys = k_ref.shape[0] // seq_count
-    block = 256
+    block = rows
 
     @pl.when(group == 0)
     def _():
@@ -573,7 +573,7 @@
             *scratch,
         ],
         cost_estimate=pl.CostEstimate(flops=int(45 * PEAK), bytes_accessed=40 << 20, transcendentals=0),
-        compiler_params=pltpu.CompilerParams(vmem_limit_bytes=VMEM_BYTES),
+        compiler_params=pltpu.CompilerParams(vmem_limit_bytes=(36 if causal else 46) * MEGABYTE),
         name="self_backward" if causal else "cross_backward",
     )(lengths, where, x, source, grad, gain, weights, weights, wave, *kept, mix, past)
 
@@ -602,7 +602,7 @@
         out_specs=[rowwise, whole((1, width))],
         out_shape=[jax.ShapeDtypeStruct((rows, width), WIDE), jax.ShapeDtypeStruct((1, width), WIDE)],
         cost_estimate=pl.CostEstimate(flops=int(8 * PEAK), bytes_accessed=12 << 20, transcendentals=0),
-        compiler_params=pltpu.CompilerParams(vmem_limit_bytes=VMEM_BYTES),
+        compiler_params=pltpu.CompilerParams(vmem_limit_bytes=24 * MEGABYTE),
         name="input_gradient",
     )(*grads, weights, weights, weights, x, grad, gain)
 
@@ -623,7 +623,7 @@
         out_specs=rowwise,
         out_shape=jax.ShapeDtypeStruct((rows, width), WIDE),
         cost_estimate=pl.CostEstimate(flops=int(7 * PEAK), bytes_accessed=10 << 20, transcendentals=0),
-        compiler_params=pltpu.CompilerParams(vmem_limit_bytes=VMEM_BYTES),
+        compiler_params=pltpu.CompilerParams(vmem_limit_bytes=24 * MEGABYTE),
         name="memory_gradient",
     )(grad_key, grad_value, weights, weights)
 
@@ -698,7 +698,7 @@
         out_shape=jax.ShapeDtypeStruct(shape, LOW),
         scratch_shapes=[pltpu.SemaphoreType.DMA((8 * hops,))],
         cost_estimate=pl.CostEstimate(flops=int(4 * PEAK), bytes_accessed=8 << 20, transcendentals=0),
-        compiler_params=pltpu.CompilerParams(vmem_limit_bytes=VMEM_BYTES),
+        compiler_params=pltpu.CompilerParams(vmem_limit_bytes=24 * MEGABYTE),
         name=name,
     )(where, *parts)
 

time: 469 us -> 462 us (0.985)
  Pallas kernels: 212 us -> 176 us
  local copies, waits for them, and re-layouts: 20.5 us -> 49.7 us
    unnamed x144 -> x190, local copies, waits for them, and re-layouts: 9.63 us -> 41.8 us
    pallas_call x2, Pallas kernels: 55.1 us -> 39.5 us  [attention_forward(): pl.pallas_call(functools.partial(forward_kernel, causal, seq_count), grid...]
    pallas_call x2, Pallas kernels: 82.9 us -> 70.2 us  [attention_backward(): pl.pallas_call(functools.partial(backward_kernel, causal, seq_count), gri...]
  transfers between devices with their start and end apart: 56 -> 56, of which waited for: 22 -> 21; matrix products, arithmetic and copies ran while one was open for 7% -> 6% of each run, Pallas kernels for 36% -> 29%
where the time goes in v8:
time: 462 us; the launch traced here: 454 us
  Pallas kernels  176 us (38%)
  starting transfers between devices  82.2 us (18%)
  waiting for transfers between devices  77.5 us (17%)
  local copies, waits for them, and re-layouts  49.7 us (11%)
  other arithmetic  34.3 us (7%)
  between operations  17.7 us (4%)
  blocking collectives  16.7 us (4%)
    ppermute x51, starting transfers between devices, flat_permute(): return lax.ppermute(value, ('rep', 'fsdp'), pairs)  82 us
    ppermute x51, waiting for transfers between devices, flat_permute(): return lax.ppermute(value, ('rep', 'fsdp'), pairs)  74.9 us
    pallas_call x2, Pallas kernels, attention_backward(): pl.pallas_call(functools.partial(backward_kernel, causal, seq_count), gri...  70.2 us
    pallas_call x1, Pallas kernels, feed_forward_both(): pl.pallas_call(functools.partial(feed_kernel, seq_count), grid=(hidden //...  45.8 us
    unnamed x190, local copies, waits for them, and re-layouts  41.8 us
    pallas_call x2, Pallas kernels, attention_forward(): pl.pallas_call(functools.partial(forward_kernel, causal, seq_count), grid...  39.5 us
    all_gather x1, blocking collectives, per_device(): lax.all_gather(gains.astype(LOW), 'fsdp', axis=1, tiled=True).astype(WIDE)  16.7 us
    convert_element_type x7, other arithmetic, add_up(): return sum((part.astype(WIDE) for part in parts)).astype(LOW)  11.2 us
  transfers between devices with their start and end apart: 56, of which 21 were waited for; matrix products, arithmetic and copies ran while one was open for 6% of the time, Pallas kernels for 29%

profile of v8, /device:TPU:0, one launch (start us, length us, event | category | flops | bytes accessed | tf_op | source)
XLA Modules:
  0.0 454.2 jit_solution(4285964424188165959)
XLA Ops:
  7.3 3.2 multiply_reduce_fusion.1
  13.5 3.1 collective-permute-start
  16.6 2.6 collective-permute-start.1
  21.1 16.7 %all-gather = bf16[8,96,3]{1,2,0:T(4,128)(2,1)S(1)} all-gather(bf16[1,96,3]{1,2,0:T(4,128)(2,1)S(1)} %get-tuple-element.378), channel_id=1, replica_groups=mesh['rep'=4,'fsdp'=8] {'fsdp'}, dimensions={0}, use_global_device_ids=true | all-gather | bytes 5184 | tf_op jit(solution)/shard_map/all_gather | solution.py:809
  44.8 11.0 %collective-permute-done.3.refs_1_ = bf16[4,96,768]{2,1,0:T(8,128)(2,1)S(1)} collective-permute-done((bf16[4,96,768]{2,1,0:T(8,128)(2,1)S(1)}, bf16[4,96,768]{2,1,0:T(8,128)(2,1)S(1)}, u32[]{:S(2)}, u32[]{:S(2)}) %collective-permute-start.3) | collective-permute-done | bytes 589856 | tf_op jit(solution)/shard_map/ppermute | solution.py:638
  55.8 13.2 %collective-permute-done.4.refs_2_ = bf16[4,96,768]{2,1,0:T(8,128)(2,1)} collective-permute-done((bf16[4,96,768]{2,1,0:T(8,128)(2,1)S(1)}, bf16[4,96,768]{2,1,0:T(8,128)(2,1)}, u32[]{:S(2)}, u32[]{:S(2)}) %collective-permute-start.4) | collective-permute-done | bytes 589856 | tf_op jit(solution)/shard_map/ppermute | solution.py:638
  69.5 2.6 all-gather.4.cloned.1.call-done.wq_ref.wk_ref.wv_ref.wo_ref
  72.1 9.6 %collective-permute-start.10 = (bf16[64,768]{1,0:T(8,128)(2,1)S(1)}, bf16[64,768]{1,0:T(8,128)(2,1)S(1)}, u32[]{:S(2)}, u32[]{:S(2)}) collective-permute-start(bf16[64,768]{1,0:T(8,128)(2,1)S(1)} %fusion.26), channel_id=1, source_target_pairs={{0,2},{1,3},{2,4},{3,5},{4,6},{5,7},{6,0},{7,1},{8,10},{9,11},{10,... | collective-permute-start | bytes 294920 | tf_op jit(solution)/shard_map/ppermute | solution.py:638
  81.7 2.7 copy-done.6
  84.4 20.7 %self_forward.1 = (bf16[1024,768]{1,0:T(8,128)(2,1)S(1)}, bf16[1024,768]{1,0:T(8,128)(2,1)S(1)}, bf16[1024,768]{1,0:T(8,128)(2,1)S(1)}, bf16[1024,768]{1,0:T(8,1...) custom-call(s32[2]{0:T(128)S(1)} %copy-done.15, bf16[1024,768]{1,0:T(8,128)(2,1)S(1)} %bitcast.112, ...), custom_call_target="tpu_custom_call" | custom-call | flops 31050000384 | bytes 20971520 | tf_op jit(solution)/shard_map/self_forward/pallas_call | solution.py:188
  110.3 4.4 assemble_cross.1.wq_ref.wk_ref.wv_ref.wo_ref
  121.9 18.8 %cross_forward.1 = (bf16[1024,768]{1,0:T(8,128)(2,1)S(1)}, bf16[1024,768]{1,0:T(8,128)(2,1)S(1)}, bf16[1024,768]{1,0:T(8,128)(2,1)S(1)}, bf16[1024,768]{1,0:T(8,...) custom-call(s32[2]{0:T(128)S(1)} %copy-done.14, f32[1024,768]{1,0:T(8,128)S(1)} %get-tuple-element.117.x_ref, ...), custom_call_target="tpu_custom_call" | custom-call | flops 31050000384 | bytes 20971520 | tf_op jit(solution)/shard_map/cross_forward/pallas_call | solution.py:188
  151.7 5.8 %assemble_out.1.wd_ref = bf16[2048,768]{1,0:T(8,128)(2,1)S(1)} custom-call(s32[3]{0:T(128)S(1)} %pad_add_fusion.where_ref, bf16[4,64,768]{2,1,0:T(8,128)(2,1)S(1)} %pad_maximum_fusion.7.refs_0_, bf16[4,64,768]{2,1,0:T(8,128)(2,1)S(1)} %collective-permute-done.13.refs_1_, bf16[4,64,768]{2,1,0:T(8,128)(2,1)S(1)} %collective-permute-done.14.refs_2_, ...), custom_call_target="tpu_custom_call" | custom-call | flops 4600000000 | bytes 8388608 | tf_op jit(solution)/shard_map/assemble_out/pallas_call | solution.py:694
  159.1 45.8 %feed_forward_both.1 = (bf16[1024,768]{1,0:T(8,128)(2,1)}, f32[1024,768]{1,0:T(8,128)S(1)}, bf16[768,2048]{1,0:T(8,128)(2,1)}, bf16[768,2048]{1,0:T(8,128)(2,1)}...) custom-call(s32[2]{0:T(128)S(1)} %copy-done.15, ...), custom_call_target="tpu_custom_call" | custom-call | flops 52899999744 | bytes 41943040 | tf_op jit(solution)/shard_map/feed_forward_both/pallas_call | solution.py:314
  212.5 39.9 %cross_backward.1 = (f32[1024,768]{1,0:T(8,128)}, bf16[1024,768]{1,0:T(8,128)(2,1)S(1)}, bf16[1024,768]{1,0:T(8,128)(2,1)S(1)}, f32[1,768]{1,0:T(1,128)S(1)}, bf...) custom-call(s32[2]{0:T(128)S(1)} %copy-done.14, ...), custom_call_target="tpu_custom_call" | custom-call | flops 51749998592 | bytes 41943040 | tf_op jit(solution)/shard_map/cross_backward/pallas_call | solution.py:546
  260.8 4.2 memory_gradient.1
  265.1 4.4 fusion
  275.8 30.2 %self_backward.1 = (bf16[1024,768]{1,0:T(8,128)(2,1)S(1)}, bf16[1024,768]{1,0:T(8,128)(2,1)S(1)}, bf16[1024,768]{1,0:T(8,128)(2,1)S(1)}, bf16[3,768,768]{2,1,0:T(8,128)(2,1)}, f32[16,512]{1,0:T(8,128)S(1)}) custom-call(s32[2]{0:T(128)S(1)} %copy-done.15, s32[3]{0:T(128)S(1)} %pad_add_fusion.where_ref, bf16[1024,768]{1,0:T(8,128)(2,1)S(1)} %bitcast.113, ...), custom_call_target="tpu_custom_call" | custom-call | flops 51749998592 | bytes 41943040 | tf_op jit(solution)/shard_map/self_backward/pallas_call | solution.py:546
  321.8 6.2 %input_gradient.1 = (f32[1024,768]{1,0:T(8,128)}, f32[1,768]{1,0:T(1,128)S(1)}) custom-call(bf16[1024,768]{1,0:T(8,128)(2,1)S(1)} %get-tuple-element.176.gq_ref, bf16[1024,768]{1,0:T(8,128)(2,1)S(1)} %copy-done.22, bf16[1024,768]{1,0:T(8,128)(2,1)S(1)} %copy-done.24, bf16[4,768,768]{2,1,0:T(8,128)(2,1)S(1)} %copy-done.7, bf16[4,768,768]{2,1,0:T(8,128)(2,1)S(1)} %copy-done.7, ...), custom_call_target="tpu_custom_call" | custom-call | flops 9200000000 | bytes 12582912 | tf_op jit(solution)/shard_map/input_gradient/pallas_call | solution.py:598
  332.6 8.2 %collective-permute-start.36 = (bf16[192,768]{1,0:T(8,128)(2,1)S(1)}, bf16[192,768]{1,0:T(8,128)(2,1)S(1)}, u32[]{:S(2)}, u32[]{:S(2)}) collective-permute-start(bf16[192,768]{1,0:T(8,128)(2,1)S(1)} %get-tuple-element.343), channel_id=1, source_target_pairs={{0,2},{1,3},{2,4},{3,5},{4,6},{5,7},{6,0},{7,1},{8,10},{9,11},{10,... | collective-permute-start | bytes 884744 | tf_op jit(solution)/shard_map/ppermute | solution.py:638
  346.3 6.1 %collective-permute-done.36 = bf16[192,768]{1,0:T(8,128)(2,1)S(1)} collective-permute-done((bf16[192,768]{1,0:T(8,128)(2,1)S(1)}, bf16[192,768]{1,0:T(8,128)(2,1)S(1)}, u32[]{:S(2)}, u32[]{:S(2)}) %collective-permute-start.36) | collective-permute-done | bytes 294944 | tf_op jit(solution)/shard_map/ppermute | solution.py:638
  352.4 17.9 %collective-permute-done.37 = bf16[192,768]{1,0:T(8,128)(2,1)S(1)} collective-permute-done((bf16[192,768]{1,0:T(8,128)(2,1)S(1)}, bf16[192,768]{1,0:T(8,128)(2,1)S(1)}, u32[]{:S(2)}, u32[]{:S(2)}) %collective-permute-start.37) | collective-permute-done | bytes 294944 | tf_op jit(solution)/shard_map/ppermute | solution.py:638
  380.9 13.2 %collective-permute-done.33 = bf16[48,2048]{1,0:T(8,128)(2,1)S(1)} collective-permute-done((bf16[48,2048]{1,0:T(8,128)(2,1)S(1)}, bf16[48,2048]{1,0:T(8,128)(2,1)S(1)}, u32[]{:S(2)}, u32[]{:S(2)}) %collective-permute-start.33) | collective-permute-done | bytes 196640 | tf_op jit(solution)/shard_map/ppermute | solution.py:638
  415.6 10.9 %collective-permute-start.49 = (f32[13721]{0:T(1024)S(1)}, f32[13721]{0:T(1024)S(1)}, u32[]{:S(2)}, u32[]{:S(2)}) collective-permute-start(f32[13721]{0:T(1024)S(1)} %add.250), channel_id=1, source_target_pairs={{0,2},{1,3},{2,0},{3,1},{4,6},{5,7},{6,4},{7,5},{8,10},{9,11},{10,... | collective-permute-start | bytes 164660 | tf_op jit(solution)/shard_map/ppermute | solution.py:638
  (388 shorter events, 135.1 us)
Async XLA Ops:
  7.2 64.9 %all-gather.4.cloned.1.call-start = ((), (), s32[]{:S(2)}) async-start(), calls=%async_computation.3 | async-start | bytes 5308416 | tf_op jit(solution)/shard_map/all_gather | solution.py:808
  10.6 148.6 %all-gather.6.cloned.1.call-start = ((), (), s32[]{:S(2)}) async-start(), calls=%async_computation.4 | async-start | bytes 7077888 | tf_op jit(solution)/shard_map/all_gather | solution.py:810
  12.3 252.7 %reduce-scatter.4.cloned.1.call-start = ((), (), s32[]{:S(2)}) async-start(), calls=%async_computation.5 | async-start | bytes 3538944 | tf_op jit(solution)/shard_map/reduce_scatter | solution.py:859
  41.0 28.0 %collective-permute-start.4 = (bf16[4,96,768]{2,1,0:T(8,128)(2,1)S(1)}, bf16[4,96,768]{2,1,0:T(8,128)(2,1)}, u32[]{:S(2)}, u32[]{:S(2)}) collective-permute-start(bf16[4,96,768]{2,1,0:T(8,128)(2,1)S(1)} %pad_maximum_fusion.4.refs_0_), channel_id=1, source_target_pairs={{0,16},{1,17},{2,18},{3,19},{4,20},{5,21},{6,22},{7,23},{8,24},{9,... | collective-permute-start | bytes 1769480 | tf_op jit(solution)/shard_map/ppermute | solution.py:638
  44.7 60.5 %collective-permute-start.6 = (bf16[4,96,768]{2,1,0:T(8,128)(2,1)S(1)}, bf16[4,96,768]{2,1,0:T(8,128)(2,1)}, u32[]{:S(2)}, u32[]{:S(2)}) collective-permute-start(bf16[4,96,768]{2,1,0:T(8,128)(2,1)S(1)} %pad_maximum_fusion.4.refs_0_), channel_id=1, source_target_pairs={{0,1},{1,0},{2,3},{3,2},{4,5},{5,4},{6,7},{7,6},{8,9},{9,8},{10,11... | collective-permute-start | bytes 1769480 | tf_op jit(solution)/shard_map/ppermute | solution.py:638
  55.8 51.9 %collective-permute-start.7 = (bf16[4,96,768]{2,1,0:T(8,128)(2,1)S(1)}, bf16[4,96,768]{2,1,0:T(8,128)(2,1)}, u32[]{:S(2)}, u32[]{:S(2)}) collective-permute-start(bf16[4,96,768]{2,1,0:T(8,128)(2,1)S(1)} %collective-permute-done.3.refs_1_), channel_id=1, source_target_pairs={{0,1},{1,0},{2,3},{3,2},{4,5},{5,4},{6,7},{7,6},{8,9},{9,8},{10,11... | collective-permute-start | bytes 1769480 | tf_op jit(solution)/shard_map/ppermute | solution.py:638
  69.0 41.2 %collective-permute-start.8 = (bf16[4,96,768]{2,1,0:T(8,128)(2,1)}, bf16[4,96,768]{2,1,0:T(8,128)(2,1)}, u32[]{:S(2)}, u32[]{:S(2)}) collective-permute-start(bf16[4,96,768]{2,1,0:T(8,128)(2,1)} %collective-permute-done.4.refs_2_), channel_id=1, source_target_pairs={{0,1},{1,0},{2,3},{3,2},{4,5},{5,4},{6,7},{7,6},{8,9},{9,8},{10,11... | collective-permute-start | bytes 1769480 | tf_op jit(solution)/shard_map/ppermute | solution.py:638
  69.0 41.2 %collective-permute-start.9 = (bf16[4,96,768]{2,1,0:T(8,128)(2,1)}, bf16[4,96,768]{2,1,0:T(8,128)(2,1)}, u32[]{:S(2)}, u32[]{:S(2)}) collective-permute-start(bf16[4,96,768]{2,1,0:T(8,128)(2,1)} %collective-permute-done.5.refs_3_), channel_id=1, source_target_pairs={{0,1},{1,0},{2,3},{3,2},{4,5},{5,4},{6,7},{7,6},{8,9},{9,8},{10,11... | collective-permute-start | bytes 1769480 | tf_op jit(solution)/shard_map/ppermute | solution.py:638
  72.1 44.9 %collective-permute-start.10 = (bf16[64,768]{1,0:T(8,128)(2,1)S(1)}, bf16[64,768]{1,0:T(8,128)(2,1)S(1)}, u32[]{:S(2)}, u32[]{:S(2)}) collective-permute-start(bf16[64,768]{1,0:T(8,128)(2,1)S(1)} %fusion.26), channel_id=1, source_target_pairs={{0,2},{1,3},{2,4},{3,5},{4,6},{5,7},{6,0},{7,1},{8,10},{9,11},{10,... | collective-permute-start | bytes 294920 | tf_op jit(solution)/shard_map/ppermute | solution.py:638
  118.3 29.9 %collective-permute-start.13 = (bf16[4,64,768]{2,1,0:T(8,128)(2,1)S(1)}, bf16[4,64,768]{2,1,0:T(8,128)(2,1)S(1)}, u32[]{:S(2)}, u32[]{:S(2)}) collective-permute-start(bf16[4,64,768]{2,1,0:T(8,128)(2,1)S(1)} %pad_maximum_fusion.7.refs_0_), channel_id=1, source_target_pairs={{0,8},{1,9},{2,10},{3,11},{4,12},{5,13},{6,14},{7,15},{8,0},{9,1},... | collective-permute-start | bytes 1179656 | tf_op jit(solution)/shard_map/ppermute | solution.py:638
  119.6 28.6 %collective-permute-start.14 = (bf16[4,64,768]{2,1,0:T(8,128)(2,1)S(1)}, bf16[4,64,768]{2,1,0:T(8,128)(2,1)S(1)}, u32[]{:S(2)}, u32[]{:S(2)}) collective-permute-start(bf16[4,64,768]{2,1,0:T(8,128)(2,1)S(1)} %pad_maximum_fusion.7.refs_0_), channel_id=1, source_target_pairs={{0,16},{1,17},{2,18},{3,19},{4,20},{5,21},{6,22},{7,23},{8,24},{9,... | collective-permute-start | bytes 1179656 | tf_op jit(solution)/shard_map/ppermute | solution.py:638
  121.0 27.2 %collective-permute-start.15 = (bf16[4,64,768]{2,1,0:T(8,128)(2,1)S(1)}, bf16[4,64,768]{2,1,0:T(8,128)(2,1)S(1)}, u32[]{:S(2)}, u32[]{:S(2)}) collective-permute-start(bf16[4,64,768]{2,1,0:T(8,128)(2,1)S(1)} %pad_maximum_fusion.7.refs_0_), channel_id=1, source_target_pairs={{0,24},{1,25},{2,26},{3,27},{4,28},{5,29},{6,30},{7,31},{8,16},{9,... | collective-permute-start | bytes 1179656 | tf_op jit(solution)/shard_map/ppermute | solution.py:638
  207.5 47.2 %collective-permute-start.20 = (bf16[2,4,64,768]{3,2,1,0:T(8,128)(2,1)}, bf16[2,4,64,768]{3,2,1,0:T(8,128)(2,1)}, u32[]{:S(2)}, u32[]{:S(2)}) collective-permute-start(bf16[2,4,64,768]{3,2,1,0:T(8,128)(2,1)} %get-tuple-element.146), channel_id=1, source_target_pairs={{0,8},{1,9},{2,10},{3,11},{4,12},{5,13},{6,14},{7,15},{8,0},{9,1},... | collective-permute-start | bytes 2359304 | tf_op jit(solution)/shard_map/ppermute | solution.py:638
  208.7 46.0 %collective-permute-start.21 = (bf16[2,4,64,768]{3,2,1,0:T(8,128)(2,1)}, bf16[2,4,64,768]{3,2,1,0:T(8,128)(2,1)}, u32[]{:S(2)}, u32[]{:S(2)}) collective-permute-start(bf16[2,4,64,768]{3,2,1,0:T(8,128)(2,1)} %get-tuple-element.147), channel_id=1, source_target_pairs={{0,16},{1,17},{2,18},{3,19},{4,20},{5,21},{6,22},{7,23},{8,24},{9,... | collective-permute-start | bytes 2359304 | tf_op jit(solution)/shard_map/ppermute | solution.py:638
  210.1 44.6 %collective-permute-start.22 = (bf16[2,4,64,768]{3,2,1,0:T(8,128)(2,1)}, bf16[2,4,64,768]{3,2,1,0:T(8,128)(2,1)}, u32[]{:S(2)}, u32[]{:S(2)}) collective-permute-start(bf16[2,4,64,768]{3,2,1,0:T(8,128)(2,1)} %get-tuple-element.148), channel_id=1, source_target_pairs={{0,24},{1,25},{2,26},{3,27},{4,28},{5,29},{6,30},{7,31},{8,16},{9,... | collective-permute-start | bytes 2359304 | tf_op jit(solution)/shard_map/ppermute | solution.py:638
  211.0 97.3 %reduce-scatter.6.cloned.1.call-start = ((), (), s32[]{:S(2)}) async-start(), calls=%async_computation.6 | async-start | bytes 3538944 | tf_op jit(solution)/shard_map/reduce_scatter | solution.py:859
  254.8 125.0 %reduce-scatter.8.cloned.1.call-start = ((), (), s32[]{:S(2)}) async-start(), calls=%async_computation.7 | async-start | bytes 3981312 | tf_op jit(solution)/shard_map/reduce_scatter | solution.py:859
  269.4 38.9 %collective-permute-start.24 = (bf16[4,128,768]{2,1,0:T(8,128)(2,1)}, bf16[4,128,768]{2,1,0:T(8,128)(2,1)S(1)}, u32[]{:S(2)}, u32[]{:S(2)}) collective-permute-start(bf16[4,128,768]{2,1,0:T(8,128)(2,1)} %get-tuple-element.169), channel_id=1, source_target_pairs={{0,8},{1,9},{2,10},{3,11},{4,12},{5,13},{6,14},{7,15},{8,0},{9,1},... | collective-permute-start | bytes 2359304 | tf_op jit(solution)/shard_map/ppermute | solution.py:638
  270.4 37.9 %collective-permute-start.25 = (bf16[4,128,768]{2,1,0:T(8,128)(2,1)}, bf16[4,128,768]{2,1,0:T(8,128)(2,1)}, u32[]{:S(2)}, u32[]{:S(2)}) collective-permute-start(bf16[4,128,768]{2,1,0:T(8,128)(2,1)} %get-tuple-element.170), channel_id=1, source_target_pairs={{0,16},{1,17},{2,18},{3,19},{4,20},{5,21},{6,22},{7,23},{8,24},{9,... | collective-permute-start | bytes 2359304 | tf_op jit(solution)/shard_map/ppermute | solution.py:638
  271.8 36.6 %collective-permute-start.26 = (bf16[4,128,768]{2,1,0:T(8,128)(2,1)}, bf16[4,128,768]{2,1,0:T(8,128)(2,1)}, u32[]{:S(2)}, u32[]{:S(2)}) collective-permute-start(bf16[4,128,768]{2,1,0:T(8,128)(2,1)} %get-tuple-element.171), channel_id=1, source_target_pairs={{0,24},{1,25},{2,26},{3,27},{4,28},{5,29},{6,30},{7,31},{8,16},{9,... | collective-permute-start | bytes 2359304 | tf_op jit(solution)/shard_map/ppermute | solution.py:638
  328.4 44.7 %collective-permute-start.27 = (f32[2688]{0:T(1024)S(1)}, f32[2688]{0:T(1024)S(1)}, u32[]{:S(2)}, u32[]{:S(2)}) collective-permute-start(f32[2688]{0:T(1024)S(1)} %pad_maximum_fusion.12), channel_id=1, source_target_pairs={{0,8},{1,9},{2,10},{3,11},{4,12},{5,13},{6,14},{7,15},{8,0},{9,1},... | collective-permute-start | bytes 32264 | tf_op jit(solution)/shard_map/ppermute | solution.py:638
  340.8 29.5 %collective-permute-start.37 = (bf16[192,768]{1,0:T(8,128)(2,1)S(1)}, bf16[192,768]{1,0:T(8,128)(2,1)S(1)}, u32[]{:S(2)}, u32[]{:S(2)}) collective-permute-start(bf16[192,768]{1,0:T(8,128)(2,1)S(1)} %get-tuple-element.345), channel_id=1, source_target_pairs={{0,4},{1,5},{2,6},{3,7},{4,0},{5,1},{6,2},{7,3},{8,12},{9,13},{10,... | collective-permute-start | bytes 884744 | tf_op jit(solution)/shard_map/ppermute | solution.py:638
  340.8 30.5 %collective-permute-start.38 = (bf16[192,768]{1,0:T(8,128)(2,1)S(1)}, bf16[192,768]{1,0:T(8,128)(2,1)S(1)}, u32[]{:S(2)}, u32[]{:S(2)}) collective-permute-start(bf16[192,768]{1,0:T(8,128)(2,1)S(1)} %get-tuple-element.344), channel_id=1, source_target_pairs={{0,6},{1,7},{2,0},{3,1},{4,2},{5,3},{6,4},{7,5},{8,14},{9,15},{10,... | collective-permute-start | bytes 884744 | tf_op jit(solution)/shard_map/ppermute | solution.py:638
  344.4 34.4 %collective-permute-start.32 = (bf16[48,2048]{1,0:T(8,128)(2,1)S(1)}, bf16[48,2048]{1,0:T(8,128)(2,1)S(1)}, u32[]{:S(2)}, u32[]{:S(2)}) collective-permute-start(bf16[48,2048]{1,0:T(8,128)(2,1)S(1)} %fusion.18), channel_id=1, source_target_pairs={{0,8},{1,9},{2,10},{3,11},{4,12},{5,13},{6,14},{7,15},{8,0},{9,1},... | collective-permute-start | bytes 589832 | tf_op jit(solution)/shard_map/ppermute | solution.py:638
  (123 other events, 1433.6 us)
Sparse Core Ops, SparseCore 0:
  10.6 61.4 all-gather.3
  74.3 69.8 all-gather.5
  211.2 45.8 reduce-scatter.3
  259.3 41.9 reduce-scatter.5
  309.4 68.2 reduce-scatter.7

commit v9 on v8

--- a/solution.py
+++ b/solution.py
@@ -217,7 +217,7 @@
             pltpu.VMEM((2, length, length) if causal else (1, 8, PAIR), WIDE),
         ],
         cost_estimate=pl.CostEstimate(flops=int(27 * PEAK), bytes_accessed=20 << 20, transcendentals=0),
-        compiler_params=pltpu.CompilerParams(vmem_limit_bytes=36 * MEGABYTE),
+        compiler_params=pltpu.CompilerParams(vmem_limit_bytes=60 * MEGABYTE),
         name="self_forward" if causal else "cross_forward",
     )(*args)
 
@@ -342,7 +342,7 @@
             pltpu.VMEM((4, block // 4, width), LOW),
         ],
         cost_estimate=pl.CostEstimate(flops=int(46 * PEAK), bytes_accessed=40 << 20, transcendentals=0),
-        compiler_params=pltpu.CompilerParams(vmem_limit_bytes=40 * MEGABYTE),
+        compiler_params=pltpu.CompilerParams(vmem_limit_bytes=60 * MEGABYTE),
         name="feed_forward_both",
     )(lengths, where, after, out_grad, gain, w_in, w_in, w_out)
 
@@ -573,7 +573,7 @@
             *scratch,
         ],
         cost_estimate=pl.CostEstimate(flops=int(45 * PEAK), bytes_accessed=40 << 20, transcendentals=0),
-        compiler_params=pltpu.CompilerParams(vmem_limit_bytes=(36 if causal else 46) * MEGABYTE),
+        compiler_params=pltpu.CompilerParams(vmem_limit_bytes=60 * MEGABYTE),
         name="self_backward" if causal else "cross_backward",
     )(lengths, where, x, source, grad, gain, weights, weights, wave, *kept, mix, past)
 
@@ -602,7 +602,7 @@
         out_specs=[rowwise, whole((1, width))],
         out_shape=[jax.ShapeDtypeStruct((rows, width), WIDE), jax.ShapeDtypeStruct((1, width), WIDE)],
         cost_estimate=pl.CostEstimate(flops=int(8 * PEAK), bytes_accessed=12 << 20, transcendentals=0),
-        compiler_params=pltpu.CompilerParams(vmem_limit_bytes=24 * MEGABYTE),
+        compiler_params=pltpu.CompilerParams(vmem_limit_bytes=60 * MEGABYTE),
         name="input_gradient",
     )(*grads, weights, weights, weights, x, grad, gain)
 
@@ -623,7 +623,7 @@
         out_specs=rowwise,
         out_shape=jax.ShapeDtypeStruct((rows, width), WIDE),
         cost_estimate=pl.CostEstimate(flops=int(7 * PEAK), bytes_accessed=10 << 20, transcendentals=0),
-        compiler_params=pltpu.CompilerParams(vmem_limit_bytes=24 * MEGABYTE),
+        compiler_params=pltpu.CompilerParams(vmem_limit_bytes=60 * MEGABYTE),
         name="memory_gradient",
     )(grad_key, grad_value, weights, weights)
 
@@ -698,14 +698,14 @@
         out_shape=jax.ShapeDtypeStruct(shape, LOW),
         scratch_shapes=[pltpu.SemaphoreType.DMA((8 * hops,))],
         cost_estimate=pl.CostEstimate(flops=int(4 * PEAK), bytes_accessed=8 << 20, transcendentals=0),
-        compiler_params=pltpu.CompilerParams(vmem_limit_bytes=24 * MEGABYTE),
+        compiler_params=pltpu.CompilerParams(vmem_limit_bytes=60 * MEGABYTE),
         name=name,
     )(where, *parts)
 
 
-def rep_parts(parts):
+def rep_parts(parts, axis):
     rep = lax.axis_index("rep")
-    pick = lambda at: lax.dynamic_index_in_dim(parts, at, 0, keepdims=False)
+    pick = lambda at: lax.dynamic_index_in_dim(parts, at, axis, keepdims=False)
     return [pick(rep)] + [from_rep(pick(rep ^ way), way) for way in range(1, 4)]
 
 
@@ -719,8 +719,7 @@
 
 def rep_order(near):
     rep = lax.axis_index("rep")
-    near = jnp.stack(near)
-    return jnp.stack([lax.dynamic_index_in_dim(near, at ^ rep, 0, keepdims=False) for at in range(4)])
+    return [lax.select_n(rep, *[near[at ^ own] for own in range(4)]) for at in range(4)]
 
 
 def hold(*values):
@@ -739,30 +738,35 @@
     return lax.optimization_barrier((value, *earlier))[0]
 
 
-def factored_sums(gradient, weight, row_state):
+def row_moments(gradient, row_state):
     squares = gradient * gradient + TINY_TERM
-    row_moment = DECAY_RATE * row_state + (1.0 - DECAY_RATE) * jnp.mean(squares, axis=2)
-    local = jnp.concatenate(
-        [
-            jnp.sum(squares, axis=1).reshape(-1),
-            jnp.sum(row_moment, axis=1),
-            jnp.sum(weight * weight, axis=(1, 2)),
-        ]
-    )
-    return row_moment, local
-
-
-def factored_update(gradient, weight, row_moment, col_state, total):
+    return DECAY_RATE * row_state + (1.0 - DECAY_RATE) * jnp.mean(squares, axis=-1)
+
+
+def factored_sums(gradient, row_state):
+    squares = gradient * gradient + TINY_TERM
+    return jnp.sum(squares, axis=1), jnp.sum(row_moments(gradient, row_state), axis=1)
+
+
+def pack(values):
+    return jnp.concatenate([value.reshape(-1) for value in values])
+
+
+def unpack(vector, values):
+    out = []
+    for value in values:
+        out.append(vector[: value.size].reshape(value.shape))
+        vector = vector[value.size :]
+    return out
+
+
+def factored_update(gradient, weight, row_moment, col_state, col_sum, row_sum, square):
     count, rows, cols = weight.shape
     whole_rows = rows * lax.axis_size("fsdp")
-    col_sum = total[: count * cols].reshape(count, cols)
-    row_mean = total[count * cols : count * cols + count] / whole_rows
-    square = total[count * cols + count :] / (whole_rows * cols)
     col_moment = DECAY_RATE * col_state + (1.0 - DECAY_RATE) * col_sum / whole_rows
-    direction = gradient * lax.rsqrt(
-        row_moment[:, :, None] * col_moment[:, None, :] / row_mean[:, None, None]
-    )
-    step = STEP_RATE * jnp.sqrt(square + 1e-06)
+    scale = lax.rsqrt(row_moment / (row_sum[:, None] / whole_rows))
+    step = STEP_RATE * jnp.sqrt(square / (whole_rows * cols) + 1e-06)
+    direction = gradient * scale[:, :, None] * lax.rsqrt(col_moment)[:, None, :]
     return weight - step[:, None, None] * direction, col_moment
 
 
@@ -887,7 +891,7 @@
         own_self = scatter(grad_self_weights, 1)
         out_sum = add_up(out_near)
         out_pair = from_shard(out_sum[1], 1)
-        in_parts = rep_parts(jnp.stack([own_gate, own_up]).reshape(4, -1, hidden_width))
+        in_parts = rep_parts(jnp.stack([own_gate, own_up]).reshape(2, 4, -1, hidden_width), 1)
         line = jnp.concatenate([add_up(cross_near), add_up([out_sum[0], out_pair])], axis=1)
         line_parts = add_line(line)
         input_grad, gain_one = input_gradient(grads_one, w_self, dec_rows, grad_self, gain_full[0:1])
@@ -900,25 +904,54 @@
     small = jnp.concatenate(
         [gain_one.reshape(-1), gain_two.reshape(-1), gain_three.reshape(-1), table_part.reshape(-1)]
     )
+    grad_factor = 1.0 / math.sqrt(row_count * reps * shards)
+    wide = lambda value: value.astype(WIDE) * grad_factor
     each = model_width // (LINE * LINE_CORES)
+    small = small * grad_factor
+    square = lambda value: jnp.sum(value * value, axis=(1, 2))
+    squares = (
+        square(ffn_in), square(ffn_out[None]), square(cross_weight), square(self_weight),
+        jnp.sum(gains * gains, axis=1),
+    )
     if quarters:
-        small = butterfly(small, from_rep, reps)
-        in_near = rep_near(add_up(in_parts))
-        both_near = rep_near(add_up(line_parts))
-        self_parts = rep_parts(own_self.reshape(4, -1, model_width))
-        rest = hold(small, *in_near, *both_near, *self_parts)
-        small, in_near, both_near, self_parts = rest[0], rest[1:5], rest[5:9], rest[9:]
-        own_in = rep_order(in_near).reshape(ffn_in.shape)
-        both = rep_order(both_near)
-        own_cross = both[:, :each]
-        own_out = both[:, each + each // 3 :].reshape(ffn_out.shape)
-        own_self = jnp.concatenate(
-            [
-                rep_order(rep_near(add_up(self_parts))).reshape(3, *self_weight.shape[1:]),
-                both[:3, each : each + each // 3].reshape(1, *self_weight.shape[1:]),
-            ]
+        quarter_of = lambda value, axis: lax.dynamic_index_in_dim(value, rep, axis, keepdims=False)
+        third = each // 3
+        in_piece, line_piece = add_up(in_parts), add_up(line_parts)
+        in_near, line_near = rep_near(in_piece), rep_near(line_piece)
+        cross_piece, past_piece, out_piece = (
+            line_piece[:each], line_piece[each : each + third], line_piece[each + third :],
         )
-        over_shards = lambda vector: butterfly(vector, from_shard, shards)
+        in_sums = factored_sums(
+            wide(in_piece), quarter_of(in_rows.reshape(2, 4, -1), 1)
+        )
+        out_sums = factored_sums(wide(out_piece)[None], quarter_of(out_rows.reshape(4, -1), 0)[None])
+        mine = jnp.arange(4) == rep
+        cross_sums = factored_sums(wide(cross_piece)[None], quarter_of(cross_rows, 0)[None])
+        cross_sums = [
+            jnp.where(mine.reshape((4,) + (1,) * (member.ndim - 1)), member, 0.0) for member in cross_sums
+        ]
+        past_rows = lax.dynamic_slice_in_dim(self_rows[3], jnp.minimum(rep, 2) * third, third)
+        past_sums = factored_sums(wide(past_piece)[None], past_rows[None])
+        past_sums = [jnp.where(rep < 3, member, 0.0) for member in past_sums]
+        early = [*in_sums, *out_sums, *cross_sums, *past_sums, *[member / reps for member in squares], small]
+        over_all = lambda vector: butterfly(butterfly(vector, from_rep, reps), from_shard, shards)
+        in_sums, out_sums, cross_sums, past_sums, rest = (
+            lambda found: (found[0:2], found[2:4], found[4:6], found[6:8], found[8:])
+        )(unpack(over_all(pack(early)), early))
+        *squares, small = rest
+        self_parts = rep_parts(own_self.reshape(3, 4, -1, model_width), 1)
+        self_piece = add_up(self_parts)
+        self_near = rep_near(self_piece)
+        late = factored_sums(wide(self_piece), quarter_of(self_rows[:3].reshape(3, 4, -1), 1))
+        late = unpack(over_all(pack(late)), late)
+        self_sums = [jnp.concatenate(members) for members in zip(late, past_sums)]
+        line_all = rep_order(line_near)
+        own_in = jnp.stack(rep_order(in_near), axis=1).reshape(ffn_in.shape)
+        own_cross = jnp.stack([member[:each] for member in line_all])
+        own_out = jnp.concatenate([member[each + third :] for member in line_all])
+        own_self = jnp.stack(rep_order(self_near), axis=1).reshape(3, *self_weight.shape[1:])
+        own_past = jnp.concatenate([member[each : each + third] for member in line_all[:3]])
+        own_self = jnp.concatenate([own_self, own_past[None]])
     else:
         over_reps = lambda value: lax.psum(value, "rep")
         own_in = over_reps(scatter(jnp.stack([grad_gate, grad_up]), 1))
@@ -930,41 +963,49 @@
         past = packed[:3, ..., each:, :].transpose(1, 2, 0, 3, 4).reshape(1, model_width, model_width)
         own_cross = over_reps(scatter(cross_parts, 1))
         own_self = over_reps(scatter(jnp.concatenate([grad_self_weights, past]), 1))
-        over_shards = lambda vector: lax.psum(vector, "fsdp")
-        small = lax.psum(small, "rep")
-
-    grad_factor = 1.0 / math.sqrt(row_count * reps * shards)
     self_grad, cross_grad, ffn_in_grad, feedforward_output_gradient = [
-        member.astype(WIDE) * grad_factor for member in (own_self, own_cross, own_in, own_out)
+        wide(member) for member in (own_self, own_cross, own_in, own_out)
     ]
-    groups = (
-        (ffn_in_grad, ffn_in, in_rows, in_cols),
-        (feedforward_output_gradient[None], ffn_out[None], out_rows[None], out_cols[None]),
-        (cross_grad, cross_weight, cross_rows, cross_cols),
-        (self_grad, self_weight, self_rows, self_cols),
-    )
-    sums = [factored_sums(gradient, weight, row_state) for gradient, weight, row_state, _ in groups]
-    vectors = [member[1] for member in sums] + [jnp.sum(gains * gains, axis=1), small]
-    total = over_shards(jnp.concatenate(vectors))
-    totals = []
-    for vector in vectors:
-        totals.append(total[: vector.shape[0]])
-        total = total[vector.shape[0] :]
-    updated = [
-        factored_update(gradient, weight, sums[at][0], col_state, totals[at])
-        for at, (gradient, weight, _, col_state) in enumerate(groups)
+    if not quarters:
+        local = (
+            *factored_sums(ffn_in_grad, in_rows),
+            *factored_sums(feedforward_output_gradient[None], out_rows[None]),
+            *factored_sums(cross_grad, cross_rows),
+            *factored_sums(self_grad, self_rows),
+            *squares,
+        )
+        found = unpack(lax.psum(pack(local), "fsdp"), local)
+        in_sums, out_sums, cross_sums, self_sums, squares = (
+            found[0:2], found[2:4], found[4:6], found[6:8], found[8:],
+        )
+        small = lax.psum(small, ("rep", "fsdp"))
+    new_in_rows = row_moments(ffn_in_grad, in_rows)
+    new_out_rows = row_moments(feedforward_output_gradient, out_rows)
+    new_cross_rows = row_moments(cross_grad, cross_rows)
+    new_self_rows = row_moments(self_grad, self_rows)
+    new_ffn_in, new_in_cols = factored_update(
+        ffn_in_grad, ffn_in, new_in_rows, in_cols, *in_sums, squares[0]
+    )
+    new_ffn_out, new_out_cols = [
+        member[0]
+        for member in factored_update(
+            feedforward_output_gradient[None], ffn_out[None], new_out_rows[None], out_cols[None],
+            *out_sums, squares[1],
+        )
     ]
-    new_ffn_in, new_ffn_out, new_cross, new_self = [member[0] for member in updated]
-    new_in_cols, new_out_cols, new_cross_cols, new_self_cols = [member[1] for member in updated]
-    new_in_rows, new_out_rows, new_cross_rows, new_self_rows = [member[0] for member in sums]
-    new_ffn_out, new_out_rows, new_out_cols = new_ffn_out[0], new_out_rows[0], new_out_cols[0]
-    gain_square = totals[4] / model_width
-    small = totals[5] * grad_factor
+    new_cross, new_cross_cols = factored_update(
+        cross_grad, cross_weight, new_cross_rows, cross_cols, *cross_sums, squares[2]
+    )
+    new_self, new_self_cols = factored_update(
+        self_grad, self_weight, new_self_rows, self_cols, *self_sums, squares[3]
+    )
     gains_grad = lax.dynamic_slice_in_dim(
         small[: 3 * model_width].reshape(3, model_width), shard * gains.shape[1], gains.shape[1], axis=1
     )
     table_grad = small[3 * model_width :].reshape(BUCKETS, H)
-    new_gains, new_gain_moment = plain_update(gains_grad, gains, gain_moment, gain_square[:, None])
+    new_gains, new_gain_moment = plain_update(
+        gains_grad, gains, gain_moment, (squares[4] / model_width)[:, None]
+    )
     new_table, new_table_moment = plain_update(
         table_grad, table, table_moment, jnp.mean(table * table)
     )

time: 462 us -> 472 us (1.022)
  local copies, waits for them, and re-layouts: 49.7 us -> 19.6 us
  other arithmetic: 34.3 us -> 53.1 us
  Pallas kernels: 176 us -> 194 us
  starting transfers between devices: 82.2 us -> 91.2 us
  waiting for transfers between devices: 77.5 us -> 71.6 us
    unnamed x190 -> x128, local copies, waits for them, and re-layouts: 41.8 us -> 4.41 us
    ppermute x51 -> x56, starting transfers between devices: 82 us -> 91 us  [flat_permute(): return lax.ppermute(value, ('rep', 'fsdp'), pairs)]
    ppermute x51 -> x56, waiting for transfers between devices: 74.9 us -> 68.9 us  [flat_permute(): return lax.ppermute(value, ('rep', 'fsdp'), pairs)]
    pallas_call x2, Pallas kernels: 39.5 us -> 44.9 us  [attention_forward(): pl.pallas_call(functools.partial(forward_kernel, causal, seq_count), grid...]
    div x0 -> x5, other arithmetic: none -> 4.76 us  [the longest x4 4.04 us: per_device(): member / reps]
    reduce_sum x12 -> x18, other arithmetic: 11.4 us -> 16 us  [the longest x4 5.93 us: per_device(): square = lambda value: jnp.sum(value * value, axis=(1, 2))]
    convert_element_type x7 -> x5, other arithmetic: 11.2 us -> 8.79 us  [add_up(): return sum((part.astype(WIDE) for part in parts)).astype(LOW)]
  transfers between devices with their start and end apart: 56 -> 61, of which waited for: 21 -> 26; matrix products, arithmetic and copies ran while one was open for 6% -> 13% of each run, Pallas kernels for 29% -> 31%
where the time goes in v9:
time: 472 us; the launch traced here: 465 us
  Pallas kernels  194 us (41%)
  starting transfers between devices  91.2 us (19%)
  waiting for transfers between devices  71.6 us (15%)
  other arithmetic  53.1 us (11%)
  local copies, waits for them, and re-layouts  19.6 us (4%)
  between operations  18.7 us (4%)
  blocking collectives  16.7 us (4%)
    ppermute x56, starting transfers between devices, flat_permute(): return lax.ppermute(value, ('rep', 'fsdp'), pairs)  91 us
    pallas_call x2, Pallas kernels, attention_backward(): pl.pallas_call(functools.partial(backward_kernel, causal, seq_count), gri...  74.5 us
    ppermute x56, waiting for transfers between devices, flat_permute(): return lax.ppermute(value, ('rep', 'fsdp'), pairs)  68.9 us
    pallas_call x1, Pallas kernels, feed_forward_both(): pl.pallas_call(functools.partial(feed_kernel, seq_count), grid=(hidden //...  47.7 us
    pallas_call x2, Pallas kernels, attention_forward(): pl.pallas_call(functools.partial(forward_kernel, causal, seq_count), grid...  44.9 us
    all_gather x1, blocking collectives, per_device(): lax.all_gather(gains.astype(LOW), 'fsdp', axis=1, tiled=True).astype(WIDE)  16.7 us
    pallas_call x1, Pallas kernels, input_gradient(): pl.pallas_call(input_kernel, grid=(rows // block,), in_specs=[rowwise, ro...  10.1 us
    pallas_call x2, Pallas kernels, assemble(): pl.pallas_call(functools.partial(assemble_kernel, place, hops), in_specs=...  10.1 us
  transfers between devices with their start and end apart: 61, of which 26 were waited for; matrix products, arithmetic and copies ran while one was open for 13% of the time, Pallas kernels for 31%

profile of v9, /device:TPU:0, one launch (start us, length us, event | category | flops | bytes accessed | tf_op | source)
XLA Modules:
  0.0 465.0 jit_solution(12027044049257962556)
XLA Ops:
  7.3 3.2 multiply_reduce_fusion.1
  13.4 3.1 collective-permute-start
  21.0 16.7 %all-gather = bf16[8,96,3]{1,2,0:T(4,128)(2,1)S(1)} all-gather(bf16[1,96,3]{1,2,0:T(4,128)(2,1)S(1)} %get-tuple-element.391), channel_id=1, replica_groups=mesh['rep'=4,'fsdp'=8] {'fsdp'}, dimensions={0}, use_global_device_ids=true | all-gather | bytes 5184 | tf_op jit(solution)/shard_map/all_gather | solution.py:813
  46.6 9.4 %collective-permute-done.3.refs_1_ = bf16[4,96,768]{2,1,0:T(8,128)(2,1)S(1)} collective-permute-done((bf16[4,96,768]{2,1,0:T(8,128)(2,1)S(1)}, bf16[4,96,768]{2,1,0:T(8,128)(2,1)S(1)}, u32[]{:S(2)}, u32[]{:S(2)}) %collective-permute-start.3) | collective-permute-done | bytes 589856 | tf_op jit(solution)/shard_map/ppermute | solution.py:638
  56.0 13.0 %collective-permute-done.4.refs_2_ = bf16[4,96,768]{2,1,0:T(8,128)(2,1)S(1)} collective-permute-done((bf16[4,96,768]{2,1,0:T(8,128)(2,1)S(1)}, bf16[4,96,768]{2,1,0:T(8,128)(2,1)S(1)}, u32[]{:S(2)}, u32[]{:S(2)}) %collective-permute-start.4) | collective-permute-done | bytes 589856 | tf_op jit(solution)/shard_map/ppermute | solution.py:638
  72.1 9.7 %collective-permute-start.10 = (bf16[64,768]{1,0:T(8,128)(2,1)S(1)}, bf16[64,768]{1,0:T(8,128)(2,1)S(1)}, u32[]{:S(2)}, u32[]{:S(2)}) collective-permute-start(bf16[64,768]{1,0:T(8,128)(2,1)S(1)} %fusion.49), channel_id=1, source_target_pairs={{0,2},{1,3},{2,4},{3,5},{4,6},{5,7},{6,0},{7,1},{8,10},{9,11},{10,... | collective-permute-start | bytes 294920 | tf_op jit(solution)/shard_map/ppermute | solution.py:638
  82.3 22.0 %self_forward.1 = (bf16[1024,768]{1,0:T(8,128)(2,1)}, bf16[1024,768]{1,0:T(8,128)(2,1)}, bf16[1024,768]{1,0:T(8,128)(2,1)}, bf16[1024,768]{1,0:T(8,128)(2,1)}, f...) custom-call(s32[2]{0:T(128)} %length_ref.9, bf16[1024,768]{1,0:T(8,128)(2,1)} %bitcast.186, ...), custom_call_target="tpu_custom_call" | custom-call | flops 31050000384 | bytes 20971520 | tf_op jit(solution)/shard_map/self_forward/pallas_call | solution.py:188
  109.7 5.5 %assemble_cross.1.wq_ref.wk_ref.wv_ref.wo_ref = bf16[4,768,768]{2,1,0:T(8,128)(2,1)} custom-call(s32[3]{0:T(128)} %pad_add_fusion.where_ref, bf16[4,96,768]{2,1,0:T(8,128)(2,1)} %copy-done.18, bf16[4,96,768]{2,1,0:T(8,128)(2,1)} %copy-done.49, bf16[4,96,768]{2,1,0:T(8,128)(2,1)} %copy-done.50, bf16[4,96,768]{2,1,0:T(8,128)(2,1)} %copy-done.51, ...), custom_call_target="tpu_custom_call" | custom-call | flops 4600000000 | bytes 8388608 | tf_op jit(solution)/shard_map/assemble_cross/pallas_call | solution.py:694
  122.1 22.9 %cross_forward.1 = (bf16[1024,768]{1,0:T(8,128)(2,1)}, bf16[1024,768]{1,0:T(8,128)(2,1)}, bf16[1024,768]{1,0:T(8,128)(2,1)}, bf16[1024,768]{1,0:T(8,128)(2,1)}, ...) custom-call(s32[2]{0:T(128)} %length_ref.8, f32[1024,768]{1,0:T(8,128)} %get-tuple-element.104.x_ref, ...), custom_call_target="tpu_custom_call" | custom-call | flops 31050000384 | bytes 20971520 | tf_op jit(solution)/shard_map/cross_forward/pallas_call | solution.py:188
  149.5 4.6 assemble_out.1.wd_ref
  154.1 47.7 %feed_forward_both.1 = (bf16[1024,768]{1,0:T(8,128)(2,1)}, f32[1024,768]{1,0:T(8,128)}, bf16[768,2048]{1,0:T(8,128)(2,1)}, bf16[768,2048]{1,0:T(8,128)(2,1)}, bf...) custom-call(s32[2]{0:T(128)} %length_ref.9, ...), custom_call_target="tpu_custom_call" | custom-call | flops 52899999744 | bytes 41943040 | tf_op jit(solution)/shard_map/feed_forward_both/pallas_call | solution.py:314
  205.5 41.8 %cross_backward.1 = (f32[1024,768]{1,0:T(8,128)}, bf16[1024,768]{1,0:T(8,128)(2,1)}, bf16[1024,768]{1,0:T(8,128)(2,1)}, f32[1,768]{1,0:T(1,128)}, bf16[4,128,768...) custom-call(s32[2]{0:T(128)} %length_ref.8, ...), custom_call_target="tpu_custom_call" | custom-call | flops 51749998592 | bytes 41943040 | tf_op jit(solution)/shard_map/cross_backward/pallas_call | solution.py:546
  259.1 6.8 %memory_gradient.1 = f32[1024,768]{1,0:T(8,128)} custom-call(bf16[1024,768]{1,0:T(8,128)(2,1)} %get-tuple-element.136.gk_ref, bf16[1024,768]{1,0:T(8,128)(2,1)} %get-tuple-element.137.gv_ref, bf16[4,768,768]{2,1,0:T(8,128)(2,1)} %assemble_cross.1.wq_ref.wk_ref.wv_ref.wo_ref, bf16[4,768,768]{2,1,0:T(8,128)(2,1)} %assemble_cross.1.wq_ref.wk_ref.wv_ref.wo_ref), custom_call_target="tpu_custom_call" | custom-call | flops 8049999872 | bytes 10485760 | tf_op jit(solution)/shard_map/memory_gradient/pallas_call | solution.py:619
  266.0 4.0 fusion
  273.5 32.7 %self_backward.1 = (bf16[1024,768]{1,0:T(8,128)(2,1)}, bf16[1024,768]{1,0:T(8,128)(2,1)}, bf16[1024,768]{1,0:T(8,128)(2,1)}, bf16[3,768,768]{2,1,0:T(8,128)(2,1)}, f32[16,512]{1,0:T(8,128)}) custom-call(s32[2]{0:T(128)} %length_ref.9, s32[3]{0:T(128)} %pad_add_fusion.where_ref, bf16[1024,768]{1,0:T(8,128)(2,1)} %bitcast.187, ...), custom_call_target="tpu_custom_call" | custom-call | flops 51749998592 | bytes 41943040 | tf_op jit(solution)/shard_map/self_backward/pallas_call | solution.py:546
  310.1 10.1 %input_gradient.1 = (f32[1024,768]{1,0:T(8,128)}, f32[1,768]{1,0:T(1,128)}) custom-call(bf16[1024,768]{1,0:T(8,128)(2,1)} %get-tuple-element.163.gq_ref, bf16[1024,768]{1,0:T(8,128)(2,1)} %get-tuple-element.164.gk_ref, bf16[1024,768]{1,0:T(8,128)(2,1)} %get-tuple-element.165.gv_ref, ...), custom_call_target="tpu_custom_call" | custom-call | flops 9200000000 | bytes 12582912 | tf_op jit(solution)/shard_map/input_gradient/pallas_call | solution.py:598
  331.0 7.2 %collective-permute-start.34 = (bf16[192,768]{1,0:T(8,128)(2,1)S(1)}, bf16[192,768]{1,0:T(8,128)(2,1)S(1)}, u32[]{:S(2)}, u32[]{:S(2)}) collective-permute-start(bf16[192,768]{1,0:T(8,128)(2,1)S(1)} %get-tuple-element.359), channel_id=1, source_target_pairs={{0,2},{1,3},{2,4},{3,5},{4,6},{5,7},{6,0},{7,1},{8,10},{9,11},{10,... | collective-permute-start | bytes 884744 | tf_op jit(solution)/shard_map/ppermute | solution.py:638
  344.3 5.9 %collective-permute-done.34 = bf16[192,768]{1,0:T(8,128)(2,1)S(1)} collective-permute-done((bf16[192,768]{1,0:T(8,128)(2,1)S(1)}, bf16[192,768]{1,0:T(8,128)(2,1)S(1)}, u32[]{:S(2)}, u32[]{:S(2)}) %collective-permute-start.34) | collective-permute-done | bytes 294944 | tf_op jit(solution)/shard_map/ppermute | solution.py:638
  352.7 11.6 %collective-permute-done.35 = bf16[192,768]{1,0:T(8,128)(2,1)S(1)} collective-permute-done((bf16[192,768]{1,0:T(8,128)(2,1)S(1)}, bf16[192,768]{1,0:T(8,128)(2,1)S(1)}, u32[]{:S(2)}, u32[]{:S(2)}) %collective-permute-start.35) | collective-permute-done | bytes 294944 | tf_op jit(solution)/shard_map/ppermute | solution.py:638
  364.4 7.4 %collective-permute-done.36 = bf16[192,768]{1,0:T(8,128)(2,1)S(1)} collective-permute-done((bf16[192,768]{1,0:T(8,128)(2,1)S(1)}, bf16[192,768]{1,0:T(8,128)(2,1)S(1)}, u32[]{:S(2)}, u32[]{:S(2)}) %collective-permute-start.36) | collective-permute-done | bytes 294944 | tf_op jit(solution)/shard_map/ppermute | solution.py:638
  388.5 10.2 %collective-permute-start.49 = (f32[11414]{0:T(1024)S(1)}, f32[11414]{0:T(1024)S(1)}, u32[]{:S(2)}, u32[]{:S(2)}) collective-permute-start(f32[11414]{0:T(1024)S(1)} %add.296), channel_id=1, source_target_pairs={{0,2},{1,3},{2,0},{3,1},{4,6},{5,7},{6,4},{7,5},{8,10},{9,11},{10,... | collective-permute-start | bytes 136976 | tf_op jit(solution)/shard_map/ppermute | solution.py:638
  400.8 3.4 collective-permute-start.50
  415.1 3.6 fusion.6
  451.7 3.1 collective-permute-done.31
  (371 shorter events, 140.7 us)
Async XLA Ops:
  7.2 64.8 %all-gather.4.cloned.1.call-start = ((), (), s32[]{:S(2)}) async-start(), calls=%async_computation.3 | async-start | bytes 5308416 | tf_op jit(solution)/shard_map/all_gather | solution.py:812
  10.5 143.6 %all-gather.6.cloned.1.call-start = ((), (), s32[]{:S(2)}) async-start(), calls=%async_computation.4 | async-start | bytes 7077888 | tf_op jit(solution)/shard_map/all_gather | solution.py:814
  12.3 253.6 %reduce-scatter.4.cloned.1.call-start = ((), (), s32[]{:S(2)}) async-start(), calls=%async_computation.5 | async-start | bytes 3538944 | tf_op jit(solution)/shard_map/reduce_scatter | solution.py:863
  13.4 26.2 %collective-permute-start = (bf16[96,768]{1,0:T(8,128)(2,1)S(1)}, bf16[96,768]{1,0:T(8,128)(2,1)S(1)}, u32[]{:S(2)}, u32[]{:S(2)}) collective-permute-start(bf16[96,768]{1,0:T(8,128)(2,1)S(1)} %fusion.91), channel_id=1, source_target_pairs={{0,2},{1,3},{2,4},{3,5},{4,6},{5,7},{6,0},{7,1},{8,10},{9,11},{10,... | collective-permute-start | bytes 442376 | tf_op jit(solution)/shard_map/ppermute | solution.py:638
  41.0 27.9 %collective-permute-start.4 = (bf16[4,96,768]{2,1,0:T(8,128)(2,1)S(1)}, bf16[4,96,768]{2,1,0:T(8,128)(2,1)S(1)}, u32[]{:S(2)}, u32[]{:S(2)}) collective-permute-start(bf16[4,96,768]{2,1,0:T(8,128)(2,1)S(1)} %pad_maximum_fusion.refs_0_), channel_id=1, source_target_pairs={{0,16},{1,17},{2,18},{3,19},{4,20},{5,21},{6,22},{7,23},{8,24},{9,... | collective-permute-start | bytes 1769480 | tf_op jit(solution)/shard_map/ppermute | solution.py:638
  42.6 26.4 %collective-permute-start.5 = (bf16[4,96,768]{2,1,0:T(8,128)(2,1)S(1)}, bf16[4,96,768]{2,1,0:T(8,128)(2,1)S(1)}, u32[]{:S(2)}, u32[]{:S(2)}) collective-permute-start(bf16[4,96,768]{2,1,0:T(8,128)(2,1)S(1)} %pad_maximum_fusion.refs_0_), channel_id=1, source_target_pairs={{0,24},{1,25},{2,26},{3,27},{4,28},{5,29},{6,30},{7,31},{8,16},{9,... | collective-permute-start | bytes 1769480 | tf_op jit(solution)/shard_map/ppermute | solution.py:638
  46.6 57.8 %collective-permute-start.6 = (bf16[4,96,768]{2,1,0:T(8,128)(2,1)S(1)}, bf16[4,96,768]{2,1,0:T(8,128)(2,1)S(1)}, u32[]{:S(2)}, u32[]{:S(2)}) collective-permute-start(bf16[4,96,768]{2,1,0:T(8,128)(2,1)S(1)} %pad_maximum_fusion.refs_0_), channel_id=1, source_target_pairs={{0,1},{1,0},{2,3},{3,2},{4,5},{5,4},{6,7},{7,6},{8,9},{9,8},{10,11... | collective-permute-start | bytes 1769480 | tf_op jit(solution)/shard_map/ppermute | solution.py:638
  56.0 50.9 %collective-permute-start.7 = (bf16[4,96,768]{2,1,0:T(8,128)(2,1)S(1)}, bf16[4,96,768]{2,1,0:T(8,128)(2,1)}, u32[]{:S(2)}, u32[]{:S(2)}) collective-permute-start(bf16[4,96,768]{2,1,0:T(8,128)(2,1)S(1)} %collective-permute-done.3.refs_1_), channel_id=1, source_target_pairs={{0,1},{1,0},{2,3},{3,2},{4,5},{5,4},{6,7},{7,6},{8,9},{9,8},{10,11... | collective-permute-start | bytes 1769480 | tf_op jit(solution)/shard_map/ppermute | solution.py:638
  69.0 40.8 %collective-permute-start.8 = (bf16[4,96,768]{2,1,0:T(8,128)(2,1)S(1)}, bf16[4,96,768]{2,1,0:T(8,128)(2,1)}, u32[]{:S(2)}, u32[]{:S(2)}) collective-permute-start(bf16[4,96,768]{2,1,0:T(8,128)(2,1)S(1)} %collective-permute-done.4.refs_2_), channel_id=1, source_target_pairs={{0,1},{1,0},{2,3},{3,2},{4,5},{5,4},{6,7},{7,6},{8,9},{9,8},{10,11... | collective-permute-start | bytes 1769480 | tf_op jit(solution)/shard_map/ppermute | solution.py:638
  69.0 40.8 %collective-permute-start.9 = (bf16[4,96,768]{2,1,0:T(8,128)(2,1)S(1)}, bf16[4,96,768]{2,1,0:T(8,128)(2,1)}, u32[]{:S(2)}, u32[]{:S(2)}) collective-permute-start(bf16[4,96,768]{2,1,0:T(8,128)(2,1)S(1)} %collective-permute-done.5.refs_3_), channel_id=1, source_target_pairs={{0,1},{1,0},{2,3},{3,2},{4,5},{5,4},{6,7},{7,6},{8,9},{9,8},{10,11... | collective-permute-start | bytes 1769480 | tf_op jit(solution)/shard_map/ppermute | solution.py:638
  72.1 43.2 %collective-permute-start.10 = (bf16[64,768]{1,0:T(8,128)(2,1)S(1)}, bf16[64,768]{1,0:T(8,128)(2,1)S(1)}, u32[]{:S(2)}, u32[]{:S(2)}) collective-permute-start(bf16[64,768]{1,0:T(8,128)(2,1)S(1)} %fusion.49), channel_id=1, source_target_pairs={{0,2},{1,3},{2,4},{3,5},{4,6},{5,7},{6,0},{7,1},{8,10},{9,11},{10,... | collective-permute-start | bytes 294920 | tf_op jit(solution)/shard_map/ppermute | solution.py:638
  118.0 27.1 %collective-permute-start.13 = (bf16[4,64,768]{2,1,0:T(8,128)(2,1)S(1)}, bf16[4,64,768]{2,1,0:T(8,128)(2,1)S(1)}, u32[]{:S(2)}, u32[]{:S(2)}) collective-permute-start(bf16[4,64,768]{2,1,0:T(8,128)(2,1)S(1)} %pad_maximum_fusion.4.refs_0_), channel_id=1, source_target_pairs={{0,8},{1,9},{2,10},{3,11},{4,12},{5,13},{6,14},{7,15},{8,0},{9,1},... | collective-permute-start | bytes 1179656 | tf_op jit(solution)/shard_map/ppermute | solution.py:638
  201.8 45.5 %collective-permute-start.20 = (bf16[2,4,64,768]{3,2,1,0:T(8,128)(2,1)}, bf16[2,4,64,768]{3,2,1,0:T(8,128)(2,1)S(1)}, u32[]{:S(2)}, u32[]{:S(2)}) collective-permute-start(bf16[2,4,64,768]{3,2,1,0:T(8,128)(2,1)} %get-tuple-element.133), channel_id=1, source_target_pairs={{0,8},{1,9},{2,10},{3,11},{4,12},{5,13},{6,14},{7,15},{8,0},{9,1},... | collective-permute-start | bytes 2359304 | tf_op jit(solution)/shard_map/ppermute | solution.py:638
  203.3 44.0 %collective-permute-start.21 = (bf16[2,4,64,768]{3,2,1,0:T(8,128)(2,1)}, bf16[2,4,64,768]{3,2,1,0:T(8,128)(2,1)S(1)}, u32[]{:S(2)}, u32[]{:S(2)}) collective-permute-start(bf16[2,4,64,768]{3,2,1,0:T(8,128)(2,1)} %get-tuple-element.134), channel_id=1, source_target_pairs={{0,16},{1,17},{2,18},{3,19},{4,20},{5,21},{6,22},{7,23},{8,24},{9,... | collective-permute-start | bytes 2359304 | tf_op jit(solution)/shard_map/ppermute | solution.py:638
  204.7 42.7 %collective-permute-start.22 = (bf16[2,4,64,768]{3,2,1,0:T(8,128)(2,1)}, bf16[2,4,64,768]{3,2,1,0:T(8,128)(2,1)}, u32[]{:S(2)}, u32[]{:S(2)}) collective-permute-start(bf16[2,4,64,768]{3,2,1,0:T(8,128)(2,1)} %get-tuple-element.135), channel_id=1, source_target_pairs={{0,24},{1,25},{2,26},{3,27},{4,28},{5,29},{6,30},{7,31},{8,16},{9,... | collective-permute-start | bytes 2359304 | tf_op jit(solution)/shard_map/ppermute | solution.py:638
  205.4 100.8 %reduce-scatter.6.cloned.1.call-start = ((), (), s32[]{:S(2)}) async-start(), calls=%async_computation.6 | async-start | bytes 3538944 | tf_op jit(solution)/shard_map/reduce_scatter | solution.py:863
  258.0 166.1 %reduce-scatter.8.cloned.1.call-start = ((), (), s32[]{:S(2)}) async-start(), calls=%async_computation.7 | async-start | bytes 3981312 | tf_op jit(solution)/shard_map/reduce_scatter | solution.py:863
  270.0 36.2 %collective-permute-start.24 = (bf16[4,128,768]{2,1,0:T(8,128)(2,1)}, bf16[4,128,768]{2,1,0:T(8,128)(2,1)S(1)}, u32[]{:S(2)}, u32[]{:S(2)}) collective-permute-start(bf16[4,128,768]{2,1,0:T(8,128)(2,1)} %get-tuple-element.156), channel_id=1, source_target_pairs={{0,8},{1,9},{2,10},{3,11},{4,12},{5,13},{6,14},{7,15},{8,0},{9,1},... | collective-permute-start | bytes 2359304 | tf_op jit(solution)/shard_map/ppermute | solution.py:638
  271.4 36.7 %collective-permute-start.25 = (bf16[4,128,768]{2,1,0:T(8,128)(2,1)}, bf16[4,128,768]{2,1,0:T(8,128)(2,1)}, u32[]{:S(2)}, u32[]{:S(2)}) collective-permute-start(bf16[4,128,768]{2,1,0:T(8,128)(2,1)} %get-tuple-element.157), channel_id=1, source_target_pairs={{0,16},{1,17},{2,18},{3,19},{4,20},{5,21},{6,22},{7,23},{8,24},{9,... | collective-permute-start | bytes 2359304 | tf_op jit(solution)/shard_map/ppermute | solution.py:638
  272.8 35.3 %collective-permute-start.26 = (bf16[4,128,768]{2,1,0:T(8,128)(2,1)}, bf16[4,128,768]{2,1,0:T(8,128)(2,1)}, u32[]{:S(2)}, u32[]{:S(2)}) collective-permute-start(bf16[4,128,768]{2,1,0:T(8,128)(2,1)} %get-tuple-element.158), channel_id=1, source_target_pairs={{0,24},{1,25},{2,26},{3,27},{4,28},{5,29},{6,30},{7,31},{8,16},{9,... | collective-permute-start | bytes 2359304 | tf_op jit(solution)/shard_map/ppermute | solution.py:638
  338.2 33.6 %collective-permute-start.36 = (bf16[192,768]{1,0:T(8,128)(2,1)S(1)}, bf16[192,768]{1,0:T(8,128)(2,1)S(1)}, u32[]{:S(2)}, u32[]{:S(2)}) collective-permute-start(bf16[192,768]{1,0:T(8,128)(2,1)S(1)} %get-tuple-element.360), channel_id=1, source_target_pairs={{0,6},{1,7},{2,0},{3,1},{4,2},{5,3},{6,4},{7,5},{8,14},{9,15},{10,... | collective-permute-start | bytes 884744 | tf_op jit(solution)/shard_map/ppermute | solution.py:638
  342.1 43.0 %collective-permute-start.43 = (bf16[2,24,2048]{2,1,0:T(8,128)(2,1)S(1)}, bf16[2,24,2048]{2,1,0:T(8,128)(2,1)S(1)}, u32[]{:S(2)}, u32[]{:S(2)}) collective-permute-start(bf16[2,24,2048]{2,1,0:T(8,128)(2,1)S(1)} %get-tuple-element.344), channel_id=1, source_target_pairs={{0,8},{1,9},{2,10},{3,11},{4,12},{5,13},{6,14},{7,15},{8,0},{9,1},... | collective-permute-start | bytes 589832 | tf_op jit(solution)/shard_map/ppermute | solution.py:638
  343.3 41.8 %collective-permute-start.44 = (bf16[2,24,2048]{2,1,0:T(8,128)(2,1)S(1)}, bf16[2,24,2048]{2,1,0:T(8,128)(2,1)S(1)}, u32[]{:S(2)}, u32[]{:S(2)}) collective-permute-start(bf16[2,24,2048]{2,1,0:T(8,128)(2,1)S(1)} %get-tuple-element.344), channel_id=1, source_target_pairs={{0,16},{1,17},{2,18},{3,19},{4,20},{5,21},{6,22},{7,23},{8,24},{9,... | collective-permute-start | bytes 589832 | tf_op jit(solution)/shard_map/ppermute | solution.py:638
  350.2 34.9 %collective-permute-start.45 = (bf16[2,24,2048]{2,1,0:T(8,128)(2,1)S(1)}, bf16[2,24,2048]{2,1,0:T(8,128)(2,1)S(1)}, u32[]{:S(2)}, u32[]{:S(2)}) collective-permute-start(bf16[2,24,2048]{2,1,0:T(8,128)(2,1)S(1)} %get-tuple-element.344), channel_id=1, source_target_pairs={{0,24},{1,25},{2,26},{3,27},{4,28},{5,29},{6,30},{7,31},{8,16},{9,... | collective-permute-start | bytes 589832 | tf_op jit(solution)/shard_map/ppermute | solution.py:638
  (97 other events, 1539.2 us)
Sparse Core Ops, SparseCore 0:
  10.6 61.3 all-gather.3
  74.2 69.8 all-gather.5
  205.5 44.6 reduce-scatter.3
  258.1 44.8 reduce-scatter.5
  326.9 69.7 reduce-scatter.7

commit v10 on v9

--- a/solution.py
+++ b/solution.py
@@ -628,6 +628,249 @@
     )(grad_key, grad_value, weights, weights)
 
 
+LANES = 128
+IN_AT, OUT_AT, CROSS_AT, PAST_AT, SELF_AT, SMALL_AT = 0, 1, 2, 3, 4, 5
+
+
+def vector_rows(width, hidden, small):
+    one, big = width // LANES, hidden // LANES
+    starts = [0]
+    for size in (2 * big, one, 4 * one, one, 3 * one, small // LANES):
+        starts.append(starts[-1] + size)
+    return starts
+
+
+def spill(ref, at, row):
+    for part in range(row.shape[1] // LANES):
+        ref[pl.ds(at + part, 1), :] = row[:, part * LANES : (part + 1) * LANES]
+
+
+def fetch(ref, at, width):
+    return jnp.concatenate([ref[at + part : at + part + 1, :] for part in range(width // LANES)], axis=1)
+
+
+def column_sums(rows):
+    return jnp.sum(rows * rows + TINY_TERM, axis=0, keepdims=True)
+
+
+def in_kernel(factor, *refs):
+    in_refs, in_ref, sums_ref = refs[:4], refs[4], refs[5]
+    big = in_ref.shape[2] // LANES
+    for matrix in range(2):
+        piece = sum(ref[matrix].astype(WIDE) for ref in in_refs).astype(LOW)
+        in_ref[matrix] = piece
+        spill(sums_ref, matrix * big, column_sums(piece.astype(WIDE) * factor))
+
+
+def gated_sums(factor, in_parts):
+    shape = in_parts[0].shape
+    return pl.pallas_call(
+        functools.partial(in_kernel, factor),
+        in_specs=[pl.BlockSpec(memory_space=pltpu.VMEM)] * 4,
+        out_specs=[pl.BlockSpec(memory_space=pltpu.VMEM)] * 2,
+        out_shape=[
+            jax.ShapeDtypeStruct(shape, LOW),
+            jax.ShapeDtypeStruct((2 * shape[2] // LANES, LANES), WIDE),
+        ],
+        cost_estimate=pl.CostEstimate(flops=int(2 * PEAK), bytes_accessed=2 << 20, transcendentals=0),
+        compiler_params=pltpu.CompilerParams(vmem_limit_bytes=60 * MEGABYTE),
+        name="gated_sums",
+    )(*in_parts)
+
+
+def early_kernel(factor, starts, where_ref, *refs):
+    line_refs, sums_ref, constant_ref, line_ref, vector_ref = refs[0:4], *refs[4:]
+    rep = where_ref[0]
+    one = line_ref.shape[1] // LANES
+    each = line_ref.shape[0] // 2
+    third = each // 3
+    line = sum(ref[...].astype(WIDE) for ref in line_refs).astype(LOW)
+    line_ref[...] = line
+    vector_ref[...] = jnp.zeros_like(vector_ref)
+    vector_ref[starts[IN_AT] : starts[OUT_AT], :] = sums_ref[...]
+    line = line.astype(WIDE) * factor
+    spill(vector_ref, starts[OUT_AT], column_sums(line[each + third :]))
+    spill(vector_ref, starts[CROSS_AT] + rep * one, column_sums(line[:each]))
+    past = column_sums(line[each : each + third])
+    spill(vector_ref, starts[PAST_AT], past * (rep < 3).astype(WIDE))
+    vector_ref[starts[-1] : starts[-1] + 1, :] = constant_ref[...]
+
+
+def early_sums(factor, starts, where, line_parts, sums, constants):
+    rows = -(-(starts[-1] + 1) // 8) * 8
+    return pl.pallas_call(
+        functools.partial(early_kernel, factor, starts),
+        in_specs=[pl.BlockSpec(memory_space=pltpu.SMEM)] + [pl.BlockSpec(memory_space=pltpu.VMEM)] * 6,
+        out_specs=[pl.BlockSpec(memory_space=pltpu.VMEM)] * 2,
+        out_shape=[
+            jax.ShapeDtypeStruct(line_parts[0].shape, LOW),
+            jax.ShapeDtypeStruct((rows, LANES), WIDE),
+        ],
+        cost_estimate=pl.CostEstimate(flops=int(2 * PEAK), bytes_accessed=2 << 20, transcendentals=0),
+        compiler_params=pltpu.CompilerParams(vmem_limit_bytes=60 * MEGABYTE),
+        name="early_sums",
+    )(where, *line_parts, sums, constants)
+
+
+def late_kernel(factor, starts, *refs):
+    part_refs, small_ref, early_ref, piece_ref, vector_ref = refs[0:4], refs[4], refs[5], refs[6], refs[7]
+    vector_ref[...] = early_ref[...]
+    one = piece_ref.shape[2] // LANES
+    for matrix in range(3):
+        piece = sum(ref[matrix].astype(WIDE) for ref in part_refs).astype(LOW)
+        piece_ref[matrix] = piece
+        spill(vector_ref, starts[SELF_AT] + matrix * one, column_sums(piece.astype(WIDE) * factor))
+    vector_ref[starts[SMALL_AT] : starts[SMALL_AT + 1], :] = small_ref[...]
+
+
+def late_sums(factor, starts, self_parts, small, early):
+    return pl.pallas_call(
+        functools.partial(late_kernel, factor, starts),
+        in_specs=[pl.BlockSpec(memory_space=pltpu.VMEM)] * 6,
+        out_specs=[pl.BlockSpec(memory_space=pltpu.VMEM)] * 2,
+        out_shape=[
+            jax.ShapeDtypeStruct(self_parts[0].shape, LOW),
+            jax.ShapeDtypeStruct(early.shape, WIDE),
+        ],
+        cost_estimate=pl.CostEstimate(flops=int(2 * PEAK), bytes_accessed=1 << 20, transcendentals=0),
+        compiler_params=pltpu.CompilerParams(vmem_limit_bytes=60 * MEGABYTE),
+        name="late_sums",
+    )(*self_parts, small, early)
+
+
+def to_column(row):
+    size = row.shape[1]
+    same = lax.broadcasted_iota(jnp.int32, (size, size), 0) == lax.broadcasted_iota(jnp.int32, (size, size), 1)
+    return jnp.sum(jnp.where(same, jnp.broadcast_to(row, (size, size)), 0.0), axis=1, keepdims=True)
+
+
+def to_row(column):
+    size = column.shape[0]
+    same = lax.broadcasted_iota(jnp.int32, (size, size), 0) == lax.broadcasted_iota(jnp.int32, (size, size), 1)
+    return jnp.sum(jnp.where(same, jnp.broadcast_to(column, (size, size)), 0.0), axis=0, keepdims=True)
+
+
+def update_kernel(factor, starts, shards, where_ref, total_ref, *refs):
+    in_near, line_near, self_near = refs[0:4], refs[4:8], refs[8:12]
+    (
+        in_ref, out_ref, cross_ref, self_ref, in_rows_ref, out_rows_ref, cross_rows_ref, self_rows_ref,
+        in_cols_ref, out_cols_ref, cross_cols_ref, self_cols_ref,
+    ) = refs[12:24]
+    (
+        in_grad, out_grad, cross_grad, self_grad, new_in, new_out, new_cross, new_self,
+        new_in_rows, new_out_rows, new_cross_rows, new_self_rows,
+        new_in_cols, new_out_cols, new_cross_cols, new_self_cols,
+        gains_grad, table_grad, new_gains, new_table, new_gain_moment, new_table_moment,
+    ) = refs[28:50]
+    gains_ref, table_ref, gain_moment_ref, table_moment_ref = refs[24:28]
+    in_held, line_held, self_held = refs[50:]
+    rep = where_ref[0]
+    for way in range(4):
+        in_held[rep ^ way] = in_near[way][...]
+        line_held[rep ^ way] = line_near[way][...]
+        self_held[rep ^ way] = self_near[way][...]
+    width = cross_ref.shape[2]
+    one, big = width // LANES, in_ref.shape[2] // LANES
+    each = cross_ref.shape[1]
+    third = each // 3
+    scalars = total_ref[starts[-1] : starts[-1] + 1, :]
+
+    def step(at, pieces, index, weight, grad, new, rows_ref, new_rows, cols_ref, new_cols, row_at, scalar):
+        rows, cols = weight.shape[-2:]
+        spans = []
+        start = 0
+        for piece in pieces:
+            spans.append(slice(start, start + piece.shape[0]))
+            start += piece.shape[0]
+        whole_rows = rows * shards
+        col_sum = fetch(total_ref, at, cols)
+        state_sum = scalars[:, scalar : scalar + 1]
+        square = scalars[:, 16 + scalar : 17 + scalar]
+        col_moment = DECAY_RATE * cols_ref[row_at : row_at + 1, :] + (1.0 - DECAY_RATE) * col_sum / whole_rows
+        new_cols[row_at : row_at + 1, :] = col_moment
+        row_mean = (
+            DECAY_RATE * state_sum
+            + (1.0 - DECAY_RATE) / cols * jnp.sum(col_sum, axis=1, keepdims=True)
+        ) / whole_rows
+        blocks = [piece.astype(WIDE) * factor for piece in pieces]
+        means = jnp.concatenate(
+            [jnp.mean(block * block + TINY_TERM, axis=1, keepdims=True) for block in blocks], axis=0
+        )
+        row_moment = DECAY_RATE * to_column(rows_ref[row_at : row_at + 1, :]) + (1.0 - DECAY_RATE) * means
+        new_rows[row_at : row_at + 1, :] = to_row(row_moment)
+        size = STEP_RATE * jnp.sqrt(square / (whole_rows * cols) + 1e-06)
+        scale = size * lax.rsqrt(row_moment / row_mean)
+        across = lax.rsqrt(col_moment)
+        for block, span in zip(blocks, spans):
+            place = (span, slice(None)) if index is None else (index, span, slice(None))
+            grad[place] = block
+            new[place] = weight[place] - scale[span] * block * across
+
+    def plain(grad, ref, moment_ref, square, out, new, new_moment, spot):
+        moment = DECAY_RATE * moment_ref[spot] + (1.0 - DECAY_RATE) * (grad * grad + TINY_TERM)
+        out[spot] = grad
+        new_moment[spot] = moment
+        new[spot] = ref[spot] - STEP_RATE * jnp.sqrt(square + 1e-06) * grad * lax.rsqrt(moment)
+
+    part = gains_ref.shape[1]
+    for norm in range(3):
+        row = fetch(total_ref, starts[SMALL_AT] + norm * one, width)
+        mine = where_ref[1] * LINE_CORES + where_ref[2]
+        row = pltpu.roll(jnp.broadcast_to(row, (8, width)), lax.rem(width - mine * part, width), 1)
+        plain(
+            row[0:1, :part], gains_ref, gain_moment_ref, scalars[:, 27 + norm : 28 + norm] / width,
+            gains_grad, new_gains, new_gain_moment, (slice(norm, norm + 1), slice(None)),
+        )
+    table = total_ref[starts[SMALL_AT] + 3 * one : starts[SMALL_AT + 1], 0 : table_ref.shape[1]]
+    square = jnp.sum(jnp.sum(table_ref[...] * table_ref[...], axis=1, keepdims=True), axis=0, keepdims=True)
+    plain(
+        table, table_ref, table_moment_ref, square / (table_ref.shape[0] * table_ref.shape[1]),
+        table_grad, new_table, new_table_moment, (slice(None), slice(None)),
+    )
+    quarters = range(4)
+    for matrix in range(2):
+        step(
+            starts[IN_AT] + matrix * big, [in_held[at, matrix] for at in quarters], matrix,
+            in_ref, in_grad, new_in, in_rows_ref, new_in_rows, in_cols_ref, new_in_cols, matrix, matrix,
+        )
+    step(
+        starts[OUT_AT], [line_held[at, each + third :, :] for at in quarters], None,
+        out_ref, out_grad, new_out, out_rows_ref, new_out_rows, out_cols_ref, new_out_cols, 0, 2,
+    )
+    for matrix in range(4):
+        step(
+            starts[CROSS_AT] + matrix * one, [line_held[matrix, 0:each, :]], matrix,
+            cross_ref, cross_grad, new_cross, cross_rows_ref, new_cross_rows, cross_cols_ref, new_cross_cols,
+            matrix, 3 + matrix,
+        )
+        if matrix < 3:
+            at, pieces = starts[SELF_AT] + matrix * one, [self_held[at, matrix] for at in quarters]
+        else:
+            at, pieces = starts[PAST_AT], [line_held[at, each : each + third, :] for at in range(3)]
+        step(
+            at, pieces, matrix, self_ref, self_grad, new_self, self_rows_ref, new_self_rows,
+            self_cols_ref, new_self_cols, matrix, 7 + matrix,
+        )
+
+
+def update_all(
+    factor, starts, shards, where, total, in_near, line_near, self_near, weights, rows, cols, plain
+):
+    outs = (*weights, *weights, *rows, *cols, *plain[:2], *plain[:2], *plain[2:])
+    out_shape = [jax.ShapeDtypeStruct(value.shape, WIDE) for value in outs]
+    spec = pl.BlockSpec(memory_space=pltpu.VMEM)
+    return pl.pallas_call(
+        functools.partial(update_kernel, factor, starts, shards),
+        in_specs=[pl.BlockSpec(memory_space=pltpu.SMEM)] + [spec] * 29,
+        out_specs=[spec] * 22,
+        out_shape=out_shape,
+        scratch_shapes=[pltpu.VMEM((4, *near[0].shape), LOW) for near in (in_near, line_near, self_near)],
+        cost_estimate=pl.CostEstimate(flops=int(8 * PEAK), bytes_accessed=16 << 20, transcendentals=0),
+        compiler_params=pltpu.CompilerParams(vmem_limit_bytes=60 * MEGABYTE),
+        name="update_all",
+    )(where, total, *in_near, *line_near, *self_near, *weights, *rows, *cols, *plain)
+
+
 def flat_permute(value, target):
     reps, shards = lax.axis_size("rep"), lax.axis_size("fsdp")
     pairs = []
@@ -648,12 +891,11 @@
 
 def from_line(value, hops):
     shards = lax.axis_size("fsdp")
-    return flat_permute(value, lambda rep, shard: (rep, (shard + 2 * hops) % shards))
+    return flat_permute(value, lambda rep, shard: (rep, (shard + LINE_CORES * hops) % shards))
 
 
 def along_line(piece):
-    hops = lax.axis_size("fsdp") // 2
-    return jnp.stack([piece] + [from_line(piece, hop) for hop in range(1, hops)])
+    return jnp.stack([piece] + [from_line(piece, hop) for hop in range(1, LINE)])
 
 
 def across_reps(line):
@@ -675,7 +917,7 @@
     for other in range(2):
         for way in range(4):
             for hop in range(hops):
-                shard = lax.rem(line - hop + hops, hops) * 2 + (core ^ other)
+                shard = lax.rem(line - hop + hops, hops) * LINE_CORES + (core ^ other)
                 copies.append(
                     pltpu.make_async_copy(
                         parts[4 * other + way].at[hop],
@@ -808,10 +1050,34 @@
     rep, shard = lax.axis_index("rep"), lax.axis_index("fsdp")
     quarters = reps == 4 and shards == 8
     part_rows = hidden_width // shards
+    grad_factor = 1.0 / math.sqrt(row_count * reps * shards)
     where = jnp.stack([rep, shard // 2, shard % 2]).astype(jnp.int32) * int(quarters)
     w_self = lax.all_gather(self_weight.astype(LOW), "fsdp", axis=1, tiled=True)
     gain_full = lax.all_gather(gains.astype(LOW), "fsdp", axis=1, tiled=True).astype(WIDE)
     w_in = lax.all_gather(ffn_in.astype(LOW), "fsdp", axis=1, tiled=True)
+
+    each = model_width // (LINE * LINE_CORES)
+    if quarters:
+        out_each = part_rows // 4
+        cross_quarter = lax.dynamic_index_in_dim(cross_weight, rep, 0, keepdims=False).astype(LOW)
+        out_quarter = lax.dynamic_index_in_dim(
+            ffn_out.reshape(4, out_each, model_width), rep, 0, keepdims=False
+        ).astype(LOW)
+        cross_pieces = with_partner(across_reps(along_line(cross_quarter)))
+    square = lambda value: jnp.sum(value * value, axis=(1, 2))
+    squares = (
+        square(ffn_in), square(ffn_out[None]), square(cross_weight), square(self_weight),
+        jnp.sum(gains * gains, axis=1),
+    )
+    if quarters:
+        state_sums = (
+            jnp.sum(in_rows, axis=1), jnp.sum(out_rows)[None], jnp.sum(cross_rows, axis=1),
+            jnp.sum(self_rows, axis=1),
+        )
+        blank = jnp.zeros((5,), WIDE)
+        constants = pack([*state_sums, blank, *squares]) / reps
+        constants = jnp.pad(constants, (0, LANES - constants.size)).reshape(1, LANES)
+        gain_full, constants = hold(gain_full, constants)
 
     bucket_mask = (buckets[None, :] == jnp.arange(BUCKETS)[:, None]).astype(WIDE)
     by_distance = jnp.sum(table.T[:, :, None] * bucket_mask[None], axis=1)
@@ -827,17 +1093,11 @@
         True, dec_rows, no_source, dec_len, gain_full[0:1], w_self, backwards
     )
     if quarters:
-        cross_quarter = lax.dynamic_index_in_dim(cross_weight, rep, 0, keepdims=False).astype(LOW)
-        out_quarter = lax.dynamic_index_in_dim(
-            ffn_out.reshape(4, part_rows // 4, model_width), rep, 0, keepdims=False
-        ).astype(LOW)
-        cross_rows_each, out_rows_each = cross_weight.shape[1], part_rows // 4
-        cross_pieces = with_partner(across_reps(along_line(cross_quarter)))
         w_cross = assemble(
             hold(*cross_pieces, after_self)[:-1],
             where,
             (4, model_width, model_width),
-            lambda ref, quarter, at: ref.at[quarter, pl.ds(at * cross_rows_each, cross_rows_each)],
+            lambda ref, quarter, at: ref.at[quarter, pl.ds(at * each, each)],
             "assemble_cross",
         )
         out_line = along_line(after(out_quarter, w_self))
@@ -849,12 +1109,12 @@
         False, after_self, mem_rows, enc_len, gain_full[1:2], w_cross, no_bias
     )
     if quarters:
-        out_near = list(hold(*out_near, after_cross)[:-1])
+        out_near = hold(*out_near, after_cross)[:-1]
         w_out = assemble(
-            with_partner(out_near),
+            with_partner(list(out_near)),
             where,
             (hidden_width, model_width),
-            lambda ref, quarter, at: ref.at[pl.ds((at * 4 + quarter) * out_rows_each, out_rows_each)],
+            lambda ref, quarter, at: ref.at[pl.ds((at * 4 + quarter) * out_each, out_each)],
             "assemble_out",
         )
     layer_out, grad_cross, grad_gate, grad_up, *out_near, gain_three = feed_forward_both(
@@ -893,65 +1153,48 @@
         out_pair = from_shard(out_sum[1], 1)
         in_parts = rep_parts(jnp.stack([own_gate, own_up]).reshape(2, 4, -1, hidden_width), 1)
         line = jnp.concatenate([add_up(cross_near), add_up([out_sum[0], out_pair])], axis=1)
-        line_parts = add_line(line)
+        in_piece, in_columns = gated_sums(grad_factor, in_parts)
+        in_near = rep_near(in_piece)
+        *line_parts, gate = hold(*add_line(line), grads_one[0])
+        grads_one = [gate, *grads_one[1:]]
         input_grad, gain_one = input_gradient(grads_one, w_self, dec_rows, grad_self, gain_full[0:1])
     else:
         input_grad, gain_one = input_gradient(grads_one, w_self, dec_rows, grad_self, gain_full[0:1])
     layer_out = layer_out.reshape(dec_in.shape)
     input_grad = input_grad.reshape(dec_in.shape)
     memory_grad = memory_grad.reshape(memory.shape)
-    table_part = jnp.sum(bucket_mask[:, None, :] * dist_grad[None, :H, :], axis=2)
-    small = jnp.concatenate(
-        [gain_one.reshape(-1), gain_two.reshape(-1), gain_three.reshape(-1), table_part.reshape(-1)]
-    )
-    grad_factor = 1.0 / math.sqrt(row_count * reps * shards)
+    table_part = jnp.sum(dist_grad[:H, None, :] * bucket_mask[None], axis=2)
     wide = lambda value: value.astype(WIDE) * grad_factor
-    each = model_width // (LINE * LINE_CORES)
-    small = small * grad_factor
-    square = lambda value: jnp.sum(value * value, axis=(1, 2))
-    squares = (
-        square(ffn_in), square(ffn_out[None]), square(cross_weight), square(self_weight),
-        jnp.sum(gains * gains, axis=1),
-    )
+    gain_parts = jnp.concatenate([gain_one, gain_two, gain_three]) * grad_factor
+    table_part = table_part * grad_factor
     if quarters:
-        quarter_of = lambda value, axis: lax.dynamic_index_in_dim(value, rep, axis, keepdims=False)
-        third = each // 3
-        in_piece, line_piece = add_up(in_parts), add_up(line_parts)
-        in_near, line_near = rep_near(in_piece), rep_near(line_piece)
-        cross_piece, past_piece, out_piece = (
-            line_piece[:each], line_piece[each : each + third], line_piece[each + third :],
-        )
-        in_sums = factored_sums(
-            wide(in_piece), quarter_of(in_rows.reshape(2, 4, -1), 1)
-        )
-        out_sums = factored_sums(wide(out_piece)[None], quarter_of(out_rows.reshape(4, -1), 0)[None])
-        mine = jnp.arange(4) == rep
-        cross_sums = factored_sums(wide(cross_piece)[None], quarter_of(cross_rows, 0)[None])
-        cross_sums = [
-            jnp.where(mine.reshape((4,) + (1,) * (member.ndim - 1)), member, 0.0) for member in cross_sums
-        ]
-        past_rows = lax.dynamic_slice_in_dim(self_rows[3], jnp.minimum(rep, 2) * third, third)
-        past_sums = factored_sums(wide(past_piece)[None], past_rows[None])
-        past_sums = [jnp.where(rep < 3, member, 0.0) for member in past_sums]
-        early = [*in_sums, *out_sums, *cross_sums, *past_sums, *[member / reps for member in squares], small]
-        over_all = lambda vector: butterfly(butterfly(vector, from_rep, reps), from_shard, shards)
-        in_sums, out_sums, cross_sums, past_sums, rest = (
-            lambda found: (found[0:2], found[2:4], found[4:6], found[6:8], found[8:])
-        )(unpack(over_all(pack(early)), early))
-        *squares, small = rest
+        starts = vector_rows(model_width, hidden_width, 3 * model_width + H * LANES)
+        small = jnp.concatenate(
+            [gain_parts.reshape(-1, LANES), jnp.pad(table_part, ((0, 0), (0, LANES - BUCKETS)))]
+        )
+        line_piece, early = early_sums(grad_factor, starts, where, line_parts, in_columns, constants)
+        line_near = rep_near(line_piece)
+        own_self, early, *near = hold(own_self, early, *in_near, *line_near[:3])
+        in_near, line_near = near[:4], near[4:] + line_near[3:]
         self_parts = rep_parts(own_self.reshape(3, 4, -1, model_width), 1)
-        self_piece = add_up(self_parts)
-        self_near = rep_near(self_piece)
-        late = factored_sums(wide(self_piece), quarter_of(self_rows[:3].reshape(3, 4, -1), 1))
-        late = unpack(over_all(pack(late)), late)
-        self_sums = [jnp.concatenate(members) for members in zip(late, past_sums)]
-        line_all = rep_order(line_near)
-        own_in = jnp.stack(rep_order(in_near), axis=1).reshape(ffn_in.shape)
-        own_cross = jnp.stack([member[:each] for member in line_all])
-        own_out = jnp.concatenate([member[each + third :] for member in line_all])
-        own_self = jnp.stack(rep_order(self_near), axis=1).reshape(3, *self_weight.shape[1:])
-        own_past = jnp.concatenate([member[each : each + third] for member in line_all[:3]])
-        own_self = jnp.concatenate([own_self, own_past[None]])
+        self_piece, vector = late_sums(grad_factor, starts, self_parts, small, early)
+        vector, *self_near = hold(butterfly(vector, from_rep, reps), *rep_near(self_piece))
+        total = butterfly(vector, from_shard, shards)
+        (
+            ffn_in_grad, feedforward_output_gradient, cross_grad, self_grad,
+            new_ffn_in, new_ffn_out, new_cross, new_self,
+            new_in_rows, new_out_rows, new_cross_rows, new_self_rows,
+            new_in_cols, new_out_cols, new_cross_cols, new_self_cols,
+            gains_grad, table_grad, new_gains, new_table, new_gain_moment, new_table_moment,
+        ) = update_all(
+            grad_factor, starts, shards, where, total, in_near, line_near, self_near,
+            (ffn_in, ffn_out, cross_weight, self_weight),
+            (in_rows, out_rows[None], cross_rows, self_rows),
+            (in_cols, out_cols[None], cross_cols, self_cols),
+            (gains, table.T, gain_moment, table_moment.T),
+        )
+        table_grad, new_table, new_table_moment = table_grad.T, new_table.T, new_table_moment.T
+        new_out_rows, new_out_cols = new_out_rows.reshape(-1), new_out_cols.reshape(-1)
     else:
         over_reps = lambda value: lax.psum(value, "rep")
         own_in = over_reps(scatter(jnp.stack([grad_gate, grad_up]), 1))
@@ -963,10 +1206,9 @@
         past = packed[:3, ..., each:, :].transpose(1, 2, 0, 3, 4).reshape(1, model_width, model_width)
         own_cross = over_reps(scatter(cross_parts, 1))
         own_self = over_reps(scatter(jnp.concatenate([grad_self_weights, past]), 1))
-    self_grad, cross_grad, ffn_in_grad, feedforward_output_gradient = [
-        wide(member) for member in (own_self, own_cross, own_in, own_out)
-    ]
-    if not quarters:
+        self_grad, cross_grad, ffn_in_grad, feedforward_output_gradient = [
+            wide(member) for member in (own_self, own_cross, own_in, own_out)
+        ]
         local = (
             *factored_sums(ffn_in_grad, in_rows),
             *factored_sums(feedforward_output_gradient[None], out_rows[None]),
@@ -978,37 +1220,34 @@
         in_sums, out_sums, cross_sums, self_sums, squares = (
             found[0:2], found[2:4], found[4:6], found[6:8], found[8:],
         )
-        small = lax.psum(small, ("rep", "fsdp"))
-    new_in_rows = row_moments(ffn_in_grad, in_rows)
-    new_out_rows = row_moments(feedforward_output_gradient, out_rows)
-    new_cross_rows = row_moments(cross_grad, cross_rows)
-    new_self_rows = row_moments(self_grad, self_rows)
-    new_ffn_in, new_in_cols = factored_update(
-        ffn_in_grad, ffn_in, new_in_rows, in_cols, *in_sums, squares[0]
-    )
-    new_ffn_out, new_out_cols = [
-        member[0]
-        for member in factored_update(
-            feedforward_output_gradient[None], ffn_out[None], new_out_rows[None], out_cols[None],
-            *out_sums, squares[1],
-        )
-    ]
-    new_cross, new_cross_cols = factored_update(
-        cross_grad, cross_weight, new_cross_rows, cross_cols, *cross_sums, squares[2]
-    )
-    new_self, new_self_cols = factored_update(
-        self_grad, self_weight, new_self_rows, self_cols, *self_sums, squares[3]
-    )
-    gains_grad = lax.dynamic_slice_in_dim(
-        small[: 3 * model_width].reshape(3, model_width), shard * gains.shape[1], gains.shape[1], axis=1
-    )
-    table_grad = small[3 * model_width :].reshape(BUCKETS, H)
-    new_gains, new_gain_moment = plain_update(
-        gains_grad, gains, gain_moment, (squares[4] / model_width)[:, None]
-    )
-    new_table, new_table_moment = plain_update(
-        table_grad, table, table_moment, jnp.mean(table * table)
-    )
+        gain_total, table_grad = lax.psum((gain_parts, table_part.T), ("rep", "fsdp"))
+        gains_grad = lax.dynamic_slice_in_dim(gain_total, shard * gains.shape[1], gains.shape[1], axis=1)
+        new_gains, new_gain_moment = plain_update(
+            gains_grad, gains, gain_moment, (squares[4] / model_width)[:, None]
+        )
+        new_table, new_table_moment = plain_update(
+            table_grad, table, table_moment, jnp.mean(table * table)
+        )
+        new_in_rows = row_moments(ffn_in_grad, in_rows)
+        new_out_rows = row_moments(feedforward_output_gradient, out_rows)
+        new_cross_rows = row_moments(cross_grad, cross_rows)
+        new_self_rows = row_moments(self_grad, self_rows)
+        new_ffn_in, new_in_cols = factored_update(
+            ffn_in_grad, ffn_in, new_in_rows, in_cols, *in_sums, squares[0]
+        )
+        new_ffn_out, new_out_cols = [
+            member[0]
+            for member in factored_update(
+                feedforward_output_gradient[None], ffn_out[None], new_out_rows[None], out_cols[None],
+                *out_sums, squares[1],
+            )
+        ]
+        new_cross, new_cross_cols = factored_update(
+            cross_grad, cross_weight, new_cross_rows, cross_cols, *cross_sums, squares[2]
+        )
+        new_self, new_self_cols = factored_update(
+            self_grad, self_weight, new_self_rows, self_cols, *self_sums, squares[3]
+        )
     return (
         layer_out,
         input_grad,

time: 472 us -> 436 us (0.924)
  other arithmetic: 53.1 us -> 20.2 us
  starting transfers between devices: 91.2 us -> 73.1 us
  Pallas kernels: 194 us -> 209 us
  waiting for transfers between devices: 71.6 us -> 83.7 us
  blocking collectives: 16.7 us -> 11.1 us
    ppermute x56 -> x51, starting transfers between devices: 91 us -> 72.9 us  [flat_permute(): return lax.ppermute(value, ('rep', 'fsdp'), pairs)]
    pallas_call x0 -> x4, Pallas kernels: none -> 15 us  [the longest x1 8.83 us: update_all(): pl.pallas_call(functools.partial(update_kernel, factor, starts, shards),...]
    sub x5 -> x0, other arithmetic: 8.56 us -> none  [the longest x4 7.21 us: factored_update(): return (weight - step[:, None, None] * direction, col_moment)]
    reduce_sum x16 -> x5, other arithmetic: 10.8 us -> 2.45 us  [the longest x1 1.29 us: per_device(): jnp.sum(out_rows)[None]]
    reduce_scatter x3, waiting for transfers between devices: 0.03 us -> 6.55 us  [per_device(): lax.psum_scatter(value, 'fsdp', scatter_dimension=at, tiled=True)]
    unnamed x128 -> x130, local copies, waits for them, and re-layouts: 4.41 us -> 10.1 us
    all_gather x1, blocking collectives: 16.7 us -> 11.1 us  [per_device(): lax.all_gather(gains.astype(LOW), 'fsdp', axis=1, tiled=True).astype(WIDE)]
    reduce_sum x4 -> x2, other arithmetic: 5.93 us -> 1.01 us  [per_device(): square = lambda value: jnp.sum(value * value, axis=(1, 2))]
  transfers between devices with their start and end apart: 61 -> 56, of which waited for: 26 -> 21; matrix products, arithmetic and copies ran while one was open for 13% -> 5% of each run, Pallas kernels for 31% -> 35%
where the time goes in v10:
time: 436 us; the launch traced here: 429 us
  Pallas kernels  209 us (48%)
  waiting for transfers between devices  83.7 us (19%)
  starting transfers between devices  73.1 us (17%)
  other arithmetic  20.2 us (5%)
  local copies, waits for them, and re-layouts  16.9 us (4%)
  between operations  15.1 us (3%)
  blocking collectives  11.1 us (3%)
    pallas_call x2, Pallas kernels, attention_backward(): pl.pallas_call(functools.partial(backward_kernel, causal, seq_count), gri...  74.5 us
    ppermute x51, waiting for transfers between devices, flat_permute(): return lax.ppermute(value, ('rep', 'fsdp'), pairs)  73.2 us
    ppermute x51, starting transfers between devices, flat_permute(): return lax.ppermute(value, ('rep', 'fsdp'), pairs)  72.9 us
    pallas_call x1, Pallas kernels, feed_forward_both(): pl.pallas_call(functools.partial(feed_kernel, seq_count), grid=(hidden //...  47.7 us
    pallas_call x2, Pallas kernels, attention_forward(): pl.pallas_call(functools.partial(forward_kernel, causal, seq_count), grid...  45.3 us
    all_gather x1, blocking collectives, per_device(): lax.all_gather(gains.astype(LOW), 'fsdp', axis=1, tiled=True).astype(WIDE)  11.1 us
    unnamed x130, local copies, waits for them, and re-layouts  10.1 us
    pallas_call x2, Pallas kernels, assemble(): pl.pallas_call(functools.partial(assemble_kernel, place, hops), in_specs=...  9.99 us
  transfers between devices with their start and end apart: 56, of which 21 were waited for; matrix products, arithmetic and copies ran while one was open for 5% of the time, Pallas kernels for 35%

profile of v10, /device:TPU:0, one launch (start us, length us, event | category | flops | bytes accessed | tf_op | source)
XLA Modules:
  0.0 429.2 jit_solution(18278350241902723284)
XLA Ops:
  7.3 3.2 fusion.23
  23.8 11.1 %all-gather = bf16[8,96,3]{1,2,0:T(4,128)(2,1)S(1)} all-gather(bf16[1,96,3]{1,2,0:T(4,128)(2,1)S(1)} %get-tuple-element.305), channel_id=1, replica_groups=mesh['rep'=4,'fsdp'=8] {'fsdp'}, dimensions={0}, use_global_device_ids=true | all-gather | bytes 5184 | tf_op jit(solution)/shard_map/all_gather | solution.py:1056
  42.4 10.3 %collective-permute-done.3.refs_1_ = bf16[4,96,768]{2,1,0:T(8,128)(2,1)S(1)} collective-permute-done((bf16[4,96,768]{2,1,0:T(8,128)(2,1)S(1)}, bf16[4,96,768]{2,1,0:T(8,128)(2,1)S(1)}, u32[]{:S(2)}, u32[]{:S(2)}) %collective-permute-start.3) | collective-permute-done | bytes 589856 | tf_op jit(solution)/shard_map/ppermute | solution.py:881
  52.7 13.0 %collective-permute-done.4.refs_2_ = bf16[4,96,768]{2,1,0:T(8,128)(2,1)S(1)} collective-permute-done((bf16[4,96,768]{2,1,0:T(8,128)(2,1)S(1)}, bf16[4,96,768]{2,1,0:T(8,128)(2,1)S(1)}, u32[]{:S(2)}, u32[]{:S(2)}) %collective-permute-start.4) | collective-permute-done | bytes 589856 | tf_op jit(solution)/shard_map/ppermute | solution.py:881
  66.2 3.9 all-gather.4.cloned.1.call-done.wq_ref.wk_ref.wv_ref.wo_ref
  70.1 8.9 %collective-permute-start.10 = (bf16[64,768]{1,0:T(8,128)(2,1)S(1)}, bf16[64,768]{1,0:T(8,128)(2,1)S(1)}, u32[]{:S(2)}, u32[]{:S(2)}) collective-permute-start(bf16[64,768]{1,0:T(8,128)(2,1)S(1)} %fusion.20), channel_id=1, source_target_pairs={{0,2},{1,3},{2,4},{3,5},{4,6},{5,7},{6,0},{7,1},{8,10},{9,11},{10,... | collective-permute-start | bytes 294920 | tf_op jit(solution)/shard_map/ppermute | solution.py:881
  79.6 22.5 %self_forward.1 = (bf16[1024,768]{1,0:T(8,128)(2,1)}, bf16[1024,768]{1,0:T(8,128)(2,1)}, bf16[1024,768]{1,0:T(8,128)(2,1)}, bf16[1024,768]{1,0:T(8,128)(2,1)}, f...) custom-call(s32[2]{0:T(128)} %length_ref.9, bf16[1024,768]{1,0:T(8,128)(2,1)} %bitcast.119, ...), custom_call_target="tpu_custom_call" | custom-call | flops 31050000384 | bytes 20971520 | tf_op jit(solution)/shard_map/self_forward/pallas_call | solution.py:188
  107.1 5.5 %assemble_cross.1.wq_ref.wk_ref.wv_ref.wo_ref = bf16[4,768,768]{2,1,0:T(8,128)(2,1)} custom-call(s32[3]{0:T(128)} %pad_add_fusion.where_ref, bf16[4,96,768]{2,1,0:T(8,128)(2,1)} %copy-done.17, bf16[4,96,768]{2,1,0:T(8,128)(2,1)} %copy-done.35, bf16[4,96,768]{2,1,0:T(8,128)(2,1)} %copy-done.36, bf16[4,96,768]{2,1,0:T(8,128)(2,1)} %collective-permute-done.5.refs_3_, ...), custom_call_target="tpu_custom_call" | custom-call | flops 4600000000 | bytes 8388608 | tf_op jit(solution)/shard_map/assemble_cross/pallas_call | solution.py:936
  112.6 3.5 collective-permute-done.11
  120.4 22.8 %cross_forward.1 = (bf16[1024,768]{1,0:T(8,128)(2,1)}, bf16[1024,768]{1,0:T(8,128)(2,1)}, bf16[1024,768]{1,0:T(8,128)(2,1)}, bf16[1024,768]{1,0:T(8,128)(2,1)}, ...) custom-call(s32[2]{0:T(128)} %length_ref.8, f32[1024,768]{1,0:T(8,128)} %get-tuple-element.154.x_ref, ...), custom_call_target="tpu_custom_call" | custom-call | flops 31050000384 | bytes 20971520 | tf_op jit(solution)/shard_map/cross_forward/pallas_call | solution.py:188
  147.7 4.5 %assemble_out.1.wd_ref = bf16[2048,768]{1,0:T(8,128)(2,1)} custom-call(s32[3]{0:T(128)} %pad_add_fusion.where_ref, bf16[4,64,768]{2,1,0:T(8,128)(2,1)} %copy-done.22, bf16[4,64,768]{2,1,0:T(8,128)(2,1)} %copy-done.38, bf16[4,64,768]{2,1,0:T(8,128)(2,1)} %copy-done.39, bf16[4,64,768]{2,1,0:T(8,128)(2,1)} %copy-done.40, bf16[4,64,768]{2,1,0:T(8,128)(2,1)} %copy-done.41, ...), custom_call_target="tpu_custom_call" | custom-call | flops 4600000000 | bytes 8388608 | tf_op jit(solution)/shard_map/assemble_out/pallas_call | solution.py:936
  152.2 47.7 %feed_forward_both.1 = (bf16[1024,768]{1,0:T(8,128)(2,1)}, f32[1024,768]{1,0:T(8,128)}, bf16[768,2048]{1,0:T(8,128)(2,1)}, bf16[768,2048]{1,0:T(8,128)(2,1)}, bf...) custom-call(s32[2]{0:T(128)} %length_ref.9, ...), custom_call_target="tpu_custom_call" | custom-call | flops 52899999744 | bytes 41943040 | tf_op jit(solution)/shard_map/feed_forward_both/pallas_call | solution.py:314
  203.6 41.7 %cross_backward.1 = (f32[1024,768]{1,0:T(8,128)}, bf16[1024,768]{1,0:T(8,128)(2,1)}, bf16[1024,768]{1,0:T(8,128)(2,1)}, f32[1,768]{1,0:T(1,128)}, bf16[4,128,768...) custom-call(s32[2]{0:T(128)} %length_ref.8, ...), custom_call_target="tpu_custom_call" | custom-call | flops 51749998592 | bytes 41943040 | tf_op jit(solution)/shard_map/cross_backward/pallas_call | solution.py:546
  248.0 6.7 %memory_gradient.1 = f32[1024,768]{1,0:T(8,128)} custom-call(bf16[1024,768]{1,0:T(8,128)(2,1)} %get-tuple-element.186.gk_ref, bf16[1024,768]{1,0:T(8,128)(2,1)} %get-tuple-element.187.gv_ref, bf16[4,768,768]{2,1,0:T(8,128)(2,1)} %assemble_cross.1.wq_ref.wk_ref.wv_ref.wo_ref, bf16[4,768,768]{2,1,0:T(8,128)(2,1)} %assemble_cross.1.wq_ref.wk_ref.wv_ref.wo_ref), custom_call_target="tpu_custom_call" | custom-call | flops 8049999872 | bytes 10485760 | tf_op jit(solution)/shard_map/memory_gradient/pallas_call | solution.py:619
  254.7 4.0 fusion
  262.3 32.8 %self_backward.1 = (bf16[1024,768]{1,0:T(8,128)(2,1)}, bf16[1024,768]{1,0:T(8,128)(2,1)}, bf16[1024,768]{1,0:T(8,128)(2,1)}, bf16[3,768,768]{2,1,0:T(8,128)(2,1)}, f32[16,512]{1,0:T(8,128)}) custom-call(s32[2]{0:T(128)} %length_ref.9, s32[3]{0:T(128)} %pad_add_fusion.where_ref, bf16[1024,768]{1,0:T(8,128)(2,1)} %bitcast.120, ...), custom_call_target="tpu_custom_call" | custom-call | flops 51749998592 | bytes 41943040 | tf_op jit(solution)/shard_map/self_backward/pallas_call | solution.py:546
  306.3 7.2 %collective-permute-start.28 = (bf16[192,768]{1,0:T(8,128)(2,1)S(1)}, bf16[192,768]{1,0:T(8,128)(2,1)S(1)}, u32[]{:S(2)}, u32[]{:S(2)}) collective-permute-start(bf16[192,768]{1,0:T(8,128)(2,1)S(1)} %get-tuple-element.289), channel_id=1, source_target_pairs={{0,2},{1,3},{2,4},{3,5},{4,6},{5,7},{6,0},{7,1},{8,10},{9,11},{10,... | collective-permute-start | bytes 884744 | tf_op jit(solution)/shard_map/ppermute | solution.py:881
  321.2 3.4 collective-permute-done.28.refs_1_
  326.2 14.3 %collective-permute-done.29.refs_2_ = bf16[192,768]{1,0:T(8,128)(2,1)S(1)} collective-permute-done((bf16[192,768]{1,0:T(8,128)(2,1)S(1)}, bf16[192,768]{1,0:T(8,128)(2,1)S(1)}, u32[]{:S(2)}, u32[]{:S(2)}) %collective-permute-start.29) | collective-permute-done | bytes 294944 | tf_op jit(solution)/shard_map/ppermute | solution.py:881
  349.7 10.0 %input_gradient.1 = (f32[1024,768]{1,0:T(8,128)}, f32[1,768]{1,0:T(1,128)}) custom-call(bf16[1024,768]{1,0:T(8,128)(2,1)} %get-tuple-element.222.gq_ref, bf16[1024,768]{1,0:T(8,128)(2,1)} %get-tuple-element.223.gk_ref, bf16[1024,768]{1,0:T(8,128)(2,1)} %get-tuple-element.224.gv_ref, ...), custom_call_target="tpu_custom_call" | custom-call | flops 9200000000 | bytes 12582912 | tf_op jit(solution)/shard_map/input_gradient/pallas_call | solution.py:598
  360.5 6.5 %reduce-scatter.8.cloned.1.call-done = bf16[3,96,768]{2,1,0:T(8,128)(2,1)} async-done(((bf16[3,768,768]{2,1,0:T(8,128)(2,1)}), bf16[3,96,768]{2,1,0:T(8,128)(2,1)}) %reduce-scatter.8.cloned.1.call-update) | async-done | bytes 442384 | tf_op jit(solution)/shard_map/reduce_scatter | solution.py:1123
  374.4 4.0 collective-permute-done.40.refs_2_
  390.2 9.6 %collective-permute-done.43 = f32[120,128]{1,0:T(8,128)S(1)} collective-permute-done((f32[120,128]{1,0:T(8,128)S(1)}, f32[120,128]{1,0:T(8,128)S(1)}, u32[]{:S(2)}, u32[]{:S(2)}) %collective-permute-start.43) | collective-permute-done | bytes 61472 | tf_op jit(solution)/shard_map/ppermute | solution.py:881
  412.1 8.8 %update_all.1 = (f32[2,96,2048]{2,1,0:T(8,128)}, f32[256,768]{1,0:T(8,128)}, f32[4,96,768]{2,1,0:T(8,128)}, f32[4,96,768]{2,1,0:T(8,128)}, f32[2,96,2048]{2,1,0:...) custom-call(s32[3]{0:T(128)} %pad_add_fusion.where_ref, ...), custom_call_target="tpu_custom_call" | custom-call | flops 9200000000 | bytes 16777216 | tf_op jit(solution)/shard_map/update_all/pallas_call | solution.py:862
  (287 shorter events, 108.2 us)
Async XLA Ops:
  7.2 62.9 %all-gather.4.cloned.1.call-start = ((), (), s32[]{:S(2)}) async-start(), calls=%async_computation.3 | async-start | bytes 5308416 | tf_op jit(solution)/shard_map/all_gather | solution.py:1055
  10.6 141.7 %all-gather.6.cloned.1.call-start = ((), (), s32[]{:S(2)}) async-start(), calls=%async_computation.4 | async-start | bytes 7077888 | tf_op jit(solution)/shard_map/all_gather | solution.py:1057
  11.9 242.9 %reduce-scatter.4.cloned.1.call-start = ((), (), s32[]{:S(2)}) async-start(), calls=%async_computation.5 | async-start | bytes 3538944 | tf_op jit(solution)/shard_map/reduce_scatter | solution.py:1123
  37.8 27.9 %collective-permute-start.4 = (bf16[4,96,768]{2,1,0:T(8,128)(2,1)S(1)}, bf16[4,96,768]{2,1,0:T(8,128)(2,1)S(1)}, u32[]{:S(2)}, u32[]{:S(2)}) collective-permute-start(bf16[4,96,768]{2,1,0:T(8,128)(2,1)S(1)} %pad_maximum_fusion.refs_0_), channel_id=1, source_target_pairs={{0,16},{1,17},{2,18},{3,19},{4,20},{5,21},{6,22},{7,23},{8,24},{9,... | collective-permute-start | bytes 1769480 | tf_op jit(solution)/shard_map/ppermute | solution.py:881
  39.3 26.4 %collective-permute-start.5 = (bf16[4,96,768]{2,1,0:T(8,128)(2,1)S(1)}, bf16[4,96,768]{2,1,0:T(8,128)(2,1)}, u32[]{:S(2)}, u32[]{:S(2)}) collective-permute-start(bf16[4,96,768]{2,1,0:T(8,128)(2,1)S(1)} %pad_maximum_fusion.refs_0_), channel_id=1, source_target_pairs={{0,24},{1,25},{2,26},{3,27},{4,28},{5,29},{6,30},{7,31},{8,16},{9,... | collective-permute-start | bytes 1769480 | tf_op jit(solution)/shard_map/ppermute | solution.py:881
  42.4 59.8 %collective-permute-start.6 = (bf16[4,96,768]{2,1,0:T(8,128)(2,1)S(1)}, bf16[4,96,768]{2,1,0:T(8,128)(2,1)S(1)}, u32[]{:S(2)}, u32[]{:S(2)}) collective-permute-start(bf16[4,96,768]{2,1,0:T(8,128)(2,1)S(1)} %pad_maximum_fusion.refs_0_), channel_id=1, source_target_pairs={{0,1},{1,0},{2,3},{3,2},{4,5},{5,4},{6,7},{7,6},{8,9},{9,8},{10,11... | collective-permute-start | bytes 1769480 | tf_op jit(solution)/shard_map/ppermute | solution.py:881
  52.7 51.6 %collective-permute-start.7 = (bf16[4,96,768]{2,1,0:T(8,128)(2,1)S(1)}, bf16[4,96,768]{2,1,0:T(8,128)(2,1)}, u32[]{:S(2)}, u32[]{:S(2)}) collective-permute-start(bf16[4,96,768]{2,1,0:T(8,128)(2,1)S(1)} %collective-permute-done.3.refs_1_), channel_id=1, source_target_pairs={{0,1},{1,0},{2,3},{3,2},{4,5},{5,4},{6,7},{7,6},{8,9},{9,8},{10,11... | collective-permute-start | bytes 1769480 | tf_op jit(solution)/shard_map/ppermute | solution.py:881
  65.7 41.4 %collective-permute-start.8 = (bf16[4,96,768]{2,1,0:T(8,128)(2,1)S(1)}, bf16[4,96,768]{2,1,0:T(8,128)(2,1)}, u32[]{:S(2)}, u32[]{:S(2)}) collective-permute-start(bf16[4,96,768]{2,1,0:T(8,128)(2,1)S(1)} %collective-permute-done.4.refs_2_), channel_id=1, source_target_pairs={{0,1},{1,0},{2,3},{3,2},{4,5},{5,4},{6,7},{7,6},{8,9},{9,8},{10,11... | collective-permute-start | bytes 1769480 | tf_op jit(solution)/shard_map/ppermute | solution.py:881
  65.7 41.4 %collective-permute-start.9 = (bf16[4,96,768]{2,1,0:T(8,128)(2,1)}, bf16[4,96,768]{2,1,0:T(8,128)(2,1)}, u32[]{:S(2)}, u32[]{:S(2)}) collective-permute-start(bf16[4,96,768]{2,1,0:T(8,128)(2,1)} %collective-permute-done.5.refs_3_), channel_id=1, source_target_pairs={{0,1},{1,0},{2,3},{3,2},{4,5},{5,4},{6,7},{7,6},{8,9},{9,8},{10,11... | collective-permute-start | bytes 1769480 | tf_op jit(solution)/shard_map/ppermute | solution.py:881
  70.1 42.5 %collective-permute-start.10 = (bf16[64,768]{1,0:T(8,128)(2,1)S(1)}, bf16[64,768]{1,0:T(8,128)(2,1)S(1)}, u32[]{:S(2)}, u32[]{:S(2)}) collective-permute-start(bf16[64,768]{1,0:T(8,128)(2,1)S(1)} %fusion.20), channel_id=1, source_target_pairs={{0,2},{1,3},{2,4},{3,5},{4,6},{5,7},{6,0},{7,1},{8,10},{9,11},{10,... | collective-permute-start | bytes 294920 | tf_op jit(solution)/shard_map/ppermute | solution.py:881
  116.2 27.0 %collective-permute-start.13 = (bf16[4,64,768]{2,1,0:T(8,128)(2,1)S(1)}, bf16[4,64,768]{2,1,0:T(8,128)(2,1)S(1)}, u32[]{:S(2)}, u32[]{:S(2)}) collective-permute-start(bf16[4,64,768]{2,1,0:T(8,128)(2,1)S(1)} %pad_maximum_fusion.1.refs_0_), channel_id=1, source_target_pairs={{0,8},{1,9},{2,10},{3,11},{4,12},{5,13},{6,14},{7,15},{8,0},{9,1},... | collective-permute-start | bytes 1179656 | tf_op jit(solution)/shard_map/ppermute | solution.py:881
  199.9 45.3 %collective-permute-start.20 = (bf16[2,4,64,768]{3,2,1,0:T(8,128)(2,1)}, bf16[2,4,64,768]{3,2,1,0:T(8,128)(2,1)S(1)}, u32[]{:S(2)}, u32[]{:S(2)}) collective-permute-start(bf16[2,4,64,768]{3,2,1,0:T(8,128)(2,1)} %get-tuple-element.183), channel_id=1, source_target_pairs={{0,8},{1,9},{2,10},{3,11},{4,12},{5,13},{6,14},{7,15},{8,0},{9,1},... | collective-permute-start | bytes 2359304 | tf_op jit(solution)/shard_map/ppermute | solution.py:881
  201.2 44.1 %collective-permute-start.21 = (bf16[2,4,64,768]{3,2,1,0:T(8,128)(2,1)}, bf16[2,4,64,768]{3,2,1,0:T(8,128)(2,1)S(1)}, u32[]{:S(2)}, u32[]{:S(2)}) collective-permute-start(bf16[2,4,64,768]{3,2,1,0:T(8,128)(2,1)} %get-tuple-element.184), channel_id=1, source_target_pairs={{0,16},{1,17},{2,18},{3,19},{4,20},{5,21},{6,22},{7,23},{8,24},{9,... | collective-permute-start | bytes 2359304 | tf_op jit(solution)/shard_map/ppermute | solution.py:881
  202.0 43.3 %collective-permute-start.22 = (bf16[2,4,64,768]{3,2,1,0:T(8,128)(2,1)}, bf16[2,4,64,768]{3,2,1,0:T(8,128)(2,1)S(1)}, u32[]{:S(2)}, u32[]{:S(2)}) collective-permute-start(bf16[2,4,64,768]{3,2,1,0:T(8,128)(2,1)} %get-tuple-element.185), channel_id=1, source_target_pairs={{0,24},{1,25},{2,26},{3,27},{4,28},{5,29},{6,30},{7,31},{8,16},{9,... | collective-permute-start | bytes 2359304 | tf_op jit(solution)/shard_map/ppermute | solution.py:881
  203.5 91.6 %reduce-scatter.6.cloned.1.call-start = ((), (), s32[]{:S(2)}) async-start(), calls=%async_computation.6 | async-start | bytes 3538944 | tf_op jit(solution)/shard_map/reduce_scatter | solution.py:1123
  246.7 120.3 %reduce-scatter.8.cloned.1.call-start = ((), (), s32[]{:S(2)}) async-start(), calls=%async_computation.7 | async-start | bytes 3981312 | tf_op jit(solution)/shard_map/reduce_scatter | solution.py:1123
  258.8 36.3 %collective-permute-start.24 = (bf16[4,128,768]{2,1,0:T(8,128)(2,1)}, bf16[4,128,768]{2,1,0:T(8,128)(2,1)S(1)}, u32[]{:S(2)}, u32[]{:S(2)}) collective-permute-start(bf16[4,128,768]{2,1,0:T(8,128)(2,1)} %get-tuple-element.206), channel_id=1, source_target_pairs={{0,8},{1,9},{2,10},{3,11},{4,12},{5,13},{6,14},{7,15},{8,0},{9,1},... | collective-permute-start | bytes 2359304 | tf_op jit(solution)/shard_map/ppermute | solution.py:881
  260.0 35.2 %collective-permute-start.25 = (bf16[4,128,768]{2,1,0:T(8,128)(2,1)}, bf16[4,128,768]{2,1,0:T(8,128)(2,1)S(1)}, u32[]{:S(2)}, u32[]{:S(2)}) collective-permute-start(bf16[4,128,768]{2,1,0:T(8,128)(2,1)} %get-tuple-element.207), channel_id=1, source_target_pairs={{0,16},{1,17},{2,18},{3,19},{4,20},{5,21},{6,22},{7,23},{8,24},{9,... | collective-permute-start | bytes 2359304 | tf_op jit(solution)/shard_map/ppermute | solution.py:881
  260.8 35.9 %collective-permute-start.26 = (bf16[4,128,768]{2,1,0:T(8,128)(2,1)}, bf16[4,128,768]{2,1,0:T(8,128)(2,1)S(1)}, u32[]{:S(2)}, u32[]{:S(2)}) collective-permute-start(bf16[4,128,768]{2,1,0:T(8,128)(2,1)} %get-tuple-element.208), channel_id=1, source_target_pairs={{0,24},{1,25},{2,26},{3,27},{4,28},{5,29},{6,30},{7,31},{8,16},{9,... | collective-permute-start | bytes 2359304 | tf_op jit(solution)/shard_map/ppermute | solution.py:881
  313.5 27.0 %collective-permute-start.29 = (bf16[192,768]{1,0:T(8,128)(2,1)S(1)}, bf16[192,768]{1,0:T(8,128)(2,1)S(1)}, u32[]{:S(2)}, u32[]{:S(2)}) collective-permute-start(bf16[192,768]{1,0:T(8,128)(2,1)S(1)} %get-tuple-element.290), channel_id=1, source_target_pairs={{0,4},{1,5},{2,6},{3,7},{4,0},{5,1},{6,2},{7,3},{8,12},{9,13},{10,... | collective-permute-start | bytes 884744 | tf_op jit(solution)/shard_map/ppermute | solution.py:881
  313.5 29.3 %collective-permute-start.30 = (bf16[192,768]{1,0:T(8,128)(2,1)S(1)}, bf16[192,768]{1,0:T(8,128)(2,1)S(1)}, u32[]{:S(2)}, u32[]{:S(2)}) collective-permute-start(bf16[192,768]{1,0:T(8,128)(2,1)S(1)} %get-tuple-element.287), channel_id=1, source_target_pairs={{0,6},{1,7},{2,0},{3,1},{4,2},{5,3},{6,4},{7,5},{8,14},{9,15},{10,... | collective-permute-start | bytes 884744 | tf_op jit(solution)/shard_map/ppermute | solution.py:881
  318.7 41.7 %collective-permute-start.34 = (bf16[2,24,2048]{2,1,0:T(8,128)(2,1)}, bf16[2,24,2048]{2,1,0:T(8,128)(2,1)S(1)}, u32[]{:S(2)}, u32[]{:S(2)}) collective-permute-start(bf16[2,24,2048]{2,1,0:T(8,128)(2,1)} %get-tuple-element.248.refs_0_), channel_id=1, source_target_pairs={{0,8},{1,9},{2,10},{3,11},{4,12},{5,13},{6,14},{7,15},{8,0},{9,1},... | collective-permute-start | bytes 589832 | tf_op jit(solution)/shard_map/ppermute | solution.py:881
  319.6 40.8 %collective-permute-start.35 = (bf16[2,24,2048]{2,1,0:T(8,128)(2,1)}, bf16[2,24,2048]{2,1,0:T(8,128)(2,1)S(1)}, u32[]{:S(2)}, u32[]{:S(2)}) collective-permute-start(bf16[2,24,2048]{2,1,0:T(8,128)(2,1)} %get-tuple-element.248.refs_0_), channel_id=1, source_target_pairs={{0,16},{1,17},{2,18},{3,19},{4,20},{5,21},{6,22},{7,23},{8,24},{9,... | collective-permute-start | bytes 589832 | tf_op jit(solution)/shard_map/ppermute | solution.py:881
  324.6 35.8 %collective-permute-start.36 = (bf16[2,24,2048]{2,1,0:T(8,128)(2,1)}, bf16[2,24,2048]{2,1,0:T(8,128)(2,1)S(1)}, u32[]{:S(2)}, u32[]{:S(2)}) collective-permute-start(bf16[2,24,2048]{2,1,0:T(8,128)(2,1)} %get-tuple-element.248.refs_0_), channel_id=1, source_target_pairs={{0,24},{1,25},{2,26},{3,27},{4,28},{5,29},{6,30},{7,31},{8,16},{9,... | collective-permute-start | bytes 589832 | tf_op jit(solution)/shard_map/ppermute | solution.py:881
  (96 other events, 1037.3 us)
Sparse Core Ops, SparseCore 0:
  10.6 59.4 all-gather.3
  72.3 70.3 all-gather.5
  203.6 44.2 reduce-scatter.3
  250.1 41.3 reduce-scatter.5
  297.7 69.2 reduce-scatter.7

commit v11 on v10

--- a/solution.py
+++ b/solution.py
@@ -82,6 +82,18 @@
             lane == 1, wide(middle), jnp.where(lane == 2, wide(low), jnp.where(lane == 3, last, 0.0))
         ),
     ).astype(LOW)
+
+
+def piece_copies(parts, where_ref, place, sems):
+    rep, line, core = where_ref[0], where_ref[1], where_ref[2]
+    copies = []
+    for other in range(LINE_CORES):
+        for way in range(4):
+            for hop in range(LINE):
+                shard = lax.rem(line - hop + LINE, LINE) * LINE_CORES + (core ^ other)
+                source = parts[4 * other + way].at[hop]
+                copies.append(pltpu.make_async_copy(source, place(rep ^ way, shard), sems.at[len(copies)]))
+    return copies
 
 
 def forward_body(causal, seq_count, length_ref, wave_ref, bias_ref, q_ref, k_ref, v_ref, mix_ref, total_ref, group):
@@ -245,11 +257,11 @@
 
 
 def feed_kernel(
-    seq_count, length_ref, where_ref, after_ref, out_grad_ref, gain_ref, wg_ref, wu_ref, wd_ref,
-    layer_ref, grad_cross_ref, dwg_ref, dwu_ref, *refs,
+    seq_count, pieces, length_ref, where_ref, after_ref, out_grad_ref, gain_ref, wg_ref, wu_ref, *refs,
 ):
-    near_refs = refs[:4]
-    dgain_ref, normed, normed_t, down, out_total, grad_total, cut = refs[4:]
+    wd_refs, (layer_ref, grad_cross_ref, dwg_ref, dwu_ref) = refs[:pieces], refs[pieces : pieces + 4]
+    near_refs = refs[pieces + 4 : pieces + 8]
+    dgain_ref, normed, normed_t, down, out_total, grad_total, cut, *held = refs[pieces + 8 :]
     step = pl.program_id(0)
     row_count = after_ref.shape[0]
     length = row_count // seq_count
@@ -260,6 +272,11 @@
 
     @pl.when(step == 0)
     def _():
+        if pieces > 1:
+            place = lambda quarter, at: held[0].at[pl.ds((at * 4 + quarter) * cut.shape[2], cut.shape[2])]
+            copies = piece_copies(wd_refs, where_ref, place, held[1])
+            for copy in copies:
+                copy.start()
         for at, size in chunks(row_count, 256):
             rows = after_ref[at : at + size, :]
             low = (rows * rms_rate(rows) * gain_ref[...]).astype(LOW)
@@ -270,7 +287,15 @@
             ).astype(LOW)
             out_total[at : at + size, :] = rows
             grad_total[at : at + size, :] = jnp.zeros((size, rows.shape[1]), WIDE)
-
+        if pieces > 1:
+            for copy in copies:
+                copy.wait()
+
+    block = wg_ref.shape[1]
+    if pieces > 1:
+        wd_ref = held[0].at[pl.ds(pl.multiple_of(step * block, block), block)]
+    else:
+        wd_ref = wd_refs[0]
     gate = nn(normed[...], wg_ref[...])
     up = nn(normed[...], wu_ref[...])
     value, slope = gelu_parts(gate)
@@ -278,9 +303,10 @@
     out_total[...] += nn(hidden, wd_ref[...])
     grad_hidden = nt(down[...], wd_ref[...])
     cut[...] = tn(hidden, down[...]).astype(LOW).reshape(cut.shape)
-    core, hop = shard_slot(where_ref, step)
-    for way in range(4):
-        near_refs[way][core, hop] = cut[where_ref[0] ^ way]
+    for part in range(cut.shape[0]):
+        core, hop = shard_slot(where_ref, step * cut.shape[0] + part)
+        for way in range(4):
+            near_refs[way][core, hop] = cut[part, where_ref[0] ^ way]
     grad_gate = (grad_hidden * up * slope).astype(LOW)
     grad_up = (grad_hidden * value).astype(LOW)
     dwg_ref[...] = nn(normed_t[...], grad_gate).astype(LOW)
@@ -303,16 +329,19 @@
 
 def feed_forward_both(after, out_grad, lengths, where, gain, w_in, w_out):
     row_count, width = after.shape
-    hidden = w_out.shape[0]
-    block = hidden // (LINE * LINE_CORES)
+    hidden = w_in.shape[2]
+    each = hidden // (LINE * LINE_CORES)
+    block = 2 * each
     seq_count = lengths.shape[0]
     wide = pl.BlockSpec((None, width, block), lambda g: (0, 0, g))
     wide_up = pl.BlockSpec((None, width, block), lambda g: (1, 0, g))
     tall = pl.BlockSpec((block, width), lambda g: (g, 0))
     flat = pl.BlockSpec((width, block), lambda g: (0, g))
-    near = (LINE_CORES, LINE, block // 4, width)
+    near = (LINE_CORES, LINE, each // 4, width)
+    pieces = len(w_out)
+    held = [pltpu.VMEM((hidden, width), LOW), pltpu.SemaphoreType.DMA((pieces * LINE,))] if pieces > 1 else []
     return pl.pallas_call(
-        functools.partial(feed_kernel, seq_count),
+        functools.partial(feed_kernel, seq_count, pieces),
         grid=(hidden // block,),
         in_specs=[
             pl.BlockSpec(memory_space=pltpu.SMEM),
@@ -322,7 +351,7 @@
             whole(gain.shape),
             wide,
             wide_up,
-            tall,
+            *([pl.BlockSpec(memory_space=pl.ANY)] * pieces if pieces > 1 else [tall]),
         ],
         out_specs=[whole(after.shape), whole(after.shape), flat, flat, *[whole(near)] * 4, whole((1, width))],
         out_shape=[
@@ -339,12 +368,13 @@
             pltpu.VMEM((row_count, width), LOW),
             pltpu.VMEM((row_count, width), WIDE),
             pltpu.VMEM((row_count, width), WIDE),
-            pltpu.VMEM((4, block // 4, width), LOW),
+            pltpu.VMEM((2, 4, each // 4, width), LOW),
+            *held,
         ],
         cost_estimate=pl.CostEstimate(flops=int(46 * PEAK), bytes_accessed=40 << 20, transcendentals=0),
         compiler_params=pltpu.CompilerParams(vmem_limit_bytes=60 * MEGABYTE),
         name="feed_forward_both",
-    )(lengths, where, after, out_grad, gain, w_in, w_in, w_out)
+    )(lengths, where, after, out_grad, gain, w_in, w_in, *w_out)
 
 
 def backward_kernel(
@@ -910,21 +940,8 @@
     return [parts[0]] + [from_line(parts[hop], hop) for hop in range(1, LINE)]
 
 
-def assemble_kernel(place, hops, where_ref, *refs):
-    parts, out_ref, sems = refs[:8], refs[8], refs[9]
-    rep, line, core = where_ref[0], where_ref[1], where_ref[2]
-    copies = []
-    for other in range(2):
-        for way in range(4):
-            for hop in range(hops):
-                shard = lax.rem(line - hop + hops, hops) * LINE_CORES + (core ^ other)
-                copies.append(
-                    pltpu.make_async_copy(
-                        parts[4 * other + way].at[hop],
-                        place(out_ref, rep ^ way, shard),
-                        sems.at[len(copies)],
-                    )
-                )
+def assemble_kernel(place, where_ref, *refs):
+    copies = piece_copies(refs[:8], where_ref, functools.partial(place, refs[8]), refs[9])
     for copy in copies:
         copy.start()
     for copy in copies:
@@ -934,7 +951,7 @@
 def assemble(parts, where, shape, place, name):
     hops = parts[0].shape[0]
     return pl.pallas_call(
-        functools.partial(assemble_kernel, place, hops),
+        functools.partial(assemble_kernel, place),
         in_specs=[pl.BlockSpec(memory_space=pltpu.SMEM)] + [pl.BlockSpec(memory_space=pl.ANY)] * 8,
         out_specs=pl.BlockSpec(memory_space=pltpu.VMEM),
         out_shape=jax.ShapeDtypeStruct(shape, LOW),
@@ -1104,19 +1121,13 @@
         out_near = across_reps(after(out_line, after_self))
     else:
         w_cross = lax.all_gather(cross_weight.astype(LOW), "fsdp", axis=1, tiled=True)
-        w_out = lax.all_gather(ffn_out.astype(LOW), "fsdp", axis=0, tiled=True)
+        w_out = [lax.all_gather(ffn_out.astype(LOW), "fsdp", axis=0, tiled=True)]
     *kept_two, after_cross = attention_forward(
         False, after_self, mem_rows, enc_len, gain_full[1:2], w_cross, no_bias
     )
     if quarters:
         out_near = hold(*out_near, after_cross)[:-1]
-        w_out = assemble(
-            with_partner(list(out_near)),
-            where,
-            (hidden_width, model_width),
-            lambda ref, quarter, at: ref.at[pl.ds((at * 4 + quarter) * out_each, out_each)],
-            "assemble_out",
-        )
+        w_out = with_partner(list(out_near))
     layer_out, grad_cross, grad_gate, grad_up, *out_near, gain_three = feed_forward_both(
         after_cross, grad_rows, dec_len, where, gain_full[2:3], w_in, w_out
     )
@@ -1178,8 +1189,8 @@
         in_near, line_near = near[:4], near[4:] + line_near[3:]
         self_parts = rep_parts(own_self.reshape(3, 4, -1, model_width), 1)
         self_piece, vector = late_sums(grad_factor, starts, self_parts, small, early)
-        vector, *self_near = hold(butterfly(vector, from_rep, reps), *rep_near(self_piece))
-        total = butterfly(vector, from_shard, shards)
+        vector, *self_near = hold(butterfly(vector, from_shard, shards), *rep_near(self_piece))
+        total = butterfly(vector, from_rep, reps)
         (
             ffn_in_grad, feedforward_output_gradient, cross_grad, self_grad,
             new_ffn_in, new_ffn_out, new_cross, new_self,

time: 436 us -> 426 us (0.977)
  waiting for transfers between devices: 83.7 us -> 76.7 us
  Pallas kernels: 209 us -> 203 us
    ppermute x51, waiting for transfers between devices: 73.2 us -> 66.2 us  [flat_permute(): return lax.ppermute(value, ('rep', 'fsdp'), pairs)]
    pallas_call x3 -> x2, Pallas kernels: 57.7 us -> 51.5 us  [the longest x1 46 us: feed_forward_both(): pl.pallas_call(functools.partial(feed_kernel, seq_count, pieces), grid=(h...]
    unnamed x130 -> x128, local copies, waits for them, and re-layouts: 10.1 us -> 9.9 us
  transfers between devices with their start and end apart: 56 -> 56, of which waited for: 21 -> 20; matrix products, arithmetic and copies ran while one was open for 5% -> 5% of each run, Pallas kernels for 35% -> 35%
where the time goes in v11:
time: 426 us; the launch traced here: 418 us
  Pallas kernels  203 us (48%)
  waiting for transfers between devices  76.7 us (18%)
  starting transfers between devices  75.6 us (18%)
  other arithmetic  20.2 us (5%)
  local copies, waits for them, and re-layouts  16.7 us (4%)
  between operations  15.1 us (4%)
  blocking collectives  11.1 us (3%)
    ppermute x51, starting transfers between devices, flat_permute(): return lax.ppermute(value, ('rep', 'fsdp'), pairs)  75.3 us
    pallas_call x2, Pallas kernels, attention_backward(): pl.pallas_call(functools.partial(backward_kernel, causal, seq_count), gri...  74.3 us
    ppermute x51, waiting for transfers between devices, flat_permute(): return lax.ppermute(value, ('rep', 'fsdp'), pairs)  66.2 us
    pallas_call x1, Pallas kernels, feed_forward_both(): pl.pallas_call(functools.partial(feed_kernel, seq_count, pieces), grid=(h...  46 us
    pallas_call x2, Pallas kernels, attention_forward(): pl.pallas_call(functools.partial(forward_kernel, causal, seq_count), grid...  45.3 us
    all_gather x1, blocking collectives, per_device(): lax.all_gather(gains.astype(LOW), 'fsdp', axis=1, tiled=True).astype(WIDE)  11.1 us
    pallas_call x1, Pallas kernels, input_gradient(): pl.pallas_call(input_kernel, grid=(rows // block,), in_specs=[rowwise, ro...  9.97 us
    unnamed x128, local copies, waits for them, and re-layouts  9.9 us
  transfers between devices with their start and end apart: 56, of which 20 were waited for; matrix products, arithmetic and copies ran while one was open for 5% of the time, Pallas kernels for 35%

profile of v11, /device:TPU:0, one launch (start us, length us, event | category | flops | bytes accessed | tf_op | source)
XLA Modules:
  0.0 418.3 jit_solution(16581300854742116301)
XLA Ops:
  7.3 3.2 fusion.23
  23.8 11.1 %all-gather = bf16[8,96,3]{1,2,0:T(4,128)(2,1)S(1)} all-gather(bf16[1,96,3]{1,2,0:T(4,128)(2,1)S(1)} %get-tuple-element.305), channel_id=1, replica_groups=mesh['rep'=4,'fsdp'=8] {'fsdp'}, dimensions={0}, use_global_device_ids=true | all-gather | bytes 5184 | tf_op jit(solution)/shard_map/all_gather | solution.py:1073
  42.4 10.2 %collective-permute-done.3.refs_1_ = bf16[4,96,768]{2,1,0:T(8,128)(2,1)S(1)} collective-permute-done((bf16[4,96,768]{2,1,0:T(8,128)(2,1)S(1)}, bf16[4,96,768]{2,1,0:T(8,128)(2,1)S(1)}, u32[]{:S(2)}, u32[]{:S(2)}) %collective-permute-start.3) | collective-permute-done | bytes 589856 | tf_op jit(solution)/shard_map/ppermute | solution.py:911
  52.7 13.0 %collective-permute-done.4.refs_2_ = bf16[4,96,768]{2,1,0:T(8,128)(2,1)S(1)} collective-permute-done((bf16[4,96,768]{2,1,0:T(8,128)(2,1)S(1)}, bf16[4,96,768]{2,1,0:T(8,128)(2,1)S(1)}, u32[]{:S(2)}, u32[]{:S(2)}) %collective-permute-start.4) | collective-permute-done | bytes 589856 | tf_op jit(solution)/shard_map/ppermute | solution.py:911
  66.2 3.9 all-gather.4.cloned.1.call-done.wq_ref.wk_ref.wv_ref.wo_ref
  70.1 8.9 %collective-permute-start.10 = (bf16[64,768]{1,0:T(8,128)(2,1)S(1)}, bf16[64,768]{1,0:T(8,128)(2,1)S(1)}, u32[]{:S(2)}, u32[]{:S(2)}) collective-permute-start(bf16[64,768]{1,0:T(8,128)(2,1)S(1)} %fusion.20), channel_id=1, source_target_pairs={{0,2},{1,3},{2,4},{3,5},{4,6},{5,7},{6,0},{7,1},{8,10},{9,11},{10,... | collective-permute-start | bytes 294920 | tf_op jit(solution)/shard_map/ppermute | solution.py:911
  79.6 22.5 %self_forward.1 = (bf16[1024,768]{1,0:T(8,128)(2,1)}, bf16[1024,768]{1,0:T(8,128)(2,1)}, bf16[1024,768]{1,0:T(8,128)(2,1)}, bf16[1024,768]{1,0:T(8,128)(2,1)}, f...) custom-call(s32[2]{0:T(128)} %length_ref.9, bf16[1024,768]{1,0:T(8,128)(2,1)} %bitcast.119, ...), custom_call_target="tpu_custom_call" | custom-call | flops 31050000384 | bytes 20971520 | tf_op jit(solution)/shard_map/self_forward/pallas_call | solution.py:200
  107.1 5.5 %assemble_cross.1.wq_ref.wk_ref.wv_ref.wo_ref = bf16[4,768,768]{2,1,0:T(8,128)(2,1)} custom-call(s32[3]{0:T(128)} %pad_add_fusion.where_ref, bf16[4,96,768]{2,1,0:T(8,128)(2,1)} %copy-done.17, bf16[4,96,768]{2,1,0:T(8,128)(2,1)} %copy-done.35, bf16[4,96,768]{2,1,0:T(8,128)(2,1)} %copy-done.36, bf16[4,96,768]{2,1,0:T(8,128)(2,1)} %collective-permute-done.5.refs_3_, ...), custom_call_target="tpu_custom_call" | custom-call | flops 4600000000 | bytes 8388608 | tf_op jit(solution)/shard_map/assemble_cross/pallas_call | solution.py:953
  112.6 3.5 collective-permute-done.11
  120.4 22.8 %cross_forward.1 = (bf16[1024,768]{1,0:T(8,128)(2,1)}, bf16[1024,768]{1,0:T(8,128)(2,1)}, bf16[1024,768]{1,0:T(8,128)(2,1)}, bf16[1024,768]{1,0:T(8,128)(2,1)}, ...) custom-call(s32[2]{0:T(128)} %length_ref.8, f32[1024,768]{1,0:T(8,128)} %get-tuple-element.154.x_ref, ...), custom_call_target="tpu_custom_call" | custom-call | flops 31050000384 | bytes 20971520 | tf_op jit(solution)/shard_map/cross_forward/pallas_call | solution.py:200
  147.5 46.0 %feed_forward_both.1 = (bf16[1024,768]{1,0:T(8,128)(2,1)}, f32[1024,768]{1,0:T(8,128)}, bf16[768,2048]{1,0:T(8,128)(2,1)}, bf16[768,2048]{1,0:T(8,128)(2,1)}, bf...) custom-call(s32[2]{0:T(128)} %length_ref.9, ...), custom_call_target="tpu_custom_call" | custom-call | flops 52899999744 | bytes 41943040 | tf_op jit(solution)/shard_map/feed_forward_both/pallas_call | solution.py:343
  197.2 41.7 %cross_backward.1 = (f32[1024,768]{1,0:T(8,128)}, bf16[1024,768]{1,0:T(8,128)(2,1)}, bf16[1024,768]{1,0:T(8,128)(2,1)}, f32[1,768]{1,0:T(1,128)}, bf16[4,128,768...) custom-call(s32[2]{0:T(128)} %length_ref.8, ...), custom_call_target="tpu_custom_call" | custom-call | flops 51749998592 | bytes 41943040 | tf_op jit(solution)/shard_map/cross_backward/pallas_call | solution.py:576
  241.6 6.7 %memory_gradient.1 = f32[1024,768]{1,0:T(8,128)} custom-call(bf16[1024,768]{1,0:T(8,128)(2,1)} %get-tuple-element.186.gk_ref, bf16[1024,768]{1,0:T(8,128)(2,1)} %get-tuple-element.187.gv_ref, bf16[4,768,768]{2,1,0:T(8,128)(2,1)} %assemble_cross.1.wq_ref.wk_ref.wv_ref.wo_ref, bf16[4,768,768]{2,1,0:T(8,128)(2,1)} %assemble_cross.1.wq_ref.wk_ref.wv_ref.wo_ref), custom_call_target="tpu_custom_call" | custom-call | flops 8049999872 | bytes 10485760 | tf_op jit(solution)/shard_map/memory_gradient/pallas_call | solution.py:649
  248.3 4.0 fusion
  255.8 32.7 %self_backward.1 = (bf16[1024,768]{1,0:T(8,128)(2,1)}, bf16[1024,768]{1,0:T(8,128)(2,1)}, bf16[1024,768]{1,0:T(8,128)(2,1)}, bf16[3,768,768]{2,1,0:T(8,128)(2,1)}, f32[16,512]{1,0:T(8,128)}) custom-call(s32[2]{0:T(128)} %length_ref.9, s32[3]{0:T(128)} %pad_add_fusion.where_ref, bf16[1024,768]{1,0:T(8,128)(2,1)} %bitcast.120, ...), custom_call_target="tpu_custom_call" | custom-call | flops 51749998592 | bytes 41943040 | tf_op jit(solution)/shard_map/self_backward/pallas_call | solution.py:576
  299.9 7.2 %collective-permute-start.28 = (bf16[192,768]{1,0:T(8,128)(2,1)S(1)}, bf16[192,768]{1,0:T(8,128)(2,1)S(1)}, u32[]{:S(2)}, u32[]{:S(2)}) collective-permute-start(bf16[192,768]{1,0:T(8,128)(2,1)S(1)} %get-tuple-element.289), channel_id=1, source_target_pairs={{0,2},{1,3},{2,4},{3,5},{4,6},{5,7},{6,0},{7,1},{8,10},{9,11},{10,... | collective-permute-start | bytes 884744 | tf_op jit(solution)/shard_map/ppermute | solution.py:911
  314.8 3.3 collective-permute-done.28.refs_1_
  319.8 14.3 %collective-permute-done.29.refs_2_ = bf16[192,768]{1,0:T(8,128)(2,1)S(1)} collective-permute-done((bf16[192,768]{1,0:T(8,128)(2,1)S(1)}, bf16[192,768]{1,0:T(8,128)(2,1)S(1)}, u32[]{:S(2)}, u32[]{:S(2)}) %collective-permute-start.29) | collective-permute-done | bytes 294944 | tf_op jit(solution)/shard_map/ppermute | solution.py:911
  343.3 10.0 %input_gradient.1 = (f32[1024,768]{1,0:T(8,128)}, f32[1,768]{1,0:T(1,128)}) custom-call(bf16[1024,768]{1,0:T(8,128)(2,1)} %get-tuple-element.222.gq_ref, bf16[1024,768]{1,0:T(8,128)(2,1)} %get-tuple-element.223.gk_ref, bf16[1024,768]{1,0:T(8,128)(2,1)} %get-tuple-element.224.gv_ref, ...), custom_call_target="tpu_custom_call" | custom-call | flops 9200000000 | bytes 12582912 | tf_op jit(solution)/shard_map/input_gradient/pallas_call | solution.py:628
  354.1 6.5 %reduce-scatter.8.cloned.1.call-done = bf16[3,96,768]{2,1,0:T(8,128)(2,1)} async-done(((bf16[3,768,768]{2,1,0:T(8,128)(2,1)}), bf16[3,96,768]{2,1,0:T(8,128)(2,1)}) %reduce-scatter.8.cloned.1.call-update) | async-done | bytes 442384 | tf_op jit(solution)/shard_map/reduce_scatter | solution.py:1134
  368.1 4.0 collective-permute-done.40.refs_2_
  378.3 3.5 collective-permute-start.43
  388.1 3.1 collective-permute-done.44
  401.2 8.8 %update_all.1 = (f32[2,96,2048]{2,1,0:T(8,128)}, f32[256,768]{1,0:T(8,128)}, f32[4,96,768]{2,1,0:T(8,128)}, f32[4,96,768]{2,1,0:T(8,128)}, f32[2,96,2048]{2,1,0:...) custom-call(s32[3]{0:T(128)} %pad_add_fusion.where_ref, ...), custom_call_target="tpu_custom_call" | custom-call | flops 9200000000 | bytes 16777216 | tf_op jit(solution)/shard_map/update_all/pallas_call | solution.py:892
  (284 shorter events, 106.7 us)
Async XLA Ops:
  7.2 62.9 %all-gather.4.cloned.1.call-start = ((), (), s32[]{:S(2)}) async-start(), calls=%async_computation.3 | async-start | bytes 5308416 | tf_op jit(solution)/shard_map/all_gather | solution.py:1072
  10.6 136.2 %all-gather.6.cloned.1.call-start = ((), (), s32[]{:S(2)}) async-start(), calls=%async_computation.4 | async-start | bytes 7077888 | tf_op jit(solution)/shard_map/all_gather | solution.py:1074
  11.9 236.4 %reduce-scatter.4.cloned.1.call-start = ((), (), s32[]{:S(2)}) async-start(), calls=%async_computation.5 | async-start | bytes 3538944 | tf_op jit(solution)/shard_map/reduce_scatter | solution.py:1134
  37.8 27.9 %collective-permute-start.4 = (bf16[4,96,768]{2,1,0:T(8,128)(2,1)S(1)}, bf16[4,96,768]{2,1,0:T(8,128)(2,1)S(1)}, u32[]{:S(2)}, u32[]{:S(2)}) collective-permute-start(bf16[4,96,768]{2,1,0:T(8,128)(2,1)S(1)} %pad_maximum_fusion.refs_0_), channel_id=1, source_target_pairs={{0,16},{1,17},{2,18},{3,19},{4,20},{5,21},{6,22},{7,23},{8,24},{9,... | collective-permute-start | bytes 1769480 | tf_op jit(solution)/shard_map/ppermute | solution.py:911
  39.3 26.4 %collective-permute-start.5 = (bf16[4,96,768]{2,1,0:T(8,128)(2,1)S(1)}, bf16[4,96,768]{2,1,0:T(8,128)(2,1)}, u32[]{:S(2)}, u32[]{:S(2)}) collective-permute-start(bf16[4,96,768]{2,1,0:T(8,128)(2,1)S(1)} %pad_maximum_fusion.refs_0_), channel_id=1, source_target_pairs={{0,24},{1,25},{2,26},{3,27},{4,28},{5,29},{6,30},{7,31},{8,16},{9,... | collective-permute-start | bytes 1769480 | tf_op jit(solution)/shard_map/ppermute | solution.py:911
  42.4 59.7 %collective-permute-start.6 = (bf16[4,96,768]{2,1,0:T(8,128)(2,1)S(1)}, bf16[4,96,768]{2,1,0:T(8,128)(2,1)}, u32[]{:S(2)}, u32[]{:S(2)}) collective-permute-start(bf16[4,96,768]{2,1,0:T(8,128)(2,1)S(1)} %pad_maximum_fusion.refs_0_), channel_id=1, source_target_pairs={{0,1},{1,0},{2,3},{3,2},{4,5},{5,4},{6,7},{7,6},{8,9},{9,8},{10,11... | collective-permute-start | bytes 1769480 | tf_op jit(solution)/shard_map/ppermute | solution.py:911
  52.7 51.6 %collective-permute-start.7 = (bf16[4,96,768]{2,1,0:T(8,128)(2,1)S(1)}, bf16[4,96,768]{2,1,0:T(8,128)(2,1)}, u32[]{:S(2)}, u32[]{:S(2)}) collective-permute-start(bf16[4,96,768]{2,1,0:T(8,128)(2,1)S(1)} %collective-permute-done.3.refs_1_), channel_id=1, source_target_pairs={{0,1},{1,0},{2,3},{3,2},{4,5},{5,4},{6,7},{7,6},{8,9},{9,8},{10,11... | collective-permute-start | bytes 1769480 | tf_op jit(solution)/shard_map/ppermute | solution.py:911
  65.7 41.4 %collective-permute-start.8 = (bf16[4,96,768]{2,1,0:T(8,128)(2,1)S(1)}, bf16[4,96,768]{2,1,0:T(8,128)(2,1)}, u32[]{:S(2)}, u32[]{:S(2)}) collective-permute-start(bf16[4,96,768]{2,1,0:T(8,128)(2,1)S(1)} %collective-permute-done.4.refs_2_), channel_id=1, source_target_pairs={{0,1},{1,0},{2,3},{3,2},{4,5},{5,4},{6,7},{7,6},{8,9},{9,8},{10,11... | collective-permute-start | bytes 1769480 | tf_op jit(solution)/shard_map/ppermute | solution.py:911
  65.7 41.4 %collective-permute-start.9 = (bf16[4,96,768]{2,1,0:T(8,128)(2,1)}, bf16[4,96,768]{2,1,0:T(8,128)(2,1)}, u32[]{:S(2)}, u32[]{:S(2)}) collective-permute-start(bf16[4,96,768]{2,1,0:T(8,128)(2,1)} %collective-permute-done.5.refs_3_), channel_id=1, source_target_pairs={{0,1},{1,0},{2,3},{3,2},{4,5},{5,4},{6,7},{7,6},{8,9},{9,8},{10,11... | collective-permute-start | bytes 1769480 | tf_op jit(solution)/shard_map/ppermute | solution.py:911
  70.1 42.5 %collective-permute-start.10 = (bf16[64,768]{1,0:T(8,128)(2,1)S(1)}, bf16[64,768]{1,0:T(8,128)(2,1)S(1)}, u32[]{:S(2)}, u32[]{:S(2)}) collective-permute-start(bf16[64,768]{1,0:T(8,128)(2,1)S(1)} %fusion.20), channel_id=1, source_target_pairs={{0,2},{1,3},{2,4},{3,5},{4,6},{5,7},{6,0},{7,1},{8,10},{9,11},{10,... | collective-permute-start | bytes 294920 | tf_op jit(solution)/shard_map/ppermute | solution.py:911
  116.2 27.0 %collective-permute-start.13 = (bf16[4,64,768]{2,1,0:T(8,128)(2,1)S(1)}, bf16[4,64,768]{2,1,0:T(8,128)(2,1)S(1)}, u32[]{:S(2)}, u32[]{:S(2)}) collective-permute-start(bf16[4,64,768]{2,1,0:T(8,128)(2,1)S(1)} %pad_maximum_fusion.1.refs_0_), channel_id=1, source_target_pairs={{0,8},{1,9},{2,10},{3,11},{4,12},{5,13},{6,14},{7,15},{8,0},{9,1},... | collective-permute-start | bytes 1179656 | tf_op jit(solution)/shard_map/ppermute | solution.py:911
  193.5 45.3 %collective-permute-start.20 = (bf16[2,4,64,768]{3,2,1,0:T(8,128)(2,1)}, bf16[2,4,64,768]{3,2,1,0:T(8,128)(2,1)S(1)}, u32[]{:S(2)}, u32[]{:S(2)}) collective-permute-start(bf16[2,4,64,768]{3,2,1,0:T(8,128)(2,1)} %get-tuple-element.183), channel_id=1, source_target_pairs={{0,8},{1,9},{2,10},{3,11},{4,12},{5,13},{6,14},{7,15},{8,0},{9,1},... | collective-permute-start | bytes 2359304 | tf_op jit(solution)/shard_map/ppermute | solution.py:911
  194.8 44.1 %collective-permute-start.21 = (bf16[2,4,64,768]{3,2,1,0:T(8,128)(2,1)}, bf16[2,4,64,768]{3,2,1,0:T(8,128)(2,1)S(1)}, u32[]{:S(2)}, u32[]{:S(2)}) collective-permute-start(bf16[2,4,64,768]{3,2,1,0:T(8,128)(2,1)} %get-tuple-element.184), channel_id=1, source_target_pairs={{0,16},{1,17},{2,18},{3,19},{4,20},{5,21},{6,22},{7,23},{8,24},{9,... | collective-permute-start | bytes 2359304 | tf_op jit(solution)/shard_map/ppermute | solution.py:911
  195.6 43.3 %collective-permute-start.22 = (bf16[2,4,64,768]{3,2,1,0:T(8,128)(2,1)}, bf16[2,4,64,768]{3,2,1,0:T(8,128)(2,1)S(1)}, u32[]{:S(2)}, u32[]{:S(2)}) collective-permute-start(bf16[2,4,64,768]{3,2,1,0:T(8,128)(2,1)} %get-tuple-element.185), channel_id=1, source_target_pairs={{0,24},{1,25},{2,26},{3,27},{4,28},{5,29},{6,30},{7,31},{8,16},{9,... | collective-permute-start | bytes 2359304 | tf_op jit(solution)/shard_map/ppermute | solution.py:911
  197.1 91.4 %reduce-scatter.6.cloned.1.call-start = ((), (), s32[]{:S(2)}) async-start(), calls=%async_computation.6 | async-start | bytes 3538944 | tf_op jit(solution)/shard_map/reduce_scatter | solution.py:1134
  240.3 120.3 %reduce-scatter.8.cloned.1.call-start = ((), (), s32[]{:S(2)}) async-start(), calls=%async_computation.7 | async-start | bytes 3981312 | tf_op jit(solution)/shard_map/reduce_scatter | solution.py:1134
  252.4 36.2 %collective-permute-start.24 = (bf16[4,128,768]{2,1,0:T(8,128)(2,1)}, bf16[4,128,768]{2,1,0:T(8,128)(2,1)S(1)}, u32[]{:S(2)}, u32[]{:S(2)}) collective-permute-start(bf16[4,128,768]{2,1,0:T(8,128)(2,1)} %get-tuple-element.206), channel_id=1, source_target_pairs={{0,8},{1,9},{2,10},{3,11},{4,12},{5,13},{6,14},{7,15},{8,0},{9,1},... | collective-permute-start | bytes 2359304 | tf_op jit(solution)/shard_map/ppermute | solution.py:911
  253.6 35.0 %collective-permute-start.25 = (bf16[4,128,768]{2,1,0:T(8,128)(2,1)}, bf16[4,128,768]{2,1,0:T(8,128)(2,1)S(1)}, u32[]{:S(2)}, u32[]{:S(2)}) collective-permute-start(bf16[4,128,768]{2,1,0:T(8,128)(2,1)} %get-tuple-element.207), channel_id=1, source_target_pairs={{0,16},{1,17},{2,18},{3,19},{4,20},{5,21},{6,22},{7,23},{8,24},{9,... | collective-permute-start | bytes 2359304 | tf_op jit(solution)/shard_map/ppermute | solution.py:911
  254.4 35.9 %collective-permute-start.26 = (bf16[4,128,768]{2,1,0:T(8,128)(2,1)}, bf16[4,128,768]{2,1,0:T(8,128)(2,1)S(1)}, u32[]{:S(2)}, u32[]{:S(2)}) collective-permute-start(bf16[4,128,768]{2,1,0:T(8,128)(2,1)} %get-tuple-element.208), channel_id=1, source_target_pairs={{0,24},{1,25},{2,26},{3,27},{4,28},{5,29},{6,30},{7,31},{8,16},{9,... | collective-permute-start | bytes 2359304 | tf_op jit(solution)/shard_map/ppermute | solution.py:911
  307.1 27.0 %collective-permute-start.29 = (bf16[192,768]{1,0:T(8,128)(2,1)S(1)}, bf16[192,768]{1,0:T(8,128)(2,1)S(1)}, u32[]{:S(2)}, u32[]{:S(2)}) collective-permute-start(bf16[192,768]{1,0:T(8,128)(2,1)S(1)} %get-tuple-element.290), channel_id=1, source_target_pairs={{0,4},{1,5},{2,6},{3,7},{4,0},{5,1},{6,2},{7,3},{8,12},{9,13},{10,... | collective-permute-start | bytes 884744 | tf_op jit(solution)/shard_map/ppermute | solution.py:911
  307.1 29.4 %collective-permute-start.30 = (bf16[192,768]{1,0:T(8,128)(2,1)S(1)}, bf16[192,768]{1,0:T(8,128)(2,1)S(1)}, u32[]{:S(2)}, u32[]{:S(2)}) collective-permute-start(bf16[192,768]{1,0:T(8,128)(2,1)S(1)} %get-tuple-element.287), channel_id=1, source_target_pairs={{0,6},{1,7},{2,0},{3,1},{4,2},{5,3},{6,4},{7,5},{8,14},{9,15},{10,... | collective-permute-start | bytes 884744 | tf_op jit(solution)/shard_map/ppermute | solution.py:911
  312.3 41.8 %collective-permute-start.34 = (bf16[2,24,2048]{2,1,0:T(8,128)(2,1)}, bf16[2,24,2048]{2,1,0:T(8,128)(2,1)S(1)}, u32[]{:S(2)}, u32[]{:S(2)}) collective-permute-start(bf16[2,24,2048]{2,1,0:T(8,128)(2,1)} %get-tuple-element.248.refs_0_), channel_id=1, source_target_pairs={{0,8},{1,9},{2,10},{3,11},{4,12},{5,13},{6,14},{7,15},{8,0},{9,1},... | collective-permute-start | bytes 589832 | tf_op jit(solution)/shard_map/ppermute | solution.py:911
  313.2 40.9 %collective-permute-start.35 = (bf16[2,24,2048]{2,1,0:T(8,128)(2,1)}, bf16[2,24,2048]{2,1,0:T(8,128)(2,1)S(1)}, u32[]{:S(2)}, u32[]{:S(2)}) collective-permute-start(bf16[2,24,2048]{2,1,0:T(8,128)(2,1)} %get-tuple-element.248.refs_0_), channel_id=1, source_target_pairs={{0,16},{1,17},{2,18},{3,19},{4,20},{5,21},{6,22},{7,23},{8,24},{9,... | collective-permute-start | bytes 589832 | tf_op jit(solution)/shard_map/ppermute | solution.py:911
  318.2 35.9 %collective-permute-start.36 = (bf16[2,24,2048]{2,1,0:T(8,128)(2,1)}, bf16[2,24,2048]{2,1,0:T(8,128)(2,1)S(1)}, u32[]{:S(2)}, u32[]{:S(2)}) collective-permute-start(bf16[2,24,2048]{2,1,0:T(8,128)(2,1)} %get-tuple-element.248.refs_0_), channel_id=1, source_target_pairs={{0,24},{1,25},{2,26},{3,27},{4,28},{5,29},{6,30},{7,31},{8,16},{9,... | collective-permute-start | bytes 589832 | tf_op jit(solution)/shard_map/ppermute | solution.py:911
  (95 other events, 990.9 us)
Sparse Core Ops, SparseCore 0:
  10.6 59.4 all-gather.3
  72.3 70.3 all-gather.5
  197.2 44.2 reduce-scatter.3
  243.7 41.3 reduce-scatter.5
  291.3 69.2 reduce-scatter.7

commit v12 on v11

--- a/solution.py
+++ b/solution.py
@@ -155,18 +155,36 @@
             ).astype(LOW)
 
 
-def forward_kernel(
-    causal, seq_count, length_ref, x_ref, source_ref, gain_ref, wq_ref, wk_ref, wv_ref, wo_ref, wave_ref,
-    q_ref, k_ref, v_ref, mix_ref, total_ref, after_ref, normed, bias,
-):
+def forward_kernel(causal, seq_count, pieces, length_ref, where_ref, x_ref, source_ref, gain_ref, *refs):
     group = pl.program_id(0)
+    if pieces:
+        w_refs, wave_ref, refs = refs[:8], refs[8], refs[9:]
+        q_ref, k_ref, v_ref, mix_ref, total_ref, after_ref, whole_ref = refs[:7]
+        normed, bias, held, sems, whole_sem = refs[7:]
+        each = held.shape[1] // (LINE * LINE_CORES)
+        place = lambda quarter, at: held.at[quarter, pl.ds(at * each, each)]
+        copies = piece_copies(w_refs, where_ref, place, sems)
+        keep = pltpu.make_async_copy(held, whole_ref, whole_sem)
+        across = pl.ds(pl.multiple_of(group * GROUP, GROUP), GROUP)
+        wq_ref, wk_ref, wv_ref = [held.at[at, :, across] for at in range(3)]
+        wo_ref = held.at[3, across, :]
+    else:
+        wq_ref, wk_ref, wv_ref, wo_ref, wave_ref = refs[:5]
+        q_ref, k_ref, v_ref, mix_ref, total_ref, after_ref, normed, bias = refs[5:]
 
     @pl.when(group == 0)
     def _():
+        if pieces:
+            for copy in copies:
+                copy.start()
         for at, size in chunks(x_ref.shape[0], 256):
             rows = x_ref[at : at + size, :].astype(WIDE)
             normed[at : at + size, :] = (rows * rms_rate(rows) * gain_ref[...]).astype(LOW)
             after_ref[at : at + size, :] = rows
+        if pieces:
+            for copy in copies:
+                copy.wait()
+            keep.start()
 
     source = normed if causal else source_ref
     q_ref[...] = nn(normed[...], wq_ref[...]).astype(LOW)
@@ -175,6 +193,11 @@
     forward_body(causal, seq_count, length_ref, wave_ref, bias, q_ref, k_ref, v_ref, mix_ref, total_ref, group)
     after_ref[...] += nn(mix_ref[...], wo_ref[...])
 
+    @pl.when(group == pl.num_programs(0) - 1)
+    def _():
+        if pieces:
+            keep.wait()
+
 
 def weight_specs(width):
     across = lambda at: pl.BlockSpec((None, width, GROUP), lambda g, at=at: (at, 0, g))
@@ -189,23 +212,26 @@
     return pl.BlockSpec((rows, GROUP), lambda g: (0, g))
 
 
-def attention_forward(causal, x, source, lengths, gain, weights, wave):
+def attention_forward(causal, x, source, lengths, where, gain, weights, wave):
     row_count, width = x.shape
     seq_count = lengths.shape[0]
     source_rows = row_count if causal else source.shape[0]
     length = row_count // seq_count
     groups = width // GROUP
     low = lambda rows: jax.ShapeDtypeStruct((rows, width), LOW)
-    args = [lengths, x, source, gain, weights, weights, weights, weights, wave]
+    pieces = isinstance(weights, list)
+    everything = jax.ShapeDtypeStruct((4, width, width), LOW)
+    anywhere = pl.BlockSpec(memory_space=pl.ANY)
     return pl.pallas_call(
-        functools.partial(forward_kernel, causal, seq_count),
+        functools.partial(forward_kernel, causal, seq_count, pieces),
         grid=(groups,),
         in_specs=[
+            pl.BlockSpec(memory_space=pltpu.SMEM),
             pl.BlockSpec(memory_space=pltpu.SMEM),
             whole(x.shape),
             whole(source.shape),
             whole(gain.shape),
-            *weight_specs(width),
+            *([anywhere] * 8 if pieces else weight_specs(width)),
             whole(wave.shape),
         ],
         out_specs=[
@@ -215,6 +241,7 @@
             columns(row_count),
             pl.BlockSpec((None, row_count, PAIR), lambda g: (g, 0, 0)),
             whole((row_count, width)),
+            *([anywhere] if pieces else []),
         ],
         out_shape=[
             low(row_count),
@@ -223,15 +250,25 @@
             low(row_count),
             jax.ShapeDtypeStruct((groups, row_count, PAIR), WIDE),
             jax.ShapeDtypeStruct((row_count, width), WIDE),
+            *([everything] if pieces else []),
         ],
         scratch_shapes=[
             pltpu.VMEM((row_count, width), LOW),
             pltpu.VMEM((2, length, length) if causal else (1, 8, PAIR), WIDE),
+            *(
+                [
+                    pltpu.VMEM(everything.shape, LOW),
+                    pltpu.SemaphoreType.DMA((8 * LINE,)),
+                    pltpu.SemaphoreType.DMA(()),
+                ]
+                if pieces
+                else []
+            ),
         ],
         cost_estimate=pl.CostEstimate(flops=int(27 * PEAK), bytes_accessed=20 << 20, transcendentals=0),
         compiler_params=pltpu.CompilerParams(vmem_limit_bytes=60 * MEGABYTE),
         name="self_forward" if causal else "cross_forward",
-    )(*args)
+    )(lengths, where, x, source, gain, *(weights if pieces else [weights] * 4), wave)
 
 
 def gelu_parts(gate):
@@ -940,28 +977,6 @@
     return [parts[0]] + [from_line(parts[hop], hop) for hop in range(1, LINE)]
 
 
-def assemble_kernel(place, where_ref, *refs):
-    copies = piece_copies(refs[:8], where_ref, functools.partial(place, refs[8]), refs[9])
-    for copy in copies:
-        copy.start()
-    for copy in copies:
-        copy.wait()
-
-
-def assemble(parts, where, shape, place, name):
-    hops = parts[0].shape[0]
-    return pl.pallas_call(
-        functools.partial(assemble_kernel, place),
-        in_specs=[pl.BlockSpec(memory_space=pltpu.SMEM)] + [pl.BlockSpec(memory_space=pl.ANY)] * 8,
-        out_specs=pl.BlockSpec(memory_space=pltpu.VMEM),
-        out_shape=jax.ShapeDtypeStruct(shape, LOW),
-        scratch_shapes=[pltpu.SemaphoreType.DMA((8 * hops,))],
-        cost_estimate=pl.CostEstimate(flops=int(4 * PEAK), bytes_accessed=8 << 20, transcendentals=0),
-        compiler_params=pltpu.CompilerParams(vmem_limit_bytes=60 * MEGABYTE),
-        name=name,
-    )(where, *parts)
-
-
 def rep_parts(parts, axis):
     rep = lax.axis_index("rep")
     pick = lambda at: lax.dynamic_index_in_dim(parts, at, axis, keepdims=False)
@@ -1107,24 +1122,20 @@
     mem_rows = memory.reshape(seq_count * mem_length, model_width)
     grad_rows = out_grad.reshape(row_count, model_width)
     *kept_one, after_self = attention_forward(
-        True, dec_rows, no_source, dec_len, gain_full[0:1], w_self, backwards
+        True, dec_rows, no_source, dec_len, where, gain_full[0:1], w_self, backwards
     )
     if quarters:
-        w_cross = assemble(
-            hold(*cross_pieces, after_self)[:-1],
-            where,
-            (4, model_width, model_width),
-            lambda ref, quarter, at: ref.at[quarter, pl.ds(at * each, each)],
-            "assemble_cross",
-        )
+        w_cross = list(hold(*cross_pieces, after_self)[:-1])
         out_line = along_line(after(out_quarter, w_self))
         out_near = across_reps(after(out_line, after_self))
     else:
         w_cross = lax.all_gather(cross_weight.astype(LOW), "fsdp", axis=1, tiled=True)
         w_out = [lax.all_gather(ffn_out.astype(LOW), "fsdp", axis=0, tiled=True)]
     *kept_two, after_cross = attention_forward(
-        False, after_self, mem_rows, enc_len, gain_full[1:2], w_cross, no_bias
+        False, after_self, mem_rows, enc_len, where, gain_full[1:2], w_cross, no_bias
     )
+    if quarters:
+        *kept_two, after_cross, w_cross = (*kept_two, after_cross)
     if quarters:
         out_near = hold(*out_near, after_cross)[:-1]
         w_out = with_partner(list(out_near))

time: 426 us -> 417 us (0.979)
  starting transfers between devices: 75.6 us -> 60.8 us
  blocking collectives: 11.1 us -> 21.7 us
  waiting for transfers between devices: 76.7 us -> 82.9 us
    ppermute x51, starting transfers between devices: 75.3 us -> 60.6 us  [flat_permute(): return lax.ppermute(value, ('rep', 'fsdp'), pairs)]
    all_gather x1, blocking collectives: 11.1 us -> 21.7 us  [per_device(): lax.all_gather(gains.astype(LOW), 'fsdp', axis=1, tiled=True).astype(WIDE)]
    ppermute x51, waiting for transfers between devices: 66.2 us -> 76.5 us  [flat_permute(): return lax.ppermute(value, ('rep', 'fsdp'), pairs)]
    pallas_call x3 -> x2, Pallas kernels: 50.8 us -> 46.7 us  [attention_forward(): pl.pallas_call(functools.partial(forward_kernel, causal, seq_count, piece...]
    unnamed x128 -> x130, local copies, waits for them, and re-layouts: 9.9 us -> 9.02 us
  transfers between devices with their start and end apart: 56 -> 56, of which waited for: 20 -> 21; matrix products, arithmetic and copies ran while one was open for 5% -> 5% of each run, Pallas kernels for 35% -> 34%
where the time goes in v12:
time: 417 us; the launch traced here: 413 us
  Pallas kernels  199 us (48%)
  waiting for transfers between devices  82.9 us (20%)
  starting transfers between devices  60.8 us (15%)
  blocking collectives  21.7 us (5%)
  other arithmetic  18.3 us (4%)
  local copies, waits for them, and re-layouts  15.9 us (4%)
  between operations  15.1 us (4%)
    ppermute x51, waiting for transfers between devices, flat_permute(): return lax.ppermute(value, ('rep', 'fsdp'), pairs)  76.5 us
    pallas_call x2, Pallas kernels, attention_backward(): pl.pallas_call(functools.partial(backward_kernel, causal, seq_count), gri...  74.6 us
    ppermute x51, starting transfers between devices, flat_permute(): return lax.ppermute(value, ('rep', 'fsdp'), pairs)  60.6 us
    pallas_call x2, Pallas kernels, attention_forward(): pl.pallas_call(functools.partial(forward_kernel, causal, seq_count, piece...  46.7 us
    pallas_call x1, Pallas kernels, feed_forward_both(): pl.pallas_call(functools.partial(feed_kernel, seq_count, pieces), grid=(h...  45.6 us
    all_gather x1, blocking collectives, per_device(): lax.all_gather(gains.astype(LOW), 'fsdp', axis=1, tiled=True).astype(WIDE)  21.7 us
    pallas_call x1, Pallas kernels, input_gradient(): pl.pallas_call(input_kernel, grid=(rows // block,), in_specs=[rowwise, ro...  9.91 us
    unnamed x130, local copies, waits for them, and re-layouts  9.02 us
  transfers between devices with their start and end apart: 56, of which 21 were waited for; matrix products, arithmetic and copies ran while one was open for 5% of the time, Pallas kernels for 34%

profile of v12, /device:TPU:0, one launch (start us, length us, event | category | flops | bytes accessed | tf_op | source)
XLA Modules:
  0.0 413.1 jit_solution(16724420840302835738)
XLA Ops:
  7.3 2.7 fusion.23
  11.4 3.1 collective-permute-start
  14.5 2.6 collective-permute-start.1
  22.0 10.0 %collective-permute-done.1 = bf16[96,768]{1,0:T(8,128)(2,1)S(1)} collective-permute-done((bf16[96,768]{1,0:T(8,128)(2,1)S(1)}, bf16[96,768]{1,0:T(8,128)(2,1)S(1)}, u32[]{:S(2)}, u32[]{:S(2)}) %collective-permute-start.1) | collective-permute-done | bytes 147488 | tf_op jit(solution)/shard_map/ppermute | solution.py:948
  33.6 21.7 %all-gather = bf16[8,96,3]{1,2,0:T(4,128)(2,1)S(1)} all-gather(bf16[1,96,3]{1,2,0:T(4,128)(2,1)S(1)} %get-tuple-element.307), channel_id=1, replica_groups=mesh['rep'=4,'fsdp'=8] {'fsdp'}, dimensions={0}, use_global_device_ids=true | all-gather | bytes 5184 | tf_op jit(solution)/shard_map/all_gather | solution.py:1088
  60.9 23.4 %collective-permute-done.4.refs_2_ = bf16[4,96,768]{2,1,0:T(8,128)(2,1)S(1)} collective-permute-done((bf16[4,96,768]{2,1,0:T(8,128)(2,1)S(1)}, bf16[4,96,768]{2,1,0:T(8,128)(2,1)S(1)}, u32[]{:S(2)}, u32[]{:S(2)}) %collective-permute-start.4) | collective-permute-done | bytes 589856 | tf_op jit(solution)/shard_map/ppermute | solution.py:948
  85.3 3.6 collective-permute-start.12
  89.5 22.1 %self_forward.1 = (bf16[1024,768]{1,0:T(8,128)(2,1)}, bf16[1024,768]{1,0:T(8,128)(2,1)}, bf16[1024,768]{1,0:T(8,128)(2,1)}, bf16[1024,768]{1,0:T(8,128)(2,1)}, f...) custom-call(s32[2]{0:T(128)} %length_ref.9, s32[3]{0:T(128)} %pad_add_fusion.where_ref, bf16[1024,768]{1,0:T(8,128)(2,1)} %bitcast.119, ...), custom_call_target="tpu_custom_call" | custom-call | flops 31050000384 | bytes 20971520 | tf_op jit(solution)/shard_map/self_forward/pallas_call | solution.py:225
  115.9 24.6 %cross_forward.1 = (bf16[1024,768]{1,0:T(8,128)(2,1)}, bf16[1024,768]{1,0:T(8,128)(2,1)}, bf16[1024,768]{1,0:T(8,128)(2,1)}, bf16[1024,768]{1,0:T(8,128)(2,1)}, ...) custom-call(s32[2]{0:T(128)} %length_ref.8, s32[3]{0:T(128)} %pad_add_fusion.where_ref, ...), custom_call_target="tpu_custom_call" | custom-call | flops 31050000384 | bytes 20971520 | tf_op jit(solution)/shard_map/cross_forward/pallas_call | solution.py:225
  144.8 45.6 %feed_forward_both.1 = (bf16[1024,768]{1,0:T(8,128)(2,1)}, f32[1024,768]{1,0:T(8,128)}, bf16[768,2048]{1,0:T(8,128)(2,1)}, bf16[768,2048]{1,0:T(8,128)(2,1)}, bf...) custom-call(s32[2]{0:T(128)} %length_ref.9, ...), custom_call_target="tpu_custom_call" | custom-call | flops 52899999744 | bytes 41943040 | tf_op jit(solution)/shard_map/feed_forward_both/pallas_call | solution.py:380
  194.1 42.0 %cross_backward.1 = (f32[1024,768]{1,0:T(8,128)}, bf16[1024,768]{1,0:T(8,128)(2,1)}, bf16[1024,768]{1,0:T(8,128)(2,1)}, f32[1,768]{1,0:T(1,128)}, bf16[4,128,768...) custom-call(s32[2]{0:T(128)} %length_ref.8, ...), custom_call_target="tpu_custom_call" | custom-call | flops 51749998592 | bytes 41943040 | tf_op jit(solution)/shard_map/cross_backward/pallas_call | solution.py:613
  238.8 6.7 %memory_gradient.1 = f32[1024,768]{1,0:T(8,128)} custom-call(bf16[1024,768]{1,0:T(8,128)(2,1)} %get-tuple-element.188.gk_ref, bf16[1024,768]{1,0:T(8,128)(2,1)} %get-tuple-element.189.gv_ref, bf16[4,768,768]{2,1,0:T(8,128)(2,1)} %get-tuple-element.173.wq_ref.wo_ref.wk_ref.wv_ref, bf16[4,768,768]{2,1,0:T(8,128)(2,1)} %get-tuple-element.173.wq_ref.wo_ref.wk_ref.wv_ref), custom_call_target="tpu_custom_call" | custom-call | flops 8049999872 | bytes 10485760 | tf_op jit(solution)/shard_map/memory_gradient/pallas_call | solution.py:686
  245.5 4.0 fusion
  253.1 32.6 %self_backward.1 = (bf16[1024,768]{1,0:T(8,128)(2,1)}, bf16[1024,768]{1,0:T(8,128)(2,1)}, bf16[1024,768]{1,0:T(8,128)(2,1)}, bf16[3,768,768]{2,1,0:T(8,128)(2,1)}, f32[16,512]{1,0:T(8,128)}) custom-call(s32[2]{0:T(128)} %length_ref.9, s32[3]{0:T(128)} %pad_add_fusion.where_ref, bf16[1024,768]{1,0:T(8,128)(2,1)} %bitcast.120, ...), custom_call_target="tpu_custom_call" | custom-call | flops 51749998592 | bytes 41943040 | tf_op jit(solution)/shard_map/self_backward/pallas_call | solution.py:613
  309.3 5.9 %collective-permute-done.28.refs_1_ = bf16[192,768]{1,0:T(8,128)(2,1)S(1)} collective-permute-done((bf16[192,768]{1,0:T(8,128)(2,1)S(1)}, bf16[192,768]{1,0:T(8,128)(2,1)S(1)}, u32[]{:S(2)}, u32[]{:S(2)}) %collective-permute-start.28) | collective-permute-done | bytes 294944 | tf_op jit(solution)/shard_map/ppermute | solution.py:948
  317.1 13.7 %collective-permute-done.29.refs_2_ = bf16[192,768]{1,0:T(8,128)(2,1)S(1)} collective-permute-done((bf16[192,768]{1,0:T(8,128)(2,1)S(1)}, bf16[192,768]{1,0:T(8,128)(2,1)S(1)}, u32[]{:S(2)}, u32[]{:S(2)}) %collective-permute-start.29) | collective-permute-done | bytes 294944 | tf_op jit(solution)/shard_map/ppermute | solution.py:948
  336.6 9.9 %input_gradient.1 = (f32[1024,768]{1,0:T(8,128)}, f32[1,768]{1,0:T(1,128)}) custom-call(bf16[1024,768]{1,0:T(8,128)(2,1)} %get-tuple-element.224.gq_ref, bf16[1024,768]{1,0:T(8,128)(2,1)} %get-tuple-element.225.gk_ref, bf16[1024,768]{1,0:T(8,128)(2,1)} %get-tuple-element.226.gv_ref, ...), custom_call_target="tpu_custom_call" | custom-call | flops 9200000000 | bytes 12582912 | tf_op jit(solution)/shard_map/input_gradient/pallas_call | solution.py:665
  347.3 5.9 %reduce-scatter.8.cloned.1.call-done = bf16[3,96,768]{2,1,0:T(8,128)(2,1)} async-done(((bf16[3,768,768]{2,1,0:T(8,128)(2,1)}), bf16[3,96,768]{2,1,0:T(8,128)(2,1)}) %reduce-scatter.8.cloned.1.call-update) | async-done | bytes 442384 | tf_op jit(solution)/shard_map/reduce_scatter | solution.py:1145
  359.8 2.4 collective-permute-done.40.refs_2_
  369.5 7.2 %collective-permute-start.43 = (f32[120,128]{1,0:T(8,128)S(1)}, f32[120,128]{1,0:T(8,128)S(1)}, u32[]{:S(2)}, u32[]{:S(2)}) collective-permute-start(f32[120,128]{1,0:T(8,128)S(1)} %add.103), channel_id=1, source_target_pairs={{0,2},{1,3},{2,0},{3,1},{4,6},{5,7},{6,4},{7,5},{8,10},{9,11},{10,... | collective-permute-start | bytes 184328 | tf_op jit(solution)/shard_map/ppermute | solution.py:948
  380.3 5.8 %collective-permute-done.44 = f32[120,128]{1,0:T(8,128)S(1)} collective-permute-done((f32[120,128]{1,0:T(8,128)S(1)}, f32[120,128]{1,0:T(8,128)S(1)}, u32[]{:S(2)}, u32[]{:S(2)}) %collective-permute-start.44) | collective-permute-done | bytes 61472 | tf_op jit(solution)/shard_map/ppermute | solution.py:948
  387.5 2.9 collective-permute-done.48
  392.2 2.5 collective-permute-done.49
  396.1 8.8 %update_all.1 = (f32[2,96,2048]{2,1,0:T(8,128)}, f32[256,768]{1,0:T(8,128)}, f32[4,96,768]{2,1,0:T(8,128)}, f32[4,96,768]{2,1,0:T(8,128)}, f32[2,96,2048]{2,1,0:...) custom-call(s32[3]{0:T(128)} %pad_add_fusion.where_ref, ...), custom_call_target="tpu_custom_call" | custom-call | flops 9200000000 | bytes 16777216 | tf_op jit(solution)/shard_map/update_all/pallas_call | solution.py:929
  (285 shorter events, 88.4 us)
Async XLA Ops:
  7.2 77.6 %all-gather.4.cloned.1.call-start = ((), (), s32[]{:S(2)}) async-start(), calls=%async_computation.3 | async-start | bytes 5308416 | tf_op jit(solution)/shard_map/all_gather | solution.py:1087
  10.0 134.3 %all-gather.6.cloned.1.call-start = ((), (), s32[]{:S(2)}) async-start(), calls=%async_computation.4 | async-start | bytes 7077888 | tf_op jit(solution)/shard_map/all_gather | solution.py:1089
  11.3 234.2 %reduce-scatter.4.cloned.1.call-start = ((), (), s32[]{:S(2)}) async-start(), calls=%async_computation.5 | async-start | bytes 3538944 | tf_op jit(solution)/shard_map/reduce_scatter | solution.py:1145
  56.1 28.2 %collective-permute-start.4 = (bf16[4,96,768]{2,1,0:T(8,128)(2,1)S(1)}, bf16[4,96,768]{2,1,0:T(8,128)(2,1)S(1)}, u32[]{:S(2)}, u32[]{:S(2)}) collective-permute-start(bf16[4,96,768]{2,1,0:T(8,128)(2,1)S(1)} %pad_maximum_fusion.refs_0_), channel_id=1, source_target_pairs={{0,16},{1,17},{2,18},{3,19},{4,20},{5,21},{6,22},{7,23},{8,24},{9,... | collective-permute-start | bytes 1769480 | tf_op jit(solution)/shard_map/ppermute | solution.py:948
  58.0 27.3 %collective-permute-start.7 = (bf16[4,96,768]{2,1,0:T(8,128)(2,1)S(1)}, bf16[4,96,768]{2,1,0:T(8,128)(2,1)}, u32[]{:S(2)}, u32[]{:S(2)}) collective-permute-start(bf16[4,96,768]{2,1,0:T(8,128)(2,1)S(1)} %collective-permute-done.3.refs_1_), channel_id=1, source_target_pairs={{0,1},{1,0},{2,3},{3,2},{4,5},{5,4},{6,7},{7,6},{8,9},{9,8},{10,11... | collective-permute-start | bytes 1769480 | tf_op jit(solution)/shard_map/ppermute | solution.py:948
  84.3 27.3 %collective-permute-start.8 = (bf16[4,96,768]{2,1,0:T(8,128)(2,1)S(1)}, bf16[4,96,768]{2,1,0:T(8,128)(2,1)}, u32[]{:S(2)}, u32[]{:S(2)}) collective-permute-start(bf16[4,96,768]{2,1,0:T(8,128)(2,1)S(1)} %collective-permute-done.4.refs_2_), channel_id=1, source_target_pairs={{0,1},{1,0},{2,3},{3,2},{4,5},{5,4},{6,7},{7,6},{8,9},{9,8},{10,11... | collective-permute-start | bytes 1769480 | tf_op jit(solution)/shard_map/ppermute | solution.py:948
  84.3 27.3 %collective-permute-start.9 = (bf16[4,96,768]{2,1,0:T(8,128)(2,1)}, bf16[4,96,768]{2,1,0:T(8,128)(2,1)}, u32[]{:S(2)}, u32[]{:S(2)}) collective-permute-start(bf16[4,96,768]{2,1,0:T(8,128)(2,1)} %collective-permute-done.5.refs_3_), channel_id=1, source_target_pairs={{0,1},{1,0},{2,3},{3,2},{4,5},{5,4},{6,7},{7,6},{8,9},{9,8},{10,11... | collective-permute-start | bytes 1769480 | tf_op jit(solution)/shard_map/ppermute | solution.py:948
  84.8 26.8 %collective-permute-start.11 = (bf16[64,768]{1,0:T(8,128)(2,1)S(1)}, bf16[64,768]{1,0:T(8,128)(2,1)S(1)}, u32[]{:S(2)}, u32[]{:S(2)}) collective-permute-start(bf16[64,768]{1,0:T(8,128)(2,1)S(1)} %fusion.20), channel_id=1, source_target_pairs={{0,4},{1,5},{2,6},{3,7},{4,0},{5,1},{6,2},{7,3},{8,12},{9,13},{10,... | collective-permute-start | bytes 294920 | tf_op jit(solution)/shard_map/ppermute | solution.py:948
  111.7 28.8 %collective-permute-start.13 = (bf16[4,64,768]{2,1,0:T(8,128)(2,1)S(1)}, bf16[4,64,768]{2,1,0:T(8,128)(2,1)S(1)}, u32[]{:S(2)}, u32[]{:S(2)}) collective-permute-start(bf16[4,64,768]{2,1,0:T(8,128)(2,1)S(1)} %pad_maximum_fusion.1.refs_0_), channel_id=1, source_target_pairs={{0,8},{1,9},{2,10},{3,11},{4,12},{5,13},{6,14},{7,15},{8,0},{9,1},... | collective-permute-start | bytes 1179656 | tf_op jit(solution)/shard_map/ppermute | solution.py:948
  112.5 28.0 %collective-permute-start.14 = (bf16[4,64,768]{2,1,0:T(8,128)(2,1)S(1)}, bf16[4,64,768]{2,1,0:T(8,128)(2,1)S(1)}, u32[]{:S(2)}, u32[]{:S(2)}) collective-permute-start(bf16[4,64,768]{2,1,0:T(8,128)(2,1)S(1)} %pad_maximum_fusion.1.refs_0_), channel_id=1, source_target_pairs={{0,16},{1,17},{2,18},{3,19},{4,20},{5,21},{6,22},{7,23},{8,24},{9,... | collective-permute-start | bytes 1179656 | tf_op jit(solution)/shard_map/ppermute | solution.py:948
  190.5 45.6 %collective-permute-start.20 = (bf16[2,4,64,768]{3,2,1,0:T(8,128)(2,1)}, bf16[2,4,64,768]{3,2,1,0:T(8,128)(2,1)S(1)}, u32[]{:S(2)}, u32[]{:S(2)}) collective-permute-start(bf16[2,4,64,768]{3,2,1,0:T(8,128)(2,1)} %get-tuple-element.185), channel_id=1, source_target_pairs={{0,8},{1,9},{2,10},{3,11},{4,12},{5,13},{6,14},{7,15},{8,0},{9,1},... | collective-permute-start | bytes 2359304 | tf_op jit(solution)/shard_map/ppermute | solution.py:948
  191.6 44.5 %collective-permute-start.21 = (bf16[2,4,64,768]{3,2,1,0:T(8,128)(2,1)}, bf16[2,4,64,768]{3,2,1,0:T(8,128)(2,1)S(1)}, u32[]{:S(2)}, u32[]{:S(2)}) collective-permute-start(bf16[2,4,64,768]{3,2,1,0:T(8,128)(2,1)} %get-tuple-element.186), channel_id=1, source_target_pairs={{0,16},{1,17},{2,18},{3,19},{4,20},{5,21},{6,22},{7,23},{8,24},{9,... | collective-permute-start | bytes 2359304 | tf_op jit(solution)/shard_map/ppermute | solution.py:948
  193.1 43.0 %collective-permute-start.22 = (bf16[2,4,64,768]{3,2,1,0:T(8,128)(2,1)}, bf16[2,4,64,768]{3,2,1,0:T(8,128)(2,1)S(1)}, u32[]{:S(2)}, u32[]{:S(2)}) collective-permute-start(bf16[2,4,64,768]{3,2,1,0:T(8,128)(2,1)} %get-tuple-element.187), channel_id=1, source_target_pairs={{0,24},{1,25},{2,26},{3,27},{4,28},{5,29},{6,30},{7,31},{8,16},{9,... | collective-permute-start | bytes 2359304 | tf_op jit(solution)/shard_map/ppermute | solution.py:948
  194.0 91.7 %reduce-scatter.6.cloned.1.call-start = ((), (), s32[]{:S(2)}) async-start(), calls=%async_computation.6 | async-start | bytes 3538944 | tf_op jit(solution)/shard_map/reduce_scatter | solution.py:1145
  237.5 115.7 %reduce-scatter.8.cloned.1.call-start = ((), (), s32[]{:S(2)}) async-start(), calls=%async_computation.7 | async-start | bytes 3981312 | tf_op jit(solution)/shard_map/reduce_scatter | solution.py:1145
  249.6 36.2 %collective-permute-start.24 = (bf16[4,128,768]{2,1,0:T(8,128)(2,1)}, bf16[4,128,768]{2,1,0:T(8,128)(2,1)S(1)}, u32[]{:S(2)}, u32[]{:S(2)}) collective-permute-start(bf16[4,128,768]{2,1,0:T(8,128)(2,1)} %get-tuple-element.208), channel_id=1, source_target_pairs={{0,8},{1,9},{2,10},{3,11},{4,12},{5,13},{6,14},{7,15},{8,0},{9,1},... | collective-permute-start | bytes 2359304 | tf_op jit(solution)/shard_map/ppermute | solution.py:948
  250.6 35.9 %collective-permute-start.25 = (bf16[4,128,768]{2,1,0:T(8,128)(2,1)}, bf16[4,128,768]{2,1,0:T(8,128)(2,1)S(1)}, u32[]{:S(2)}, u32[]{:S(2)}) collective-permute-start(bf16[4,128,768]{2,1,0:T(8,128)(2,1)} %get-tuple-element.209), channel_id=1, source_target_pairs={{0,16},{1,17},{2,18},{3,19},{4,20},{5,21},{6,22},{7,23},{8,24},{9,... | collective-permute-start | bytes 2359304 | tf_op jit(solution)/shard_map/ppermute | solution.py:948
  252.1 35.5 %collective-permute-start.26 = (bf16[4,128,768]{2,1,0:T(8,128)(2,1)}, bf16[4,128,768]{2,1,0:T(8,128)(2,1)S(1)}, u32[]{:S(2)}, u32[]{:S(2)}) collective-permute-start(bf16[4,128,768]{2,1,0:T(8,128)(2,1)} %get-tuple-element.210), channel_id=1, source_target_pairs={{0,24},{1,25},{2,26},{3,27},{4,28},{5,29},{6,30},{7,31},{8,16},{9,... | collective-permute-start | bytes 2359304 | tf_op jit(solution)/shard_map/ppermute | solution.py:948
  297.4 33.4 %collective-permute-start.29 = (bf16[192,768]{1,0:T(8,128)(2,1)S(1)}, bf16[192,768]{1,0:T(8,128)(2,1)S(1)}, u32[]{:S(2)}, u32[]{:S(2)}) collective-permute-start(bf16[192,768]{1,0:T(8,128)(2,1)S(1)} %get-tuple-element.292), channel_id=1, source_target_pairs={{0,4},{1,5},{2,6},{3,7},{4,0},{5,1},{6,2},{7,3},{8,12},{9,13},{10,... | collective-permute-start | bytes 884744 | tf_op jit(solution)/shard_map/ppermute | solution.py:948
  299.9 30.9 %collective-permute-start.30 = (bf16[192,768]{1,0:T(8,128)(2,1)S(1)}, bf16[192,768]{1,0:T(8,128)(2,1)S(1)}, u32[]{:S(2)}, u32[]{:S(2)}) collective-permute-start(bf16[192,768]{1,0:T(8,128)(2,1)S(1)} %get-tuple-element.289), channel_id=1, source_target_pairs={{0,6},{1,7},{2,0},{3,1},{4,2},{5,3},{6,4},{7,5},{8,14},{9,15},{10,... | collective-permute-start | bytes 884744 | tf_op jit(solution)/shard_map/ppermute | solution.py:948
  306.9 40.3 %collective-permute-start.34 = (bf16[2,24,2048]{2,1,0:T(8,128)(2,1)}, bf16[2,24,2048]{2,1,0:T(8,128)(2,1)S(1)}, u32[]{:S(2)}, u32[]{:S(2)}) collective-permute-start(bf16[2,24,2048]{2,1,0:T(8,128)(2,1)} %get-tuple-element.250.refs_0_), channel_id=1, source_target_pairs={{0,8},{1,9},{2,10},{3,11},{4,12},{5,13},{6,14},{7,15},{8,0},{9,1},... | collective-permute-start | bytes 589832 | tf_op jit(solution)/shard_map/ppermute | solution.py:948
  307.9 39.3 %collective-permute-start.35 = (bf16[2,24,2048]{2,1,0:T(8,128)(2,1)}, bf16[2,24,2048]{2,1,0:T(8,128)(2,1)S(1)}, u32[]{:S(2)}, u32[]{:S(2)}) collective-permute-start(bf16[2,24,2048]{2,1,0:T(8,128)(2,1)} %get-tuple-element.250.refs_0_), channel_id=1, source_target_pairs={{0,16},{1,17},{2,18},{3,19},{4,20},{5,21},{6,22},{7,23},{8,24},{9,... | collective-permute-start | bytes 589832 | tf_op jit(solution)/shard_map/ppermute | solution.py:948
  315.1 32.1 %collective-permute-start.36 = (bf16[2,24,2048]{2,1,0:T(8,128)(2,1)}, bf16[2,24,2048]{2,1,0:T(8,128)(2,1)S(1)}, u32[]{:S(2)}, u32[]{:S(2)}) collective-permute-start(bf16[2,24,2048]{2,1,0:T(8,128)(2,1)} %get-tuple-element.250.refs_0_), channel_id=1, source_target_pairs={{0,24},{1,25},{2,26},{3,27},{4,28},{5,29},{6,30},{7,31},{8,16},{9,... | collective-permute-start | bytes 589832 | tf_op jit(solution)/shard_map/ppermute | solution.py:948
  367.3 28.0 %collective-permute-start.50 = (bf16[192,768]{1,0:T(8,128)(2,1)S(1)}, bf16[192,768]{1,0:T(8,128)(2,1)S(1)}, u32[]{:S(2)}, u32[]{:S(2)}) collective-permute-start(bf16[192,768]{1,0:T(8,128)(2,1)S(1)} %copy-done.45), channel_id=1, source_target_pairs={{0,24},{1,25},{2,26},{3,27},{4,28},{5,29},{6,30},{7,31},{8,16},{9,... | collective-permute-start | bytes 884744 | tf_op jit(solution)/shard_map/ppermute | solution.py:948
  (96 other events, 1077.0 us)
Sparse Core Ops, SparseCore 0:
  10.2 59.2 all-gather.3
  71.7 72.6 all-gather.5
  194.2 39.0 reduce-scatter.3
  237.6 39.1 reduce-scatter.5
  288.6 64.5 reduce-scatter.7

commit v13 on v12

--- a/solution.py
+++ b/solution.py
@@ -854,7 +854,10 @@
         state_sum = scalars[:, scalar : scalar + 1]
         square = scalars[:, 16 + scalar : 17 + scalar]
         col_moment = DECAY_RATE * cols_ref[row_at : row_at + 1, :] + (1.0 - DECAY_RATE) * col_sum / whole_rows
-        new_cols[row_at : row_at + 1, :] = col_moment
+        if index is None:
+            spill(new_cols, 0, col_moment)
+        else:
+            new_cols[row_at : row_at + 1, :] = col_moment
         row_mean = (
             DECAY_RATE * state_sum
             + (1.0 - DECAY_RATE) / cols * jnp.sum(col_sum, axis=1, keepdims=True)
@@ -925,6 +928,8 @@
 ):
     outs = (*weights, *weights, *rows, *cols, *plain[:2], *plain[:2], *plain[2:])
     out_shape = [jax.ShapeDtypeStruct(value.shape, WIDE) for value in outs]
+    flat_cols = 2 * len(weights) + len(rows) + 1
+    out_shape[flat_cols] = jax.ShapeDtypeStruct((cols[1].size // LANES, LANES), WIDE)
     spec = pl.BlockSpec(memory_space=pltpu.VMEM)
     return pl.pallas_call(
         functools.partial(update_kernel, factor, starts, shards),
@@ -1117,6 +1122,10 @@
     backwards = jnp.roll(by_distance[:, ::-1], 1, axis=1)
     no_bias = jnp.zeros((8, PAIR), WIDE)
     no_source = jnp.zeros((16, PAIR), LOW)
+    if quarters:
+        gain_full, by_distance, backwards, no_bias, no_source = hold(
+            gain_full, by_distance, backwards, no_bias, no_source
+        )
 
     dec_rows = dec_in.reshape(row_count, model_width)
     mem_rows = memory.reshape(seq_count * mem_length, model_width)

time: 417 us -> 416 us (level)
    ppermute x51, waiting for transfers between devices: 76.5 us -> 81 us  [flat_permute(): return lax.ppermute(value, ('rep', 'fsdp'), pairs)]
    unnamed x130 -> x128, local copies, waits for them, and re-layouts: 9.02 us -> 8.71 us
  transfers between devices with their start and end apart: 56 -> 56, of which waited for: 21 -> 20; matrix products, arithmetic and copies ran while one was open for 5% -> 5% of each run, Pallas kernels for 34% -> 34%
where the time goes in v13:
time: 416 us; the launch traced here: 413 us
  Pallas kernels  199 us (48%)
  waiting for transfers between devices  86.6 us (21%)
  starting transfers between devices  58.2 us (14%)
  blocking collectives  21.6 us (5%)
  other arithmetic  17 us (4%)
  local copies, waits for them, and re-layouts  15.6 us (4%)
  between operations  15.2 us (4%)
    ppermute x51, waiting for transfers between devices, flat_permute(): return lax.ppermute(value, ('rep', 'fsdp'), pairs)  81 us
    pallas_call x2, Pallas kernels, attention_backward(): pl.pallas_call(functools.partial(backward_kernel, causal, seq_count), gri...  74.6 us
    ppermute x51, starting transfers between devices, flat_permute(): return lax.ppermute(value, ('rep', 'fsdp'), pairs)  58 us
    pallas_call x2, Pallas kernels, attention_forward(): pl.pallas_call(functools.partial(forward_kernel, causal, seq_count, piece...  46.6 us
    pallas_call x1, Pallas kernels, feed_forward_both(): pl.pallas_call(functools.partial(feed_kernel, seq_count, pieces), grid=(h...  45.6 us
    all_gather x1, blocking collectives, per_device(): lax.all_gather(gains.astype(LOW), 'fsdp', axis=1, tiled=True).astype(WIDE)  21.6 us
    pallas_call x1, Pallas kernels, input_gradient(): pl.pallas_call(input_kernel, grid=(rows // block,), in_specs=[rowwise, ro...  9.94 us
    pallas_call x1, Pallas kernels, update_all(): pl.pallas_call(functools.partial(update_kernel, factor, starts, shards),...  8.83 us
  transfers between devices with their start and end apart: 56, of which 20 were waited for; matrix products, arithmetic and copies ran while one was open for 5% of the time, Pallas kernels for 34%

profile of v13, /device:TPU:0, one launch (start us, length us, event | category | flops | bytes accessed | tf_op | source)
XLA Modules:
  0.0 412.8 jit_solution(9168091757178001424)
XLA Ops:
  7.3 2.7 fusion.23
  11.4 3.1 collective-permute-start
  14.5 2.6 collective-permute-start.1
  21.3 10.7 %collective-permute-done.1 = bf16[96,768]{1,0:T(8,128)(2,1)S(1)} collective-permute-done((bf16[96,768]{1,0:T(8,128)(2,1)S(1)}, bf16[96,768]{1,0:T(8,128)(2,1)S(1)}, u32[]{:S(2)}, u32[]{:S(2)}) %collective-permute-start.1) | collective-permute-done | bytes 147488 | tf_op jit(solution)/shard_map/ppermute | solution.py:953
  36.1 21.6 %all-gather = bf16[8,96,3]{1,2,0:T(4,128)(2,1)S(1)} all-gather(bf16[1,96,3]{1,2,0:T(4,128)(2,1)S(1)} %get-tuple-element.317), channel_id=1, replica_groups=mesh['rep'=4,'fsdp'=8] {'fsdp'}, dimensions={0}, use_global_device_ids=true | all-gather | bytes 5184 | tf_op jit(solution)/shard_map/all_gather | solution.py:1093
  63.9 22.1 %collective-permute-done.4.refs_2_ = bf16[4,96,768]{2,1,0:T(8,128)(2,1)S(1)} collective-permute-done((bf16[4,96,768]{2,1,0:T(8,128)(2,1)S(1)}, bf16[4,96,768]{2,1,0:T(8,128)(2,1)S(1)}, u32[]{:S(2)}, u32[]{:S(2)}) %collective-permute-start.4) | collective-permute-done | bytes 589856 | tf_op jit(solution)/shard_map/ppermute | solution.py:953
  87.6 3.1 collective-permute-start.12
  91.2 22.0 %self_forward.1 = (bf16[1024,768]{1,0:T(8,128)(2,1)}, bf16[1024,768]{1,0:T(8,128)(2,1)}, bf16[1024,768]{1,0:T(8,128)(2,1)}, bf16[1024,768]{1,0:T(8,128)(2,1)}, f...) custom-call(s32[2]{0:T(128)} %length_ref.9, s32[3]{0:T(128)} %pad_add_fusion.where_ref, bf16[1024,768]{1,0:T(8,128)(2,1)} %bitcast.120, ...), custom_call_target="tpu_custom_call" | custom-call | flops 31050000384 | bytes 20971520 | tf_op jit(solution)/shard_map/self_forward/pallas_call | solution.py:225
  117.5 24.6 %cross_forward.1 = (bf16[1024,768]{1,0:T(8,128)(2,1)}, bf16[1024,768]{1,0:T(8,128)(2,1)}, bf16[1024,768]{1,0:T(8,128)(2,1)}, bf16[1024,768]{1,0:T(8,128)(2,1)}, ...) custom-call(s32[2]{0:T(128)} %length_ref.8, s32[3]{0:T(128)} %pad_add_fusion.where_ref, ...), custom_call_target="tpu_custom_call" | custom-call | flops 31050000384 | bytes 20971520 | tf_op jit(solution)/shard_map/cross_forward/pallas_call | solution.py:225
  146.6 45.6 %feed_forward_both.1 = (bf16[1024,768]{1,0:T(8,128)(2,1)}, f32[1024,768]{1,0:T(8,128)}, bf16[768,2048]{1,0:T(8,128)(2,1)}, bf16[768,2048]{1,0:T(8,128)(2,1)}, bf...) custom-call(s32[2]{0:T(128)} %length_ref.9, ...), custom_call_target="tpu_custom_call" | custom-call | flops 52899999744 | bytes 41943040 | tf_op jit(solution)/shard_map/feed_forward_both/pallas_call | solution.py:380
  195.9 42.0 %cross_backward.1 = (f32[1024,768]{1,0:T(8,128)}, bf16[1024,768]{1,0:T(8,128)(2,1)}, bf16[1024,768]{1,0:T(8,128)(2,1)}, f32[1,768]{1,0:T(1,128)}, bf16[4,128,768...) custom-call(s32[2]{0:T(128)} %length_ref.8, ...), custom_call_target="tpu_custom_call" | custom-call | flops 51749998592 | bytes 41943040 | tf_op jit(solution)/shard_map/cross_backward/pallas_call | solution.py:613
  239.4 6.8 %memory_gradient.1 = f32[1024,768]{1,0:T(8,128)} custom-call(bf16[1024,768]{1,0:T(8,128)(2,1)} %get-tuple-element.197.gk_ref, bf16[1024,768]{1,0:T(8,128)(2,1)} %get-tuple-element.198.gv_ref, bf16[4,768,768]{2,1,0:T(8,128)(2,1)} %get-tuple-element.182.wq_ref.wo_ref.wk_ref.wv_ref, bf16[4,768,768]{2,1,0:T(8,128)(2,1)} %get-tuple-element.182.wq_ref.wo_ref.wk_ref.wv_ref), custom_call_target="tpu_custom_call" | custom-call | flops 8049999872 | bytes 10485760 | tf_op jit(solution)/shard_map/memory_gradient/pallas_call | solution.py:686
  246.2 4.0 fusion
  253.7 32.7 %self_backward.1 = (bf16[1024,768]{1,0:T(8,128)(2,1)}, bf16[1024,768]{1,0:T(8,128)(2,1)}, bf16[1024,768]{1,0:T(8,128)(2,1)}, bf16[3,768,768]{2,1,0:T(8,128)(2,1)}, f32[16,512]{1,0:T(8,128)}) custom-call(s32[2]{0:T(128)} %length_ref.9, s32[3]{0:T(128)} %pad_add_fusion.where_ref, bf16[1024,768]{1,0:T(8,128)(2,1)} %bitcast.121, ...), custom_call_target="tpu_custom_call" | custom-call | flops 51749998592 | bytes 41943040 | tf_op jit(solution)/shard_map/self_backward/pallas_call | solution.py:613
  309.1 6.6 %collective-permute-done.28.refs_1_ = bf16[192,768]{1,0:T(8,128)(2,1)S(1)} collective-permute-done((bf16[192,768]{1,0:T(8,128)(2,1)S(1)}, bf16[192,768]{1,0:T(8,128)(2,1)S(1)}, u32[]{:S(2)}, u32[]{:S(2)}) %collective-permute-start.28) | collective-permute-done | bytes 294944 | tf_op jit(solution)/shard_map/ppermute | solution.py:953
  317.7 13.6 %collective-permute-done.29.refs_2_ = bf16[192,768]{1,0:T(8,128)(2,1)S(1)} collective-permute-done((bf16[192,768]{1,0:T(8,128)(2,1)S(1)}, bf16[192,768]{1,0:T(8,128)(2,1)S(1)}, u32[]{:S(2)}, u32[]{:S(2)}) %collective-permute-start.29) | collective-permute-done | bytes 294944 | tf_op jit(solution)/shard_map/ppermute | solution.py:953
  337.1 9.9 %input_gradient.1 = (f32[1024,768]{1,0:T(8,128)}, f32[1,768]{1,0:T(1,128)}) custom-call(bf16[1024,768]{1,0:T(8,128)(2,1)} %get-tuple-element.234.gq_ref, bf16[1024,768]{1,0:T(8,128)(2,1)} %get-tuple-element.235.gk_ref, bf16[1024,768]{1,0:T(8,128)(2,1)} %get-tuple-element.236.gv_ref, ...), custom_call_target="tpu_custom_call" | custom-call | flops 9200000000 | bytes 12582912 | tf_op jit(solution)/shard_map/input_gradient/pallas_call | solution.py:665
  347.8 5.5 %reduce-scatter.8.cloned.1.call-done = bf16[3,96,768]{2,1,0:T(8,128)(2,1)} async-done(((bf16[3,768,768]{2,1,0:T(8,128)(2,1)}), bf16[3,96,768]{2,1,0:T(8,128)(2,1)}) %reduce-scatter.8.cloned.1.call-update) | async-done | bytes 442384 | tf_op jit(solution)/shard_map/reduce_scatter | solution.py:1154
  359.9 3.8 collective-permute-done.40.refs_2_
  369.9 7.7 %collective-permute-start.43 = (f32[120,128]{1,0:T(8,128)S(1)}, f32[120,128]{1,0:T(8,128)S(1)}, u32[]{:S(2)}, u32[]{:S(2)}) collective-permute-start(f32[120,128]{1,0:T(8,128)S(1)} %add.103), channel_id=1, source_target_pairs={{0,2},{1,3},{2,0},{3,1},{4,6},{5,7},{6,4},{7,5},{8,10},{9,11},{10,... | collective-permute-start | bytes 184328 | tf_op jit(solution)/shard_map/ppermute | solution.py:953
  381.2 5.8 %collective-permute-done.44 = f32[120,128]{1,0:T(8,128)S(1)} collective-permute-done((f32[120,128]{1,0:T(8,128)S(1)}, f32[120,128]{1,0:T(8,128)S(1)}, u32[]{:S(2)}, u32[]{:S(2)}) %collective-permute-start.44) | collective-permute-done | bytes 61472 | tf_op jit(solution)/shard_map/ppermute | solution.py:953
  387.6 3.7 collective-permute-done.48
  392.6 3.1 collective-permute-done.49
  397.0 8.8 %update_all.1 = (f32[2,96,2048]{2,1,0:T(8,128)}, f32[256,768]{1,0:T(8,128)}, f32[4,96,768]{2,1,0:T(8,128)}, f32[4,96,768]{2,1,0:T(8,128)}, f32[2,96,2048]{2,1,0:...) custom-call(s32[3]{0:T(128)} %pad_add_fusion.where_ref, ...), custom_call_target="tpu_custom_call" | custom-call | flops 9200000000 | bytes 16777216 | tf_op jit(solution)/shard_map/update_all/pallas_call | solution.py:934
  (282 shorter events, 85.5 us)
Async XLA Ops:
  7.2 79.3 %all-gather.4.cloned.1.call-start = ((), (), s32[]{:S(2)}) async-start(), calls=%async_computation.3 | async-start | bytes 5308416 | tf_op jit(solution)/shard_map/all_gather | solution.py:1092
  10.0 135.8 %all-gather.6.cloned.1.call-start = ((), (), s32[]{:S(2)}) async-start(), calls=%async_computation.4 | async-start | bytes 7077888 | tf_op jit(solution)/shard_map/all_gather | solution.py:1094
  11.3 234.9 %reduce-scatter.4.cloned.1.call-start = ((), (), s32[]{:S(2)}) async-start(), calls=%async_computation.5 | async-start | bytes 3538944 | tf_op jit(solution)/shard_map/reduce_scatter | solution.py:1154
  32.1 27.8 %collective-permute-start.3 = (bf16[4,96,768]{2,1,0:T(8,128)(2,1)S(1)}, bf16[4,96,768]{2,1,0:T(8,128)(2,1)S(1)}, u32[]{:S(2)}, u32[]{:S(2)}) collective-permute-start(bf16[4,96,768]{2,1,0:T(8,128)(2,1)S(1)} %pad_maximum_fusion.refs_0_), channel_id=1, source_target_pairs={{0,8},{1,9},{2,10},{3,11},{4,12},{5,13},{6,14},{7,15},{8,0},{9,1},... | collective-permute-start | bytes 1769480 | tf_op jit(solution)/shard_map/ppermute | solution.py:953
  57.7 28.3 %collective-permute-start.4 = (bf16[4,96,768]{2,1,0:T(8,128)(2,1)S(1)}, bf16[4,96,768]{2,1,0:T(8,128)(2,1)S(1)}, u32[]{:S(2)}, u32[]{:S(2)}) collective-permute-start(bf16[4,96,768]{2,1,0:T(8,128)(2,1)S(1)} %pad_maximum_fusion.refs_0_), channel_id=1, source_target_pairs={{0,16},{1,17},{2,18},{3,19},{4,20},{5,21},{6,22},{7,23},{8,24},{9,... | collective-permute-start | bytes 1769480 | tf_op jit(solution)/shard_map/ppermute | solution.py:953
  59.9 27.7 %collective-permute-start.7 = (bf16[4,96,768]{2,1,0:T(8,128)(2,1)S(1)}, bf16[4,96,768]{2,1,0:T(8,128)(2,1)}, u32[]{:S(2)}, u32[]{:S(2)}) collective-permute-start(bf16[4,96,768]{2,1,0:T(8,128)(2,1)S(1)} %collective-permute-done.3.refs_1_), channel_id=1, source_target_pairs={{0,1},{1,0},{2,3},{3,2},{4,5},{5,4},{6,7},{7,6},{8,9},{9,8},{10,11... | collective-permute-start | bytes 1769480 | tf_op jit(solution)/shard_map/ppermute | solution.py:953
  86.0 27.3 %collective-permute-start.8 = (bf16[4,96,768]{2,1,0:T(8,128)(2,1)S(1)}, bf16[4,96,768]{2,1,0:T(8,128)(2,1)}, u32[]{:S(2)}, u32[]{:S(2)}) collective-permute-start(bf16[4,96,768]{2,1,0:T(8,128)(2,1)S(1)} %collective-permute-done.4.refs_2_), channel_id=1, source_target_pairs={{0,1},{1,0},{2,3},{3,2},{4,5},{5,4},{6,7},{7,6},{8,9},{9,8},{10,11... | collective-permute-start | bytes 1769480 | tf_op jit(solution)/shard_map/ppermute | solution.py:953
  86.0 27.3 %collective-permute-start.9 = (bf16[4,96,768]{2,1,0:T(8,128)(2,1)S(1)}, bf16[4,96,768]{2,1,0:T(8,128)(2,1)}, u32[]{:S(2)}, u32[]{:S(2)}) collective-permute-start(bf16[4,96,768]{2,1,0:T(8,128)(2,1)S(1)} %collective-permute-done.5.refs_3_), channel_id=1, source_target_pairs={{0,1},{1,0},{2,3},{3,2},{4,5},{5,4},{6,7},{7,6},{8,9},{9,8},{10,11... | collective-permute-start | bytes 1769480 | tf_op jit(solution)/shard_map/ppermute | solution.py:953
  113.4 28.8 %collective-permute-start.13 = (bf16[4,64,768]{2,1,0:T(8,128)(2,1)S(1)}, bf16[4,64,768]{2,1,0:T(8,128)(2,1)S(1)}, u32[]{:S(2)}, u32[]{:S(2)}) collective-permute-start(bf16[4,64,768]{2,1,0:T(8,128)(2,1)S(1)} %pad_maximum_fusion.1.refs_0_), channel_id=1, source_target_pairs={{0,8},{1,9},{2,10},{3,11},{4,12},{5,13},{6,14},{7,15},{8,0},{9,1},... | collective-permute-start | bytes 1179656 | tf_op jit(solution)/shard_map/ppermute | solution.py:953
  114.1 28.1 %collective-permute-start.14 = (bf16[4,64,768]{2,1,0:T(8,128)(2,1)S(1)}, bf16[4,64,768]{2,1,0:T(8,128)(2,1)S(1)}, u32[]{:S(2)}, u32[]{:S(2)}) collective-permute-start(bf16[4,64,768]{2,1,0:T(8,128)(2,1)S(1)} %pad_maximum_fusion.1.refs_0_), channel_id=1, source_target_pairs={{0,16},{1,17},{2,18},{3,19},{4,20},{5,21},{6,22},{7,23},{8,24},{9,... | collective-permute-start | bytes 1179656 | tf_op jit(solution)/shard_map/ppermute | solution.py:953
  192.3 45.6 %collective-permute-start.20 = (bf16[2,4,64,768]{3,2,1,0:T(8,128)(2,1)}, bf16[2,4,64,768]{3,2,1,0:T(8,128)(2,1)S(1)}, u32[]{:S(2)}, u32[]{:S(2)}) collective-permute-start(bf16[2,4,64,768]{3,2,1,0:T(8,128)(2,1)} %get-tuple-element.194), channel_id=1, source_target_pairs={{0,8},{1,9},{2,10},{3,11},{4,12},{5,13},{6,14},{7,15},{8,0},{9,1},... | collective-permute-start | bytes 2359304 | tf_op jit(solution)/shard_map/ppermute | solution.py:953
  192.9 45.0 %collective-permute-start.21 = (bf16[2,4,64,768]{3,2,1,0:T(8,128)(2,1)}, bf16[2,4,64,768]{3,2,1,0:T(8,128)(2,1)S(1)}, u32[]{:S(2)}, u32[]{:S(2)}) collective-permute-start(bf16[2,4,64,768]{3,2,1,0:T(8,128)(2,1)} %get-tuple-element.195), channel_id=1, source_target_pairs={{0,16},{1,17},{2,18},{3,19},{4,20},{5,21},{6,22},{7,23},{8,24},{9,... | collective-permute-start | bytes 2359304 | tf_op jit(solution)/shard_map/ppermute | solution.py:953
  194.5 43.5 %collective-permute-start.22 = (bf16[2,4,64,768]{3,2,1,0:T(8,128)(2,1)}, bf16[2,4,64,768]{3,2,1,0:T(8,128)(2,1)S(1)}, u32[]{:S(2)}, u32[]{:S(2)}) collective-permute-start(bf16[2,4,64,768]{3,2,1,0:T(8,128)(2,1)} %get-tuple-element.196), channel_id=1, source_target_pairs={{0,24},{1,25},{2,26},{3,27},{4,28},{5,29},{6,30},{7,31},{8,16},{9,... | collective-permute-start | bytes 2359304 | tf_op jit(solution)/shard_map/ppermute | solution.py:953
  195.9 90.5 %reduce-scatter.6.cloned.1.call-start = ((), (), s32[]{:S(2)}) async-start(), calls=%async_computation.6 | async-start | bytes 3538944 | tf_op jit(solution)/shard_map/reduce_scatter | solution.py:1154
  239.3 114.0 %reduce-scatter.8.cloned.1.call-start = ((), (), s32[]{:S(2)}) async-start(), calls=%async_computation.7 | async-start | bytes 3981312 | tf_op jit(solution)/shard_map/reduce_scatter | solution.py:1154
  250.2 36.2 %collective-permute-start.24 = (bf16[4,128,768]{2,1,0:T(8,128)(2,1)}, bf16[4,128,768]{2,1,0:T(8,128)(2,1)S(1)}, u32[]{:S(2)}, u32[]{:S(2)}) collective-permute-start(bf16[4,128,768]{2,1,0:T(8,128)(2,1)} %get-tuple-element.218), channel_id=1, source_target_pairs={{0,8},{1,9},{2,10},{3,11},{4,12},{5,13},{6,14},{7,15},{8,0},{9,1},... | collective-permute-start | bytes 2359304 | tf_op jit(solution)/shard_map/ppermute | solution.py:953
  250.5 36.0 %collective-permute-start.25 = (bf16[4,128,768]{2,1,0:T(8,128)(2,1)}, bf16[4,128,768]{2,1,0:T(8,128)(2,1)S(1)}, u32[]{:S(2)}, u32[]{:S(2)}) collective-permute-start(bf16[4,128,768]{2,1,0:T(8,128)(2,1)} %get-tuple-element.219), channel_id=1, source_target_pairs={{0,16},{1,17},{2,18},{3,19},{4,20},{5,21},{6,22},{7,23},{8,24},{9,... | collective-permute-start | bytes 2359304 | tf_op jit(solution)/shard_map/ppermute | solution.py:953
  252.0 36.2 %collective-permute-start.26 = (bf16[4,128,768]{2,1,0:T(8,128)(2,1)}, bf16[4,128,768]{2,1,0:T(8,128)(2,1)S(1)}, u32[]{:S(2)}, u32[]{:S(2)}) collective-permute-start(bf16[4,128,768]{2,1,0:T(8,128)(2,1)} %get-tuple-element.220), channel_id=1, source_target_pairs={{0,24},{1,25},{2,26},{3,27},{4,28},{5,29},{6,30},{7,31},{8,16},{9,... | collective-permute-start | bytes 2359304 | tf_op jit(solution)/shard_map/ppermute | solution.py:953
  297.8 33.6 %collective-permute-start.29 = (bf16[192,768]{1,0:T(8,128)(2,1)S(1)}, bf16[192,768]{1,0:T(8,128)(2,1)S(1)}, u32[]{:S(2)}, u32[]{:S(2)}) collective-permute-start(bf16[192,768]{1,0:T(8,128)(2,1)S(1)} %get-tuple-element.302), channel_id=1, source_target_pairs={{0,4},{1,5},{2,6},{3,7},{4,0},{5,1},{6,2},{7,3},{8,12},{9,13},{10,... | collective-permute-start | bytes 884744 | tf_op jit(solution)/shard_map/ppermute | solution.py:953
  300.6 30.8 %collective-permute-start.30 = (bf16[192,768]{1,0:T(8,128)(2,1)S(1)}, bf16[192,768]{1,0:T(8,128)(2,1)S(1)}, u32[]{:S(2)}, u32[]{:S(2)}) collective-permute-start(bf16[192,768]{1,0:T(8,128)(2,1)S(1)} %get-tuple-element.299), channel_id=1, source_target_pairs={{0,6},{1,7},{2,0},{3,1},{4,2},{5,3},{6,4},{7,5},{8,14},{9,15},{10,... | collective-permute-start | bytes 884744 | tf_op jit(solution)/shard_map/ppermute | solution.py:953
  307.4 40.3 %collective-permute-start.34 = (bf16[2,24,2048]{2,1,0:T(8,128)(2,1)}, bf16[2,24,2048]{2,1,0:T(8,128)(2,1)S(1)}, u32[]{:S(2)}, u32[]{:S(2)}) collective-permute-start(bf16[2,24,2048]{2,1,0:T(8,128)(2,1)} %get-tuple-element.260.refs_0_), channel_id=1, source_target_pairs={{0,8},{1,9},{2,10},{3,11},{4,12},{5,13},{6,14},{7,15},{8,0},{9,1},... | collective-permute-start | bytes 589832 | tf_op jit(solution)/shard_map/ppermute | solution.py:953
  308.5 39.2 %collective-permute-start.35 = (bf16[2,24,2048]{2,1,0:T(8,128)(2,1)}, bf16[2,24,2048]{2,1,0:T(8,128)(2,1)S(1)}, u32[]{:S(2)}, u32[]{:S(2)}) collective-permute-start(bf16[2,24,2048]{2,1,0:T(8,128)(2,1)} %get-tuple-element.260.refs_0_), channel_id=1, source_target_pairs={{0,16},{1,17},{2,18},{3,19},{4,20},{5,21},{6,22},{7,23},{8,24},{9,... | collective-permute-start | bytes 589832 | tf_op jit(solution)/shard_map/ppermute | solution.py:953
  315.7 32.0 %collective-permute-start.36 = (bf16[2,24,2048]{2,1,0:T(8,128)(2,1)}, bf16[2,24,2048]{2,1,0:T(8,128)(2,1)S(1)}, u32[]{:S(2)}, u32[]{:S(2)}) collective-permute-start(bf16[2,24,2048]{2,1,0:T(8,128)(2,1)} %get-tuple-element.260.refs_0_), channel_id=1, source_target_pairs={{0,24},{1,25},{2,26},{3,27},{4,28},{5,29},{6,30},{7,31},{8,16},{9,... | collective-permute-start | bytes 589832 | tf_op jit(solution)/shard_map/ppermute | solution.py:953
  367.8 28.5 %collective-permute-start.50 = (bf16[192,768]{1,0:T(8,128)(2,1)S(1)}, bf16[192,768]{1,0:T(8,128)(2,1)S(1)}, u32[]{:S(2)}, u32[]{:S(2)}) collective-permute-start(bf16[192,768]{1,0:T(8,128)(2,1)S(1)} %copy-done.44), channel_id=1, source_target_pairs={{0,24},{1,25},{2,26},{3,27},{4,28},{5,29},{6,30},{7,31},{8,16},{9,... | collective-permute-start | bytes 884744 | tf_op jit(solution)/shard_map/ppermute | solution.py:953
  (95 other events, 976.9 us)
Sparse Core Ops, SparseCore 0:
  10.2 59.3 all-gather.3
  71.8 72.9 all-gather.5
  196.0 38.8 reduce-scatter.3
  239.5 38.8 reduce-scatter.5
  289.2 64.0 reduce-scatter.7
